TPU v7x, 32 devices: a whole 2x2x4 slice. The times are simulated.
32 devices in a mesh: rows: 4 (over y, x), cols: 8 (over z, core).
Axes of the slice: x: 2, y: 2, z: 4, core: 2. Of those that a mesh axis runs over, the one named last changes fastest.
Arguments:
- layer_in: bfloat16 [1, 4096, 2560], P(None, 'cols', 'rows'), may hold values from -6 to 6
- norm1_gain: bfloat16 [2560], P('cols'), may hold values from 0.25 to 1.75
- w_query: bfloat16 [2560, 2560], P('cols', 'rows'), may hold values from -0.125 to 0.125
- key_matrix: bfloat16 [2560, 512], P('cols', 'rows'), may hold values from -0.125 to 0.125
- value_matrix: bfloat16 [2560, 512], P('cols', 'rows'), may hold values from -0.125 to 0.125
- w_out: bfloat16 [2560, 2560], P('rows', 'cols'), may hold values from -2 to 2
- norm2_gain: bfloat16 [2560], P('cols'), may hold values from 0.25 to 1.75
- w_router: bfloat16 [2560, 16], P('cols'), may hold values from -0.0625 to 0.0625
- shared_gate: bfloat16 [2560, 3072], P('cols', 'rows'), may hold values from -0.125 to 0.125
- shared_up: bfloat16 [2560, 3072], P('cols', 'rows'), may hold values from -0.125 to 0.125
- shared_down: bfloat16 [3072, 2560], P('rows', 'cols'), may hold values from -0.109375 to 0.109375
- expert_gate: bfloat16 [32, 2560, 768], P(('rows', 'cols')), may hold values from -0.125 to 0.125
- expert_up: bfloat16 [32, 2560, 768], P(('rows', 'cols')), may hold values from -0.125 to 0.125
- expert_down: bfloat16 [32, 768, 2560], P(('rows', 'cols')), may hold values from -0.3125 to 0.3125
- routes: int32 [8, 4, 128, 6], P('cols', 'rows'), may hold values from 0 to 15, all different within a row; in each aligned block of 128 rows (0 to 127, 128 to 255, ..., all dimensions but the last counted through in order) at most 60 rows name the same one
- cotangent: bfloat16 [1, 4096, 2560], P(None, 'cols', 'rows'), may hold values from -6 to 6
Outputs:
- layer_out: bfloat16 [1, 4096, 2560], P(None, 'cols', 'rows')
- grad_in: float32 [1, 4096, 2560], P(None, 'cols', 'rows')
- grad_norm1_gain: float32 [2560], P('cols')
- grad_w_query: float32 [2560, 2560], P('cols', 'rows')
- grad_w_key: float32 [2560, 512], P('cols', 'rows')
- grad_w_value: float32 [2560, 512], P('cols', 'rows')
- grad_w_out: float32 [2560, 2560], P('rows', 'cols')
- grad_norm2_gain: float32 [2560], P('cols')
- grad_w_router: float32 [2560, 16], P('cols')
- grad_shared_gate: float32 [2560, 3072], P('cols', 'rows')
- grad_shared_up: float32 [2560, 3072], P('cols', 'rows')
- grad_shared_down: float32 [3072, 2560], P('rows', 'cols')
- grad_expert_gate: float32 [32, 2560, 768], P(('rows', 'cols'))
- grad_expert_up: float32 [32, 2560, 768], P(('rows', 'cols'))
- grad_expert_down: float32 [32, 768, 2560], P(('rows', 'cols'))
Inputs may be any that keep to these rules, and one draw needn't show every extreme that they name: The 6 experts of a token differ. Among the 128 tokens of one device's block of routes no expert is named more than 60 times, and in every draw some expert is named exactly 60 times in some block.
All inputs are finite; a program needn't handle non-finite values.
Results may differ from a plain program's by a relative error of at most 0.03.
Values may be sent and summed in bfloat16 or wider, within the bound.
A program may use at most 320 MiB of HBM per device.

v0:
```python
import math

import jax
import jax.numpy as jnp
from jax import lax
from jax.sharding import PartitionSpec as P

HEAD_DIM = 128


NORM_EPS = 1e-05
ROPE_BASE = 500000.0
NEG_LARGE = -1e30
PRECISE = lax.Precision.HIGHEST


def rope_tables(positions, head_size):
    half_size = head_size // 2
    inv_freq = ROPE_BASE ** (-(2.0 * jnp.arange(half_size, dtype=jnp.float32)) / head_size)
    angles = positions.astype(jnp.float32)[:, None] * inv_freq[None, :]
    return (jnp.cos(angles), jnp.sin(angles))


def apply_rotary(values, cosine_table, sine_table):
    half_size = values.shape[-1] // 2
    first_half = values[..., :half_size]
    second = values[..., half_size:]
    cos_b = cosine_table[:, None, :]
    sin_b = sine_table[:, None, :]
    return jnp.concatenate(
        [first_half * cos_b - second * sin_b, second * cos_b + first_half * sin_b], -1
    )


def matmul(left_op, right_op):
    return jnp.dot(left_op, right_op, preferred_element_type=jnp.float32)


def matmul_tn(left_op, right_op):
    return lax.dot_general(
        left_op, right_op, (((0,), (0,)), ((), ())), preferred_element_type=jnp.float32
    )


def matmul_nt(left_op, right_op):
    return lax.dot_general(
        left_op, right_op, (((1,), (1,)), ((), ())), preferred_element_type=jnp.float32
    )


def silu_parts(pre_act):
    sigma = jax.nn.sigmoid(pre_act)
    return (pre_act * sigma, sigma * (1.0 + pre_act * (1.0 - sigma)))


def keep_same(carry_in):
    return carry_in


def per_device(
    layer_in,
    norm1_gain,
    w_query,
    key_matrix,
    value_matrix,
    w_out,
    norm2_gain,
    w_router,
    shared_gate,
    shared_up,
    shared_down,
    expert_gate,
    expert_up,
    expert_down,
    routes,
    cotangent,
):
    n_rows = lax.axis_size("rows")
    n_cols = lax.axis_size("cols")
    row_idx = lax.axis_index("rows")
    col_idx = lax.axis_index("cols")
    sequence_count, len_dev, row_width = layer_in.shape
    tok_dev = sequence_count * len_dev
    rows_dev = routes.shape[2]
    top_k = routes.shape[3]
    experts = w_router.shape[1]
    devices = n_rows * n_cols
    capacity = 2 * max(1, 5 * rows_dev * top_k // (8 * experts))
    full_in = lax.all_gather(layer_in, "rows", axis=2, tiled=True)
    (
        gain_one,
        wq_full,
        wk_full,
        wv_full,
        wo_full,
        gain_two,
        router_full,
        sg_full,
        su_full,
        sd_full,
    ) = (
        lax.all_gather(norm1_gain, "cols", axis=0, tiled=True),
        lax.all_gather(w_query, "cols", axis=0, tiled=True),
        lax.all_gather(key_matrix, "cols", axis=0, tiled=True),
        lax.all_gather(value_matrix, "cols", axis=0, tiled=True),
        lax.all_gather(w_out, "cols", axis=1, tiled=True),
        lax.all_gather(norm2_gain, "cols", axis=0, tiled=True),
        lax.all_gather(w_router, "cols", axis=0, tiled=True),
        lax.all_gather(shared_gate, "cols", axis=0, tiled=True),
        lax.all_gather(shared_up, "cols", axis=0, tiled=True),
        lax.all_gather(shared_down, "cols", axis=1, tiled=True),
    )
    model_width = full_in.shape[2]
    token_input = full_in.reshape(tok_dev, model_width).astype(jnp.float32)
    first_inverse_deviation = lax.rsqrt(
        jnp.mean(token_input * token_input, -1, keepdims=True) + NORM_EPS
    )
    first_unit_rows = token_input * first_inverse_deviation
    first_gain_float = gain_one.astype(jnp.float32)
    first_normed = (first_unit_rows * first_gain_float).astype(jnp.bfloat16)
    q_pre = matmul(first_normed, wq_full)
    key_unrotated = matmul(first_normed, wk_full)
    value_projected = matmul(first_normed, wv_full).astype(jnp.bfloat16)
    q_heads = q_pre.shape[1] // HEAD_DIM
    positions = col_idx * len_dev + jnp.arange(len_dev, dtype=jnp.int32)
    cosine_table, sine_table = rope_tables(positions, HEAD_DIM)
    rotated_queries = apply_rotary(
        q_pre.reshape(sequence_count, len_dev, q_heads, HEAD_DIM), cosine_table, sine_table
    ).astype(jnp.bfloat16)
    rotated_keys = apply_rotary(
        key_unrotated.reshape(sequence_count, len_dev, 1, HEAD_DIM), cosine_table, sine_table
    ).astype(jnp.bfloat16)
    kv_local = jnp.concatenate(
        [
            rotated_keys.reshape(sequence_count, len_dev, HEAD_DIM),
            value_projected.reshape(sequence_count, len_dev, HEAD_DIM),
        ],
        -1,
    )
    kv_local = jnp.swapaxes(kv_local, 0, 1)
    query_t = jnp.transpose(rotated_queries, (0, 2, 1, 3))
    score_scale = 1.0 / math.sqrt(HEAD_DIM)
    q_last = col_idx * len_dev + len_dev - 1

    def online_update(carry_in, key_part, k_start):
        run_max, run_sum, run_acc = carry_in
        block_len = key_part.shape[0]
        scores = (
            jnp.einsum(
                "shqd,bsd->shqb",
                query_t,
                key_part[:, :, :HEAD_DIM],
                preferred_element_type=jnp.float32,
            )
            * score_scale
        )
        key_pos = k_start + jnp.arange(block_len, dtype=jnp.int32)
        causal = positions[:, None] >= key_pos[None, :]
        scores = jnp.where(causal, scores, NEG_LARGE)
        new_max = jnp.maximum(run_max, jnp.max(scores, -1))
        prob_vals = jnp.where(causal, jnp.exp(scores - new_max[..., None]), 0.0)
        rescale = jnp.exp(run_max - new_max)
        run_sum = run_sum * rescale + jnp.sum(prob_vals, -1)
        run_acc = run_acc * rescale[..., None] + jnp.einsum(
            "shqb,bsd->shqd",
            prob_vals.astype(jnp.bfloat16),
            key_part[:, :, HEAD_DIM:],
            preferred_element_type=jnp.float32,
        )
        return (new_max, run_sum, run_acc)

    fold_start = (
        jnp.full((sequence_count, q_heads, len_dev), NEG_LARGE, jnp.float32),
        jnp.zeros((sequence_count, q_heads, len_dev), jnp.float32),
        jnp.zeros((sequence_count, q_heads, len_dev, HEAD_DIM), jnp.float32),
    )
    carry_in = fold_start
    piece = lax.all_gather(kv_local, "cols", axis=0, tiled=True)
    start = jnp.int32(0)
    piece_len = piece.shape[0]
    step_len = min(512, piece_len)
    for offset in range(0, piece_len, step_len):
        key_part = piece[offset : offset + step_len]
        k_start = start + offset

        def updated(state_in, key_part=key_part, k_start=k_start):
            return online_update(state_in, key_part, k_start)

        carry_in = lax.cond(k_start <= q_last, updated, keep_same, carry_in)
    run_max, run_sum, run_acc = carry_in
    attn_f32 = run_acc / run_sum[..., None]
    log_total = run_max + jnp.log(run_sum)
    attn_bf = attn_f32.astype(jnp.bfloat16)
    attn_rows = jnp.transpose(attn_bf, (0, 2, 1, 3)).reshape(tok_dev, q_heads * HEAD_DIM)
    attn_proj = lax.psum(matmul(attn_rows, wo_full).astype(jnp.bfloat16), "rows").astype(
        jnp.float32
    )
    residual_stream = token_input + attn_proj
    second_inverse_deviation = lax.rsqrt(
        jnp.mean(residual_stream * residual_stream, -1, keepdims=True) + NORM_EPS
    )
    second_unit_rows = residual_stream * second_inverse_deviation
    second_gain_float = gain_two.astype(jnp.float32)
    second_normed = (second_unit_rows * second_gain_float).astype(jnp.bfloat16)
    gate_pre = matmul(second_normed, sg_full)
    up_pre = matmul(second_normed, su_full)
    silu_gate, silu_slope = silu_parts(gate_pre)
    shared_act = (silu_gate * up_pre).astype(jnp.bfloat16)
    ffn_part = matmul(shared_act, sd_full)
    my_rows = row_idx * rows_dev
    normed_mine = lax.dynamic_slice_in_dim(second_normed, my_rows, rows_dev, 0)
    route_mine = routes.reshape(rows_dev, top_k)
    logits = matmul(normed_mine, router_full)
    expert_ids = jnp.arange(experts, dtype=jnp.int32)
    chosen_hot = (route_mine[:, :, None] == expert_ids[None, None, :]).astype(jnp.float32)
    chosen = jnp.sum(chosen_hot * logits[:, None, :], -1)
    gate_probs = jax.nn.softmax(chosen, -1)
    assign_count = rows_dev * top_k
    flat_routes = route_mine.reshape(assign_count)
    assign_hot = (flat_routes[:, None] == expert_ids[None, :]).astype(jnp.int32)
    rank_in = jnp.sum((jnp.cumsum(assign_hot, 0) - assign_hot) * assign_hot, 1)
    slot_of = flat_routes * capacity + rank_in
    assign_of_slot = (
        jnp.zeros((experts * capacity,), jnp.int32)
        .at[slot_of]
        .set(jnp.arange(assign_count, dtype=jnp.int32))
    )
    slot_used = jnp.zeros((experts * capacity,), jnp.int32).at[slot_of].set(1)
    slot_row = assign_of_slot // top_k

    def send_rows(slot_vals):
        slot_vals = slot_vals.reshape(experts, capacity, model_width)
        outgoing = jnp.broadcast_to(
            slot_vals[:, None], (experts, 2, capacity, model_width)
        ).reshape(devices, capacity, model_width)
        received = lax.all_to_all(
            outgoing, ("rows", "cols"), split_axis=0, concat_axis=0, tiled=True
        )
        return received.reshape(devices * capacity, model_width)

    def return_rows(slot_vals):
        returned = lax.all_to_all(
            slot_vals.reshape(devices, capacity, model_width),
            ("rows", "cols"),
            split_axis=0,
            concat_axis=0,
            tiled=True,
        )
        returned = returned.reshape(experts, 2, capacity, model_width).astype(jnp.float32)
        summed = (returned[:, 0] + returned[:, 1]).astype(jnp.bfloat16)
        return summed.reshape(experts * capacity, model_width).astype(jnp.float32)

    slot_inputs = jnp.where(slot_used[:, None] > 0, normed_mine[slot_row], 0)
    expert_rows = send_rows(slot_inputs)
    eg_mat = expert_gate.reshape(model_width, -1)
    eu_mat = expert_up.reshape(model_width, -1)
    ed_mat = expert_down.reshape(-1, model_width)
    e_gate = matmul(expert_rows, eg_mat)
    e_up = matmul(expert_rows, eu_mat)
    e_silu, e_slope = silu_parts(e_gate)
    e_act = (e_silu * e_up).astype(jnp.bfloat16)
    e_out = matmul(e_act, ed_mat).astype(jnp.bfloat16)
    expert_sum = return_rows(e_out)
    picked = expert_sum[slot_of].reshape(rows_dev, top_k, model_width)
    routed = jnp.sum(gate_probs[:, :, None] * picked, 1)
    ffn_full = lax.dynamic_update_slice_in_dim(
        ffn_part, lax.dynamic_slice_in_dim(ffn_part, my_rows, rows_dev, 0) + routed, my_rows, 0
    )
    ffn_mine = lax.psum_scatter(
        ffn_full.reshape(sequence_count, len_dev, model_width).astype(jnp.bfloat16),
        "rows",
        scatter_dimension=2,
        tiled=True,
    ).astype(jnp.float32)
    resid_mine = lax.dynamic_slice_in_dim(
        residual_stream.reshape(sequence_count, len_dev, model_width),
        row_idx * row_width,
        row_width,
        2,
    )
    layer_out = (resid_mine + ffn_mine).astype(jnp.bfloat16)
    grad_full = lax.all_gather(cotangent, "rows", axis=2, tiled=True).reshape(tok_dev, model_width)
    d_shared_act = matmul_nt(grad_full, sd_full)
    grad_sd = matmul_tn(shared_act, grad_full)
    d_gate_pre = (d_shared_act * up_pre * silu_slope).astype(jnp.bfloat16)
    d_up_pre = (d_shared_act * silu_gate).astype(jnp.bfloat16)
    grad_sg = matmul_tn(second_normed, d_gate_pre)
    grad_su = matmul_tn(second_normed, d_up_pre)
    grad_second_normed = matmul_nt(d_gate_pre, sg_full) + matmul_nt(d_up_pre, su_full)
    grad_mine = lax.dynamic_slice_in_dim(grad_full, my_rows, rows_dev, 0).astype(jnp.float32)
    d_gates = jnp.sum(grad_mine[:, None, :] * picked, -1)
    to_experts = (
        (gate_probs[:, :, None] * grad_mine[:, None, :])
        .reshape(assign_count, model_width)
        .astype(jnp.bfloat16)
    )
    slot_grads = jnp.where(slot_used[:, None] > 0, to_experts[assign_of_slot], 0)
    d_expert_out = send_rows(slot_grads)
    grad_ed = matmul_tn(e_act, d_expert_out)
    d_e_act = matmul_nt(d_expert_out, ed_mat)
    d_e_gate = (d_e_act * e_up * e_slope).astype(jnp.bfloat16)
    d_e_up = (d_e_act * e_silu).astype(jnp.bfloat16)
    grad_eg = matmul_tn(expert_rows, d_e_gate)
    grad_eu = matmul_tn(expert_rows, d_e_up)
    d_rows = (matmul_nt(d_e_gate, eg_mat) + matmul_nt(d_e_up, eu_mat)).astype(jnp.bfloat16)
    d_assign = return_rows(d_rows)[slot_of].reshape(rows_dev, top_k, model_width)
    d_routed_in = jnp.sum(d_assign, 1)
    d_chosen = gate_probs * (d_gates - jnp.sum(gate_probs * d_gates, -1, keepdims=True))
    d_logits = jnp.sum(chosen_hot * d_chosen[:, :, None], 1)
    router_f = router_full.astype(jnp.float32)
    grad_router_part = jnp.dot(normed_mine.astype(jnp.float32).T, d_logits, precision=PRECISE)
    d_router_in = jnp.dot(d_logits, router_f.T, precision=PRECISE)
    d_mine = (
        lax.dynamic_slice_in_dim(grad_second_normed, my_rows, rows_dev, 0)
        + d_routed_in
        + d_router_in
    )
    grad_second_normed = lax.dynamic_update_slice_in_dim(grad_second_normed, d_mine, my_rows, 0)
    grad_second_normed, grad_router = (
        lax.psum(grad_second_normed.astype(jnp.bfloat16), "rows").astype(jnp.float32),
        lax.psum(grad_router_part.astype(jnp.bfloat16), "rows").astype(jnp.float32),
    )
    grad_second_unit = grad_second_normed * second_gain_float
    second_gain_gradient = jnp.sum(grad_second_normed * second_unit_rows, 0)
    d_resid = grad_full.astype(jnp.float32) + second_inverse_deviation * (
        grad_second_unit
        - second_unit_rows * jnp.mean(grad_second_unit * second_unit_rows, -1, keepdims=True)
    )
    d_attn = d_resid.astype(jnp.bfloat16)
    grad_wo = matmul_tn(attn_rows, d_attn)
    d_heads = matmul_nt(d_attn, wo_full).astype(jnp.bfloat16)
    d_heads_t = jnp.transpose(
        d_heads.reshape(sequence_count, len_dev, q_heads, HEAD_DIM), (0, 2, 1, 3)
    )
    delta_rows = jnp.sum(d_heads_t.astype(jnp.float32) * attn_f32, -1)
    kv_all = lax.all_gather(kv_local, "cols", axis=0, tiled=True)
    seq_len = kv_all.shape[0]
    key_block = min(512, seq_len)

    def key_step(block_no, carry_in):
        k_start = block_no * key_block
        key_part = lax.dynamic_slice_in_dim(kv_all, k_start, key_block, 0)

        def contribute(state_in):
            d_query_in, d_kv_in = state_in
            keys_bf = key_part[:, :, :HEAD_DIM]
            values_bf = key_part[:, :, HEAD_DIM:]
            scores = (
                jnp.einsum("shqd,bsd->shqb", query_t, keys_bf, preferred_element_type=jnp.float32)
                * score_scale
            )
            key_pos = k_start + jnp.arange(key_block, dtype=jnp.int32)
            causal = positions[:, None] >= key_pos[None, :]
            prob_vals = jnp.where(causal, jnp.exp(scores - log_total[..., None]), 0.0)
            d_prob = jnp.einsum(
                "shqd,bsd->shqb", d_heads_t, values_bf, preferred_element_type=jnp.float32
            )
            d_scores = (prob_vals * (d_prob - delta_rows[..., None])).astype(jnp.bfloat16)
            d_query_in = (
                d_query_in
                + jnp.einsum(
                    "shqb,bsd->shqd", d_scores, keys_bf, preferred_element_type=jnp.float32
                )
                * score_scale
            )
            d_key = (
                jnp.einsum("shqb,shqd->bsd", d_scores, query_t, preferred_element_type=jnp.float32)
                * score_scale
            )
            d_value = jnp.einsum(
                "shqb,shqd->bsd",
                prob_vals.astype(jnp.bfloat16),
                d_heads_t,
                preferred_element_type=jnp.float32,
            )
            d_kv_in = lax.dynamic_update_slice_in_dim(
                d_kv_in, jnp.concatenate([d_key, d_value], -1), k_start, 0
            )
            return (d_query_in, d_kv_in)

        return lax.cond(k_start <= q_last, contribute, keep_same, carry_in)

    grad_start = (
        jnp.zeros((sequence_count, q_heads, len_dev, HEAD_DIM), jnp.float32),
        jnp.zeros((seq_len, sequence_count, 2 * HEAD_DIM), jnp.float32),
    )
    d_query, d_kv_all = lax.fori_loop(0, seq_len // key_block, key_step, grad_start)
    d_kv = lax.psum_scatter(
        d_kv_all.astype(jnp.bfloat16), "cols", scatter_dimension=0, tiled=True
    ).astype(jnp.float32)
    d_query_rows = (
        apply_rotary(jnp.transpose(d_query, (0, 2, 1, 3)), cosine_table, -sine_table)
        .reshape(tok_dev, q_heads * HEAD_DIM)
        .astype(jnp.bfloat16)
    )
    d_kv_t = jnp.swapaxes(d_kv, 0, 1)
    d_key_rows = (
        apply_rotary(
            d_kv_t[:, :, :HEAD_DIM].reshape(sequence_count, len_dev, 1, HEAD_DIM),
            cosine_table,
            -sine_table,
        )
        .reshape(tok_dev, HEAD_DIM)
        .astype(jnp.bfloat16)
    )
    d_value_rows = d_kv_t[:, :, HEAD_DIM:].reshape(tok_dev, HEAD_DIM).astype(jnp.bfloat16)
    grad_wq = matmul_tn(first_normed, d_query_rows)
    grad_wk = matmul_tn(first_normed, d_key_rows)
    grad_wv = matmul_tn(first_normed, d_value_rows)
    grad_first_normed = (
        matmul_nt(d_query_rows, wq_full)
        + matmul_nt(d_key_rows, wk_full)
        + matmul_nt(d_value_rows, wv_full)
    )
    grad_first_normed = lax.psum(grad_first_normed.astype(jnp.bfloat16), "rows").astype(jnp.float32)
    grad_first_unit = grad_first_normed * first_gain_float
    first_gain_gradient = jnp.sum(grad_first_normed * first_unit_rows, 0)
    d_input = d_resid + first_inverse_deviation * (
        grad_first_unit
        - first_unit_rows * jnp.mean(grad_first_unit * first_unit_rows, -1, keepdims=True)
    )
    grad_in = lax.dynamic_slice_in_dim(
        d_input.reshape(sequence_count, len_dev, model_width), row_idx * row_width, row_width, 2
    )
    g_gain_one, g_wq, g_wk, g_wv, g_wo, g_gain_two, g_router, g_sg, g_su, g_sd = (
        lax.psum_scatter(
            first_gain_gradient.astype(jnp.bfloat16), "cols", scatter_dimension=0, tiled=True
        ).astype(jnp.float32),
        lax.psum_scatter(
            grad_wq.astype(jnp.bfloat16), "cols", scatter_dimension=0, tiled=True
        ).astype(jnp.float32),
        lax.psum_scatter(
            grad_wk.astype(jnp.bfloat16), "cols", scatter_dimension=0, tiled=True
        ).astype(jnp.float32),
        lax.psum_scatter(
            grad_wv.astype(jnp.bfloat16), "cols", scatter_dimension=0, tiled=True
        ).astype(jnp.float32),
        lax.psum_scatter(
            grad_wo.astype(jnp.bfloat16), "cols", scatter_dimension=1, tiled=True
        ).astype(jnp.float32),
        lax.psum_scatter(
            second_gain_gradient.astype(jnp.bfloat16), "cols", scatter_dimension=0, tiled=True
        ).astype(jnp.float32),
        lax.psum_scatter(
            grad_router.astype(jnp.bfloat16), "cols", scatter_dimension=0, tiled=True
        ).astype(jnp.float32),
        lax.psum_scatter(
            grad_sg.astype(jnp.bfloat16), "cols", scatter_dimension=0, tiled=True
        ).astype(jnp.float32),
        lax.psum_scatter(
            grad_su.astype(jnp.bfloat16), "cols", scatter_dimension=0, tiled=True
        ).astype(jnp.float32),
        lax.psum_scatter(
            grad_sd.astype(jnp.bfloat16), "cols", scatter_dimension=1, tiled=True
        ).astype(jnp.float32),
    )
    return (
        layer_out,
        grad_in,
        g_gain_one,
        g_wq,
        g_wk,
        g_wv,
        g_wo,
        g_gain_two,
        g_router,
        g_sg,
        g_su,
        g_sd,
        grad_eg.reshape(expert_gate.shape),
        grad_eu.reshape(expert_up.shape),
        grad_ed.reshape(expert_down.shape),
    )


def solution(mesh):
    placed = (
        P(None, "cols", "rows"),
        P("cols"),
        P("cols", "rows"),
        P("cols", "rows"),
        P("cols", "rows"),
        P("rows", "cols"),
        P("cols"),
        P("cols", None),
        P("cols", "rows"),
        P("cols", "rows"),
        P("rows", "cols"),
        P(("rows", "cols"), None, None),
        P(("rows", "cols"), None, None),
        P(("rows", "cols"), None, None),
        P("cols", "rows", None, None),
        P(None, "cols", "rows"),
    )
    return jax.shard_map(
        per_device,
        mesh=mesh,
        in_specs=placed,
        out_specs=(
            P(None, "cols", "rows"),
            P(None, "cols", "rows"),
            P("cols"),
            P("cols", "rows"),
            P("cols", "rows"),
            P("cols", "rows"),
            P("rows", "cols"),
            P("cols"),
            P("cols", None),
            P("cols", "rows"),
            P("cols", "rows"),
            P("rows", "cols"),
            P(("rows", "cols"), None, None),
            P(("rows", "cols"), None, None),
            P(("rows", "cols"), None, None),
        ),
        check_vma=False,
    )
```

profile of v0, /device:TPU:18, one launch (start us, length us, event | category | flops | bytes accessed | tf_op | source)
XLA Modules:
  0.0 2309.9 jit_solution(470671953778792149)
XLA Ops:
  12.5 22.2 all-reduce.5
  34.7 20.3 all_gather.43
  54.9 19.2 all_gather.44
  104.1 21.0 all-gather.25.cloned.1.call-done
  195.0 50.2 %all-gather.1 = bf16[8,320,16]{1,2,0:T(8,128)(2,1)S(1)} all-gather(bf16[1,320,16]{1,2,0:T(8,128)(2,1)S(1)} %bitcast.593), channel_id=1, replica_groups=mesh['rows'=4,'cols'=8] {'cols'}, dimensions={0}, use_global_device_ids=true | all-gather | bytes 92160 | tf_op jit(solution)/shard_map/all_gather | solution.py:108
  272.0 40.2 %all-reduce.10.cloned.1.call-done = bf16[512,2560]{1,0:T(8,128)(2,1)} async-done(((bf16[512,2560]{1,0:T(8,128)(2,1)}), bf16[512,2560]{1,0:T(8,128)(2,1)}) %all-reduce.10.cloned.1.call-update) | async-done | bytes 2621456 | tf_op jit(solution)/shard_map/psum | solution.py:195
  376.2 230.9 %all_to_all.20 = bf16[32,60,2560]{2,1,0:T(8,128)(2,1)} all-to-all(bf16[32,60,2560]{2,1,0:T(8,128)(2,1)} %bitcast.561), channel_id=1, replica_groups=mesh['rows'=4,'cols'=8] {'rows','cols'}, dimensions={0} | all-to-all | bytes 19660800 | tf_op jit(solution)/shard_map/all_to_all | solution.py:236
  659.2 189.1 %all-to-all-done.2 = bf16[32,60,2560]{2,1,0:T(8,128)(2,1)} async-done(((bf16[32,60,2560]{2,1,0:T(8,128)(2,1)}), bf16[32,60,2560]{2,1,0:T(8,128)(2,1)}, u32[]{:S(2)}, u32[]{:S(2)}) %all-to-all-start.2) | async-done | bytes 9830432 | tf_op jit(solution)/shard_map/all_to_all | solution.py:236
  861.6 18.0 multiply_convert_fusion.1
  956.4 231.0 %all-to-all-done.3 = bf16[32,60,2560]{2,1,0:T(8,128)(2,1)} async-done(((bf16[32,60,2560]{2,1,0:T(8,128)(2,1)}), bf16[32,60,2560]{2,1,0:T(8,128)(2,1)}, u32[]{:S(2)}, u32[]{:S(2)}) %all-to-all-start.3) | async-done | bytes 9830432 | tf_op jit(solution)/shard_map/all_to_all | solution.py:242
  1202.7 77.4 %all-gather.19.cloned.1.call-done = bf16[2560,768]{1,0:T(8,128)(2,1)} async-done(((bf16[320,768]{1,0:T(8,128)(2,1)}), bf16[2560,768]{1,0:T(8,128)(2,1)}) %all-gather.19.cloned.1.call-update) | async-done | bytes 3932176 | tf_op jit(solution)/shard_map/all_gather | solution.py:110
  1286.3 117.3 %all-gather.21.cloned.1.call-done = bf16[768,2560]{0,1:T(8,128)(2,1)} async-done(((bf16[768,320]{0,1:T(8,128)(2,1)}), bf16[768,2560]{0,1:T(8,128)(2,1)}) %all-gather.21.cloned.1.call-update) | async-done | bytes 3932176 | tf_op jit(solution)/shard_map/all_gather | solution.py:111
  1570.9 75.9 %all-reduce.12.cloned.1.call-done = bf16[512,2560]{1,0:T(8,128)(2,1)} async-done(((bf16[512,2560]{1,0:T(8,128)(2,1)}), bf16[512,2560]{1,0:T(8,128)(2,1)}) %all-reduce.12.cloned.1.call-update) | async-done | bytes 2621456 | tf_op jit(solution)/shard_map/psum | solution.py:320
  1665.6 75.7 %while.16 = (s32[]{:T(128)}, f32[1,5,512,128]{3,2,1,0:T(8,128)S(1)}, bf16[4096,1,256]{0,2,1:T(8,128)(2,1)}, s32[]{:T(128)}, bf16[4096,1,256]{2,0,1:T(8,128)(2,1)...) while((s32[]{:T(128)}, ...), condition=%wide.region_55.56_spmd.clone, body=%wide.region_52.55_spmd.clone.sunk | while | flops 1692402688 | bytes 46580096 | solution.py:387
  1788.1 27.3 %reduce-scatter.15.cloned.1.call-done = bf16[512,1,256]{0,2,1:T(8,128)(2,1)} async-done(((bf16[4096,1,256]{0,2,1:T(8,128)(2,1)}), bf16[512,1,256]{0,2,1:T(8,128)(2,1)}) %reduce-scatter.15.cloned.1.call-update) | async-done | bytes 262160 | tf_op jit(solution)/shard_map/reduce_scatter | solution.py:388
  1838.2 29.3 %reduce-scatter.25.cloned.1.call-done = bf16[320,768]{1,0:T(8,128)(2,1)} async-done(((bf16[2560,768]{1,0:T(8,128)(2,1)}), bf16[320,768]{1,0:T(8,128)(2,1)}) %reduce-scatter.25.cloned.1.call-update) | async-done | bytes 491536 | tf_op jit(solution)/shard_map/reduce_scatter | solution.py:447
  1869.5 46.0 %reduce-scatter.27.cloned.1.call-done = bf16[320,768]{1,0:T(8,128)(2,1)} async-done(((bf16[2560,768]{1,0:T(8,128)(2,1)}), bf16[320,768]{1,0:T(8,128)(2,1)}) %reduce-scatter.27.cloned.1.call-update) | async-done | bytes 491536 | tf_op jit(solution)/shard_map/reduce_scatter | solution.py:450
  1917.5 45.8 %reduce-scatter.29.cloned.1.call-done = bf16[768,320]{0,1:T(8,128)(2,1)} async-done(((bf16[768,2560]{0,1:T(8,128)(2,1)}), bf16[768,320]{0,1:T(8,128)(2,1)}) %reduce-scatter.29.cloned.1.call-update) | async-done | bytes 491536 | tf_op jit(solution)/shard_map/reduce_scatter | solution.py:453
  2046.7 20.3 reduce-scatter.19.cloned.1.call-done
  2068.6 30.4 %reduce-scatter.21.cloned.1.call-done = bf16[320,128]{1,0:T(8,128)(2,1)} async-done(((bf16[2560,128]{1,0:T(8,128)(2,1)}), bf16[320,128]{1,0:T(8,128)(2,1)}) %reduce-scatter.21.cloned.1.call-update) | async-done | bytes 81936 | tf_op jit(solution)/shard_map/reduce_scatter | solution.py:435
  2100.6 44.0 %reduce-scatter.23.cloned.1.call-done = bf16[640,320]{0,1:T(8,128)(2,1)} async-done(((bf16[640,2560]{0,1:T(8,128)(2,1)}), bf16[640,320]{0,1:T(8,128)(2,1)}) %reduce-scatter.23.cloned.1.call-update) | async-done | bytes 409616 | tf_op jit(solution)/shard_map/reduce_scatter | solution.py:438
  2146.5 40.5 %reduce-scatter.17.cloned.1.call-done = bf16[320,640]{1,0:T(8,128)(2,1)} async-done(((bf16[2560,640]{1,0:T(8,128)(2,1)}), bf16[320,640]{1,0:T(8,128)(2,1)}) %reduce-scatter.17.cloned.1.call-update) | async-done | bytes 409616 | tf_op jit(solution)/shard_map/reduce_scatter | solution.py:429
  2189.0 81.0 %all-reduce.14.cloned.1.call-done = bf16[512,2560]{1,0:T(8,128)(2,1)} async-done(((bf16[512,2560]{1,0:T(8,128)(2,1)}), bf16[512,2560]{1,0:T(8,128)(2,1)}) %all-reduce.14.cloned.1.call-update) | async-done | bytes 2621456 | tf_op jit(solution)/shard_map/psum | solution.py:415
  2277.2 21.5 all-reduce.4
  (505 shorter events, 927.2 us)
Async XLA Ops:
  7.2 67.0 %all-gather.11.cloned.1.call-start = ((), (), s32[]{:S(2)}) async-start(), calls=%async_computation.14 | async-start | bytes 3276800 | tf_op jit(solution)/shard_map/all_gather | solution.py:89
  7.9 86.3 %all-gather.13.cloned.1.call-start = ((), (), s32[]{:S(2)}) async-start(), calls=%async_computation.15 | async-start | bytes 3686400 | tf_op jit(solution)/shard_map/all_gather | solution.py:103
  8.7 116.4 %all-gather.25.cloned.1.call-start = ((), (), s32[]{:S(2)}) async-start(), calls=%async_computation.32 | async-start | bytes 2359296 | tf_op jit(solution)/shard_map/all_gather | solution.py:178
  81.9 106.4 %all-gather.15.cloned.1.call-start = ((), (), s32[]{:S(2)}) async-start(), calls=%async_computation.16 | async-start | bytes 3686400 | tf_op jit(solution)/shard_map/all_gather | solution.py:106
  82.5 172.4 %all-gather.23.cloned.1.call-start = ((), (), s32[]{:S(2)}) async-start(), calls=%async_computation.21 | async-start | bytes 3276800 | tf_op jit(solution)/shard_map/all_gather | solution.py:282
  83.1 229.2 %all-reduce.10.cloned.1.call-start = ((), (), s32[]{:S(2)}) async-start(), calls=%async_computation.17 | async-start | bytes 5242880 | tf_op jit(solution)/shard_map/psum | solution.py:195
  614.9 233.4 %all-to-all-start.2 = ((bf16[32,60,2560]{2,1,0:T(8,128)(2,1)}), bf16[32,60,2560]{2,1,0:T(8,128)(2,1)}, u32[]{:S(2)}, u32[]{:S(2)}) async-start(bf16[32,60,2560]{2,1,0:T(8,128)(2,1)} %bitcast.560), calls=%async_computation.2 | async-start | bytes 20971520 | tf_op jit(solution)/shard_map/all_to_all | solution.py:236
  922.0 265.5 %all-to-all-start.3 = ((bf16[32,60,2560]{2,1,0:T(8,128)(2,1)}), bf16[32,60,2560]{2,1,0:T(8,128)(2,1)}, u32[]{:S(2)}, u32[]{:S(2)}) async-start(bf16[32,60,2560]{2,1,0:T(8,128)(2,1)} %reshape.1063), calls=%async_computation.3 | async-start | bytes 20971520 | tf_op jit(solution)/shard_map/all_to_all | solution.py:242
  930.4 266.8 %all-gather.17.cloned.1.call-start = ((), (), s32[]{:S(2)}) async-start(), calls=%async_computation.18 | async-start | bytes 4423680 | tf_op jit(solution)/shard_map/all_gather | solution.py:109
  1187.5 296.7 %all-to-all-start.1 = ((bf16[32,60,2560]{2,1,0:T(8,128)(2,1)}), bf16[32,60,2560]{2,1,0:T(8,128)(2,1)}, u32[]{:S(2)}, u32[]{:S(2)}) async-start(bf16[32,60,2560]{2,1,0:T(8,128)(2,1)} %reshape.1057), calls=%async_computation.1 | async-start | bytes 20971520 | tf_op jit(solution)/shard_map/all_to_all | solution.py:242
  1195.6 84.4 %all-gather.19.cloned.1.call-start = ((), (), s32[]{:S(2)}) async-start(), calls=%async_computation.19 | async-start | bytes 4423680 | tf_op jit(solution)/shard_map/all_gather | solution.py:110
  1196.4 207.2 %all-gather.21.cloned.1.call-start = ((), (), s32[]{:S(2)}) async-start(), calls=%async_computation.20 | async-start | bytes 4423680 | tf_op jit(solution)/shard_map/all_gather | solution.py:111
  1197.1 449.7 %all-reduce.12.cloned.1.call-start = ((), (), s32[]{:S(2)}) async-start(), calls=%async_computation.22 | async-start | bytes 5242880 | tf_op jit(solution)/shard_map/psum | solution.py:320
  1566.5 248.9 %reduce-scatter.15.cloned.1.call-start = ((), (), s32[]{:S(2)}) async-start(), calls=%async_computation.23 | async-start | bytes 2359296 | tf_op jit(solution)/shard_map/reduce_scatter | solution.py:388
  1741.4 126.0 %reduce-scatter.25.cloned.1.call-start = ((), (), s32[]{:S(2)}) async-start(), calls=%async_computation.29 | async-start | bytes 4423680 | tf_op jit(solution)/shard_map/reduce_scatter | solution.py:447
  1748.0 167.5 %reduce-scatter.27.cloned.1.call-start = ((), (), s32[]{:S(2)}) async-start(), calls=%async_computation.30 | async-start | bytes 4423680 | tf_op jit(solution)/shard_map/reduce_scatter | solution.py:450
  1754.3 209.0 %reduce-scatter.29.cloned.1.call-start = ((), (), s32[]{:S(2)}) async-start(), calls=%async_computation.31 | async-start | bytes 4423680 | tf_op jit(solution)/shard_map/reduce_scatter | solution.py:453
  1759.7 253.1 %reduce-scatter.33.cloned.1.call-start = ((), (), s32[]{:S(2)}) async-start(), calls=%async_computation.34 | async-start | bytes 737280
  1769.9 269.2 %reduce-scatter.31.cloned.1.call-start = ((), (), s32[]{:S(2)}) async-start(), calls=%async_computation.33 | async-start | bytes 3276800
  1788.1 279.0 %reduce-scatter.19.cloned.1.call-start = ((), (), s32[]{:S(2)}) async-start(), calls=%async_computation.26 | async-start | bytes 737280 | tf_op jit(solution)/shard_map/reduce_scatter | solution.py:432
  1819.0 280.0 %reduce-scatter.21.cloned.1.call-start = ((), (), s32[]{:S(2)}) async-start(), calls=%async_computation.27 | async-start | bytes 737280 | tf_op jit(solution)/shard_map/reduce_scatter | solution.py:435
  1821.4 323.1 %reduce-scatter.23.cloned.1.call-start = ((), (), s32[]{:S(2)}) async-start(), calls=%async_computation.28 | async-start | bytes 3686400 | tf_op jit(solution)/shard_map/reduce_scatter | solution.py:438
  1828.2 358.8 %reduce-scatter.17.cloned.1.call-start = ((), (), s32[]{:S(2)}) async-start(), calls=%async_computation.25 | async-start | bytes 3686400 | tf_op jit(solution)/shard_map/reduce_scatter | solution.py:429
  1837.5 432.4 %all-reduce.14.cloned.1.call-start = ((), (), s32[]{:S(2)}) async-start(), calls=%async_computation.24 | async-start | bytes 5242880 | tf_op jit(solution)/shard_map/psum | solution.py:415
  (91 other events, 2276.3 us)
Sparse Core Ops, SparseCore 0:
  9.9 40.6 all-gather.10
  52.2 41.9 all-gather.12
  96.4 28.6 all-gather.24
  126.6 38.2 all-gather.14
  166.5 39.6 all-gather.22
  209.7 102.4 all-reduce.9
  933.0 81.7 all-gather.16
  1198.2 81.7 all-gather.18
  1281.8 121.7 all-gather.20
  1566.6 80.1 all-reduce.11
  1741.5 73.8 reduce-scatter.14
  1818.1 49.2 reduce-scatter.24
  1869.7 45.6 reduce-scatter.26
  1917.6 45.6 reduce-scatter.28
  1965.4 26.6 reduce-scatter.32
  1995.0 44.0 reduce-scatter.30
  2041.8 25.2 reduce-scatter.18
  2069.7 29.2 reduce-scatter.20
  2101.3 43.1 reduce-scatter.22
  2146.8 40.1 reduce-scatter.16
  2190.1 79.8 all-reduce.13
where the time goes:
time: 2330 us; the launch traced here: 2310 us
  waiting for transfers between devices  1150 us (49%)
  blocking collectives  378 us (16%)
  matrix products  309 us (13%)
  local copies, waits for them, and re-layouts  255 us (11%)
  other arithmetic  173 us (7%)
  starting transfers between devices  26.2 us (1%)
    all_to_all x2, waiting for transfers between devices, return_rows(): lax.all_to_all(slot_vals.reshape(devices, capacity, model_width), ('rows'...  238 us
    all_to_all x1, blocking collectives, send_rows(): lax.all_to_all(outgoing, ('rows', 'cols'), split_axis=0, concat_axis=0, t...  231 us
    all_to_all x1, waiting for transfers between devices, send_rows(): lax.all_to_all(outgoing, ('rows', 'cols'), split_axis=0, concat_axis=0, t...  189 us
    all_gather x1, waiting for transfers between devices, per_device(): lax.all_gather(shared_down, 'cols', axis=1, tiled=True)  117 us
    psum x1, waiting for transfers between devices, per_device(): lax.psum(grad_first_normed.astype(jnp.bfloat16), 'rows').astype(jnp.float32)  81 us
    all_gather x1, waiting for transfers between devices, per_device(): lax.all_gather(shared_up, 'cols', axis=0, tiled=True)  77.4 us
    psum x1, waiting for transfers between devices, per_device(): lax.psum(grad_second_normed.astype(jnp.bfloat16), 'rows')  75.9 us
    dot_general x10, matrix products, matmul_tn(): lax.dot_general(left_op, right_op, (((0,), (0,)), ((), ())), preferred_el...  73.9 us
  transfers between devices with their start and end apart: 24, of which 19 were waited for; matrix products, arithmetic and copies ran while one was open for 17% of the time, Pallas kernels for 0%

commit v1 on v0

--- a/solution.py
+++ b/solution.py
@@ -3,6 +3,8 @@
 import jax
 import jax.numpy as jnp
 from jax import lax
+from jax.experimental import pallas as pl
+from jax.experimental.pallas import tpu as pltpu
 from jax.sharding import PartitionSpec as P
 
 HEAD_DIM = 128
@@ -57,7 +59,7 @@
     return carry_in
 
 
-def per_device(
+def routed_layer(
     layer_in,
     norm1_gain,
     w_query,
@@ -473,6 +475,650 @@
     )
 
 
+def scores_of(keys, queries, scale):
+    return matmul_nt(keys, queries) * scale
+
+
+def causal_mask(scores):
+    key_pos = lax.broadcasted_iota(jnp.int32, scores.shape, 0)
+    query_pos = lax.broadcasted_iota(jnp.int32, scores.shape, 1)
+    return query_pos >= key_pos
+
+
+def attention_forward_kernel(
+    scale, block_ref, q_ref, k_ref, vt_ref, out_ref, lse_ref, top, total, acc
+):
+    length = q_ref.shape[0]
+    own = block_ref[0]
+    queries = q_ref[...]
+
+    def part(block):
+        start = pl.multiple_of(block * length, length)
+        scores = scores_of(k_ref[pl.ds(start, length), :], queries, scale)
+        return scores, vt_ref[:, pl.ds(start, length)]
+
+    scores, values_t = part(own)
+    scores = jnp.where(causal_mask(scores), scores, NEG_LARGE)
+    high = jnp.max(scores, 0, keepdims=True)
+    probs = jnp.exp(scores - high)
+    top[...] = high
+    total[...] = jnp.sum(probs, 0, keepdims=True)
+    acc[...] = matmul(values_t, probs.astype(jnp.bfloat16))
+
+    @pl.loop(0, own)
+    def _(block):
+        scores, values_t = part(block)
+        high = jnp.maximum(top[...], jnp.max(scores, 0, keepdims=True))
+        probs = jnp.exp(scores - high)
+        shrink = jnp.exp(top[...] - high)
+        top[...] = high
+        total[...] = total[...] * shrink + jnp.sum(probs, 0, keepdims=True)
+        acc[...] = acc[...] * shrink + matmul(values_t, probs.astype(jnp.bfloat16))
+
+    out_ref[...] = (acc[...] / total[...]).T
+    lse_ref[0] = top[...] + jnp.log(total[...])
+
+
+def attention_forward(block, queries, keys, values_t):
+    length, width = queries.shape
+    heads = width // HEAD_DIM
+    whole = keys.shape[0]
+    return pl.pallas_call(
+        lambda *refs: attention_forward_kernel(1.0 / math.sqrt(HEAD_DIM), *refs),
+        grid_spec=pltpu.PrefetchScalarGridSpec(
+            num_scalar_prefetch=1,
+            grid=(heads,),
+            in_specs=[
+                pl.BlockSpec((length, HEAD_DIM), lambda h, s: (0, h)),
+                pl.BlockSpec((whole, HEAD_DIM), lambda h, s: (0, 0)),
+                pl.BlockSpec((HEAD_DIM, whole), lambda h, s: (0, 0)),
+            ],
+            out_specs=[
+                pl.BlockSpec((length, HEAD_DIM), lambda h, s: (0, h)),
+                pl.BlockSpec((1, 1, length), lambda h, s: (h, 0, 0)),
+            ],
+            scratch_shapes=[
+                pltpu.VMEM((1, length), jnp.float32),
+                pltpu.VMEM((1, length), jnp.float32),
+                pltpu.VMEM((HEAD_DIM, length), jnp.float32),
+            ],
+        ),
+        out_shape=[
+            jax.ShapeDtypeStruct((length, width), jnp.float32),
+            jax.ShapeDtypeStruct((heads, 1, length), jnp.float32),
+        ],
+        compiler_params=pltpu.CompilerParams(vmem_limit_bytes=48 * 1024 * 1024),
+        cost_estimate=pl.CostEstimate(
+            flops=4 * length * width * whole,
+            bytes_accessed=2 * whole * HEAD_DIM * 2 + length * width * 6,
+            transcendentals=length * heads * whole,
+        ),
+        name="attention_forward",
+    )(block, queries, keys, values_t)
+
+
+def attention_backward_kernel(
+    scale, block_ref, q_ref, k_ref, kt_ref, v_ref, go_ref, lse_ref, delta_ref, dq_ref, dkv_ref, dqt
+):
+    length, width = q_ref.shape
+    heads = width // HEAD_DIM
+    step = pl.program_id(0)
+    own = block_ref[0]
+
+    @pl.when(step == 0)
+    def _():
+        dqt[...] = jnp.zeros_like(dqt)
+
+    def one_block(masked):
+        keys = k_ref[...]
+        keys_t = kt_ref[...]
+        values = v_ref[...]
+        d_key = jnp.zeros((length, HEAD_DIM), jnp.float32)
+        d_value = jnp.zeros((length, HEAD_DIM), jnp.float32)
+        for head in range(heads):
+            columns = slice(head * HEAD_DIM, (head + 1) * HEAD_DIM)
+            queries = q_ref[:, columns]
+            grads = go_ref[:, columns]
+            probs = jnp.exp(scores_of(keys, queries, scale) - lse_ref[head])
+            if masked:
+                probs = jnp.where(causal_mask(probs), probs, 0.0)
+            d_probs = matmul_nt(values, grads)
+            d_scores = (probs * (d_probs - delta_ref[head])).astype(jnp.bfloat16)
+            d_value = d_value + matmul(probs.astype(jnp.bfloat16), grads)
+            d_key = d_key + matmul(d_scores, queries)
+            dqt[head] = dqt[head] + matmul(keys_t, d_scores)
+        dkv_ref[:, :HEAD_DIM] = (d_key * scale).astype(dkv_ref.dtype)
+        dkv_ref[:, HEAD_DIM:] = d_value.astype(dkv_ref.dtype)
+
+    @pl.when(step < own)
+    def _():
+        one_block(False)
+
+    @pl.when(step == own)
+    def _():
+        one_block(True)
+
+    @pl.when(step > own)
+    def _():
+        dkv_ref[...] = jnp.zeros_like(dkv_ref)
+
+    @pl.when(step == pl.num_programs(0) - 1)
+    def _():
+        for head in range(heads):
+            dq_ref[:, head * HEAD_DIM : (head + 1) * HEAD_DIM] = (dqt[head] * scale).T
+
+
+def attention_backward(block, queries, keys, keys_t, values, grads, lse, delta):
+    length, width = queries.shape
+    heads = width // HEAD_DIM
+    whole = keys.shape[0]
+    fixed = lambda b, s: (0, 0)
+    fixed_three = lambda b, s: (0, 0, 0)
+    return pl.pallas_call(
+        lambda *refs: attention_backward_kernel(1.0 / math.sqrt(HEAD_DIM), *refs),
+        grid_spec=pltpu.PrefetchScalarGridSpec(
+            num_scalar_prefetch=1,
+            grid=(whole // length,),
+            in_specs=[
+                pl.BlockSpec((length, width), fixed),
+                pl.BlockSpec((length, HEAD_DIM), lambda b, s: (jnp.minimum(b, s[0]), 0)),
+                pl.BlockSpec((HEAD_DIM, length), lambda b, s: (0, jnp.minimum(b, s[0]))),
+                pl.BlockSpec((length, HEAD_DIM), lambda b, s: (jnp.minimum(b, s[0]), 0)),
+                pl.BlockSpec((length, width), fixed),
+                pl.BlockSpec((heads, 1, length), fixed_three),
+                pl.BlockSpec((heads, 1, length), fixed_three),
+            ],
+            out_specs=[
+                pl.BlockSpec((length, width), fixed),
+                pl.BlockSpec((length, 2 * HEAD_DIM), lambda b, s: (b, 0)),
+            ],
+            scratch_shapes=[pltpu.VMEM((heads, HEAD_DIM, length), jnp.float32)],
+        ),
+        out_shape=[
+            jax.ShapeDtypeStruct((length, width), jnp.float32),
+            jax.ShapeDtypeStruct((whole, 2 * HEAD_DIM), jnp.bfloat16),
+        ],
+        compiler_params=pltpu.CompilerParams(vmem_limit_bytes=48 * 1024 * 1024),
+        cost_estimate=pl.CostEstimate(
+            flops=10 * length * width * whole,
+            bytes_accessed=6 * whole * HEAD_DIM * 2 + length * width * 8,
+            transcendentals=length * heads * whole,
+        ),
+        name="attention_backward",
+    )(block, queries, keys, keys_t, values, grads, lse, delta)
+
+
+def add_bf16(left, right):
+    return (left.astype(jnp.float32) + right.astype(jnp.float32)).astype(jnp.bfloat16)
+
+
+class Exchange:
+    def __init__(self):
+        self.n_rows = lax.axis_size("rows")
+        self.n_cols = lax.axis_size("cols")
+        self.ring = self.n_cols // 2
+        self.r = lax.axis_index("rows")
+        self.c = lax.axis_index("cols")
+        self.z = self.c // 2
+        self.k = self.c % 2
+
+    def move(self, values, target):
+        pairs = []
+        for r in range(self.n_rows):
+            for c in range(self.n_cols):
+                to_r, to_c = target(r, c)
+                pairs.append((r * self.n_cols + c, to_r * self.n_cols + to_c))
+        return lax.ppermute(values, ("rows", "cols"), pairs)
+
+    def along_x(self, values):
+        return self.move(values, lambda r, c: (r ^ 1, c))
+
+    def along_y(self, values):
+        return self.move(values, lambda r, c: (r ^ 2, c))
+
+    def along_z(self, values, hops=1):
+        return self.move(values, lambda r, c: (r, (c + 2 * hops) % self.n_cols))
+
+    def across_z(self, values, bit):
+        return self.move(values, lambda r, c: (r, c ^ (2 * bit)))
+
+    def sibling(self, values):
+        return self.move(values, lambda r, c: (r, c ^ 1))
+
+    def chip(self, hops):
+        return (self.z - hops + self.ring) % self.ring
+
+    def place(self, hops):
+        return self.r ^ self.chip(hops)
+
+    def mixed(self, values, axis):
+        width = values.shape[axis] // self.n_rows
+
+        def branch(row):
+            return lambda whole: jnp.concatenate(
+                [
+                    lax.slice_in_dim(whole, (row ^ j) * width, ((row ^ j) + 1) * width, axis=axis)
+                    for j in range(self.n_rows)
+                ],
+                axis,
+            )
+
+        return lax.switch(self.r, [branch(row) for row in range(self.n_rows)], values)
+
+    def rows_gather(self, block):
+        half = block.shape[0] // 2
+        from_x = self.along_x(block)
+        from_y = self.along_y(block)
+        first = self.along_y(from_x[:half])
+        second = self.along_x(from_y[half:])
+        return [block, from_x, from_y, jnp.concatenate([first, second], 0)]
+
+    def rows_scatter(self, blocks):
+        half = blocks[0].shape[0] // 2
+        upper = [block[:half] for block in blocks]
+        lower = [block[half:] for block in blocks]
+        sent = self.along_x(jnp.stack([upper[1], upper[3]]))
+        forward = add_bf16(upper[2], sent[1])
+        upper_sum = upper[0].astype(jnp.float32) + sent[0].astype(jnp.float32)
+        upper_sum = upper_sum + self.along_y(forward).astype(jnp.float32)
+        sent = self.along_y(jnp.stack([lower[2], lower[3]]))
+        forward = add_bf16(lower[1], sent[1])
+        lower_sum = lower[0].astype(jnp.float32) + sent[0].astype(jnp.float32)
+        lower_sum = lower_sum + self.along_x(forward).astype(jnp.float32)
+        return jnp.concatenate([upper_sum, lower_sum], 0)
+
+    def cols_gather(self, block, place):
+        shape = (self.ring, 2) + block.shape
+        whole = jnp.zeros(shape, block.dtype)
+        rest = (0,) * block.ndim
+        for hops in range(self.ring):
+            twin = self.sibling(block)
+            spot = place(hops)
+            whole = lax.dynamic_update_slice(whole, block[None, None], (spot, self.k) + rest)
+            whole = lax.dynamic_update_slice(whole, twin[None, None], (spot, 1 - self.k) + rest)
+            if hops < self.ring - 1:
+                block = self.along_z(block)
+        return whole
+
+    def pair_sum(self, parts):
+        mine = lax.dynamic_index_in_dim(parts, self.k, 1, False)
+        other = lax.dynamic_index_in_dim(parts, 1 - self.k, 1, False)
+        return add_bf16(mine, self.sibling(other))
+
+    def cols_scatter(self, parts, place):
+        summed = self.pair_sum(parts)
+        pick = lambda hops: lax.dynamic_index_in_dim(summed, place(hops), 0, False)
+        run = pick(1)
+        for hops in range(2, self.ring):
+            run = add_bf16(self.along_z(run), pick(hops))
+        return self.along_z(run).astype(jnp.float32) + pick(0).astype(jnp.float32)
+
+
+def split_terms(values):
+    high = lax.reduce_precision(values, 8, 7)
+    return high.astype(jnp.bfloat16), (values - high).astype(jnp.bfloat16)
+
+
+def gathered_layer(
+    layer_in,
+    norm1_gain,
+    w_query,
+    key_matrix,
+    value_matrix,
+    w_out,
+    norm2_gain,
+    w_router,
+    shared_gate,
+    shared_up,
+    shared_down,
+    expert_gate,
+    expert_up,
+    expert_down,
+    routes,
+    cotangent,
+):
+    net = Exchange()
+    n_rows, ring = net.n_rows, net.ring
+    r, c, z, k = net.r, net.c, net.z, net.k
+    length, row_width = layer_in.shape[1:]
+    rows_dev, top_k = routes.shape[2:]
+    experts = w_router.shape[1]
+    model_width = row_width * n_rows
+    col_width = w_query.shape[0]
+    q_width = w_query.shape[1]
+    q_heads = q_width // HEAD_DIM
+    kv_width = key_matrix.shape[1]
+    shared_hidden = shared_gate.shape[1] // ring
+    half_hidden = expert_gate.shape[2]
+    slots = -(-2 * max(1, 5 * rows_dev * top_k // (8 * experts)) // 16) * 16
+    index = lax.dynamic_index_in_dim
+
+    expert_ids = jnp.arange(experts, dtype=jnp.int32)
+    hot = jnp.sum(
+        (routes.reshape(rows_dev, top_k)[:, :, None] == expert_ids).astype(jnp.float32), 1
+    )
+    earlier = jnp.tril(jnp.ones((rows_dev, rows_dev), jnp.float32), -1)
+    rank = jnp.dot(earlier, hot, precision=PRECISE)
+    slot_map = jnp.where(hot > 0, rank, -1.0).T
+    slot_maps = lax.all_gather(slot_map, ("cols", "rows"), axis=0, tiled=False)
+    slot_maps = slot_maps.reshape(ring, 2, n_rows, experts, rows_dev)
+    slot_maps = index(slot_maps, k, 1, False)
+
+    small = jnp.concatenate([w_router, norm1_gain[:, None], norm2_gain[:, None]], 1)
+    small = jnp.pad(small, ((0, 0), (0, 128 - small.shape[1])))
+    small = net.mixed(lax.all_gather(small, "cols", axis=0, tiled=True), 0)
+    router_full = small[:, :experts]
+    gains = small[:, experts : experts + 2].astype(jnp.float32).T
+    first_gain, second_gain = gains[0][None], gains[1][None]
+
+    token_input = jnp.concatenate(net.rows_gather(layer_in[0]), 1).astype(jnp.float32)
+    weights_in = net.cols_gather(
+        jnp.concatenate([w_query, key_matrix, value_matrix], 1), net.place
+    ).reshape(model_width, -1)
+    weights_out_t = net.cols_gather(w_out.T, net.place).reshape(model_width, -1)
+    first_inverse = lax.rsqrt(jnp.mean(token_input * token_input, -1, keepdims=True) + NORM_EPS)
+    first_unit = token_input * first_inverse
+    first_normed = (first_unit * first_gain).astype(jnp.bfloat16)
+    projected = matmul(first_normed, weights_in)
+    positions = c * length + jnp.arange(length, dtype=jnp.int32)
+    cosine_table, sine_table = rope_tables(positions, HEAD_DIM)
+    rotated = apply_rotary(
+        projected[:, : q_width + kv_width].reshape(length, -1, HEAD_DIM), cosine_table, sine_table
+    ).astype(jnp.bfloat16)
+    queries = rotated[:, :q_heads].reshape(length, q_width)
+    kv_local = jnp.concatenate(
+        [rotated[:, q_heads], projected[:, q_width + kv_width :].astype(jnp.bfloat16)], 1
+    )
+    kv_all = net.cols_gather(kv_local, net.chip).reshape(-1, 2 * HEAD_DIM)
+    keys_all, values_all = kv_all[:, :HEAD_DIM], kv_all[:, HEAD_DIM:]
+    block_no = c.astype(jnp.int32)[None]
+    attn_f32, log_total = attention_forward(block_no, queries, keys_all, values_all.T)
+    attn_rows = attn_f32.astype(jnp.bfloat16)
+    proj = matmul_nt(attn_rows, weights_out_t).astype(jnp.bfloat16)
+    blocks_of = lambda whole: [
+        whole[:, j * row_width : (j + 1) * row_width] for j in range(n_rows)
+    ]
+    proj_mine = net.rows_scatter(blocks_of(proj)).astype(jnp.bfloat16)
+    attn_proj = jnp.concatenate(net.rows_gather(proj_mine), 1).astype(jnp.float32)
+    residual = token_input + attn_proj
+    second_inverse = lax.rsqrt(jnp.mean(residual * residual, -1, keepdims=True) + NORM_EPS)
+    second_unit = residual * second_inverse
+    second_normed = (second_unit * second_gain).astype(jnp.bfloat16)
+
+    pair = lambda own, axis: jnp.concatenate([own, net.sibling(own)], axis)
+    e_gate_w = net.mixed(pair(expert_gate[0], 1), 0)
+    e_up_w = net.mixed(pair(expert_up[0], 1), 0)
+    e_down_w = net.mixed(pair(expert_down[0], 0), 1)
+    packed = jnp.concatenate(
+        [
+            shared_gate.reshape(col_width, ring, shared_hidden),
+            shared_up.reshape(col_width, ring, shared_hidden),
+            shared_down.T.reshape(col_width, ring, shared_hidden),
+        ],
+        2,
+    )
+    packed = jnp.swapaxes(packed, 0, 1)
+    shared_w = jnp.zeros((ring, 2) + packed.shape[1:], jnp.bfloat16)
+    for hops in range(ring):
+        piece = index(packed, net.chip(-hops), 0, False)
+        piece = net.along_z(piece, hops) if hops else piece
+        twin = net.sibling(piece)
+        spot = net.place(hops)
+        shared_w = lax.dynamic_update_slice(shared_w, piece[None, None], (spot, k, 0, 0))
+        shared_w = lax.dynamic_update_slice(shared_w, twin[None, None], (spot, 1 - k, 0, 0))
+    shared_w = shared_w.reshape(model_width, 3 * shared_hidden)
+    shared_in, shared_down_t = shared_w[:, : 2 * shared_hidden], shared_w[:, 2 * shared_hidden :]
+    token_w = jnp.concatenate([shared_in, router_full], 1)
+
+    my_expert = r * ring + z
+    mine_hot = (expert_ids == my_expert).astype(jnp.float32)
+    slot_ids = jnp.arange(slots, dtype=jnp.float32)
+
+    def routing(hops):
+        maps = index(slot_maps, net.chip(hops), 0, False)
+        my_map = index(maps, my_expert, 1, False)
+        pick = my_map[:, None, :] == slot_ids[None, :, None]
+        chosen = jnp.swapaxes(maps >= 0, 1, 2).reshape(length, experts)
+        return pick, chosen
+
+    def take(pick, rows):
+        return jnp.einsum(
+            "bst,btd->bsd",
+            pick.astype(jnp.bfloat16),
+            rows.reshape(n_rows, rows_dev, model_width),
+            preferred_element_type=jnp.float32,
+        ).astype(jnp.bfloat16).reshape(n_rows * slots, model_width)
+
+    def spread(pick, rows):
+        return jnp.einsum(
+            "bst,bsd->btd",
+            pick.astype(jnp.bfloat16),
+            rows.reshape(n_rows, slots, model_width),
+            preferred_element_type=jnp.float32,
+        ).reshape(length, model_width)
+
+    grad_block = cotangent[0]
+    early = []
+    for hops in range(ring):
+        grad_rows = jnp.concatenate(net.rows_gather(grad_block), 1)
+        if hops < ring - 1:
+            grad_block = net.along_z(grad_block)
+        pick, chosen = routing(hops)
+        slot_grads = take(pick, grad_rows)
+        through = matmul_nt(slot_grads, e_down_w)
+        shared_through = matmul(grad_rows, shared_down_t)
+        early.append((pick, chosen, grad_rows, slot_grads, through, shared_through))
+
+    normed_block = second_normed[:, :row_width]
+    done = []
+    for hops in range(ring):
+        pick, chosen, grad_rows, slot_grads, through, shared_through = early[hops]
+        if hops == 0:
+            rows = second_normed
+        else:
+            normed_block = net.along_z(normed_block)
+            rows = jnp.concatenate(net.rows_gather(normed_block), 1)
+        from_tokens = matmul(rows, token_w)
+        s_gate = from_tokens[:, :shared_hidden]
+        s_up = from_tokens[:, shared_hidden : 2 * shared_hidden]
+        logits = from_tokens[:, 2 * shared_hidden :]
+        gate_probs = jax.nn.softmax(jnp.where(chosen, logits, NEG_LARGE), -1)
+        my_gate = jnp.sum(gate_probs * mine_hot, -1).reshape(n_rows, 1, rows_dev)
+        slot_gate = jnp.sum(jnp.where(pick, my_gate, 0.0), -1).reshape(-1, 1)
+        slot_rows = take(pick, rows)
+        e_gate = matmul(slot_rows, e_gate_w)
+        e_up = matmul(slot_rows, e_up_w)
+        e_silu, e_slope = silu_parts(e_gate)
+        e_act_f = e_silu * e_up
+        e_act = e_act_f.astype(jnp.bfloat16)
+        d_gate_slot = jnp.sum(e_act_f * through, -1).reshape(n_rows, slots, 1)
+        d_gate_token = jnp.sum(jnp.where(pick, d_gate_slot, 0.0), 1).reshape(1, length)
+        d_e_act = through * slot_gate
+        d_e_gate = (d_e_act * e_up * e_slope).astype(jnp.bfloat16)
+        d_e_up = (d_e_act * e_silu).astype(jnp.bfloat16)
+        d_part = (slot_grads.astype(jnp.float32) * slot_gate).astype(jnp.bfloat16)
+        s_silu, s_slope = silu_parts(s_gate)
+        s_act = (s_silu * s_up).astype(jnp.bfloat16)
+        d_s_gate = (shared_through * s_up * s_slope).astype(jnp.bfloat16)
+        d_s_up = (shared_through * s_silu).astype(jnp.bfloat16)
+        d_shared = jnp.concatenate([d_s_gate, d_s_up], 1)
+        d_slot_rows = (matmul_nt(d_e_gate, e_gate_w) + matmul_nt(d_e_up, e_up_w)).astype(
+            jnp.bfloat16
+        )
+        d_rows = (spread(pick, d_slot_rows) + matmul_nt(d_shared, shared_in)).astype(jnp.bfloat16)
+        part = (matmul(e_act, e_down_w) * slot_gate).astype(jnp.bfloat16)
+        out_rows = (spread(pick, part) + matmul_nt(s_act, shared_down_t)).astype(jnp.bfloat16)
+        done.append(
+            dict(
+                rows=rows, slot_rows=slot_rows, e_act=e_act, d_e_gate=d_e_gate, d_e_up=d_e_up,
+                d_part=d_part, s_act=s_act, d_shared=d_shared, d_rows=d_rows, out_rows=out_rows,
+                gate_probs=gate_probs, d_gate_token=d_gate_token, grad_rows=grad_rows,
+            )
+        )
+
+    def ring_scatter(name):
+        run = None
+        for hops in list(range(1, ring)) + [0]:
+            here = net.rows_scatter(blocks_of(done[hops][name]))
+            if run is not None:
+                here = here + net.along_z(run).astype(jnp.float32)
+            run = here.astype(jnp.bfloat16)
+        return here
+
+    d_gate_all = jnp.zeros((ring, length), jnp.float32)
+    for hops in range(ring):
+        d_gate_all = lax.dynamic_update_slice(
+            d_gate_all, done[hops]["d_gate_token"], (net.chip(hops), 0)
+        )
+    d_gate_all = lax.all_gather(d_gate_all, ("rows", "cols"), axis=0, tiled=False)
+    d_gate_all = index(d_gate_all.reshape(experts, 2, ring, length), k, 1, False)
+    grad_router = jnp.zeros((row_width, experts), jnp.float32)
+    d_logits_own = None
+    for hops in range(ring):
+        gate_probs = done[hops]["gate_probs"]
+        d_gates = index(d_gate_all, net.chip(hops), 1, False).T
+        d_logits = gate_probs * (d_gates - jnp.sum(gate_probs * d_gates, -1, keepdims=True))
+        if hops == 0:
+            d_logits_own = d_logits
+        quarter = lax.dynamic_slice_in_dim(done[hops]["rows"], r * rows_dev, rows_dev, 0)
+        quarter = lax.switch(
+            r ^ z,
+            [
+                lambda rows, j=j: rows[:, j * row_width : (j + 1) * row_width]
+                for j in range(n_rows)
+            ],
+            quarter,
+        )
+        d_quarter = lax.dynamic_slice_in_dim(d_logits, r * rows_dev, rows_dev, 0)
+        high, low = split_terms(d_quarter)
+        both = matmul_tn(quarter, jnp.concatenate([high, low], 1))
+        grad_router = grad_router + both[:, :experts] + both[:, experts:]
+    grad_router = grad_router.reshape(2, col_width, experts)
+    g_router = index(grad_router, k, 0, False) + net.sibling(index(grad_router, 1 - k, 0, False))
+    g_router = g_router + net.along_x(g_router)
+    g_router = g_router + net.along_y(g_router)
+    high, low = split_terms(d_logits_own)
+    d_router_in = matmul_nt(
+        jnp.concatenate([high, low], 1), jnp.concatenate([router_full, router_full], 1)
+    )
+
+    d_second_mine = ring_scatter("d_rows").astype(jnp.bfloat16)
+    d_second = jnp.concatenate(net.rows_gather(d_second_mine), 1).astype(jnp.float32)
+    d_second = d_second + d_router_in
+    d_second_unit = d_second * second_gain
+    second_gain_grad = jnp.sum((d_second * second_unit)[:, :row_width], 0)
+    d_resid = done[0]["grad_rows"].astype(jnp.float32) + second_inverse * (
+        d_second_unit
+        - second_unit * jnp.mean(d_second_unit * second_unit, -1, keepdims=True)
+    )
+    d_attn = d_resid.astype(jnp.bfloat16)
+
+    d_heads = matmul(d_attn, weights_out_t).astype(jnp.bfloat16)
+    delta = jnp.sum(
+        (d_heads.astype(jnp.float32) * attn_f32).reshape(length, q_heads, HEAD_DIM), -1
+    ).T[:, None, :]
+    d_query, d_kv_all = attention_backward(
+        block_no, queries, keys_all, keys_all.T, values_all, d_heads, log_total, delta
+    )
+    d_kv = net.cols_scatter(d_kv_all.reshape(ring, 2, length, 2 * HEAD_DIM), net.chip)
+    d_rotated = jnp.concatenate([d_query, d_kv[:, :HEAD_DIM]], 1).reshape(length, -1, HEAD_DIM)
+    d_rotated = apply_rotary(d_rotated, cosine_table, -sine_table).reshape(length, -1)
+    d_projected = jnp.concatenate([d_rotated, d_kv[:, HEAD_DIM:]], 1).astype(jnp.bfloat16)
+    d_first = matmul_nt(d_projected, weights_in).astype(jnp.bfloat16)
+    d_first = net.rows_scatter(blocks_of(d_first))
+    unit_mine = first_unit[:, :row_width]
+    d_first_unit = d_first * first_gain[:, :row_width]
+    moment = jnp.sum(d_first_unit * unit_mine, -1).reshape(-1, 128)
+    moment = moment + net.along_x(moment)
+    moment = moment + net.along_y(moment)
+    moment = moment.reshape(length, 1) / model_width
+    grad_in = d_resid[:, :row_width] + first_inverse * (d_first_unit - unit_mine * moment)
+    first_gain_grad = jnp.sum(d_first * unit_mine, 0)
+    gain_grads = jnp.stack([first_gain_grad, second_gain_grad])
+    gain_grads = gain_grads + net.sibling(gain_grads)
+    bit = 1
+    while bit < ring:
+        gain_grads = gain_grads + net.across_z(gain_grads, bit)
+        bit *= 2
+    gain_grads = jnp.stack([gain_grads, net.along_x(gain_grads)])
+    gain_grads = jnp.concatenate([gain_grads, net.along_y(gain_grads)])
+    gain_grads = index(gain_grads, r ^ z, 0, False).reshape(2, 2, col_width)
+    gain_grads = index(gain_grads, k, 1, False)
+
+    column_parts = lambda whole: whole.astype(jnp.bfloat16).reshape(ring, 2, col_width, -1)
+    g_in = net.cols_scatter(column_parts(matmul_tn(first_normed, d_projected)), net.place)
+    g_out = net.cols_scatter(column_parts(matmul_tn(d_attn, attn_rows)), net.place).T
+    joined = lambda name: jnp.concatenate([part[name] for part in done], 0)
+    slot_rows, e_act = joined("slot_rows"), joined("e_act")
+    d_e_gate, d_e_up, d_part = joined("d_e_gate"), joined("d_e_up"), joined("d_part")
+
+    def halves(left, right, axis):
+        whole_width = half_hidden
+        own = lambda v: v[:, :whole_width]
+        other = lambda v: v[:, whole_width:]
+        if axis == 0:
+            mine = matmul_tn(left, own(right))
+            sent = matmul_tn(left, other(right)).astype(jnp.bfloat16)
+        else:
+            mine = matmul_tn(own(left), right)
+            sent = matmul_tn(other(left), right).astype(jnp.bfloat16)
+        return net.mixed(mine + net.sibling(sent).astype(jnp.float32), axis)[None]
+
+    g_expert_gate = halves(slot_rows, d_e_gate, 0)
+    g_expert_up = halves(slot_rows, d_e_up, 0)
+    g_expert_down = halves(e_act, d_part, 1)
+
+    rows_all, grads_all = joined("rows"), joined("grad_rows")
+    shared_parts = jnp.concatenate(
+        [matmul_tn(rows_all, joined("d_shared")), matmul_tn(grads_all, joined("s_act"))], 1
+    )
+    shared_parts = net.pair_sum(column_parts(shared_parts))
+    g_shared = jnp.zeros(shared_parts.shape, jnp.bfloat16)
+    for hops in range(ring):
+        piece = index(shared_parts, net.place(-hops), 0, False)
+        piece = net.along_z(piece, hops) if hops else piece
+        g_shared = lax.dynamic_update_slice(g_shared, piece[None], (net.chip(hops), 0, 0))
+    g_shared = g_shared.astype(jnp.float32)
+    shared_cols = lambda n: jnp.swapaxes(
+        g_shared[:, :, n * shared_hidden : (n + 1) * shared_hidden], 0, 1
+    ).reshape(col_width, -1)
+
+    out_mine = ring_scatter("out_rows")
+    layer_out = (residual[:, :row_width] + out_mine).astype(jnp.bfloat16)
+    return (
+        layer_out[None],
+        grad_in[None],
+        gain_grads[0],
+        g_in[:, :q_width],
+        g_in[:, q_width : q_width + kv_width],
+        g_in[:, q_width + kv_width :],
+        g_out,
+        gain_grads[1],
+        g_router,
+        shared_cols(0),
+        shared_cols(1),
+        shared_cols(2).T,
+        g_expert_gate,
+        g_expert_up,
+        g_expert_down,
+    )
+
+
+def per_device(layer_in, *others):
+    routes = others[13]
+    w_router = others[6]
+    n_rows, n_cols = lax.axis_size("rows"), lax.axis_size("cols")
+    experts, top_k = w_router.shape[1], routes.shape[3]
+    gathers = (
+        experts <= 4 * top_k
+        and layer_in.shape[0] == 1
+        and n_rows == 4
+        and n_cols == 2 * n_rows
+        and 2 * experts == n_rows * n_cols
+    )
+    return (gathered_layer if gathers else routed_layer)(layer_in, *others)
+
+
 def solution(mesh):
     placed = (
         P(None, "cols", "rows"),

time: 2330 us -> 1500 us (0.64)
  waiting for transfers between devices: 1150 us -> 346 us
  blocking collectives: 378 us -> 132 us
  starting transfers between devices: 26.2 us -> 213 us
  other arithmetic: 173 us -> 255 us
  local copies, waits for them, and re-layouts: 255 us -> 192 us
  Pallas kernels: 0 us -> 37.9 us
    all_to_all x3 -> x0, waiting for transfers between devices: 427 us -> none  [the longest x2 238 us: return_rows(): lax.all_to_all(slot_vals.reshape(devices, capacity, model_width), ('rows'...]
    ppermute x0 -> x152, waiting for transfers between devices: none -> 346 us  [move(): return lax.ppermute(values, ('rows', 'cols'), pairs)]
    reduce_scatter x8 -> x0, waiting for transfers between devices: 284 us -> none  [the longest x1 46 us: per_device(): lax.psum_scatter(grad_su.astype(jnp.bfloat16), 'cols', scatter_dimension=...]
    all_to_all x1 -> x0, blocking collectives: 231 us -> none  [send_rows(): lax.all_to_all(outgoing, ('rows', 'cols'), split_axis=0, concat_axis=0, t...]
    all_gather x8 -> x0, waiting for transfers between devices: 226 us -> none  [the longest x1 117 us: per_device(): lax.all_gather(shared_down, 'cols', axis=1, tiled=True)]
    ppermute x0 -> x152, starting transfers between devices: none -> 213 us  [move(): return lax.ppermute(values, ('rows', 'cols'), pairs)]
    psum x3 -> x0, waiting for transfers between devices: 197 us -> none  [the longest x1 81 us: per_device(): lax.psum(grad_first_normed.astype(jnp.bfloat16), 'rows').astype(jnp.float32)]
    concatenate x1 -> x23, other arithmetic: 0.72 us -> 84.8 us  [the longest x3 28.7 us: gathered_layer(): rows = jnp.concatenate(net.rows_gather(normed_block), 1)]
  transfers between devices with their start and end apart: 24 -> 152, of which waited for: 19 -> 63; matrix products, arithmetic and copies ran while one was open for 17% -> 34% of each run, Pallas kernels for 0% -> 3%
where the time goes in v1:
time: 1500 us; the launch traced here: 1480 us
  waiting for transfers between devices  346 us (23%)
  matrix products  299 us (20%)
  other arithmetic  255 us (17%)
  starting transfers between devices  213 us (14%)
  local copies, waits for them, and re-layouts  192 us (13%)
  blocking collectives  132 us (9%)
  Pallas kernels  37.9 us (3%)
    ppermute x152, waiting for transfers between devices, move(): return lax.ppermute(values, ('rows', 'cols'), pairs)  346 us
    ppermute x152, starting transfers between devices, move(): return lax.ppermute(values, ('rows', 'cols'), pairs)  213 us
    dot_general x14, matrix products, matmul_tn(): lax.dot_general(left_op, right_op, (((0,), (0,)), ((), ())), preferred_el...  139 us
    dot_general x22, matrix products, matmul(): return jnp.dot(left_op, right_op, preferred_element_type=jnp.float32)  72.3 us
    all_gather x1, blocking collectives, gathered_layer(): slot_maps = lax.all_gather(slot_map, ('cols', 'rows'), axis=0, tiled=False)  66.3 us
    dot_general x23, matrix products, matmul_nt(): lax.dot_general(left_op, right_op, (((1,), (1,)), ((), ())), preferred_el...  64.1 us
    unnamed x581, local copies, waits for them, and re-layouts  48.4 us
    all_gather x1, blocking collectives, gathered_layer(): lax.all_gather(d_gate_all, ('rows', 'cols'), axis=0, tiled=False)  37.7 us
  transfers between devices with their start and end apart: 152, of which 63 were waited for; matrix products, arithmetic and copies ran while one was open for 34% of the time, Pallas kernels for 3%

profile of v1, /device:TPU:18, one launch (start us, length us, event | category | flops | bytes accessed | tf_op | source)
XLA Modules:
  0.0 1481.4 jit_solution(17891566347156476243)
XLA Ops:
  14.8 66.3 %all-gather = f32[512,128]{1,0:T(8,128)S(1)} all-gather(f32[16,128]{1,0:T(8,128)S(1)} %convolution_select_fusion), channel_id=2, replica_groups=mesh['rows'=4,'cols'=8] {'cols','rows'}, dimensions={0}, use_global_device_ids=true | all-gather | bytes 270336 | tf_op jit(solution)/shard_map/all_gather | solution.py:803
  81.2 28.1 %all_gather.35 = bf16[2560,128]{1,0:T(8,128)(2,1)S(1)} all-gather(bf16[320,128]{1,0:T(8,128)(2,1)S(1)} %pad.4), channel_id=1, replica_groups=mesh['rows'=4,'cols'=8] {'cols'}, dimensions={0}, use_global_device_ids=true | all-gather | bytes 737280 | tf_op jit(solution)/shard_map/all_gather | solution.py:809
  160.0 12.7 collective-permute-start.85
  178.7 18.0 %collective-permute-done.21 = bf16[320,640]{1,0:T(8,128)(2,1)S(1)} collective-permute-done((bf16[320,640]{1,0:T(8,128)(2,1)}, bf16[320,640]{1,0:T(8,128)(2,1)S(1)}, u32[]{:S(2)}, u32[]{:S(2)}) %collective-permute-start.21) | collective-permute-done | bytes 409632 | tf_op jit(solution)/shard_map/ppermute | solution.py:671
  223.3 11.8 collective-permute-done.9
  295.2 18.4 %attention_forward.1 = (f32[512,640]{1,0:T(8,128)S(1)}, f32[5,1,512]{2,1,0:T(1,128)S(1)}) custom-call(s32[1]{0:T(128)} %bitcast.13.refs_0_, bf16[512,640]{1,0:T(8,128)(2,1)S(1)} %copy.183.refs_1_, bf16[4096,128]{1,0:T(8,128)(2,1)S(1)} %get-tuple-element.432.refs_2_, bf16[128,4096]{1,0:T(8,128)(2,1)S(1)} %copy.184.refs_3_), custom_call_target="tpu_custom_call" | custom-call | flops 5368709120 | bytes 4063232 | tf_op jit(solution)/shard_map/attention_forward/pallas_call | solution.py:526
  318.4 10.8 collective-permute-start.87
  491.0 17.1 %collective-permute-start.66 = (bf16[512,640]{1,0:T(8,128)(2,1)}, bf16[512,640]{1,0:T(8,128)(2,1)}, u32[]{:S(2)}, u32[]{:S(2)}) collective-permute-start(bf16[512,640]{1,0:T(8,128)(2,1)} %collective-permute-done.47), channel_id=1, source_target_pairs={{0,8},{1,9},{2,10},{3,11},{4,12},{5,13},{6,14},{7,15},{8,0},{9,1},... | collective-permute-start | bytes 1966088 | tf_op jit(solution)/shard_map/ppermute | solution.py:671
  634.8 37.7 %all_gather.43 = f32[32,4,512]{2,1,0:T(4,128)S(1)} all-gather(f32[1,4,512]{2,1,0:T(4,128)S(1)} %dynamic_update_slice.159), channel_id=1, replica_groups=mesh['rows'=4,'cols'=8] {'rows','cols'}, dimensions={0}, use_global_device_ids=true | all-gather | bytes 270336 | tf_op jit(solution)/shard_map/all_gather | solution.py:973
  776.8 63.3 %fusion.91 = bf16[2560,192]{0,1:T(8,128)(2,1)} fusion(bf16[256,640]{1,0:T(8,128)(2,1)} %copy-done.194, bf16[256,640]{1,0:T(8,128)(2,1)} %copy-done.195, bf16[512,640]{1,0:T(8,128)(2,1)} %copy-done.116, bf16[512,640]{1,0:T(8,128)(2,1)} %copy-done.117, bf16[512,640]{1,0:T(8,128)(2,1)} %copy-done.172, bf16[256,640]{1,0:T(8,128)(2,1)S(1)} %copy-done.192, ...), kind=kOutput, calls=%fused_computation.162 | convolution fusion | flops 2216132608 | bytes 12255232 | tf_op jit(solution)/shard_map/dot_general | solution.py:42
  902.0 10.5 fusion.510
  920.9 26.2 %fusion.80 = bf16[2560,384]{1,0:T(8,128)(2,1)S(1)} fusion(bf16[256,640]{1,0:T(8,128)(2,1)} %copy-done.200, bf16[256,640]{1,0:T(8,128)(2,1)} %copy-done.201, bf16[512,640]{1,0:T(8,128)(2,1)} %collective-permute-done.51, bf16[512,640]{1,0:T(8,128)(2,1)} %collective-permute-done.50, bf16[512,640]{1,0:T(8,128)(2,1)} %collective-permute-done.49, ...), kind=kOutput, calls=%fused_computation.135 | convolution fusion | flops 4195287040 | bytes 14024704 | tf_op jit(solution)/shard_map/dot_general | solution.py:42
  966.9 11.7 collective-permute-done.70
  980.1 12.5 collective-permute-done.100
  1010.7 16.0 %collective-permute-done.101 = bf16[256,640]{1,0:T(8,128)(2,1)S(1)} collective-permute-done((bf16[256,640]{1,0:T(8,128)(2,1)S(1)}, bf16[256,640]{1,0:T(8,128)(2,1)S(1)}, u32[]{:S(2)}, u32[]{:S(2)}) %collective-permute-start.101) | collective-permute-done | bytes 327712 | tf_op jit(solution)/shard_map/ppermute | solution.py:671
  1062.4 29.2 %collective-permute-done.55 = bf16[256,640]{1,0:T(8,128)(2,1)S(1)} collective-permute-done((bf16[256,640]{1,0:T(8,128)(2,1)S(1)}, bf16[256,640]{1,0:T(8,128)(2,1)S(1)}, u32[]{:S(2)}, u32[]{:S(2)}) %collective-permute-start.55) | collective-permute-done | bytes 327712 | tf_op jit(solution)/shard_map/ppermute | solution.py:671
  1107.1 15.6 %collective-permute-done.44 = bf16[256,640]{1,0:T(8,128)(2,1)S(1)} collective-permute-done((bf16[256,640]{1,0:T(8,128)(2,1)S(1)}, bf16[256,640]{1,0:T(8,128)(2,1)S(1)}, u32[]{:S(2)}, u32[]{:S(2)}) %collective-permute-start.44) | collective-permute-done | bytes 327712 | tf_op jit(solution)/shard_map/ppermute | solution.py:671
  1146.6 11.2 collective-permute-done.118
  1179.8 19.5 %attention_backward.1 = (f32[512,640]{1,0:T(8,128)S(1)}, bf16[4096,256]{1,0:T(8,128)(2,1)}) custom-call(s32[1]{0:T(128)} %bitcast.13.refs_0_, bf16[512,640]{1,0:T(8,128)(2,1)S(1)} %copy-done.7, bf16[4096,128]{1,0:T(8,128)(2,1)S(1)} %copy-done.5, bf16[128,4096]{1,0:T(8,128)(2,1)S(1)} %copy-done.2, bf16[4096,128]{1,0:T(8,128)(2,1)S(1)} %copy-done.3, ...), custom_call_target="tpu_custom_call" | custom-call | flops 13421772800 | bytes 8912896 | tf_op jit(solution)/shard_map/attention_backward/pallas_call | solution.py:617
  1209.0 11.6 collective-permute-start.147
  1233.8 33.4 %collective-permute-done.147 = bf16[320,576]{1,0:T(8,128)(2,1)} collective-permute-done((bf16[320,576]{1,0:T(8,128)(2,1)}, bf16[320,576]{1,0:T(8,128)(2,1)}, u32[]{:S(2)}, u32[]{:S(2)}) %collective-permute-start.147) | collective-permute-done | bytes 368672 | tf_op jit(solution)/shard_map/ppermute | solution.py:671
  1365.9 16.2 %conditional.21 = (f32[1,768,2560]{2,1,0:T(8,128)}) conditional(s32[]{:T(128)} %clamp.127, (f32[768,2560]{1,0:T(8,128)}, f32[768,2560]{1,0:T(8,128)S(1)}) %tuple.166, (f32[768,2560]{1,0:T(8,128)}, f32[768,2560]{1,0:T(8,128)S(1)}) %tuple.166, (f32[768,2560]{1,0:T(8,128)}, f32[768,2560]{1,0:T(8,128)S(1)}) %tuple.166, ...), branch_computations={%region_76.77_spmd, %region_77.78_spmd, %region_78.79_spmd, %regio... | conditional | flops 7864320 | bytes 55050248 | solution.py:706
  1384.9 15.1 %conditional.20 = (f32[1,2560,768]{2,1,0:T(8,128)}) conditional(s32[]{:T(128)} %clamp.127, (f32[2560,768]{1,0:T(8,128)}, f32[2560,768]{1,0:T(8,128)S(1)}) %tuple.165, (f32[2560,768]{1,0:T(8,128)}, f32[2560,768]{1,0:T(8,128)S(1)}) %tuple.165, (f32[2560,768]{1,0:T(8,128)}, f32[2560,768]{1,0:T(8,128)S(1)}) %tuple.165, ...), branch_computations={%region_72.73_spmd, %region_73.74_spmd, %region_74.75_spmd, %regio... | conditional | flops 7864320 | bytes 55050248 | solution.py:706
  1402.7 15.0 %conditional.19 = (f32[1,2560,768]{2,1,0:T(8,128)}) conditional(s32[]{:T(128)} %clamp.127, (f32[2560,768]{1,0:T(8,128)}, f32[2560,768]{1,0:T(8,128)S(1)}) %tuple.164, (f32[2560,768]{1,0:T(8,128)}, f32[2560,768]{1,0:T(8,128)S(1)}) %tuple.164, (f32[2560,768]{1,0:T(8,128)}, f32[2560,768]{1,0:T(8,128)S(1)}) %tuple.164, ...), branch_computations={%region_68.69_spmd, %region_69.70_spmd, %region_70.71_spmd, %regio... | conditional | flops 7864320 | bytes 55050248 | solution.py:706
  (1300 shorter events, 1017.6 us)
Async XLA Ops:
  0.7 133.3 %collective-permute-start.18 = (bf16[320,640]{1,0:T(8,128)(2,1)}, bf16[320,640]{1,0:T(8,128)(2,1)}, u32[]{:S(2)}, u32[]{:S(2)}) collective-permute-start(bf16[320,640]{1,0:T(8,128)(2,1)} %bitcast.912), channel_id=1, source_target_pairs={{0,1},{1,0},{2,3},{3,2},{4,5},{5,4},{6,7},{7,6},{8,9},{9,8},{10,11... | collective-permute-start | bytes 1228808 | tf_op jit(solution)/shard_map/ppermute | solution.py:671
  0.7 137.0 %collective-permute-start.19 = (bf16[320,640]{1,0:T(8,128)(2,1)}, bf16[320,640]{1,0:T(8,128)(2,1)}, u32[]{:S(2)}, u32[]{:S(2)}) collective-permute-start(bf16[320,640]{1,0:T(8,128)(2,1)} %bitcast.913), channel_id=1, source_target_pairs={{0,2},{1,3},{2,4},{3,5},{4,6},{5,7},{6,0},{7,1},{8,10},{9,11},{10,... | collective-permute-start | bytes 1228808 | tf_op jit(solution)/shard_map/ppermute | solution.py:671
  7.2 132.5 %collective-permute-start.5 = (bf16[320,896]{1,0:T(8,128)(2,1)}, bf16[320,896]{1,0:T(8,128)(2,1)}, u32[]{:S(2)}, u32[]{:S(2)}) collective-permute-start(bf16[320,896]{1,0:T(8,128)(2,1)} %constant_dynamic-update-slice_fusion.6), channel_id=1, source_target_pairs={{0,2},{1,3},{2,4},{3,5},{4,6},{5,7},{6,0},{7,1},{8,10},{9,11},{10,... | collective-permute-start | bytes 1720328 | tf_op jit(solution)/shard_map/ppermute | solution.py:671
  11.7 122.2 %collective-permute-start.37 = (bf16[320,576]{1,0:T(8,128)(2,1)}, bf16[320,576]{1,0:T(8,128)(2,1)}, u32[]{:S(2)}, u32[]{:S(2)}) collective-permute-start(bf16[320,576]{1,0:T(8,128)(2,1)} %bitcast.80), channel_id=1, source_target_pairs={{0,2},{1,3},{2,4},{3,5},{4,6},{5,7},{6,0},{7,1},{8,10},{9,11},{10,... | collective-permute-start | bytes 1105928 | tf_op jit(solution)/shard_map/ppermute | solution.py:671
  14.3 118.2 %collective-permute-start.36 = (bf16[320,576]{1,0:T(8,128)(2,1)}, bf16[320,576]{1,0:T(8,128)(2,1)}, u32[]{:S(2)}, u32[]{:S(2)}) collective-permute-start(bf16[320,576]{1,0:T(8,128)(2,1)} %bitcast.78), channel_id=1, source_target_pairs={{0,1},{1,0},{2,3},{3,2},{4,5},{5,4},{6,7},{7,6},{8,9},{9,8},{10,11... | collective-permute-start | bytes 1105928 | tf_op jit(solution)/shard_map/ppermute | solution.py:671
  223.3 175.4 %collective-permute-start.33 = (bf16[2560,768]{1,0:T(8,128)(2,1)}, bf16[2560,768]{1,0:T(8,128)(2,1)}, u32[]{:S(2)}, u32[]{:S(2)}) collective-permute-start(bf16[2560,768]{1,0:T(8,128)(2,1)} %bitcast.68), channel_id=1, source_target_pairs={{0,1},{1,0},{2,3},{3,2},{4,5},{5,4},{6,7},{7,6},{8,9},{9,8},{10,11... | collective-permute-start | bytes 11796488 | tf_op jit(solution)/shard_map/ppermute | solution.py:671
  241.5 76.8 %collective-permute-start.107 = (bf16[256,640]{1,0:T(8,128)(2,1)}, bf16[256,640]{1,0:T(8,128)(2,1)}, u32[]{:S(2)}, u32[]{:S(2)}) collective-permute-start(bf16[256,640]{1,0:T(8,128)(2,1)} %slice.1409), channel_id=1, source_target_pairs={{0,8},{1,9},{2,10},{3,11},{4,12},{5,13},{6,14},{7,15},{8,0},{9,1},... | collective-permute-start | bytes 983048 | tf_op jit(solution)/shard_map/ppermute | solution.py:671
  333.5 76.0 %collective-permute-start.34 = (bf16[2560,768]{1,0:T(8,128)(2,1)}, bf16[2560,768]{1,0:T(8,128)(2,1)}, u32[]{:S(2)}, u32[]{:S(2)}) collective-permute-start(bf16[2560,768]{1,0:T(8,128)(2,1)} %bitcast.69), channel_id=1, source_target_pairs={{0,1},{1,0},{2,3},{3,2},{4,5},{5,4},{6,7},{7,6},{8,9},{9,8},{10,11... | collective-permute-start | bytes 11796488 | tf_op jit(solution)/shard_map/ppermute | solution.py:671
  365.0 61.1 %collective-permute-start.35 = (bf16[768,2560]{1,0:T(8,128)(2,1)}, bf16[768,2560]{1,0:T(8,128)(2,1)}, u32[]{:S(2)}, u32[]{:S(2)}) collective-permute-start(bf16[768,2560]{1,0:T(8,128)(2,1)} %bitcast.70), channel_id=1, source_target_pairs={{0,1},{1,0},{2,3},{3,2},{4,5},{5,4},{6,7},{7,6},{8,9},{9,8},{10,11... | collective-permute-start | bytes 11796488 | tf_op jit(solution)/shard_map/ppermute | solution.py:671
  852.8 98.9 %collective-permute-start.142 = (f32[320,16]{0,1:T(8,128)S(1)}, f32[320,16]{0,1:T(8,128)S(1)}, u32[]{:S(2)}, u32[]{:S(2)}) collective-permute-start(f32[320,16]{0,1:T(8,128)S(1)} %bitcast.932), channel_id=1, source_target_pairs={{0,1},{1,0},{2,3},{3,2},{4,5},{5,4},{6,7},{7,6},{8,9},{9,8},{10,11... | collective-permute-start | bytes 61448 | tf_op jit(solution)/shard_map/ppermute | solution.py:671
  871.7 159.9 %collective-permute-start.94 = (bf16[2,256,640]{2,1,0:T(8,128)(2,1)}, bf16[2,256,640]{2,1,0:T(8,128)(2,1)}, u32[]{:S(2)}, u32[]{:S(2)}) collective-permute-start(bf16[2,256,640]{2,1,0:T(8,128)(2,1)} %pad_maximum_fusion.44), channel_id=1, source_target_pairs={{0,16},{1,17},{2,18},{3,19},{4,20},{5,21},{6,22},{7,23},{8,24},{9,... | collective-permute-start | bytes 1966088 | tf_op jit(solution)/shard_map/ppermute | solution.py:671
  873.3 87.6 %collective-permute-start.92 = (bf16[2,256,640]{2,1,0:T(8,128)(2,1)}, bf16[2,256,640]{2,1,0:T(8,128)(2,1)}, u32[]{:S(2)}, u32[]{:S(2)}) collective-permute-start(bf16[2,256,640]{2,1,0:T(8,128)(2,1)} %pad_maximum_fusion.43), channel_id=1, source_target_pairs={{0,8},{1,9},{2,10},{3,11},{4,12},{5,13},{6,14},{7,15},{8,0},{9,1},... | collective-permute-start | bytes 1966088 | tf_op jit(solution)/shard_map/ppermute | solution.py:671
  880.3 82.1 %collective-permute-start.54 = (bf16[2,256,640]{2,1,0:T(8,128)(2,1)}, bf16[2,256,640]{2,1,0:T(8,128)(2,1)}, u32[]{:S(2)}, u32[]{:S(2)}) collective-permute-start(bf16[2,256,640]{2,1,0:T(8,128)(2,1)} %pad_maximum_fusion.34), channel_id=1, source_target_pairs={{0,8},{1,9},{2,10},{3,11},{4,12},{5,13},{6,14},{7,15},{8,0},{9,1},... | collective-permute-start | bytes 1966088 | tf_op jit(solution)/shard_map/ppermute | solution.py:671
  885.8 79.4 %collective-permute-start.108 = (bf16[2,256,640]{2,1,0:T(8,128)(2,1)}, bf16[2,256,640]{2,1,0:T(8,128)(2,1)}, u32[]{:S(2)}, u32[]{:S(2)}) collective-permute-start(bf16[2,256,640]{2,1,0:T(8,128)(2,1)} %pad_maximum_fusion.47), channel_id=1, source_target_pairs={{0,8},{1,9},{2,10},{3,11},{4,12},{5,13},{6,14},{7,15},{8,0},{9,1},... | collective-permute-start | bytes 1966088 | tf_op jit(solution)/shard_map/ppermute | solution.py:671
  994.2 67.1 %collective-permute-start.56 = (bf16[2,256,640]{2,1,0:T(8,128)(2,1)S(1)}, bf16[2,256,640]{2,1,0:T(8,128)(2,1)S(1)}, u32[]{:S(2)}, u32[]{:S(2)}) collective-permute-start(bf16[2,256,640]{2,1,0:T(8,128)(2,1)S(1)} %pad_maximum_fusion.35), channel_id=1, source_target_pairs={{0,16},{1,17},{2,18},{3,19},{4,20},{5,21},{6,22},{7,23},{8,24},{9,... | collective-permute-start | bytes 1966088 | tf_op jit(solution)/shard_map/ppermute | solution.py:671
  1126.0 79.7 %collective-permute-start.145 = (bf16[4,320,576]{2,1,0:T(8,128)(2,1)}, bf16[4,320,576]{2,1,0:T(8,128)(2,1)}, u32[]{:S(2)}, u32[]{:S(2)}) collective-permute-start(bf16[4,320,576]{2,1,0:T(8,128)(2,1)} %fusion.121), channel_id=1, source_target_pairs={{0,1},{1,0},{2,3},{3,2},{4,5},{5,4},{6,7},{7,6},{8,9},{9,8},{10,11... | collective-permute-start | bytes 4423688 | tf_op jit(solution)/shard_map/ppermute | solution.py:671
  1129.8 72.0 %collective-permute-start.46 = (bf16[256,640]{1,0:T(8,128)(2,1)}, bf16[256,640]{1,0:T(8,128)(2,1)}, u32[]{:S(2)}, u32[]{:S(2)}) collective-permute-start(bf16[256,640]{1,0:T(8,128)(2,1)} %get-tuple-element.401), channel_id=1, source_target_pairs={{0,8},{1,9},{2,10},{3,11},{4,12},{5,13},{6,14},{7,15},{8,0},{9,1},... | collective-permute-start | bytes 983048 | tf_op jit(solution)/shard_map/ppermute | solution.py:671
  1157.9 64.8 %collective-permute-start.74 = (bf16[512,640]{1,0:T(8,128)(2,1)}, bf16[512,640]{1,0:T(8,128)(2,1)}, u32[]{:S(2)}, u32[]{:S(2)}) collective-permute-start(bf16[512,640]{1,0:T(8,128)(2,1)} %pad_maximum_fusion.40), channel_id=1, source_target_pairs={{0,2},{1,3},{2,4},{3,5},{4,6},{5,7},{6,0},{7,1},{8,10},{9,11},{10,... | collective-permute-start | bytes 1966088 | tf_op jit(solution)/shard_map/ppermute | solution.py:671
  1231.9 127.3 %collective-permute-start.151 = (bf16[768,2560]{1,0:T(8,128)(2,1)}, bf16[768,2560]{1,0:T(8,128)(2,1)}, u32[]{:S(2)}, u32[]{:S(2)}) collective-permute-start(bf16[768,2560]{1,0:T(8,128)(2,1)} %convolution_convert_fusion.1), channel_id=1, source_target_pairs={{0,1},{1,0},{2,3},{3,2},{4,5},{5,4},{6,7},{7,6},{8,9},{9,8},{10,11... | collective-permute-start | bytes 11796488 | tf_op jit(solution)/shard_map/ppermute | solution.py:671
  1267.2 132.8 %collective-permute-start.149 = (bf16[2560,768]{1,0:T(8,128)(2,1)}, bf16[2560,768]{1,0:T(8,128)(2,1)}, u32[]{:S(2)}, u32[]{:S(2)}) collective-permute-start(bf16[2560,768]{1,0:T(8,128)(2,1)} %convolution_convert_fusion.3), channel_id=1, source_target_pairs={{0,1},{1,0},{2,3},{3,2},{4,5},{5,4},{6,7},{7,6},{8,9},{9,8},{10,11... | collective-permute-start | bytes 11796488 | tf_op jit(solution)/shard_map/ppermute | solution.py:671
  1269.1 113.0 %collective-permute-start.150 = (bf16[2560,768]{1,0:T(8,128)(2,1)}, bf16[2560,768]{1,0:T(8,128)(2,1)}, u32[]{:S(2)}, u32[]{:S(2)}) collective-permute-start(bf16[2560,768]{1,0:T(8,128)(2,1)} %convolution_convert_fusion.2), channel_id=1, source_target_pairs={{0,1},{1,0},{2,3},{3,2},{4,5},{5,4},{6,7},{7,6},{8,9},{9,8},{10,11... | collective-permute-start | bytes 11796488 | tf_op jit(solution)/shard_map/ppermute | solution.py:671
  1337.7 89.5 %collective-permute-start.134 = (bf16[4,320,896]{2,1,0:T(8,128)(2,1)}, bf16[4,320,896]{2,1,0:T(8,128)(2,1)}, u32[]{:S(2)}, u32[]{:S(2)}) collective-permute-start(bf16[4,320,896]{2,1,0:T(8,128)(2,1)} %dynamic-slice_bitcast_fusion), channel_id=1, source_target_pairs={{0,1},{1,0},{2,3},{3,2},{4,5},{5,4},{6,7},{7,6},{8,9},{9,8},{10,11... | collective-permute-start | bytes 6881288 | tf_op jit(solution)/shard_map/ppermute | solution.py:671
  1354.6 63.1 %collective-permute-start.139 = (bf16[320,640]{1,0:T(8,128)(2,1)}, bf16[320,640]{1,0:T(8,128)(2,1)}, u32[]{:S(2)}, u32[]{:S(2)}) collective-permute-start(bf16[320,640]{1,0:T(8,128)(2,1)} %dynamic-slice_bitcast_fusion.7), channel_id=1, source_target_pairs={{0,2},{1,3},{2,4},{3,5},{4,6},{5,7},{6,0},{7,1},{8,10},{9,11},{10,... | collective-permute-start | bytes 1228808 | tf_op jit(solution)/shard_map/ppermute | solution.py:671
  1359.1 64.2 %collective-permute-start.126 = (bf16[256,640]{1,0:T(8,128)(2,1)}, bf16[256,640]{1,0:T(8,128)(2,1)}, u32[]{:S(2)}, u32[]{:S(2)}) collective-permute-start(bf16[256,640]{1,0:T(8,128)(2,1)} %get-tuple-element.370), channel_id=1, source_target_pairs={{0,8},{1,9},{2,10},{3,11},{4,12},{5,13},{6,14},{7,15},{8,0},{9,1},... | collective-permute-start | bytes 983048 | tf_op jit(solution)/shard_map/ppermute | solution.py:671
  (409 other events, 6567.5 us)

commit v2 on v1

--- a/solution.py
+++ b/solution.py
@@ -485,76 +485,769 @@
     return query_pos >= key_pos
 
 
-def attention_forward_kernel(
-    scale, block_ref, q_ref, k_ref, vt_ref, out_ref, lse_ref, top, total, acc
-):
-    length = q_ref.shape[0]
-    own = block_ref[0]
-    queries = q_ref[...]
-
-    def part(block):
-        start = pl.multiple_of(block * length, length)
-        scores = scores_of(k_ref[pl.ds(start, length), :], queries, scale)
-        return scores, vt_ref[:, pl.ds(start, length)]
-
-    scores, values_t = part(own)
-    scores = jnp.where(causal_mask(scores), scores, NEG_LARGE)
-    high = jnp.max(scores, 0, keepdims=True)
-    probs = jnp.exp(scores - high)
-    top[...] = high
-    total[...] = jnp.sum(probs, 0, keepdims=True)
-    acc[...] = matmul(values_t, probs.astype(jnp.bfloat16))
-
-    @pl.loop(0, own)
-    def _(block):
-        scores, values_t = part(block)
-        high = jnp.maximum(top[...], jnp.max(scores, 0, keepdims=True))
-        probs = jnp.exp(scores - high)
-        shrink = jnp.exp(top[...] - high)
-        top[...] = high
-        total[...] = total[...] * shrink + jnp.sum(probs, 0, keepdims=True)
-        acc[...] = acc[...] * shrink + matmul(values_t, probs.astype(jnp.bfloat16))
-
-    out_ref[...] = (acc[...] / total[...]).T
-    lse_ref[0] = top[...] + jnp.log(total[...])
-
-
-def attention_forward(block, queries, keys, values_t):
+MESH_ID = pl.DeviceIdType.MESH
+MIB = 1024 * 1024
+
+
+class Links:
+    def __init__(self, n_rows, n_cols):
+        self.n_rows, self.n_cols, self.ring = n_rows, n_cols, n_cols // 2
+        self.r = lax.axis_index("rows")
+        self.c = lax.axis_index("cols")
+        self.z = lax.div(self.c, 2)
+        self.k = lax.rem(self.c, 2)
+        self.x = (self.flip(1), self.c)
+        self.y = (self.flip(2), self.c)
+        self.up = (self.r, lax.rem(self.c + 2, n_cols))
+        self.down = (self.r, lax.rem(self.c + n_cols - 2, n_cols))
+        self.twin = (self.r, self.c + 1 - 2 * self.k)
+        self.started = []
+
+    def flip(self, bits):
+        low, high = lax.rem(self.r, 2), lax.div(self.r, 2)
+        low = 1 - low if bits & 1 else low
+        high = 1 - high if bits & 2 else high
+        return low + 2 * high
+
+    def chip(self, hops):
+        return lax.rem(self.z + (2 * self.ring - hops), self.ring)
+
+    def place(self, hops):
+        other = self.chip(hops)
+        low = lax.rem(lax.rem(self.r, 2) + lax.rem(other, 2), 2)
+        high = lax.rem(lax.div(self.r, 2) + lax.div(other, 2), 2)
+        return low + 2 * high
+
+    def spread_partners(self):
+        return [
+            (hops, bits, (self.flip(bits), lax.rem(self.c + 2 * hops, self.n_cols)))
+            for hops in range(self.ring)
+            for bits in range(self.n_rows)
+            if hops or bits
+        ]
+
+    def greet(self, partners):
+        barrier = pltpu.get_barrier_semaphore()
+        for partner in partners:
+            pl.semaphore_signal(barrier, inc=1, device_id=partner, device_id_type=MESH_ID)
+        pl.semaphore_wait(barrier, len(partners))
+
+    def send(self, src, dst, sems, number, partner):
+        copy = pltpu.make_async_remote_copy(
+            src_ref=src,
+            dst_ref=dst,
+            send_sem=sems[0].at[number],
+            recv_sem=sems[1].at[number],
+            device_id=partner,
+            device_id_type=MESH_ID,
+        )
+        copy.start()
+        self.started.append(copy)
+        return copy
+
+    def finish(self):
+        for copy in self.started:
+            copy.wait_send()
+
+
+def run_together(*steps):
+    live = list(steps)
+    while live:
+        live = [step for step in live if next(step, True) is None]
+
+
+def pair_sems(count):
+    return [pltpu.SemaphoreType.DMA((count,)), pltpu.SemaphoreType.DMA((count,))]
+
+
+def gather_square(net, src, out, sems, local_sem, chunks):
+    rows, width = src.shape
+    half = rows // 2
+
+    def block(s, j, part=None):
+        columns = pl.ds(j * width, width)
+        if part is None:
+            return out.at[s, :, columns]
+        return out.at[s, pl.ds(part * half, half), columns]
+
+    def part_of(s, part):
+        return src.at[pl.ds(part * half, half), :] if s == 0 else block(s, 0, part)
+
+    own = pltpu.make_async_copy(src, block(0, 0), local_sem)
+    own.start()
+    ups, xs, ys, lasts = [], [], [], []
+
+    def send_chunk(s):
+        if s < chunks - 1:
+            whole = src if s == 0 else block(s, 0)
+            ups.append(net.send(whole, block(s + 1, 0), sems, 7 * s, net.up))
+        xs.append([net.send(part_of(s, p), block(s, 1, p), sems, 7 * s + 1 + p, net.x) for p in (0, 1)])
+        ys.append(
+            [net.send(part_of(s, p), block(s, 2, p), sems, 7 * s + 3 + p, net.y) for p in (1, 0)][::-1]
+        )
+
+    def forward(s):
+        xs[s][0].wait_recv()
+        first = net.send(block(s, 1, 0), block(s, 3, 0), sems, 7 * s + 5, net.y)
+        ys[s][1].wait_recv()
+        second = net.send(block(s, 2, 1), block(s, 3, 1), sems, 7 * s + 6, net.x)
+        lasts.append([first, second])
+
+    send_chunk(0)
+    yield
+    for s in range(1, chunks):
+        ups[s - 1].wait_recv()
+        send_chunk(s)
+        yield
+        forward(s - 1)
+        yield
+    forward(chunks - 1)
+    yield
+    own.wait()
+    for s in range(chunks):
+        xs[s][1].wait_recv()
+        ys[s][0].wait_recv()
+        lasts[s][0].wait_recv()
+        lasts[s][1].wait_recv()
+
+
+def gather_columns(net, src, spot, sems, local_sem):
+    own = pltpu.make_async_copy(src, spot(0, net.k), local_sem)
+    own.start()
+    twins = []
+    for hops in range(net.ring):
+        if hops:
+            up.wait_recv()
+        here = src if hops == 0 else spot(hops, net.k)
+        if hops < net.ring - 1:
+            up = net.send(here, spot(hops, net.k), sems, hops, net.up)
+        twins.append(net.send(here, spot(hops, net.k), sems, net.ring + hops, net.twin))
+        yield
+    own.wait()
+    for copy in twins:
+        copy.wait_recv()
+
+
+def add_slabs(target, terms, slab=64):
+    rows = target.shape[0]
+
+    @pl.loop(0, rows // slab)
+    def _(i):
+        at = pl.ds(pl.multiple_of(i * slab, slab), slab)
+        total = terms[0](at)
+        for term in terms[1:]:
+            total = total + term(at)
+        target[at, :] = total.astype(target.dtype)
+
+
+def part_reader(ref, *lead, columns=None):
+    def read(at):
+        values = ref[(*lead, at, slice(None) if columns is None else columns)]
+        return values.astype(jnp.float32)
+
+    return read
+
+
+def scatter_scratch(chunks, rows, width):
+    half = rows // 2
+    return [
+        pltpu.VMEM((chunks, 2, half, width), jnp.bfloat16),
+        pltpu.VMEM((chunks, half, 2 * width), jnp.bfloat16),
+        pltpu.VMEM((chunks, 2, half, width), jnp.bfloat16),
+        pltpu.VMEM((chunks, half, 2 * width), jnp.bfloat16),
+        pltpu.VMEM((chunks, 2, half, width), jnp.bfloat16),
+        pltpu.VMEM((chunks, 2, half, width), jnp.bfloat16),
+        pltpu.SemaphoreType.DMA((chunks, 3)),
+    ] + pair_sems(5 * chunks)
+
+
+def scatter_square(net, src, scratch, order, finish):
+    my_up, my_low, got_x, got_y, got_last, stage, load_sems, *sems = scratch
+    half, width = my_up.shape[2:]
+    upper, lower = pl.ds(0, half), pl.ds(half, half)
+    column = lambda j, count=1: pl.ds(j * width, count * width)
+    left, right = pl.ds(0, width), pl.ds(width, width)
+    loads, sent = {}, {}
+
+    def first(s):
+        loads[s] = [
+            pltpu.make_async_copy(src.at[s, upper, column(0)], my_up.at[s, 0], load_sems.at[s, 0]),
+            pltpu.make_async_copy(src.at[s, upper, column(2)], my_up.at[s, 1], load_sems.at[s, 1]),
+            pltpu.make_async_copy(src.at[s, lower, column(0, 2)], my_low.at[s], load_sems.at[s, 2]),
+        ]
+        sent[s] = [
+            net.send(src.at[s, upper, column(3)], got_x.at[s, 1], sems, 5 * s, net.x),
+            net.send(src.at[s, lower, column(2, 2)], got_y.at[s], sems, 5 * s + 1, net.y),
+            net.send(src.at[s, upper, column(1)], got_x.at[s, 0], sems, 5 * s + 2, net.x),
+        ]
+        for load in loads[s]:
+            load.start()
+
+    def second(s):
+        loads[s][1].wait()
+        sent[s][0].wait_recv()
+        add_slabs(stage.at[s, 0], [part_reader(my_up, s, 1), part_reader(got_x, s, 1)])
+        sent[s].append(net.send(stage.at[s, 0], got_last.at[s, 0], sems, 5 * s + 3, net.y))
+        loads[s][2].wait()
+        sent[s][1].wait_recv()
+        add_slabs(
+            stage.at[s, 1],
+            [part_reader(my_low, s, columns=right), part_reader(got_y, s, columns=right)],
+        )
+        sent[s].append(net.send(stage.at[s, 1], got_last.at[s, 1], sems, 5 * s + 4, net.x))
+
+    def third(s):
+        loads[s][0].wait()
+        for copy in sent[s][2:]:
+            copy.wait_recv()
+        finish(
+            s,
+            [part_reader(my_up, s, 0), part_reader(got_x, s, 0), part_reader(got_last, s, 0)],
+            [
+                part_reader(my_low, s, columns=left),
+                part_reader(got_y, s, columns=left),
+                part_reader(got_last, s, 1),
+            ],
+        )
+
+    for i in range(len(order) + 2):
+        if i < len(order):
+            first(order[i])
+            yield
+        if 0 <= i - 1 < len(order):
+            second(order[i - 1])
+            yield
+        if 0 <= i - 2:
+            third(order[i - 2])
+            yield
+
+
+def ring_scratch(ring, rows, width):
+    return [
+        pltpu.VMEM((ring - 1, rows, width), jnp.bfloat16),
+        pltpu.VMEM((ring - 1, rows, width), jnp.bfloat16),
+    ] + pair_sems(ring - 1)
+
+
+def ring_finish(net, scratch, target):
+    landed, leaving, *sems = scratch
+    rows = landed.shape[1]
+    copies = []
+
+    def finish(s, upper, lower):
+        turn = (s - 1) % net.ring
+        for part, terms in ((0, upper), (1, lower)):
+            at = pl.ds(part * (rows // 2), rows // 2)
+            if turn and not part:
+                copies[turn - 1].wait_recv()
+            if turn:
+                terms = terms + [part_reader(landed.at[turn - 1, at, :])]
+            goal = target.at[at, :] if s == 0 else leaving.at[turn, at, :]
+            add_slabs(goal, terms)
+        if s:
+            copies.append(net.send(leaving.at[turn], landed.at[turn], sems, turn, net.up))
+
+    return finish
+
+
+def scatter_columns(net, src, out, scratch):
+    mine, got_twin, landed, leaving, load_sems, twin_send, twin_recv, *sems = scratch
+    loads, twins, copies = {}, {}, []
+    order = list(range(1, net.ring)) + [0]
+    for hops in order:
+        loads[hops] = pltpu.make_async_copy(
+            src.at[net.place(hops), net.k], mine.at[hops], load_sems.at[hops]
+        )
+        loads[hops].start()
+        twins[hops] = net.send(
+            src.at[net.place(hops), 1 - net.k],
+            got_twin.at[hops],
+            (twin_send, twin_recv),
+            hops,
+            net.twin,
+        )
+    yield
+    for turn, hops in enumerate(order):
+        loads[hops].wait()
+        twins[hops].wait_recv()
+        terms = [part_reader(mine, hops), part_reader(got_twin, hops)]
+        if turn:
+            copies[turn - 1].wait_recv()
+            terms.append(part_reader(landed, turn - 1))
+        add_slabs(leaving.at[turn] if hops else out, terms, 32)
+        if hops:
+            copies.append(net.send(leaving.at[turn], landed.at[turn], sems, turn, net.up))
+        yield
+
+
+def scatter_columns_scratch(ring, rows, width):
+    return [
+        pltpu.VMEM((ring, rows, width), jnp.bfloat16),
+        pltpu.VMEM((ring, rows, width), jnp.bfloat16),
+        pltpu.VMEM((ring - 1, rows, width), jnp.bfloat16),
+        pltpu.VMEM((ring - 1, rows, width), jnp.bfloat16),
+        pltpu.SemaphoreType.DMA((ring,)),
+    ] + pair_sems(ring) + pair_sems(ring - 1)
+
+
+def remote_call(kernel, name, collective_id, out_shape, scratch, operands, in_vmem=(), out_vmem=(), cost=None):
+    anywhere = pl.BlockSpec(memory_space=pl.ANY)
+    vmem = pl.BlockSpec(memory_space=pltpu.VMEM)
+    return pl.pallas_call(
+        kernel,
+        out_shape=out_shape,
+        in_specs=[vmem if i in in_vmem else anywhere for i in range(len(operands))],
+        out_specs=[vmem if i in out_vmem else anywhere for i in range(len(out_shape))],
+        scratch_shapes=scratch,
+        compiler_params=pltpu.CompilerParams(
+            collective_id=collective_id, has_side_effects=True, vmem_limit_bytes=60 * MIB
+        ),
+        cost_estimate=cost,
+        name=name,
+    )(*operands)
+
+
+def front_gather(n_rows, n_cols, block, weights, small):
+    ring = n_cols // 2
+    shape = lambda *dims: jax.ShapeDtypeStruct(dims, jnp.bfloat16)
+
+    def kernel(x, w, s, x_out, w_out, s_out, xs, xr, ws, wr, ss, sr, local):
+        net = Links(n_rows, n_cols)
+        net.greet([net.x, net.y, net.up, net.down, net.twin])
+        spot = lambda out: lambda hops, core: out.at[net.place(hops), core]
+        run_together(
+            gather_columns(net, s, spot(s_out), (ss, sr), local.at[2]),
+            gather_square(net, x, x_out, (xs, xr), local.at[0], 1),
+            gather_columns(net, w, spot(w_out), (ws, wr), local.at[1]),
+        )
+        net.finish()
+
+    return remote_call(
+        kernel,
+        "front_gather",
+        1,
+        [
+            shape(1, block.shape[0], n_rows * block.shape[1]),
+            shape(ring, 2, *weights.shape),
+            shape(ring, 2, *small.shape),
+        ],
+        pair_sems(7) + pair_sems(2 * ring) + pair_sems(2 * ring) + [pltpu.SemaphoreType.DMA((3,))],
+        (block, weights, small),
+    )
+
+
+def attention_gather(n_rows, n_cols, queries, kv, grads, weights, slot_map):
+    ring = n_cols // 2
     length, width = queries.shape
     heads = width // HEAD_DIM
-    whole = keys.shape[0]
+    scale = 1.0 / math.sqrt(HEAD_DIM)
+    shape = jax.ShapeDtypeStruct
+
+    def kernel(
+        q, kv_in, g, w, m, out, lse, kv_out, g_out, w_out, m_out,
+        kv_all, top, total, acc, gs, gr, ws, wr, ks, kr, ms, mr, local,
+    ):
+        net = Links(n_rows, n_cols)
+        others = net.spread_partners()
+        net.greet([device for _, _, device in others] + [net.twin])
+        kv_steps = gather_columns(
+            net, kv_in, lambda hops, core: kv_all.at[2 * net.chip(hops) + core], (ks, kr), local.at[0]
+        )
+        next(kv_steps)
+        maps = []
+        for number, (hops, bits, device) in enumerate(others):
+            maps.append(net.send(m, m_out.at[hops, net.r], (ms, mr), number, device))
+        own_map = pltpu.make_async_copy(m, m_out.at[0, net.r], local.at[1])
+        own_map.start()
+        w_steps = gather_columns(
+            net, w, lambda hops, core: w_out.at[net.place(hops), core], (ws, wr), local.at[2]
+        )
+        g_steps = gather_square(net, g, g_out, (gs, gr), local.at[3], ring)
+        next(g_steps)
+        next(w_steps)
+        run_together(kv_steps)
+        kv_save = pltpu.make_async_copy(kv_all, kv_out, local.at[4])
+        kv_save.start()
+
+        for head in range(heads):
+            columns = slice(head * HEAD_DIM, (head + 1) * HEAD_DIM)
+            queries = q[:, columns]
+
+            def part(block):
+                return scores_of(kv_all[block, :, :HEAD_DIM], queries, scale), kv_all[block, :, HEAD_DIM:]
+
+            scores, values = part(net.c)
+            scores = jnp.where(causal_mask(scores), scores, NEG_LARGE)
+            high = jnp.max(scores, 0, keepdims=True)
+            probs = jnp.exp(scores - high)
+            top[...] = high
+            total[...] = jnp.sum(probs, 0, keepdims=True)
+            acc[...] = matmul_tn(values, probs.astype(jnp.bfloat16))
+
+            @pl.loop(0, net.c)
+            def _(block):
+                scores, values = part(block)
+                high = jnp.maximum(top[...], jnp.max(scores, 0, keepdims=True))
+                probs = jnp.exp(scores - high)
+                shrink = jnp.exp(top[...] - high)
+                top[...] = high
+                total[...] = total[...] * shrink + jnp.sum(probs, 0, keepdims=True)
+                acc[...] = acc[...] * shrink + matmul_tn(values, probs.astype(jnp.bfloat16))
+
+            out[:, columns] = (acc[...] / total[...]).T
+            lse[head] = top[...] + jnp.log(total[...])
+            next(g_steps, None)
+            next(w_steps, None)
+
+        run_together(g_steps, w_steps)
+        own_map.wait()
+        for copy in maps:
+            copy.wait_recv()
+        kv_save.wait()
+        net.finish()
+
+    partners = n_rows * ring - 1
+    return remote_call(
+        kernel,
+        "attention_gather",
+        2,
+        [
+            shape((length, width), jnp.float32),
+            shape((heads, 1, length), jnp.float32),
+            shape((n_cols, *kv.shape), jnp.bfloat16),
+            shape((ring, grads.shape[0], n_rows * grads.shape[1]), jnp.bfloat16),
+            shape((ring, 2, *weights.shape), jnp.bfloat16),
+            shape((ring, n_rows, *slot_map.shape), jnp.float32),
+        ],
+        [
+            pltpu.VMEM((n_cols, *kv.shape), jnp.bfloat16),
+            pltpu.VMEM((1, length), jnp.float32),
+            pltpu.VMEM((1, length), jnp.float32),
+            pltpu.VMEM((HEAD_DIM, length), jnp.float32),
+        ]
+        + pair_sems(7 * ring)
+        + pair_sems(2 * ring)
+        + pair_sems(2 * ring)
+        + pair_sems(partners)
+        + [pltpu.SemaphoreType.DMA((5,))],
+        (queries, kv, grads, weights, slot_map),
+        in_vmem=(0,),
+        out_vmem=(0, 1),
+    )
+
+
+def rows_sum(n_rows, n_cols, parts):
+    pieces = 2
+    rows, whole = parts.shape
+    width = whole // n_rows
+    piece = rows // pieces
+    shape = jax.ShapeDtypeStruct((pieces, piece, whole), jnp.bfloat16)
+
+    def kernel(src, out, result, *rest):
+        scratch, (gs0, gr0, gs1, gr1, local) = rest[:-5], rest[-5:]
+        net = Links(n_rows, n_cols)
+        net.greet([net.x, net.y])
+        gathers = []
+
+        def finish(s, upper, lower):
+            add_slabs(result.at[s, pl.ds(0, piece // 2), :], upper)
+            add_slabs(result.at[s, pl.ds(piece // 2, piece // 2), :], lower)
+            sems = ((gs0, gr0), (gs1, gr1))[s]
+            steps = gather_square(net, result.at[s], out.at[pl.ds(s, 1)], sems, local.at[s], 1)
+            next(steps)
+            gathers.append(steps)
+
+        run_together(scatter_square(net, src, scratch, list(range(pieces)), finish))
+        run_together(*gathers)
+        net.finish()
+
+    return remote_call(
+        kernel,
+        "rows_sum",
+        3,
+        [shape],
+        [pltpu.VMEM((pieces, piece, width), jnp.bfloat16)]
+        + scatter_scratch(pieces, piece, width)
+        + pair_sems(7)
+        + pair_sems(7)
+        + [pltpu.SemaphoreType.DMA((pieces,))],
+        (parts.reshape(shape.shape),),
+    )[0].reshape(rows, whole)
+
+
+def token_gather(n_rows, n_cols, block):
+    ring = n_cols // 2
+
+    def kernel(x, out, xs, xr, local):
+        net = Links(n_rows, n_cols)
+        net.greet([net.x, net.y, net.up, net.down])
+        run_together(gather_square(net, x, out, (xs, xr), local.at[0], ring))
+        net.finish()
+
+    return remote_call(
+        kernel,
+        "token_gather",
+        4,
+        [jax.ShapeDtypeStruct((ring, block.shape[0], n_rows * block.shape[1]), jnp.bfloat16)],
+        pair_sems(7 * ring) + [pltpu.SemaphoreType.DMA((1,))],
+        (block,),
+    )[0]
+
+
+def token_sum(n_rows, n_cols, parts, gates):
+    ring = n_cols // 2
+    rows, width = parts.shape[1], parts.shape[2] // n_rows
+    experts = n_rows * ring
+
+    def kernel(src, gate, out, gate_out, result, *rest):
+        scratch, ring_parts = rest[:9], rest[9:13]
+        gs, gr, ms, mr, local = rest[13:]
+        net = Links(n_rows, n_cols)
+        others = net.spread_partners()
+        net.greet([device for _, _, device in others])
+        mine = net.r * ring + net.z
+        copies = []
+        own = pltpu.make_async_copy(gate, gate_out.at[mine], local.at[1])
+        own.start()
+        for number, (hops, bits, device) in enumerate(others):
+            copies.append(net.send(gate, gate_out.at[mine], (ms, mr), number, device))
+        order = list(range(1, ring)) + [0]
+        run_together(
+            scatter_square(net, src, scratch, order, ring_finish(net, ring_parts, result))
+        )
+        run_together(gather_square(net, result, out, (gs, gr), local.at[0], 1))
+        own.wait()
+        for copy in copies:
+            copy.wait_recv()
+        net.finish()
+
+    out, gate_out = remote_call(
+        kernel,
+        "token_sum",
+        5,
+        [
+            jax.ShapeDtypeStruct((1, rows, n_rows * width), jnp.bfloat16),
+            jax.ShapeDtypeStruct((experts, *gates.shape), jnp.float32),
+        ],
+        [pltpu.VMEM((rows, width), jnp.bfloat16)]
+        + scatter_scratch(ring, rows, width)
+        + ring_scratch(ring, rows, width)
+        + pair_sems(7)
+        + pair_sems(experts - 1)
+        + [pltpu.SemaphoreType.DMA((2,))],
+        (parts, gates),
+    )
+    return out[0], gate_out
+
+
+def last_sums(n_rows, n_cols, parts, weights):
+    ring = n_cols // 2
+    rows, width = parts.shape[1], parts.shape[2] // n_rows
+
+    def kernel(src, w, out, w_out, *rest):
+        scratch, ring_parts, column_parts = rest[:9], rest[9:13], rest[13:]
+        net = Links(n_rows, n_cols)
+        net.greet([net.x, net.y, net.up, net.down, net.twin])
+        order = list(range(1, ring)) + [0]
+        run_together(
+            scatter_columns(net, w, w_out, column_parts),
+            scatter_square(net, src, scratch, order, ring_finish(net, ring_parts, out)),
+        )
+        net.finish()
+
+    return remote_call(
+        kernel,
+        "last_sums",
+        6,
+        [
+            jax.ShapeDtypeStruct((rows, width), jnp.float32),
+            jax.ShapeDtypeStruct(weights.shape[2:], jnp.float32),
+        ],
+        scatter_scratch(ring, rows, width)
+        + ring_scratch(ring, rows, width)
+        + scatter_columns_scratch(ring, *weights.shape[2:]),
+        (parts, weights),
+        out_vmem=(0, 1),
+    )
+
+
+def expert_kernel(
+    info, rows, grads, slot_row, chosen, mine_hot, gate_own, gate_twin, up_own, up_twin, down_own,
+    down_twin, token_w, shared_down,
+    d_rows_out, rows_out, slot_rows, d_part, e_act, d_gate, d_up, s_act, d_shared, probs_out, d_gates,
+    w_gate, w_up, w_down, slot_dx, part, sems,
+):
+    tokens, model = rows.shape[1:]
+    n_slots = slot_rows.shape[1]
+    half_hidden = gate_own.shape[1]
+    hidden = 2 * half_hidden
+    pad = shared_down.shape[1]
+    row = info[0]
+    width = model // 4
+    bf16, f32 = jnp.bfloat16, jnp.float32
+
+    @pl.when(pl.program_id(0) == 0)
+    def _():
+        copies = []
+        for j in range(4):
+            flipped = row + (1 - 2 * lax.rem(row, 2)) * (j & 1) + (2 - 4 * lax.div(row, 2)) * (j >> 1)
+            there = pl.ds(pl.multiple_of(flipped * width, width), width)
+            here = pl.ds(j * width, width)
+            for h, sources in enumerate(((gate_own, up_own, down_own), (gate_twin, up_twin, down_twin))):
+                cols = pl.ds(h * half_hidden, half_hidden)
+                number = 6 * j + 3 * h
+                copies += [
+                    pltpu.make_async_copy(
+                        sources[0].at[there, :], w_gate.at[here, cols], sems.at[number]
+                    ),
+                    pltpu.make_async_copy(
+                        sources[1].at[there, :], w_up.at[here, cols], sems.at[number + 1]
+                    ),
+                    pltpu.make_async_copy(
+                        sources[2].at[:, there], w_down.at[cols, here], sems.at[number + 2]
+                    ),
+                ]
+        for copy in copies:
+            copy.start()
+        for copy in copies:
+            copy.wait()
+
+    x = rows[0]
+    pick = (
+        lax.broadcasted_iota(jnp.int32, (n_slots, tokens), 0).astype(f32) == slot_row[0]
+    ).astype(f32)
+    pick_b = pick.astype(bf16)
+    pick_t = pick.T.astype(bf16)
+    exact = lambda a, b, dims: lax.dot_general(
+        a, b, (dims, ((), ())), precision=PRECISE, preferred_element_type=f32
+    )
+
+    logits = matmul(x, token_w[:, 2 * pad :])
+    logits = jnp.where(chosen[0] > 0, logits, NEG_LARGE)
+    logits = jnp.exp(logits - jnp.max(logits, -1, keepdims=True))
+    probs = logits / jnp.sum(logits, -1, keepdims=True)
+    probs_out[0] = probs
+    my_gate = jnp.sum(probs * mine_hot[...], -1, keepdims=True)
+    slot_gate = exact(pick, jnp.broadcast_to(my_gate, (tokens, 128)), ((1,), (0,)))[:, :1]
+    s_gate = matmul(x, token_w[:, :pad])
+    s_up = matmul(x, token_w[:, pad : 2 * pad])
+    through = matmul(grads[0], shared_down[...])
+    s_silu, s_slope = silu_parts(s_gate)
+    s_act[0] = (s_silu * s_up).astype(bf16)
+    d_shared[0, :, :pad] = (through * s_up * s_slope).astype(bf16)
+    d_shared[0, :, pad:] = (through * s_silu).astype(bf16)
+
+    tile = 512
+    for t in range(model // tile):
+        at = slice(t * tile, (t + 1) * tile)
+        slot_rows[0, :, at] = matmul(pick_b, rows[0, :, at]).astype(bf16)
+        picked = matmul(pick_b, grads[0, :, at])
+        part[:, at] = picked.astype(bf16)
+        d_part[0, :, at] = (picked * slot_gate).astype(bf16)
+
+    step = 256
+
+    def hidden_tile(t, total):
+        at = pl.ds(pl.multiple_of(t * step, step), step)
+        e_gate = matmul(slot_rows[0], w_gate[:, at])
+        e_up = matmul(slot_rows[0], w_up[:, at])
+        through = matmul_nt(part[...], w_down[at, :])
+        e_silu, e_slope = silu_parts(e_gate)
+        act = e_silu * e_up
+        d_act = through * slot_gate
+        e_act[0, :, at] = act.astype(bf16)
+        d_gate[0, :, at] = (d_act * e_up * e_slope).astype(bf16)
+        d_up[0, :, at] = (d_act * e_silu).astype(bf16)
+        return total + jnp.sum(act * through, -1, keepdims=True)
+
+    d_gate_slot = lax.fori_loop(0, hidden // step, hidden_tile, jnp.zeros((n_slots, 1), f32))
+    d_gates[0] = exact(jnp.broadcast_to(d_gate_slot, (n_slots, 128)), pick, ((0,), (0,)))[:1]
+
+    @pl.loop(0, model // tile)
+    def _(t):
+        at = pl.ds(pl.multiple_of(t * tile, tile), tile)
+        d_slot = matmul_nt(d_gate[0], w_gate[at, :]) + matmul_nt(d_up[0], w_up[at, :])
+        d_rows_out[0, :, at] = (
+            matmul(pick_t, d_slot.astype(bf16)) + matmul_nt(d_shared[0], token_w[at, : 2 * pad])
+        ).astype(bf16)
+        out = (matmul(e_act[0], w_down[:, at]) * slot_gate).astype(bf16)
+        rows_out[0, :, at] = (
+            matmul(pick_t, out) + matmul_nt(s_act[0], shared_down[at, :])
+        ).astype(bf16)
+
+
+def expert_chunks(
+    info, rows, grads, slot_row, chosen, mine_hot, experts_w, token_w, shared_down, slots
+):
+    chunks, tokens, model = rows.shape
+    half_hidden = experts_w[0].shape[1]
+    hidden = 2 * half_hidden
+    pad = shared_down.shape[1]
+    by_chunk = lambda *dims: pl.BlockSpec((1, *dims), lambda i, s: (i, 0, 0))
+    once = lambda *dims: pl.BlockSpec(dims, lambda i, s: (0, 0), pipeline_mode=pl.Buffered(1))
+    anywhere = pl.BlockSpec(memory_space=pl.ANY)
+    single = lambda *dims: pl.BlockSpec(
+        (1, *dims), lambda i, s: (i, 0, 0), pipeline_mode=pl.Buffered(1)
+    )
+    bf16, f32 = jnp.bfloat16, jnp.float32
+    shape = lambda dtype, *dims: jax.ShapeDtypeStruct((chunks, *dims), dtype)
     return pl.pallas_call(
-        lambda *refs: attention_forward_kernel(1.0 / math.sqrt(HEAD_DIM), *refs),
+        expert_kernel,
         grid_spec=pltpu.PrefetchScalarGridSpec(
             num_scalar_prefetch=1,
-            grid=(heads,),
+            grid=(chunks,),
             in_specs=[
-                pl.BlockSpec((length, HEAD_DIM), lambda h, s: (0, h)),
-                pl.BlockSpec((whole, HEAD_DIM), lambda h, s: (0, 0)),
-                pl.BlockSpec((HEAD_DIM, whole), lambda h, s: (0, 0)),
-            ],
+                by_chunk(tokens, model),
+                by_chunk(tokens, model),
+                by_chunk(1, tokens),
+                by_chunk(tokens, 128),
+                once(1, 128),
+            ]
+            + [anywhere] * 6
+            + [once(*token_w.shape), once(*shared_down.shape)],
             out_specs=[
-                pl.BlockSpec((length, HEAD_DIM), lambda h, s: (0, h)),
-                pl.BlockSpec((1, 1, length), lambda h, s: (h, 0, 0)),
+                single(tokens, model),
+                single(tokens, model),
+                single(slots, model),
+                single(slots, model),
+                single(slots, hidden),
+                single(slots, hidden),
+                single(slots, hidden),
+                single(tokens, pad),
+                single(tokens, 2 * pad),
+                single(tokens, 128),
+                pl.BlockSpec((1, 1, tokens), lambda i, s: (s[1 + i], 0, 0)),
             ],
             scratch_shapes=[
-                pltpu.VMEM((1, length), jnp.float32),
-                pltpu.VMEM((1, length), jnp.float32),
-                pltpu.VMEM((HEAD_DIM, length), jnp.float32),
+                pltpu.VMEM((model, hidden), bf16),
+                pltpu.VMEM((model, hidden), bf16),
+                pltpu.VMEM((hidden, model), bf16),
+                pltpu.VMEM((8, 128), bf16),
+                pltpu.VMEM((slots, model), bf16),
+                pltpu.SemaphoreType.DMA((24,)),
             ],
         ),
         out_shape=[
-            jax.ShapeDtypeStruct((length, width), jnp.float32),
-            jax.ShapeDtypeStruct((heads, 1, length), jnp.float32),
+            shape(bf16, tokens, model),
+            shape(bf16, tokens, model),
+            shape(bf16, slots, model),
+            shape(bf16, slots, model),
+            shape(bf16, slots, hidden),
+            shape(bf16, slots, hidden),
+            shape(bf16, slots, hidden),
+            shape(bf16, tokens, pad),
+            shape(bf16, tokens, 2 * pad),
+            shape(f32, tokens, 128),
+            shape(f32, 1, tokens),
         ],
-        compiler_params=pltpu.CompilerParams(vmem_limit_bytes=48 * 1024 * 1024),
+        compiler_params=pltpu.CompilerParams(vmem_limit_bytes=63 * MIB),
         cost_estimate=pl.CostEstimate(
-            flops=4 * length * width * whole,
-            bytes_accessed=2 * whole * HEAD_DIM * 2 + length * width * 6,
-            transcendentals=length * heads * whole,
+            flops=chunks * 2 * tokens * model * (4 * hidden + 6 * pad),
+            bytes_accessed=40 * MIB,
+            transcendentals=chunks * slots * hidden,
         ),
-        name="attention_forward",
-    )(block, queries, keys, values_t)
+        name="expert_chunks",
+    )(info, rows, grads, slot_row, chosen, mine_hot, *experts_w, token_w, shared_down)
 
 
 def attention_backward_kernel(
@@ -800,22 +1493,19 @@
     earlier = jnp.tril(jnp.ones((rows_dev, rows_dev), jnp.float32), -1)
     rank = jnp.dot(earlier, hot, precision=PRECISE)
     slot_map = jnp.where(hot > 0, rank, -1.0).T
-    slot_maps = lax.all_gather(slot_map, ("cols", "rows"), axis=0, tiled=False)
-    slot_maps = slot_maps.reshape(ring, 2, n_rows, experts, rows_dev)
-    slot_maps = index(slot_maps, k, 1, False)
 
     small = jnp.concatenate([w_router, norm1_gain[:, None], norm2_gain[:, None]], 1)
     small = jnp.pad(small, ((0, 0), (0, 128 - small.shape[1])))
-    small = net.mixed(lax.all_gather(small, "cols", axis=0, tiled=True), 0)
+    token_input, weights_in, small = front_gather(
+        n_rows, net.n_cols, layer_in[0],
+        jnp.concatenate([w_query, key_matrix, value_matrix], 1), small,
+    )
+    token_input = token_input[0].astype(jnp.float32)
+    weights_in = weights_in.reshape(model_width, -1)
+    small = small.reshape(model_width, 128)
     router_full = small[:, :experts]
     gains = small[:, experts : experts + 2].astype(jnp.float32).T
     first_gain, second_gain = gains[0][None], gains[1][None]
-
-    token_input = jnp.concatenate(net.rows_gather(layer_in[0]), 1).astype(jnp.float32)
-    weights_in = net.cols_gather(
-        jnp.concatenate([w_query, key_matrix, value_matrix], 1), net.place
-    ).reshape(model_width, -1)
-    weights_out_t = net.cols_gather(w_out.T, net.place).reshape(model_width, -1)
     first_inverse = lax.rsqrt(jnp.mean(token_input * token_input, -1, keepdims=True) + NORM_EPS)
     first_unit = token_input * first_inverse
     first_normed = (first_unit * first_gain).astype(jnp.bfloat16)
@@ -829,34 +1519,29 @@
     kv_local = jnp.concatenate(
         [rotated[:, q_heads], projected[:, q_width + kv_width :].astype(jnp.bfloat16)], 1
     )
-    kv_all = net.cols_gather(kv_local, net.chip).reshape(-1, 2 * HEAD_DIM)
+    block_no = c.astype(jnp.int32)[None]
+    attn_f32, log_total, kv_all, grad_rows, weights_out_t, slot_maps = attention_gather(
+        n_rows, net.n_cols, queries, kv_local, cotangent[0], w_out.T, slot_map
+    )
+    weights_out_t = weights_out_t.reshape(model_width, -1)
+    kv_all = kv_all.reshape(-1, 2 * HEAD_DIM)
     keys_all, values_all = kv_all[:, :HEAD_DIM], kv_all[:, HEAD_DIM:]
-    block_no = c.astype(jnp.int32)[None]
-    attn_f32, log_total = attention_forward(block_no, queries, keys_all, values_all.T)
     attn_rows = attn_f32.astype(jnp.bfloat16)
     proj = matmul_nt(attn_rows, weights_out_t).astype(jnp.bfloat16)
     blocks_of = lambda whole: [
         whole[:, j * row_width : (j + 1) * row_width] for j in range(n_rows)
     ]
-    proj_mine = net.rows_scatter(blocks_of(proj)).astype(jnp.bfloat16)
-    attn_proj = jnp.concatenate(net.rows_gather(proj_mine), 1).astype(jnp.float32)
+    attn_proj = rows_sum(n_rows, net.n_cols, proj).astype(jnp.float32)
     residual = token_input + attn_proj
     second_inverse = lax.rsqrt(jnp.mean(residual * residual, -1, keepdims=True) + NORM_EPS)
     second_unit = residual * second_inverse
     second_normed = (second_unit * second_gain).astype(jnp.bfloat16)
 
-    pair = lambda own, axis: jnp.concatenate([own, net.sibling(own)], axis)
-    e_gate_w = net.mixed(pair(expert_gate[0], 1), 0)
-    e_up_w = net.mixed(pair(expert_up[0], 1), 0)
-    e_down_w = net.mixed(pair(expert_down[0], 0), 1)
-    packed = jnp.concatenate(
-        [
-            shared_gate.reshape(col_width, ring, shared_hidden),
-            shared_up.reshape(col_width, ring, shared_hidden),
-            shared_down.T.reshape(col_width, ring, shared_hidden),
-        ],
-        2,
-    )
+    pad_to = -(-shared_hidden // 128) * 128
+    padded = lambda w: jnp.pad(
+        w.reshape(col_width, ring, shared_hidden), ((0, 0), (0, 0), (0, pad_to - shared_hidden))
+    )
+    packed = jnp.concatenate([padded(shared_gate), padded(shared_up), padded(shared_down.T)], 2)
     packed = jnp.swapaxes(packed, 0, 1)
     shared_w = jnp.zeros((ring, 2) + packed.shape[1:], jnp.bfloat16)
     for hops in range(ring):
@@ -866,121 +1551,44 @@
         spot = net.place(hops)
         shared_w = lax.dynamic_update_slice(shared_w, piece[None, None], (spot, k, 0, 0))
         shared_w = lax.dynamic_update_slice(shared_w, twin[None, None], (spot, 1 - k, 0, 0))
-    shared_w = shared_w.reshape(model_width, 3 * shared_hidden)
-    shared_in, shared_down_t = shared_w[:, : 2 * shared_hidden], shared_w[:, 2 * shared_hidden :]
-    token_w = jnp.concatenate([shared_in, router_full], 1)
+    shared_w = shared_w.reshape(model_width, 3 * pad_to)
+    shared_down_t = shared_w[:, 2 * pad_to :]
+    token_w = jnp.concatenate(
+        [shared_w[:, : 2 * pad_to], jnp.pad(router_full, ((0, 0), (0, 128 - experts)))], 1
+    )
+    experts_w = []
+    for own in (expert_gate[0], expert_up[0], expert_down[0]):
+        experts_w += [own, net.sibling(own)]
 
     my_expert = r * ring + z
-    mine_hot = (expert_ids == my_expert).astype(jnp.float32)
-    slot_ids = jnp.arange(slots, dtype=jnp.float32)
-
-    def routing(hops):
-        maps = index(slot_maps, net.chip(hops), 0, False)
-        my_map = index(maps, my_expert, 1, False)
-        pick = my_map[:, None, :] == slot_ids[None, :, None]
-        chosen = jnp.swapaxes(maps >= 0, 1, 2).reshape(length, experts)
-        return pick, chosen
-
-    def take(pick, rows):
-        return jnp.einsum(
-            "bst,btd->bsd",
-            pick.astype(jnp.bfloat16),
-            rows.reshape(n_rows, rows_dev, model_width),
-            preferred_element_type=jnp.float32,
-        ).astype(jnp.bfloat16).reshape(n_rows * slots, model_width)
-
-    def spread(pick, rows):
-        return jnp.einsum(
-            "bst,bsd->btd",
-            pick.astype(jnp.bfloat16),
-            rows.reshape(n_rows, slots, model_width),
-            preferred_element_type=jnp.float32,
-        ).reshape(length, model_width)
-
-    grad_block = cotangent[0]
-    early = []
-    for hops in range(ring):
-        grad_rows = jnp.concatenate(net.rows_gather(grad_block), 1)
-        if hops < ring - 1:
-            grad_block = net.along_z(grad_block)
-        pick, chosen = routing(hops)
-        slot_grads = take(pick, grad_rows)
-        through = matmul_nt(slot_grads, e_down_w)
-        shared_through = matmul(grad_rows, shared_down_t)
-        early.append((pick, chosen, grad_rows, slot_grads, through, shared_through))
-
-    normed_block = second_normed[:, :row_width]
-    done = []
-    for hops in range(ring):
-        pick, chosen, grad_rows, slot_grads, through, shared_through = early[hops]
-        if hops == 0:
-            rows = second_normed
-        else:
-            normed_block = net.along_z(normed_block)
-            rows = jnp.concatenate(net.rows_gather(normed_block), 1)
-        from_tokens = matmul(rows, token_w)
-        s_gate = from_tokens[:, :shared_hidden]
-        s_up = from_tokens[:, shared_hidden : 2 * shared_hidden]
-        logits = from_tokens[:, 2 * shared_hidden :]
-        gate_probs = jax.nn.softmax(jnp.where(chosen, logits, NEG_LARGE), -1)
-        my_gate = jnp.sum(gate_probs * mine_hot, -1).reshape(n_rows, 1, rows_dev)
-        slot_gate = jnp.sum(jnp.where(pick, my_gate, 0.0), -1).reshape(-1, 1)
-        slot_rows = take(pick, rows)
-        e_gate = matmul(slot_rows, e_gate_w)
-        e_up = matmul(slot_rows, e_up_w)
-        e_silu, e_slope = silu_parts(e_gate)
-        e_act_f = e_silu * e_up
-        e_act = e_act_f.astype(jnp.bfloat16)
-        d_gate_slot = jnp.sum(e_act_f * through, -1).reshape(n_rows, slots, 1)
-        d_gate_token = jnp.sum(jnp.where(pick, d_gate_slot, 0.0), 1).reshape(1, length)
-        d_e_act = through * slot_gate
-        d_e_gate = (d_e_act * e_up * e_slope).astype(jnp.bfloat16)
-        d_e_up = (d_e_act * e_silu).astype(jnp.bfloat16)
-        d_part = (slot_grads.astype(jnp.float32) * slot_gate).astype(jnp.bfloat16)
-        s_silu, s_slope = silu_parts(s_gate)
-        s_act = (s_silu * s_up).astype(jnp.bfloat16)
-        d_s_gate = (shared_through * s_up * s_slope).astype(jnp.bfloat16)
-        d_s_up = (shared_through * s_silu).astype(jnp.bfloat16)
-        d_shared = jnp.concatenate([d_s_gate, d_s_up], 1)
-        d_slot_rows = (matmul_nt(d_e_gate, e_gate_w) + matmul_nt(d_e_up, e_up_w)).astype(
-            jnp.bfloat16
-        )
-        d_rows = (spread(pick, d_slot_rows) + matmul_nt(d_shared, shared_in)).astype(jnp.bfloat16)
-        part = (matmul(e_act, e_down_w) * slot_gate).astype(jnp.bfloat16)
-        out_rows = (spread(pick, part) + matmul_nt(s_act, shared_down_t)).astype(jnp.bfloat16)
-        done.append(
-            dict(
-                rows=rows, slot_rows=slot_rows, e_act=e_act, d_e_gate=d_e_gate, d_e_up=d_e_up,
-                d_part=d_part, s_act=s_act, d_shared=d_shared, d_rows=d_rows, out_rows=out_rows,
-                gate_probs=gate_probs, d_gate_token=d_gate_token, grad_rows=grad_rows,
-            )
-        )
-
-    def ring_scatter(name):
-        run = None
-        for hops in list(range(1, ring)) + [0]:
-            here = net.rows_scatter(blocks_of(done[hops][name]))
-            if run is not None:
-                here = here + net.along_z(run).astype(jnp.float32)
-            run = here.astype(jnp.bfloat16)
-        return here
-
-    d_gate_all = jnp.zeros((ring, length), jnp.float32)
-    for hops in range(ring):
-        d_gate_all = lax.dynamic_update_slice(
-            d_gate_all, done[hops]["d_gate_token"], (net.chip(hops), 0)
-        )
-    d_gate_all = lax.all_gather(d_gate_all, ("rows", "cols"), axis=0, tiled=False)
-    d_gate_all = index(d_gate_all.reshape(experts, 2, ring, length), k, 1, False)
+    mine_hot = (jnp.arange(128, dtype=jnp.int32) == my_expert).astype(jnp.float32)[None]
+    my_map = index(slot_maps, my_expert, 2, False)
+    first_slot = (jnp.arange(n_rows, dtype=jnp.float32) * slots)[None, :, None]
+    slot_row = jnp.where(my_map >= 0, my_map + first_slot, -1.0).reshape(ring, 1, length)
+    chosen = jnp.swapaxes(slot_maps >= 0, 2, 3).reshape(ring, length, experts)
+    chosen = jnp.pad(chosen.astype(jnp.float32), ((0, 0), (0, 0), (0, 128 - experts)))
+    rows_all = token_gather(n_rows, net.n_cols, second_normed[:, :row_width])
+    info = jnp.stack([r] + [net.chip(hops) for hops in range(ring)]).astype(jnp.int32)
+    (
+        d_rows, out_rows, slot_rows, d_part, e_act, d_e_gate, d_e_up, s_act, d_shared, gate_probs,
+        d_gate_mine,
+    ) = expert_chunks(
+        info, rows_all, grad_rows, slot_row, chosen, mine_hot, experts_w, token_w, shared_down_t,
+        n_rows * slots,
+    )
+
+    d_second, d_gate_all = token_sum(
+        n_rows, net.n_cols, d_rows, d_gate_mine.reshape(ring, length)
+    )
     grad_router = jnp.zeros((row_width, experts), jnp.float32)
     d_logits_own = None
     for hops in range(ring):
-        gate_probs = done[hops]["gate_probs"]
+        probs = gate_probs[hops][:, :experts]
         d_gates = index(d_gate_all, net.chip(hops), 1, False).T
-        d_logits = gate_probs * (d_gates - jnp.sum(gate_probs * d_gates, -1, keepdims=True))
+        d_logits = probs * (d_gates - jnp.sum(probs * d_gates, -1, keepdims=True))
         if hops == 0:
             d_logits_own = d_logits
-        quarter = lax.dynamic_slice_in_dim(done[hops]["rows"], r * rows_dev, rows_dev, 0)
+        quarter = lax.dynamic_slice(rows_all[hops], (r * rows_dev, 0), (rows_dev, model_width))
         quarter = lax.switch(
             r ^ z,
             [
@@ -1001,13 +1609,10 @@
     d_router_in = matmul_nt(
         jnp.concatenate([high, low], 1), jnp.concatenate([router_full, router_full], 1)
     )
-
-    d_second_mine = ring_scatter("d_rows").astype(jnp.bfloat16)
-    d_second = jnp.concatenate(net.rows_gather(d_second_mine), 1).astype(jnp.float32)
-    d_second = d_second + d_router_in
+    d_second = d_second.astype(jnp.float32) + d_router_in
     d_second_unit = d_second * second_gain
     second_gain_grad = jnp.sum((d_second * second_unit)[:, :row_width], 0)
-    d_resid = done[0]["grad_rows"].astype(jnp.float32) + second_inverse * (
+    d_resid = grad_rows[0].astype(jnp.float32) + second_inverse * (
         d_second_unit
         - second_unit * jnp.mean(d_second_unit * second_unit, -1, keepdims=True)
     )
@@ -1046,16 +1651,13 @@
     gain_grads = index(gain_grads, k, 1, False)
 
     column_parts = lambda whole: whole.astype(jnp.bfloat16).reshape(ring, 2, col_width, -1)
-    g_in = net.cols_scatter(column_parts(matmul_tn(first_normed, d_projected)), net.place)
-    g_out = net.cols_scatter(column_parts(matmul_tn(d_attn, attn_rows)), net.place).T
-    joined = lambda name: jnp.concatenate([part[name] for part in done], 0)
-    slot_rows, e_act = joined("slot_rows"), joined("e_act")
-    d_e_gate, d_e_up, d_part = joined("d_e_gate"), joined("d_e_up"), joined("d_part")
+    joined = lambda whole: whole.reshape(-1, whole.shape[-1])
+    slot_rows, e_act, d_part = joined(slot_rows), joined(e_act), joined(d_part)
+    d_e_gate, d_e_up = joined(d_e_gate), joined(d_e_up)
 
     def halves(left, right, axis):
-        whole_width = half_hidden
-        own = lambda v: v[:, :whole_width]
-        other = lambda v: v[:, whole_width:]
+        own = lambda v: v[:, :half_hidden]
+        other = lambda v: v[:, half_hidden:]
         if axis == 0:
             mine = matmul_tn(left, own(right))
             sent = matmul_tn(left, other(right)).astype(jnp.bfloat16)
@@ -1068,9 +1670,12 @@
     g_expert_up = halves(slot_rows, d_e_up, 0)
     g_expert_down = halves(e_act, d_part, 1)
 
-    rows_all, grads_all = joined("rows"), joined("grad_rows")
     shared_parts = jnp.concatenate(
-        [matmul_tn(rows_all, joined("d_shared")), matmul_tn(grads_all, joined("s_act"))], 1
+        [
+            matmul_tn(joined(rows_all), joined(d_shared)),
+            matmul_tn(joined(grad_rows), joined(s_act)),
+        ],
+        1,
     )
     shared_parts = net.pair_sum(column_parts(shared_parts))
     g_shared = jnp.zeros(shared_parts.shape, jnp.bfloat16)
@@ -1080,19 +1685,23 @@
         g_shared = lax.dynamic_update_slice(g_shared, piece[None], (net.chip(hops), 0, 0))
     g_shared = g_shared.astype(jnp.float32)
     shared_cols = lambda n: jnp.swapaxes(
-        g_shared[:, :, n * shared_hidden : (n + 1) * shared_hidden], 0, 1
+        g_shared[:, :, n * pad_to : n * pad_to + shared_hidden], 0, 1
     ).reshape(col_width, -1)
 
-    out_mine = ring_scatter("out_rows")
+    weight_parts = jnp.concatenate(
+        [matmul_tn(first_normed, d_projected), matmul_tn(d_attn, attn_rows)], 1
+    )
+    out_mine, g_in = last_sums(n_rows, net.n_cols, out_rows, column_parts(weight_parts))
     layer_out = (residual[:, :row_width] + out_mine).astype(jnp.bfloat16)
+    width_in = q_width + 2 * kv_width
     return (
         layer_out[None],
         grad_in[None],
         gain_grads[0],
         g_in[:, :q_width],
         g_in[:, q_width : q_width + kv_width],
-        g_in[:, q_width + kv_width :],
-        g_out,
+        g_in[:, q_width + kv_width : width_in],
+        g_in[:, width_in:].T,
         gain_grads[1],
         g_router,
         shared_cols(0),

time: 1500 us -> 1160 us (0.77)
  Pallas kernels: 37.9 us -> 725 us
  waiting for transfers between devices: 346 us -> 53.3 us
  matrix products: 299 us -> 97.2 us
  starting transfers between devices: 213 us -> 44.1 us
  other arithmetic: 255 us -> 110 us
  blocking collectives: 132 us -> 0 us
  local copies, waits for them, and re-layouts: 192 us -> 115 us
    pallas_call x1 -> x7, Pallas kernels: 18.4 us -> 706 us  [the longest x6 575 us: remote_call(): pl.pallas_call(kernel, out_shape=out_shape, in_specs=[vmem if i in in_vme...]
    ppermute x152 -> x35, waiting for transfers between devices: 346 us -> 53.3 us  [move(): return lax.ppermute(values, ('rows', 'cols'), pairs)]
    ppermute x152 -> x35, starting transfers between devices: 213 us -> 44.1 us  [move(): return lax.ppermute(values, ('rows', 'cols'), pairs)]
    all_gather x3 -> x0, blocking collectives: 132 us -> none  [the longest x1 66.3 us: gathered_layer(): slot_maps = lax.all_gather(slot_map, ('cols', 'rows'), axis=0, tiled=False)]
    concatenate x19 -> x4, other arithmetic: 83.5 us -> 9.47 us  [the longest x1 6.34 us: gathered_layer(): jnp.concatenate([matmul_tn(first_normed, d_projected), matmul_tn(d_attn,...]
    dot_general x14, matrix products: 139 us -> 74.4 us  [matmul_tn(): lax.dot_general(left_op, right_op, (((0,), (0,)), ((), ())), preferred_el...]
    dot_general x22 -> x2, matrix products: 72.3 us -> 8.69 us  [matmul(): return jnp.dot(left_op, right_op, preferred_element_type=jnp.float32)]
    dot_general x23 -> x3, matrix products: 64.1 us -> 12.6 us  [matmul_nt(): lax.dot_general(left_op, right_op, (((1,), (1,)), ((), ())), preferred_el...]
  transfers between devices with their start and end apart: 152 -> 35, of which waited for: 63 -> 10; matrix products, arithmetic and copies ran while one was open for 34% -> 22% of each run, Pallas kernels for 3% -> 39%
where the time goes in v2:
time: 1160 us; the launch traced here: 1150 us
  Pallas kernels  725 us (62%)
  local copies, waits for them, and re-layouts  115 us (10%)
  other arithmetic  110 us (9%)
  matrix products  97.2 us (8%)
  waiting for transfers between devices  53.3 us (5%)
  starting transfers between devices  44.1 us (4%)
    pallas_call x6, Pallas kernels, remote_call(): pl.pallas_call(kernel, out_shape=out_shape, in_specs=[vmem if i in in_vme...  575 us
    pallas_call x1, Pallas kernels, expert_chunks(): pl.pallas_call(expert_kernel, grid_spec=pltpu.PrefetchScalarGridSpec(num_...  130 us
    dot_general x14, matrix products, matmul_tn(): lax.dot_general(left_op, right_op, (((0,), (0,)), ((), ())), preferred_el...  74.4 us
    ppermute x35, waiting for transfers between devices, move(): return lax.ppermute(values, ('rows', 'cols'), pairs)  53.3 us
    ppermute x35, starting transfers between devices, move(): return lax.ppermute(values, ('rows', 'cols'), pairs)  44.1 us
    unnamed x181, local copies, waits for them, and re-layouts  28.4 us
  transfers between devices with their start and end apart: 35, of which 10 were waited for; matrix products, arithmetic and copies ran while one was open for 22% of the time, Pallas kernels for 39%

profile of v2, /device:TPU:18, one launch (start us, length us, event | category | flops | bytes accessed | tf_op | source)
XLA Modules:
  0.0 1147.8 jit_solution(2544975384135904859)
XLA Ops:
  13.4 54.2 %front_gather.1 = (bf16[1,512,2560]{2,1,0:T(8,128)(2,1)}, bf16[4,2,320,896]{3,2,1,0:T(8,128)(2,1)}, bf16[4,2,320,128]{3,2,1,0:T(8,128)(2,1)}) custom-call(bf16[512,640]{1,0:T(8,128)(2,1)} %bitcast.348, bf16[320,896]{1,0:T(8,128)(2,1)} %pad_maximum_fusion.10.w, bf16[320,128]{1,0:T(8,128)(2,1)} %pad.24.s), custom_call_target="tpu_custom_call" | custom-call | tf_op jit(solution)/shard_map/front_gather/pallas_call | solution.py:796
  100.6 135.5 %attention_gather.1 = (f32[512,640]{1,0:T(8,128)}, f32[5,1,512]{2,1,0:T(1,128)}, bf16[8,512,256]{2,1,0:T(8,128)(2,1)}, bf16[4,512,2560]{2,1,0:T(8,128)(2,1)}, bf...) custom-call(bf16[512,640]{1,0:T(8,128)(2,1)} %copy.198.q.refs_1_, bf16[512,256]{1,0:T(8,128)(2,1)} %pad_maximum_fusion.11.kv_in, ...), custom_call_target="tpu_custom_call" | custom-call | tf_op jit(solution)/shard_map/attention_gather/pallas_call | solution.py:796
  242.2 46.3 %rows_sum.1 = bf16[2,256,2560]{2,1,0:T(8,128)(2,1)} custom-call(bf16[2,256,2560]{2,1,0:T(8,128)(2,1)} %bitcast.333), custom_call_target="tpu_custom_call" | custom-call | tf_op jit(solution)/shard_map/rows_sum/pallas_call | solution.py:796
  301.6 90.3 %token_gather.1.rows = bf16[4,512,2560]{2,1,0:T(8,128)(2,1)} custom-call(bf16[512,640]{1,0:T(8,128)(2,1)} %multiply_convert_fusion.1.x), custom_call_target="tpu_custom_call" | custom-call | tf_op jit(solution)/shard_map/token_gather/pallas_call | solution.py:796
  395.6 7.2 fusion.106
  425.7 18.8 %collective-permute-done.6 = bf16[320,768]{1,0:T(8,128)(2,1)S(1)} collective-permute-done((bf16[320,768]{1,0:T(8,128)(2,1)S(1)}, bf16[320,768]{1,0:T(8,128)(2,1)S(1)}, u32[]{:S(2)}, u32[]{:S(2)}) %collective-permute-start.6) | collective-permute-done | bytes 491552 | tf_op jit(solution)/shard_map/ppermute | solution.py:1364
  446.6 6.9 collective-permute-done.8
  459.5 130.1 %expert_chunks.1 = (bf16[4,512,2560]{2,1,0:T(8,128)(2,1)}, bf16[4,512,2560]{2,1,0:T(8,128)(2,1)}, bf16[4,256,2560]{2,1,0:T(8,128)(2,1)}, bf16[4,256,2560]{2,1,0:...) custom-call(s32[5]{0:T(128)} %stack.59.info, ...), custom_call_target="tpu_custom_call" | custom-call | flops 80530636800 | bytes 41943040 | tf_op jit(solution)/shard_map/expert_chunks/pallas_call | solution.py:1194
  591.0 127.0 %token_sum.1 = (bf16[1,512,2560]{2,1,0:T(8,128)(2,1)}, f32[16,4,512]{2,1,0:T(4,128)}) custom-call(bf16[4,512,2560]{2,1,0:T(8,128)(2,1)} %get-tuple-element.191.src, f32[4,512]{1,0:T(4,128)} %bitcast.357), custom_call_target="tpu_custom_call" | custom-call | tf_op jit(solution)/shard_map/token_sum/pallas_call | solution.py:796
  722.8 10.7 fusion.32
  761.6 19.6 %attention_backward.1 = (f32[512,640]{1,0:T(8,128)S(1)}, bf16[4096,256]{1,0:T(8,128)(2,1)}) custom-call(s32[1]{0:T(128)} %bitcast.58.refs_0_, bf16[512,640]{1,0:T(8,128)(2,1)S(1)} %copy-done, bf16[4096,128]{1,0:T(8,128)(2,1)S(1)} %copy-done.2, bf16[128,4096]{1,0:T(8,128)(2,1)S(1)} %copy-done.3, bf16[4096,128]{1,0:T(8,128)(2,1)S(1)} %copy-done.1, ...), custom_call_target="tpu_custom_call" | custom-call | flops 13421772800 | bytes 8912896 | tf_op jit(solution)/shard_map/attention_backward/pallas_call | solution.py:1310
  792.0 9.1 bitcast_convert_fusion
  801.1 7.9 fusion.11
  809.1 9.3 fusion.29
  890.9 122.0 %last_sums.1 = (f32[512,640]{1,0:T(8,128)}, f32[320,1536]{1,0:T(8,128)}) custom-call(bf16[4,512,2560]{2,1,0:T(8,128)(2,1)} %get-tuple-element.189.src, bf16[4,2,320,1536]{3,2,1,0:T(8,128)(2,1)} %pad_maximum_fusion.w), custom_call_target="tpu_custom_call" | custom-call | tf_op jit(solution)/shard_map/last_sums/pallas_call | solution.py:796
  1019.9 9.6 collective-permute-done.16
  1038.8 8.6 collective-permute-done.30
  1063.9 10.3 collective-permute-start.21
  1095.5 15.2 %conditional.11 = (f32[1,2560,768]{2,1,0:T(8,128)}) conditional(s32[]{:T(128)} %clamp.5, (f32[2560,768]{1,0:T(8,128)}, f32[2560,768]{1,0:T(8,128)S(1)}) %tuple.116, (f32[2560,768]{1,0:T(8,128)}, f32[2560,768]{1,0:T(8,128)S(1)}) %tuple.116, (f32[2560,768]{1,0:T(8,128)}, f32[2560,768]{1,0:T(8,128)S(1)}) %tuple.116, ...), branch_computations={%region_28.29_spmd, %region_29.30_spmd, %region_30.31_spmd, %regio... | conditional | flops 7864320 | bytes 55050248 | solution.py:1399
  1095.5 7.5 add.338
  1113.4 15.3 %conditional.12 = (f32[1,2560,768]{2,1,0:T(8,128)}) conditional(s32[]{:T(128)} %clamp.5, (f32[2560,768]{1,0:T(8,128)}, f32[2560,768]{1,0:T(8,128)S(1)}) %tuple.117, (f32[2560,768]{1,0:T(8,128)}, f32[2560,768]{1,0:T(8,128)S(1)}) %tuple.117, (f32[2560,768]{1,0:T(8,128)}, f32[2560,768]{1,0:T(8,128)S(1)}) %tuple.117, ...), branch_computations={%region_32.33_spmd, %region_33.34_spmd, %region_34.35_spmd, %regio... | conditional | flops 7864320 | bytes 55050248 | solution.py:1399
  1113.4 7.5 add.342
  1131.9 15.8 %conditional.13 = (f32[1,768,2560]{2,1,0:T(8,128)}) conditional(s32[]{:T(128)} %clamp.5, (f32[768,2560]{1,0:T(8,128)}, f32[768,2560]{1,0:T(8,128)S(1)}) %tuple.118, (f32[768,2560]{1,0:T(8,128)}, f32[768,2560]{1,0:T(8,128)S(1)}) %tuple.118, (f32[768,2560]{1,0:T(8,128)}, f32[768,2560]{1,0:T(8,128)S(1)}) %tuple.118, ...), branch_computations={%region_36.37_spmd, %region_37.38_spmd, %region_38.39_spmd, %regio... | conditional | flops 7864320 | bytes 55050248 | solution.py:1399
  1131.9 8.1 add.346
  (442 shorter events, 299.2 us)
Async XLA Ops:
  0.6 458.9 %collective-permute-start = (bf16[2560,768]{1,0:T(8,128)(2,1)}, bf16[2560,768]{1,0:T(8,128)(2,1)}, u32[]{:S(2)}, u32[]{:S(2)}) collective-permute-start(bf16[2560,768]{1,0:T(8,128)(2,1)} %bitcast.365), channel_id=1, source_target_pairs={{0,1},{1,0},{2,3},{3,2},{4,5},{5,4},{6,7},{7,6},{8,9},{9,8},{10,11... | collective-permute-start | bytes 11796488 | tf_op jit(solution)/shard_map/ppermute | solution.py:1364
  0.7 458.8 %collective-permute-start.1 = (bf16[2560,768]{1,0:T(8,128)(2,1)}, bf16[2560,768]{1,0:T(8,128)(2,1)}, u32[]{:S(2)}, u32[]{:S(2)}) collective-permute-start(bf16[2560,768]{1,0:T(8,128)(2,1)} %bitcast.367), channel_id=1, source_target_pairs={{0,1},{1,0},{2,3},{3,2},{4,5},{5,4},{6,7},{7,6},{8,9},{9,8},{10,11... | collective-permute-start | bytes 11796488 | tf_op jit(solution)/shard_map/ppermute | solution.py:1364
  1.2 458.3 %collective-permute-start.2 = (bf16[768,2560]{1,0:T(8,128)(2,1)}, bf16[768,2560]{1,0:T(8,128)(2,1)}, u32[]{:S(2)}, u32[]{:S(2)}) collective-permute-start(bf16[768,2560]{1,0:T(8,128)(2,1)} %bitcast.369), channel_id=1, source_target_pairs={{0,1},{1,0},{2,3},{3,2},{4,5},{5,4},{6,7},{7,6},{8,9},{9,8},{10,11... | collective-permute-start | bytes 11796488 | tf_op jit(solution)/shard_map/ppermute | solution.py:1364
  8.1 415.2 %collective-permute-start.3 = (bf16[320,768]{1,0:T(8,128)(2,1)}, bf16[320,768]{1,0:T(8,128)(2,1)}, u32[]{:S(2)}, u32[]{:S(2)}) collective-permute-start(bf16[320,768]{1,0:T(8,128)(2,1)} %bitcast.44), channel_id=1, source_target_pairs={{0,1},{1,0},{2,3},{3,2},{4,5},{5,4},{6,7},{7,6},{8,9},{9,8},{10,11... | collective-permute-start | bytes 1474568 | tf_op jit(solution)/shard_map/ppermute | solution.py:1364
  9.5 414.9 %collective-permute-start.4 = (bf16[320,768]{1,0:T(8,128)(2,1)}, bf16[320,768]{1,0:T(8,128)(2,1)}, u32[]{:S(2)}, u32[]{:S(2)}) collective-permute-start(bf16[320,768]{1,0:T(8,128)(2,1)} %bitcast.46), channel_id=1, source_target_pairs={{0,2},{1,3},{2,4},{3,5},{4,6},{5,7},{6,0},{7,1},{8,10},{9,11},{10,... | collective-permute-start | bytes 1474568 | tf_op jit(solution)/shard_map/ppermute | solution.py:1364
  423.3 21.2 %collective-permute-start.6 = (bf16[320,768]{1,0:T(8,128)(2,1)S(1)}, bf16[320,768]{1,0:T(8,128)(2,1)S(1)}, u32[]{:S(2)}, u32[]{:S(2)}) collective-permute-start(bf16[320,768]{1,0:T(8,128)(2,1)S(1)} %bitcast.351), channel_id=1, source_target_pairs={{0,4},{1,5},{2,6},{3,7},{4,0},{5,1},{6,2},{7,3},{8,12},{9,13},{10,... | collective-permute-start | bytes 1474568 | tf_op jit(solution)/shard_map/ppermute | solution.py:1364
  424.5 29.1 %collective-permute-start.8 = (bf16[320,768]{1,0:T(8,128)(2,1)S(1)}, bf16[320,768]{1,0:T(8,128)(2,1)S(1)}, u32[]{:S(2)}, u32[]{:S(2)}) collective-permute-start(bf16[320,768]{1,0:T(8,128)(2,1)S(1)} %bitcast.350), channel_id=1, source_target_pairs={{0,6},{1,7},{2,0},{3,1},{4,2},{5,3},{6,4},{7,5},{8,14},{9,15},{10,... | collective-permute-start | bytes 1474568 | tf_op jit(solution)/shard_map/ppermute | solution.py:1364
  782.5 41.9 %collective-permute-start.10 = (bf16[4,512,256]{2,1,0:T(8,128)(2,1)S(1)}, bf16[4,512,256]{2,1,0:T(8,128)(2,1)S(1)}, u32[]{:S(2)}, u32[]{:S(2)}) collective-permute-start(bf16[4,512,256]{2,1,0:T(8,128)(2,1)S(1)} %dynamic-slice_bitcast_fusion), channel_id=1, source_target_pairs={{0,1},{1,0},{2,3},{3,2},{4,5},{5,4},{6,7},{7,6},{8,9},{9,8},{10,11... | collective-permute-start | bytes 3145736 | tf_op jit(solution)/shard_map/ppermute | solution.py:1364
  791.9 54.4 %collective-permute-start.25 = (f32[320,16]{0,1:T(8,128)S(1)}, f32[320,16]{0,1:T(8,128)S(1)}, u32[]{:S(2)}, u32[]{:S(2)}) collective-permute-start(f32[320,16]{0,1:T(8,128)S(1)} %bitcast.358), channel_id=1, source_target_pairs={{0,1},{1,0},{2,3},{3,2},{4,5},{5,4},{6,7},{7,6},{8,9},{9,8},{10,11... | collective-permute-start | bytes 61448 | tf_op jit(solution)/shard_map/ppermute | solution.py:1364
  824.7 13.8 %collective-permute-start.11 = (bf16[512,256]{1,0:T(8,128)(2,1)S(1)}, bf16[512,256]{1,0:T(8,128)(2,1)S(1)}, u32[]{:S(2)}, u32[]{:S(2)}) collective-permute-start(bf16[512,256]{1,0:T(8,128)(2,1)S(1)} %dynamic-slice_bitcast_fusion.8), channel_id=1, source_target_pairs={{0,2},{1,3},{2,4},{3,5},{4,6},{5,7},{6,0},{7,1},{8,10},{9,11},{10,... | collective-permute-start | bytes 786440 | tf_op jit(solution)/shard_map/ppermute | solution.py:1364
  848.3 10.7 collective-permute-start.13
  856.2 22.2 %collective-permute-start.28 = (bf16[4,320,768]{2,1,0:T(8,128)(2,1)}, bf16[4,320,768]{2,1,0:T(8,128)(2,1)}, u32[]{:S(2)}, u32[]{:S(2)}) collective-permute-start(bf16[4,320,768]{2,1,0:T(8,128)(2,1)} %fusion.22), channel_id=1, source_target_pairs={{0,1},{1,0},{2,3},{3,2},{4,5},{5,4},{6,7},{7,6},{8,9},{9,8},{10,11... | collective-permute-start | bytes 5898248 | tf_op jit(solution)/shard_map/ppermute | solution.py:1364
  856.2 236.5 %collective-permute-start.32 = (bf16[2560,768]{1,0:T(8,128)(2,1)}, bf16[2560,768]{1,0:T(8,128)(2,1)}, u32[]{:S(2)}, u32[]{:S(2)}) collective-permute-start(bf16[2560,768]{1,0:T(8,128)(2,1)} %convolution_convert_fusion.2), channel_id=1, source_target_pairs={{0,1},{1,0},{2,3},{3,2},{4,5},{5,4},{6,7},{7,6},{8,9},{9,8},{10,11... | collective-permute-start | bytes 11796488 | tf_op jit(solution)/shard_map/ppermute | solution.py:1364
  856.7 253.9 %collective-permute-start.33 = (bf16[2560,768]{1,0:T(8,128)(2,1)}, bf16[2560,768]{1,0:T(8,128)(2,1)}, u32[]{:S(2)}, u32[]{:S(2)}) collective-permute-start(bf16[2560,768]{1,0:T(8,128)(2,1)} %convolution_convert_fusion.1), channel_id=1, source_target_pairs={{0,1},{1,0},{2,3},{3,2},{4,5},{5,4},{6,7},{7,6},{8,9},{9,8},{10,11... | collective-permute-start | bytes 11796488 | tf_op jit(solution)/shard_map/ppermute | solution.py:1364
  858.3 270.4 %collective-permute-start.34 = (bf16[768,2560]{1,0:T(8,128)(2,1)}, bf16[768,2560]{1,0:T(8,128)(2,1)}, u32[]{:S(2)}, u32[]{:S(2)}) collective-permute-start(bf16[768,2560]{1,0:T(8,128)(2,1)} %convolution_convert_fusion), channel_id=1, source_target_pairs={{0,1},{1,0},{2,3},{3,2},{4,5},{5,4},{6,7},{7,6},{8,9},{9,8},{10,11... | collective-permute-start | bytes 11796488 | tf_op jit(solution)/shard_map/ppermute | solution.py:1364
  872.7 140.3 %collective-permute-start.14 = (bf16[2,256,640]{2,1,0:T(8,128)(2,1)}, bf16[2,256,640]{2,1,0:T(8,128)(2,1)}, u32[]{:S(2)}, u32[]{:S(2)}) collective-permute-start(bf16[2,256,640]{2,1,0:T(8,128)(2,1)} %pad_maximum_fusion.6), channel_id=1, source_target_pairs={{0,8},{1,9},{2,10},{3,11},{4,12},{5,13},{6,14},{7,15},{8,0},{9,1},... | collective-permute-start | bytes 1966088 | tf_op jit(solution)/shard_map/ppermute | solution.py:1364
  881.8 132.9 %collective-permute-start.29 = (bf16[320,768]{1,0:T(8,128)(2,1)}, bf16[320,768]{1,0:T(8,128)(2,1)}, u32[]{:S(2)}, u32[]{:S(2)}) collective-permute-start(bf16[320,768]{1,0:T(8,128)(2,1)} %get-tuple-element.339), channel_id=1, source_target_pairs={{0,2},{1,3},{2,4},{3,5},{4,6},{5,7},{6,0},{7,1},{8,10},{9,11},{10,... | collective-permute-start | bytes 1474568 | tf_op jit(solution)/shard_map/ppermute | solution.py:1364
  1013.0 16.5 %collective-permute-start.16 = (bf16[2,256,640]{2,1,0:T(8,128)(2,1)S(1)}, bf16[2,256,640]{2,1,0:T(8,128)(2,1)S(1)}, u32[]{:S(2)}, u32[]{:S(2)}) collective-permute-start(bf16[2,256,640]{2,1,0:T(8,128)(2,1)S(1)} %pad_maximum_fusion.7), channel_id=1, source_target_pairs={{0,16},{1,17},{2,18},{3,19},{4,20},{5,21},{6,22},{7,23},{8,24},{9,... | collective-permute-start | bytes 1966088 | tf_op jit(solution)/shard_map/ppermute | solution.py:1364
  1014.7 18.3 %collective-permute-start.15 = (bf16[256,640]{1,0:T(8,128)(2,1)S(1)}, bf16[256,640]{1,0:T(8,128)(2,1)S(1)}, u32[]{:S(2)}, u32[]{:S(2)}) collective-permute-start(bf16[256,640]{1,0:T(8,128)(2,1)S(1)} %fusion.44), channel_id=1, source_target_pairs={{0,16},{1,17},{2,18},{3,19},{4,20},{5,21},{6,22},{7,23},{8,24},{9,... | collective-permute-start | bytes 983048 | tf_op jit(solution)/shard_map/ppermute | solution.py:1364
  1029.5 17.9 %collective-permute-start.30 = (bf16[320,768]{1,0:T(8,128)(2,1)S(1)}, bf16[320,768]{1,0:T(8,128)(2,1)S(1)}, u32[]{:S(2)}, u32[]{:S(2)}) collective-permute-start(bf16[320,768]{1,0:T(8,128)(2,1)S(1)} %copy-done.50), channel_id=1, source_target_pairs={{0,4},{1,5},{2,6},{3,7},{4,0},{5,1},{6,2},{7,3},{8,12},{9,13},{10,... | collective-permute-start | bytes 1474568 | tf_op jit(solution)/shard_map/ppermute | solution.py:1364
  1033.0 21.0 %collective-permute-start.31 = (bf16[320,768]{1,0:T(8,128)(2,1)S(1)}, bf16[320,768]{1,0:T(8,128)(2,1)}, u32[]{:S(2)}, u32[]{:S(2)}) collective-permute-start(bf16[320,768]{1,0:T(8,128)(2,1)S(1)} %copy-done.49), channel_id=1, source_target_pairs={{0,6},{1,7},{2,0},{3,1},{4,2},{5,3},{6,4},{7,5},{8,14},{9,15},{10,... | collective-permute-start | bytes 1474568 | tf_op jit(solution)/shard_map/ppermute | solution.py:1364
  1062.8 11.4 collective-permute-start.18
  1063.9 11.9 %collective-permute-start.21 = (f32[2,640]{1,0:T(2,128)S(1)}, f32[2,640]{1,0:T(2,128)S(1)}, u32[]{:S(2)}, u32[]{:S(2)}) collective-permute-start(f32[2,640]{1,0:T(2,128)S(1)} %fusion.95), channel_id=1, source_target_pairs={{0,2},{1,3},{2,0},{3,1},{4,6},{5,7},{6,4},{7,5},{8,10},{9,11},{10,... | collective-permute-start | bytes 15368 | tf_op jit(solution)/shard_map/ppermute | solution.py:1364
  1074.2 11.2 collective-permute-start.19
  (95 other events, 1517.4 us)

commit v3 on v2

--- a/solution.py
+++ b/solution.py
@@ -560,7 +560,7 @@
     return [pltpu.SemaphoreType.DMA((count,)), pltpu.SemaphoreType.DMA((count,))]
 
 
-def gather_square(net, src, out, sems, local_sem, chunks):
+def gather_square(net, src, out, sems, local_sem, chunks, known=None):
     rows, width = src.shape
     half = rows // 2
 
@@ -573,47 +573,58 @@
     def part_of(s, part):
         return src.at[pl.ds(part * half, half), :] if s == 0 else block(s, 0, part)
 
-    own = pltpu.make_async_copy(src, block(0, 0), local_sem)
+    if known is None:
+        own = pltpu.make_async_copy(src, block(0, 0), local_sem)
+    else:
+        own = pltpu.make_async_copy(known, out.at[0], local_sem)
     own.start()
-    ups, xs, ys, lasts = [], [], [], []
-
-    def send_chunk(s):
+    ups, xs, ys, lasts = {}, {}, {}, {}
+    first = 0 if known is None else 1
+
+    def send_up(s):
         if s < chunks - 1:
             whole = src if s == 0 else block(s, 0)
-            ups.append(net.send(whole, block(s + 1, 0), sems, 7 * s, net.up))
-        xs.append([net.send(part_of(s, p), block(s, 1, p), sems, 7 * s + 1 + p, net.x) for p in (0, 1)])
-        ys.append(
-            [net.send(part_of(s, p), block(s, 2, p), sems, 7 * s + 3 + p, net.y) for p in (1, 0)][::-1]
-        )
+            ups[s + 1] = net.send(whole, block(s + 1, 0), sems, 7 * s, net.up)
+
+    def send_chunk(s):
+        xs[s] = {p: net.send(part_of(s, p), block(s, 1, p), sems, 7 * s + 1 + p, net.x) for p in (0, 1)}
+        ys[s] = {p: net.send(part_of(s, p), block(s, 2, p), sems, 7 * s + 3 + p, net.y) for p in (1, 0)}
 
     def forward(s):
         xs[s][0].wait_recv()
-        first = net.send(block(s, 1, 0), block(s, 3, 0), sems, 7 * s + 5, net.y)
+        one = net.send(block(s, 1, 0), block(s, 3, 0), sems, 7 * s + 5, net.y)
         ys[s][1].wait_recv()
-        second = net.send(block(s, 2, 1), block(s, 3, 1), sems, 7 * s + 6, net.x)
-        lasts.append([first, second])
-
-    send_chunk(0)
-    yield
+        two = net.send(block(s, 2, 1), block(s, 3, 1), sems, 7 * s + 6, net.x)
+        lasts[s] = [one, two]
+
+    if known is None:
+        send_chunk(0)
+        yield
+    if chunks > 1:
+        send_up(0)
+        yield
+    if known is None:
+        forward(0)
+        yield
     for s in range(1, chunks):
-        ups[s - 1].wait_recv()
+        ups[s].wait_recv()
+        send_up(s)
         send_chunk(s)
         yield
-        forward(s - 1)
+        forward(s)
         yield
-    forward(chunks - 1)
-    yield
     own.wait()
-    for s in range(chunks):
+    for s in range(first, chunks):
         xs[s][1].wait_recv()
         ys[s][0].wait_recv()
         lasts[s][0].wait_recv()
         lasts[s][1].wait_recv()
 
 
-def gather_columns(net, src, spot, sems, local_sem):
-    own = pltpu.make_async_copy(src, spot(0, net.k), local_sem)
-    own.start()
+def gather_columns(net, src, spot, sems, local_sem=None):
+    if local_sem is not None:
+        own = pltpu.make_async_copy(src, spot(0, net.k), local_sem)
+        own.start()
     twins = []
     for hops in range(net.ring):
         if hops:
@@ -623,7 +634,8 @@
             up = net.send(here, spot(hops, net.k), sems, hops, net.up)
         twins.append(net.send(here, spot(hops, net.k), sems, net.ring + hops, net.twin))
         yield
-    own.wait()
+    if local_sem is not None:
+        own.wait()
     for copy in twins:
         copy.wait_recv()
 
@@ -648,11 +660,12 @@
     return read
 
 
-def scatter_scratch(chunks, rows, width):
+def scatter_scratch(chunks, rows, width, resident=False):
     half = rows // 2
+    kept = (1, 2, 16, 128) if resident else (chunks, 2, half, width)
     return [
-        pltpu.VMEM((chunks, 2, half, width), jnp.bfloat16),
-        pltpu.VMEM((chunks, half, 2 * width), jnp.bfloat16),
+        pltpu.VMEM(kept, jnp.bfloat16),
+        pltpu.VMEM(kept[:1] + kept[2:] if resident else (chunks, half, 2 * width), jnp.bfloat16),
         pltpu.VMEM((chunks, 2, half, width), jnp.bfloat16),
         pltpu.VMEM((chunks, half, 2 * width), jnp.bfloat16),
         pltpu.VMEM((chunks, 2, half, width), jnp.bfloat16),
@@ -661,64 +674,68 @@
     ] + pair_sems(5 * chunks)
 
 
-def scatter_square(net, src, scratch, order, finish):
+def scatter_square(net, src, scratch, order, finish, resident=False):
     my_up, my_low, got_x, got_y, got_last, stage, load_sems, *sems = scratch
-    half, width = my_up.shape[2:]
+    half, width = got_x.shape[2:]
     upper, lower = pl.ds(0, half), pl.ds(half, half)
     column = lambda j, count=1: pl.ds(j * width, count * width)
     left, right = pl.ds(0, width), pl.ds(width, width)
     loads, sent = {}, {}
 
-    def first(s):
-        loads[s] = [
-            pltpu.make_async_copy(src.at[s, upper, column(0)], my_up.at[s, 0], load_sems.at[s, 0]),
-            pltpu.make_async_copy(src.at[s, upper, column(2)], my_up.at[s, 1], load_sems.at[s, 1]),
-            pltpu.make_async_copy(src.at[s, lower, column(0, 2)], my_low.at[s], load_sems.at[s, 2]),
+    def mine(i, part, j):
+        if resident:
+            return part_reader(src.at[order[i], upper if part == 0 else lower, column(j)])
+        if part == 0:
+            return part_reader(my_up, i, j // 2)
+        return part_reader(my_low, i, columns=(left, right)[j])
+
+    def first(i):
+        s = order[i]
+        loads[i] = [] if resident else [
+            pltpu.make_async_copy(src.at[s, upper, column(0)], my_up.at[i, 0], load_sems.at[i, 0]),
+            pltpu.make_async_copy(src.at[s, upper, column(2)], my_up.at[i, 1], load_sems.at[i, 1]),
+            pltpu.make_async_copy(src.at[s, lower, column(0, 2)], my_low.at[i], load_sems.at[i, 2]),
         ]
-        sent[s] = [
-            net.send(src.at[s, upper, column(3)], got_x.at[s, 1], sems, 5 * s, net.x),
-            net.send(src.at[s, lower, column(2, 2)], got_y.at[s], sems, 5 * s + 1, net.y),
-            net.send(src.at[s, upper, column(1)], got_x.at[s, 0], sems, 5 * s + 2, net.x),
+        sent[i] = [
+            net.send(src.at[s, upper, column(3)], got_x.at[i, 1], sems, 5 * i, net.x),
+            net.send(src.at[s, lower, column(2, 2)], got_y.at[i], sems, 5 * i + 1, net.y),
+            net.send(src.at[s, upper, column(1)], got_x.at[i, 0], sems, 5 * i + 2, net.x),
         ]
-        for load in loads[s]:
+        for load in loads[i]:
             load.start()
 
-    def second(s):
-        loads[s][1].wait()
-        sent[s][0].wait_recv()
-        add_slabs(stage.at[s, 0], [part_reader(my_up, s, 1), part_reader(got_x, s, 1)])
-        sent[s].append(net.send(stage.at[s, 0], got_last.at[s, 0], sems, 5 * s + 3, net.y))
-        loads[s][2].wait()
-        sent[s][1].wait_recv()
-        add_slabs(
-            stage.at[s, 1],
-            [part_reader(my_low, s, columns=right), part_reader(got_y, s, columns=right)],
-        )
-        sent[s].append(net.send(stage.at[s, 1], got_last.at[s, 1], sems, 5 * s + 4, net.x))
-
-    def third(s):
-        loads[s][0].wait()
-        for copy in sent[s][2:]:
+    def second(i):
+        for load in loads[i]:
+            load.wait()
+        sent[i][0].wait_recv()
+        add_slabs(stage.at[i, 0], [mine(i, 0, 2), part_reader(got_x, i, 1)])
+        sent[i].append(net.send(stage.at[i, 0], got_last.at[i, 0], sems, 5 * i + 3, net.y))
+        sent[i][1].wait_recv()
+        add_slabs(stage.at[i, 1], [mine(i, 1, 1), part_reader(got_y, i, columns=right)])
+        sent[i].append(net.send(stage.at[i, 1], got_last.at[i, 1], sems, 5 * i + 4, net.x))
+
+    def third(i):
+        for copy in sent[i][2:]:
             copy.wait_recv()
         finish(
-            s,
-            [part_reader(my_up, s, 0), part_reader(got_x, s, 0), part_reader(got_last, s, 0)],
+            order[i],
+            [mine(i, 0, 0), part_reader(got_x, i, 0), part_reader(got_last, i, 0)],
             [
-                part_reader(my_low, s, columns=left),
-                part_reader(got_y, s, columns=left),
-                part_reader(got_last, s, 1),
+                mine(i, 1, 0),
+                part_reader(got_y, i, columns=left),
+                part_reader(got_last, i, 1),
             ],
         )
 
     for i in range(len(order) + 2):
         if i < len(order):
-            first(order[i])
+            first(i)
             yield
         if 0 <= i - 1 < len(order):
-            second(order[i - 1])
+            second(i - 1)
             yield
         if 0 <= i - 2:
-            third(order[i - 2])
+            third(i - 2)
             yield
 
 
@@ -729,10 +746,9 @@
     ] + pair_sems(ring - 1)
 
 
-def ring_finish(net, scratch, target):
+def ring_finish(net, scratch, target, copies):
     landed, leaving, *sems = scratch
     rows = landed.shape[1]
-    copies = []
 
     def finish(s, upper, lower):
         turn = (s - 1) % net.ring
@@ -750,27 +766,18 @@
     return finish
 
 
-def scatter_columns(net, src, out, scratch):
-    mine, got_twin, landed, leaving, load_sems, twin_send, twin_recv, *sems = scratch
-    loads, twins, copies = {}, {}, []
+def scatter_columns(net, part, out, scratch):
+    got_twin, landed, leaving, twin_send, twin_recv, *sems = scratch
+    twins, copies = {}, []
     order = list(range(1, net.ring)) + [0]
     for hops in order:
-        loads[hops] = pltpu.make_async_copy(
-            src.at[net.place(hops), net.k], mine.at[hops], load_sems.at[hops]
-        )
-        loads[hops].start()
         twins[hops] = net.send(
-            src.at[net.place(hops), 1 - net.k],
-            got_twin.at[hops],
-            (twin_send, twin_recv),
-            hops,
-            net.twin,
+            part(hops, 1 - net.k), got_twin.at[hops], (twin_send, twin_recv), hops, net.twin
         )
     yield
     for turn, hops in enumerate(order):
-        loads[hops].wait()
         twins[hops].wait_recv()
-        terms = [part_reader(mine, hops), part_reader(got_twin, hops)]
+        terms = [part_reader(part(hops, net.k)), part_reader(got_twin, hops)]
         if turn:
             copies[turn - 1].wait_recv()
             terms.append(part_reader(landed, turn - 1))
@@ -783,10 +790,8 @@
 def scatter_columns_scratch(ring, rows, width):
     return [
         pltpu.VMEM((ring, rows, width), jnp.bfloat16),
-        pltpu.VMEM((ring, rows, width), jnp.bfloat16),
         pltpu.VMEM((ring - 1, rows, width), jnp.bfloat16),
         pltpu.VMEM((ring - 1, rows, width), jnp.bfloat16),
-        pltpu.SemaphoreType.DMA((ring,)),
     ] + pair_sems(ring) + pair_sems(ring - 1)
 
 
@@ -800,81 +805,157 @@
         out_specs=[vmem if i in out_vmem else anywhere for i in range(len(out_shape))],
         scratch_shapes=scratch,
         compiler_params=pltpu.CompilerParams(
-            collective_id=collective_id, has_side_effects=True, vmem_limit_bytes=60 * MIB
+            collective_id=collective_id, has_side_effects=True, vmem_limit_bytes=63 * MIB
         ),
         cost_estimate=cost,
         name=name,
     )(*operands)
 
 
-def front_gather(n_rows, n_cols, block, weights, small):
+def spread_columns(net, packed, spot, sems, local_sem):
+    own = pltpu.make_async_copy(packed.at[net.chip(0)], spot(0, net.k), local_sem)
+    own.start()
+    pieces = []
+    for hops in range(1, net.ring):
+        target = (net.r, lax.rem(net.c + 2 * hops, net.n_cols))
+        pieces.append(
+            net.send(packed.at[net.chip(-hops)], spot_at(spot, net, hops), sems, hops, target)
+        )
+    yield
+    own.wait()
+    twins = [net.send(spot(0, net.k), spot(0, net.k), sems, net.ring, net.twin)]
+    yield
+    for hops in range(1, net.ring):
+        pieces[hops - 1].wait_recv()
+        here = spot(hops, net.k)
+        twins.append(net.send(here, here, sems, net.ring + hops, net.twin))
+        yield
+    for copy in twins:
+        copy.wait_recv()
+
+
+def spot_at(spot, net, hops):
+    return spot(0, net.k)
+
+
+def first_phase(n_rows, n_cols, block, grads, weights, small, weights_out, packed, slot_map, tables):
     ring = n_cols // 2
-    shape = lambda *dims: jax.ShapeDtypeStruct(dims, jnp.bfloat16)
-
-    def kernel(x, w, s, x_out, w_out, s_out, xs, xr, ws, wr, ss, sr, local):
-        net = Links(n_rows, n_cols)
-        net.greet([net.x, net.y, net.up, net.down, net.twin])
-        spot = lambda out: lambda hops, core: out.at[net.place(hops), core]
-        run_together(
-            gather_columns(net, s, spot(s_out), (ss, sr), local.at[2]),
-            gather_square(net, x, x_out, (xs, xr), local.at[0], 1),
-            gather_columns(net, w, spot(w_out), (ws, wr), local.at[1]),
-        )
-        net.finish()
-
-    return remote_call(
-        kernel,
-        "front_gather",
-        1,
-        [
-            shape(1, block.shape[0], n_rows * block.shape[1]),
-            shape(ring, 2, *weights.shape),
-            shape(ring, 2, *small.shape),
-        ],
-        pair_sems(7) + pair_sems(2 * ring) + pair_sems(2 * ring) + [pltpu.SemaphoreType.DMA((3,))],
-        (block, weights, small),
-    )
-
-
-def attention_gather(n_rows, n_cols, queries, kv, grads, weights, slot_map):
-    ring = n_cols // 2
-    length, width = queries.shape
-    heads = width // HEAD_DIM
+    length, row_width = block.shape
+    model = n_rows * row_width
+    col_width, in_width = weights.shape
+    q_width = weights_out.shape[1]
+    heads = q_width // HEAD_DIM
+    small_width = small.shape[1]
+    experts = slot_map.shape[0]
     scale = 1.0 / math.sqrt(HEAD_DIM)
+    pieces = 2
+    piece = length // pieces
+    bf16, f32 = jnp.bfloat16, jnp.float32
     shape = jax.ShapeDtypeStruct
 
     def kernel(
-        q, kv_in, g, w, m, out, lse, kv_out, g_out, w_out, m_out,
-        kv_all, top, total, acc, gs, gr, ws, wr, ks, kr, ms, mr, local,
+        x_in, g_in, w_in, small_in, wo_in, packed_in, map_in, cosine, sine,
+        x_out, normed_out, w_out, small_out, q, kv_out, out, lse, wo_out, g_out, rows_out, map_out,
+        shared_out, sum_out, gains_out,
+        x, normed, w, small_all, kv, wo, proj, proj_sum, second, result, projected, top, total, acc,
+        *sems,
     ):
+        scratch, sems = list(sems[:9]), list(sems[9:])
+        pairs = lambda: (sems.pop(0), sems.pop(0))
+        x_sems, g_sems, w_sems, small_sems, wo_sems, kv_sems = [pairs() for _ in range(6)]
+        map_sems, rows_sems, shared_sems, sum_sems, sum_sems_two = [pairs() for _ in range(5)]
+        local = sems.pop(0)
         net = Links(n_rows, n_cols)
         others = net.spread_partners()
         net.greet([device for _, _, device in others] + [net.twin])
+        by_place = lambda ref: lambda hops, core: ref.at[
+            pl.ds((net.place(hops) * 2 + core) * col_width, col_width), :
+        ]
+
+        x_steps = gather_square(net, x_in, x, x_sems, local.at[0], 1)
+        small_steps = gather_columns(net, small_in, by_place(small_all), small_sems, local.at[1])
+        w_steps = gather_columns(net, w_in, by_place(w), w_sems, local.at[2])
+        wo_steps = gather_columns(net, wo_in, by_place(wo), wo_sems, local.at[3])
+        g_steps = gather_square(net, g_in, g_out, g_sems, local.at[4], ring)
+        saves = []
+
+        def save(src, dst):
+            copy = pltpu.make_async_copy(src, dst, local.at[8 + len(saves)])
+            copy.start()
+            saves.append(copy)
+
+        next(small_steps)
+        next(x_steps)
+        next(w_steps)
+        maps = []
+        for number, (hops, bits, device) in enumerate(others):
+            maps.append(net.send(map_in, map_out.at[hops, net.r], map_sems, number, device))
+        own_map = pltpu.make_async_copy(map_in, map_out.at[0, net.r], local.at[5])
+        own_map.start()
+        next(small_steps)
+        next(w_steps)
+        next(x_steps)
+        next(g_steps)
+        next(small_steps)
+        next(small_steps)
+        next(w_steps)
+        run_together(x_steps, small_steps)
+        save(x.at[0], x_out)
+        save(small_all, small_out)
+        gains = small_all[...].astype(f32).T
+        gains_out[...] = gains[experts : experts + 8]
+        first_gain = gains[experts : experts + 1]
+        second_gain = gains[experts + 1 : experts + 2]
+
+        @pl.loop(0, length // 64)
+        def _(i):
+            at = pl.ds(pl.multiple_of(i * 64, 64), 64)
+            values = x[0, at, :].astype(f32)
+            inverse = lax.rsqrt(jnp.mean(values * values, -1, keepdims=True) + NORM_EPS)
+            normed[at, :] = (values * inverse * first_gain).astype(bf16)
+
+        save(normed, normed_out)
+        next(wo_steps)
+        next(w_steps)
+        run_together(w_steps)
+        save(w, w_out)
+        next(g_steps)
+
+        projected[...] = matmul(normed[...], w[...])
+        next(wo_steps)
+
+        def rotate(columns):
+            values = projected[:, columns]
+            turned = pltpu.roll(values, HEAD_DIM // 2, 1)
+            return (values * cosine[...] + turned * sine[...]).astype(bf16)
+
+        for head in range(heads + 1):
+            columns = slice(head * HEAD_DIM, (head + 1) * HEAD_DIM)
+            if head < heads:
+                q[:, columns] = rotate(columns)
+            else:
+                kv[net.c, :, :HEAD_DIM] = rotate(columns)
+        kv[net.c, :, HEAD_DIM:] = projected[:, q_width + HEAD_DIM :].astype(bf16)
         kv_steps = gather_columns(
-            net, kv_in, lambda hops, core: kv_all.at[2 * net.chip(hops) + core], (ks, kr), local.at[0]
+            net, kv.at[net.c], lambda hops, core: kv.at[2 * net.chip(hops) + core], kv_sems
         )
         next(kv_steps)
-        maps = []
-        for number, (hops, bits, device) in enumerate(others):
-            maps.append(net.send(m, m_out.at[hops, net.r], (ms, mr), number, device))
-        own_map = pltpu.make_async_copy(m, m_out.at[0, net.r], local.at[1])
-        own_map.start()
-        w_steps = gather_columns(
-            net, w, lambda hops, core: w_out.at[net.place(hops), core], (ws, wr), local.at[2]
-        )
-        g_steps = gather_square(net, g, g_out, (gs, gr), local.at[3], ring)
         next(g_steps)
-        next(w_steps)
+        next(kv_steps)
+        next(wo_steps)
+        next(kv_steps)
+        next(g_steps)
+        next(kv_steps)
+        next(wo_steps)
         run_together(kv_steps)
-        kv_save = pltpu.make_async_copy(kv_all, kv_out, local.at[4])
-        kv_save.start()
+        save(kv, kv_out)
 
         for head in range(heads):
             columns = slice(head * HEAD_DIM, (head + 1) * HEAD_DIM)
             queries = q[:, columns]
 
-            def part(block):
-                return scores_of(kv_all[block, :, :HEAD_DIM], queries, scale), kv_all[block, :, HEAD_DIM:]
+            def part(number):
+                return scores_of(kv[number, :, :HEAD_DIM], queries, scale), kv[number, :, HEAD_DIM:]
 
             scores, values = part(net.c)
             scores = jnp.where(causal_mask(scores), scores, NEG_LARGE)
@@ -882,209 +963,636 @@
             probs = jnp.exp(scores - high)
             top[...] = high
             total[...] = jnp.sum(probs, 0, keepdims=True)
-            acc[...] = matmul_tn(values, probs.astype(jnp.bfloat16))
+            acc[...] = matmul_tn(values, probs.astype(bf16))
 
             @pl.loop(0, net.c)
-            def _(block):
-                scores, values = part(block)
+            def _(number):
+                scores, values = part(number)
                 high = jnp.maximum(top[...], jnp.max(scores, 0, keepdims=True))
                 probs = jnp.exp(scores - high)
                 shrink = jnp.exp(top[...] - high)
                 top[...] = high
                 total[...] = total[...] * shrink + jnp.sum(probs, 0, keepdims=True)
-                acc[...] = acc[...] * shrink + matmul_tn(values, probs.astype(jnp.bfloat16))
+                acc[...] = acc[...] * shrink + matmul_tn(values, probs.astype(bf16))
 
             out[:, columns] = (acc[...] / total[...]).T
             lse[head] = top[...] + jnp.log(total[...])
-            next(g_steps, None)
-            next(w_steps, None)
-
-        run_together(g_steps, w_steps)
+            if head in (0, 3):
+                next(g_steps)
+
+        run_together(wo_steps)
+        save(wo, wo_out)
+        heads_out = out[...].astype(bf16)
+        for s in range(pieces):
+            for j in range(n_rows):
+                at = slice(j * row_width, (j + 1) * row_width)
+                proj[s, :, at] = matmul_nt(
+                    heads_out[s * piece : (s + 1) * piece], wo[at, :]
+                ).astype(bf16)
+        gathers = []
+
+        def finish(s, upper, lower):
+            add_slabs(result.at[s, pl.ds(0, piece // 2), :], upper)
+            add_slabs(result.at[s, pl.ds(piece // 2, piece // 2), :], lower)
+            steps = gather_square(
+                net, result.at[s], proj_sum.at[pl.ds(s, 1)], (sum_sems, sum_sems_two)[s],
+                local.at[6 + s], 1,
+            )
+            next(steps)
+            gathers.append(steps)
+
+        shared_steps = spread_columns(
+            net, packed_in, by_place(shared_out), shared_sems, local.at[8 + 8]
+        )
+        sum_steps = scatter_square(net, proj, scratch, list(range(pieces)), finish, resident=True)
+        next(sum_steps)
+        next(shared_steps)
+        next(sum_steps)
+        run_together(sum_steps)
+        next(shared_steps)
+
+        def second_norm(s):
+            @pl.loop(0, piece // 64)
+            def _(i):
+                at = pl.ds(pl.multiple_of(i * 64, 64), 64)
+                there = pl.ds(pl.multiple_of(s * piece + i * 64, 64), 64)
+                values = x[0, there, :].astype(f32) + proj_sum[s, at, :].astype(f32)
+                inverse = lax.rsqrt(jnp.mean(values * values, -1, keepdims=True) + NORM_EPS)
+                second[there, :] = (values * inverse * second_gain).astype(bf16)
+
+        for s in range(pieces):
+            run_together(gathers[s])
+            second_norm(s)
+        save(proj_sum, sum_out)
+        rows_steps = gather_square(
+            net, second.at[:, pl.ds(0, row_width)], rows_out, rows_sems, local.at[8 + 9], ring,
+            known=second,
+        )
+        next(rows_steps)
+        next(g_steps, None)
+        next(rows_steps)
+        next(shared_steps)
+        next(g_steps, None)
+        run_together(rows_steps, g_steps, shared_steps)
         own_map.wait()
         for copy in maps:
             copy.wait_recv()
-        kv_save.wait()
+        for copy in saves:
+            copy.wait()
         net.finish()
 
     partners = n_rows * ring - 1
+    vmem = pltpu.VMEM
     return remote_call(
         kernel,
-        "attention_gather",
-        2,
+        "first_phase",
+        1,
         [
-            shape((length, width), jnp.float32),
-            shape((heads, 1, length), jnp.float32),
-            shape((n_cols, *kv.shape), jnp.bfloat16),
-            shape((ring, grads.shape[0], n_rows * grads.shape[1]), jnp.bfloat16),
-            shape((ring, 2, *weights.shape), jnp.bfloat16),
-            shape((ring, n_rows, *slot_map.shape), jnp.float32),
+            shape((length, model), bf16),
+            shape((length, model), bf16),
+            shape((model, in_width), bf16),
+            shape((model, small_width), bf16),
+            shape((length, q_width), bf16),
+            shape((n_cols, length, 2 * HEAD_DIM), bf16),
+            shape((length, q_width), f32),
+            shape((heads, 1, length), f32),
+            shape((model, q_width), bf16),
+            shape((ring, length, model), bf16),
+            shape((ring, length, model), bf16),
+            shape((ring, n_rows, *slot_map.shape), f32),
+            shape((model, packed.shape[2]), bf16),
+            shape((pieces, piece, model), bf16),
+            shape((8, model), f32),
         ],
         [
-            pltpu.VMEM((n_cols, *kv.shape), jnp.bfloat16),
-            pltpu.VMEM((1, length), jnp.float32),
-            pltpu.VMEM((1, length), jnp.float32),
-            pltpu.VMEM((HEAD_DIM, length), jnp.float32),
+            vmem((1, length, model), bf16),
+            vmem((length, model), bf16),
+            vmem((model, in_width), bf16),
+            vmem((model, small_width), bf16),
+            vmem((n_cols, length, 2 * HEAD_DIM), bf16),
+            vmem((model, q_width), bf16),
+            vmem((pieces, piece, model), bf16),
+            vmem((pieces, piece, model), bf16),
+            vmem((length, model), bf16),
+            vmem((pieces, piece, row_width), bf16),
+            vmem((length, in_width), f32),
+            vmem((1, length), f32),
+            vmem((1, length), f32),
+            vmem((HEAD_DIM, length), f32),
         ]
+        + scatter_scratch(pieces, piece, row_width, resident=True)
+        + pair_sems(7)
         + pair_sems(7 * ring)
         + pair_sems(2 * ring)
         + pair_sems(2 * ring)
+        + pair_sems(2 * ring)
+        + pair_sems(2 * ring)
         + pair_sems(partners)
-        + [pltpu.SemaphoreType.DMA((5,))],
-        (queries, kv, grads, weights, slot_map),
-        in_vmem=(0,),
-        out_vmem=(0, 1),
-    )
-
-
-def rows_sum(n_rows, n_cols, parts):
-    pieces = 2
-    rows, whole = parts.shape
-    width = whole // n_rows
-    piece = rows // pieces
-    shape = jax.ShapeDtypeStruct((pieces, piece, whole), jnp.bfloat16)
-
-    def kernel(src, out, result, *rest):
-        scratch, (gs0, gr0, gs1, gr1, local) = rest[:-5], rest[-5:]
-        net = Links(n_rows, n_cols)
-        net.greet([net.x, net.y])
-        gathers = []
-
-        def finish(s, upper, lower):
-            add_slabs(result.at[s, pl.ds(0, piece // 2), :], upper)
-            add_slabs(result.at[s, pl.ds(piece // 2, piece // 2), :], lower)
-            sems = ((gs0, gr0), (gs1, gr1))[s]
-            steps = gather_square(net, result.at[s], out.at[pl.ds(s, 1)], sems, local.at[s], 1)
-            next(steps)
-            gathers.append(steps)
-
-        run_together(scatter_square(net, src, scratch, list(range(pieces)), finish))
-        run_together(*gathers)
-        net.finish()
-
-    return remote_call(
-        kernel,
-        "rows_sum",
-        3,
-        [shape],
-        [pltpu.VMEM((pieces, piece, width), jnp.bfloat16)]
-        + scatter_scratch(pieces, piece, width)
+        + pair_sems(7 * ring)
+        + pair_sems(2 * ring)
         + pair_sems(7)
         + pair_sems(7)
-        + [pltpu.SemaphoreType.DMA((pieces,))],
-        (parts.reshape(shape.shape),),
-    )[0].reshape(rows, whole)
-
-
-def token_gather(n_rows, n_cols, block):
+        + [pltpu.SemaphoreType.DMA((18,))],
+        (block, grads, weights, small, weights_out, packed, slot_map, *tables),
+        in_vmem=(7, 8),
+        out_vmem=(4, 6, 7, 14),
+    )
+
+
+def token_sum(n_rows, n_cols, parts, gates, expert_rows, probs, router, token_rows, gains):
     ring = n_cols // 2
-
-    def kernel(x, out, xs, xr, local):
-        net = Links(n_rows, n_cols)
-        net.greet([net.x, net.y, net.up, net.down])
-        run_together(gather_square(net, x, out, (xs, xr), local.at[0], ring))
-        net.finish()
-
-    return remote_call(
-        kernel,
-        "token_gather",
-        4,
-        [jax.ShapeDtypeStruct((ring, block.shape[0], n_rows * block.shape[1]), jnp.bfloat16)],
-        pair_sems(7 * ring) + [pltpu.SemaphoreType.DMA((1,))],
-        (block,),
-    )[0]
-
-
-def token_sum(n_rows, n_cols, parts, gates):
-    ring = n_cols // 2
-    rows, width = parts.shape[1], parts.shape[2] // n_rows
+    rows, model = parts.shape[1:]
+    width = model // n_rows
     experts = n_rows * ring
-
-    def kernel(src, gate, out, gate_out, result, *rest):
+    slot_rows, d_part, e_act, d_gate, d_up = expert_rows
+    n_slots, hidden = e_act.shape
+    half = hidden // 2
+    bf16, f32 = jnp.bfloat16, jnp.float32
+    shape = jax.ShapeDtypeStruct
+
+    def kernel(
+        src, gate, xr_in, dp_in, act_in, dg_in, du_in, probs, router, x_in, proj_in, g_in, gains,
+        d_attn, d_resid, gain_out, gate_out, out_g, out_u, out_d, land_g, land_u, land_d,
+        result, second, xr, dp, act, dg, du, leave_a, leave_b, landed_a, landed_b, full_a, full_b,
+        gate_own, high_ref, low_ref, *rest,
+    ):
         scratch, ring_parts = rest[:9], rest[9:13]
-        gs, gr, ms, mr, local = rest[13:]
+        gs, gr, ms, mr, es, er, local, sem = rest[13:]
+        leaving, landed, full = (leave_a, leave_b), (landed_a, landed_b), (full_a, full_b)
         net = Links(n_rows, n_cols)
         others = net.spread_partners()
-        net.greet([device for _, _, device in others])
+        net.greet([device for _, _, device in others] + [net.twin])
         mine = net.r * ring + net.z
+        order = list(range(1, ring)) + [0]
+        steps = scatter_square(net, src, scratch, order, ring_finish(net, ring_parts, result, []))
+        next(steps)
         copies = []
         own = pltpu.make_async_copy(gate, gate_out.at[mine], local.at[1])
         own.start()
         for number, (hops, bits, device) in enumerate(others):
             copies.append(net.send(gate, gate_out.at[mine], (ms, mr), number, device))
-        order = list(range(1, ring)) + [0]
-        run_together(
-            scatter_square(net, src, scratch, order, ring_finish(net, ring_parts, result))
-        )
-        run_together(gather_square(net, result, out, (gs, gr), local.at[0], 1))
+        next(steps)
+
+        loads = [
+            pltpu.make_async_copy(a, b, sem.at[i])
+            for i, (a, b) in enumerate(
+                ((xr_in, xr), (dg_in, dg), (du_in, du), (act_in, act), (dp_in, dp))
+            )
+        ]
+        for load in loads:
+            load.start()
+        ours, theirs = slice(0, half), slice(half, hidden)
+        sends, leaves, stores = [], {}, {}
+
+        def slot_of(kind, j):
+            return kind // 2, j % 2 if kind < 2 else 0
+
+        def tile(kind, j, part):
+            columns = slice(j * width, (j + 1) * width)
+            if kind < 2:
+                return matmul_tn(xr[:, columns], (dg, du)[kind][:, part])
+            return matmul_tn(act[:, part], dp[:, columns])
+
+        def land(kind, j, order=False):
+            place = net.flip(j) if order else j
+            at = pl.ds(pl.multiple_of(place * width, width), width)
+            if kind < 2:
+                ref = ((land_g, land_u), (out_g, out_u))[order][kind]
+                return ref.at[at, :]
+            return (land_d, out_d)[order].at[:, at]
+
+        def give(kind, j):
+            group, slot = slot_of(kind, j)
+            if (group, slot) in leaves:
+                leaves[group, slot].wait_send()
+            buffer = leaving[group]
+            buffer[slot] = tile(kind, j, theirs).astype(bf16)
+            copy = net.send(buffer.at[slot], land(kind, j), (es, er), 4 * kind + j, net.twin)
+            net.started.pop()
+            leaves[group, slot] = copy
+            sends.append(copy)
+
+        def keep(kind, j):
+            group, slot = slot_of(kind, j)
+            buffer, got = full[group], landed[group]
+            sends[4 * kind + j].wait_recv()
+            load = pltpu.make_async_copy(land(kind, j), got.at[slot], sem.at[5 + slot])
+            load.start()
+            if (group, slot) in stores:
+                stores[group, slot].wait()
+            product = tile(kind, j, ours)
+            load.wait()
+            buffer[slot] = product + got[slot].astype(f32)
+            store = pltpu.make_async_copy(
+                buffer.at[slot], land(kind, j, True), sem.at[7 + 2 * group + slot]
+            )
+            store.start()
+            stores[group, slot] = store
+
+        for load in loads[:3]:
+            load.wait()
+        for kind in (0, 1):
+            for j in range(n_rows):
+                give(kind, j)
+            next(steps)
+        for load in loads[3:]:
+            load.wait()
+        for j in range(n_rows):
+            give(2, j)
+        next(steps)
+        next(steps)
+        for kind in (0, 1, 2):
+            next(steps)
+            for j in range(n_rows):
+                keep(kind, j)
+            next(steps)
+        for copy in leaves.values():
+            copy.wait_send()
+        for store in stores.values():
+            store.wait()
+
+        run_together(steps)
+
+        x, proj, g = xr.at[pl.ds(0, rows)], xr.at[pl.ds(rows, rows)], dp.at[pl.ds(0, rows)]
+        loads = [
+            pltpu.make_async_copy(a, b, sem.at[i])
+            for i, (a, b) in enumerate(((x_in, x), (proj_in, proj), (g_in, g)))
+        ]
+        for load in loads:
+            load.start()
+        gather = gather_square(net, result, second, (gs, gr), local.at[0], 1)
+        next(gather)
         own.wait()
         for copy in copies:
             copy.wait_recv()
+        gate_load = pltpu.make_async_copy(gate_out.at[:, net.z], gate_own, sem.at[3])
+        gate_load.start()
+        gate_load.wait()
+        d_gates = jnp.concatenate([gate_own[...], jnp.zeros((128 - experts, rows), f32)], 0).T
+        d_logits = probs[...] * (d_gates - jnp.sum(probs[...] * d_gates, -1, keepdims=True))
+        high = d_logits.astype(bf16)
+        high_ref[...] = high
+        low_ref[...] = (d_logits - high.astype(f32)).astype(bf16)
+        for load in loads:
+            load.wait()
+        run_together(gather)
+        gain = gains[1:2]
+        gain_out[...] = jnp.zeros_like(gain_out)
+
+        @pl.loop(0, rows // 128)
+        def _(i):
+            at = pl.ds(pl.multiple_of(i * 128, 128), 128)
+            values = x[at, :].astype(f32) + proj[at, :].astype(f32)
+            inverse = lax.rsqrt(jnp.mean(values * values, -1, keepdims=True) + NORM_EPS)
+            unit = values * inverse
+            d_second = second[0, at, :].astype(f32)
+            d_second = d_second + matmul_nt(high_ref[at, :], router[...])
+            d_second = d_second + matmul_nt(low_ref[at, :], router[...])
+            d_unit = d_second * gain
+            moment = jnp.mean(d_unit * unit, -1, keepdims=True)
+            resid = g[at, :].astype(f32) + inverse * (d_unit - unit * moment)
+            d_attn[at, :] = resid.astype(bf16)
+            d_resid[at, :] = resid[:, :width]
+            along = (d_second[:, :width] * unit[:, :width]).reshape(16, 8, width)
+            gain_out[...] += jnp.sum(along, 0)
+
         net.finish()
 
-    out, gate_out = remote_call(
+    x, proj, g = token_rows
+    return remote_call(
         kernel,
         "token_sum",
         5,
         [
-            jax.ShapeDtypeStruct((1, rows, n_rows * width), jnp.bfloat16),
-            jax.ShapeDtypeStruct((experts, *gates.shape), jnp.float32),
+            shape((rows, model), bf16),
+            shape((rows, width), f32),
+            shape((8, width), f32),
+            shape((experts, *gates.shape), f32),
+            shape((model, half), f32),
+            shape((model, half), f32),
+            shape((half, model), f32),
+            shape((model, half), bf16),
+            shape((model, half), bf16),
+            shape((half, model), bf16),
         ],
-        [pltpu.VMEM((rows, width), jnp.bfloat16)]
+        [
+            pltpu.VMEM((rows, width), bf16),
+            pltpu.VMEM((1, rows, model), bf16),
+            pltpu.VMEM((n_slots, model), bf16),
+            pltpu.VMEM((n_slots, model), bf16),
+            pltpu.VMEM((n_slots, hidden), bf16),
+            pltpu.VMEM((n_slots, hidden), bf16),
+            pltpu.VMEM((n_slots, hidden), bf16),
+            pltpu.VMEM((2, width, half), bf16),
+            pltpu.VMEM((1, half, width), bf16),
+            pltpu.VMEM((2, width, half), bf16),
+            pltpu.VMEM((1, half, width), bf16),
+            pltpu.VMEM((2, width, half), f32),
+            pltpu.VMEM((1, half, width), f32),
+            pltpu.VMEM((experts, rows), f32),
+            pltpu.VMEM((rows, 128), bf16),
+            pltpu.VMEM((rows, 128), bf16),
+        ]
         + scatter_scratch(ring, rows, width)
         + ring_scratch(ring, rows, width)
         + pair_sems(7)
         + pair_sems(experts - 1)
-        + [pltpu.SemaphoreType.DMA((2,))],
-        (parts, gates),
-    )
-    return out[0], gate_out
-
-
-def last_sums(n_rows, n_cols, parts, weights):
+        + pair_sems(3 * n_rows)
+        + [pltpu.SemaphoreType.DMA((2,)), pltpu.SemaphoreType.DMA((10,))],
+        (parts, gates, *expert_rows, probs, router, x, proj, g, gains),
+        in_vmem=(7, 8, 12),
+        out_vmem=(0, 1, 2),
+    )
+
+
+def attention_back(
+    n_rows, n_cols, d_attn, weights_out, weights_in, queries, kv, heads_out, lse, tables, parts
+):
     ring = n_cols // 2
-    rows, width = parts.shape[1], parts.shape[2] // n_rows
-
-    def kernel(src, w, out, w_out, *rest):
-        scratch, ring_parts, column_parts = rest[:9], rest[9:13], rest[13:]
+    length, model = d_attn.shape
+    q_width = weights_out.shape[1]
+    in_width = weights_in.shape[1]
+    col_width = model // n_cols
+    width = model // n_rows
+    heads = q_width // HEAD_DIM
+    scale = 1.0 / math.sqrt(HEAD_DIM)
+    bf16, f32 = jnp.bfloat16, jnp.float32
+    shape = jax.ShapeDtypeStruct
+
+    def kernel(
+        d_attn, wo, w_in, q, kv, out, lse, cosine, sine, y_in,
+        d_proj, d_first, y_out, wo_out,
+        w, go, delta, dqt, dkv, dkv_own, wo_part, *rest,
+    ):
+        scratch, ring_parts = rest[:9], rest[9:13]
+        kv_parts, wo_parts, local = rest[13:20], rest[20:27], rest[27]
         net = Links(n_rows, n_cols)
         net.greet([net.x, net.y, net.up, net.down, net.twin])
-        order = list(range(1, ring)) + [0]
-        run_together(
-            scatter_columns(net, w, w_out, column_parts),
-            scatter_square(net, src, scratch, order, ring_finish(net, ring_parts, out)),
+        w_load = pltpu.make_async_copy(w_in, w, local.at[0])
+        w_load.start()
+        copies = []
+        y_steps = scatter_square(
+            net, y_in, scratch, list(range(1, ring)), ring_finish(net, ring_parts, None, copies)
         )
+        next(y_steps)
+        next(y_steps)
+        by_place = lambda ref: lambda hops, core: ref.at[
+            pl.ds((net.place(hops) * 2 + core) * col_width, col_width), :
+        ]
+
+        go[...] = matmul(d_attn[...], wo[...]).astype(bf16)
+        wo_part[...] = matmul_tn(d_attn[...], out[...].astype(bf16)).astype(bf16)
+        wo_steps = scatter_columns(net, by_place(wo_part), wo_out, wo_parts)
+        next(wo_steps)
+        for head in range(heads):
+            columns = slice(head * HEAD_DIM, (head + 1) * HEAD_DIM)
+            product = (go[:, columns].astype(f32) * out[:, columns]).T
+            delta[head] = jnp.sum(product, 0, keepdims=True)
+        dqt[...] = jnp.zeros_like(dqt)
+        dkv[...] = jnp.zeros_like(dkv)
+        next(wo_steps)
+        next(y_steps)
+
+        def one_block(number, masked):
+            keys = kv[number, :, :HEAD_DIM]
+            values = kv[number, :, HEAD_DIM:]
+            keys_t = keys.T
+            d_key = jnp.zeros((length, HEAD_DIM), f32)
+            d_value = jnp.zeros((length, HEAD_DIM), f32)
+            for head in range(heads):
+                columns = slice(head * HEAD_DIM, (head + 1) * HEAD_DIM)
+                queries = q[:, columns]
+                grads = go[:, columns]
+                probs = jnp.exp(scores_of(keys, queries, scale) - lse[head])
+                if masked:
+                    probs = jnp.where(causal_mask(probs), probs, 0.0)
+                d_probs = matmul_nt(values, grads)
+                d_scores = (probs * (d_probs - delta[head])).astype(bf16)
+                d_value = d_value + matmul(probs.astype(bf16), grads)
+                d_key = d_key + matmul(d_scores, queries)
+                dqt[head] = dqt[head] + matmul(keys_t, d_scores)
+            dkv[number, :, :HEAD_DIM] = (d_key * scale).astype(bf16)
+            dkv[number, :, HEAD_DIM:] = d_value.astype(bf16)
+
+        one_block(net.c, True)
+
+        @pl.loop(0, net.c)
+        def _(number):
+            one_block(number, False)
+
+        kv_steps = scatter_columns(
+            net, lambda hops, core: dkv.at[2 * net.chip(hops) + core], dkv_own, kv_parts
+        )
+        next(kv_steps)
+        next(kv_steps)
+        next(y_steps)
+        next(wo_steps)
+
+        def turned_back(values):
+            return (values * cosine[...] - pltpu.roll(values, HEAD_DIM // 2, 1) * sine[...]).astype(bf16)
+
+        for head in range(heads):
+            columns = slice(head * HEAD_DIM, (head + 1) * HEAD_DIM)
+            d_proj[:, columns] = turned_back((dqt[head] * scale).T)
+        next(kv_steps)
+        next(y_steps)
+        next(kv_steps)
+        run_together(kv_steps)
+        d_proj[:, q_width : q_width + HEAD_DIM] = turned_back(dkv_own[:, :HEAD_DIM])
+        d_proj[:, q_width + HEAD_DIM :] = dkv_own[:, HEAD_DIM:].astype(bf16)
+        w_load.wait()
+        for j in range(n_rows):
+            at = slice(j * width, (j + 1) * width)
+            d_first[:, at] = matmul_nt(d_proj[...], w[at, :]).astype(bf16)
+        run_together(y_steps, wo_steps)
+        copies[-1].wait_recv()
+        y_out[...] = ring_parts[0][ring - 2]
         net.finish()
 
+    vmem = pltpu.VMEM
     return remote_call(
         kernel,
-        "last_sums",
+        "attention_back",
         6,
         [
-            jax.ShapeDtypeStruct((rows, width), jnp.float32),
-            jax.ShapeDtypeStruct(weights.shape[2:], jnp.float32),
+            shape((length, in_width), bf16),
+            shape((length, model), bf16),
+            shape((length, width), bf16),
+            shape((col_width, q_width), f32),
         ],
-        scatter_scratch(ring, rows, width)
-        + ring_scratch(ring, rows, width)
-        + scatter_columns_scratch(ring, *weights.shape[2:]),
-        (parts, weights),
-        out_vmem=(0, 1),
+        [
+            vmem((model, in_width), bf16),
+            vmem((length, q_width), bf16),
+            vmem((heads, 1, length), f32),
+            vmem((heads, HEAD_DIM, length), f32),
+            vmem((n_cols, length, 2 * HEAD_DIM), bf16),
+            vmem((length, 2 * HEAD_DIM), f32),
+            vmem((model, q_width), bf16),
+        ]
+        + scatter_scratch(ring - 1, length, width)
+        + ring_scratch(ring, length, width)
+        + scatter_columns_scratch(ring, length, 2 * HEAD_DIM)
+        + scatter_columns_scratch(ring, col_width, q_width)
+        + [pltpu.SemaphoreType.DMA((1,))],
+        (d_attn, weights_out, weights_in, queries, kv, heads_out, lse, *tables, parts),
+        in_vmem=(0, 1, 3, 4, 5, 6, 7, 8),
+        out_vmem=(0, 1, 2, 3),
+    )
+
+
+def last_phase(n_rows, n_cols, d_first, d_proj, normed, parts, part_sum, x, proj, d_resid, gains, gain_part):
+    ring = n_cols // 2
+    length, model = d_first.shape
+    width = model // n_rows
+    in_width = d_proj.shape[1]
+    col_width = model // n_cols
+    pieces = 2
+    piece = length // pieces
+    bf16, f32 = jnp.bfloat16, jnp.float32
+    shape = jax.ShapeDtypeStruct
+    chips = n_rows * ring
+
+    def kernel(
+        d_first, d_proj, normed, y_in, y_sum, x, proj, d_resid, gains, gain_two,
+        layer_out, grad_in, gain_out, w_out,
+        d_own, w_part, moment, moments, gain_own, gain_twin, gain_sums, *rest,
+    ):
+        scratch, y_scratch = rest[:9], rest[9:18]
+        w_parts = rest[18:25]
+        mo_s, mo_r, ga_s, ga_r, gt_s, gt_r = rest[25:]
+        net = Links(n_rows, n_cols)
+        others = net.spread_partners()
+        net.greet([device for _, _, device in others] + [net.twin])
+
+        def finish(s, upper, lower):
+            at = lambda p: pl.ds(s * piece + p * (piece // 2), piece // 2)
+            add_slabs(d_own.at[at(0), :], upper)
+            add_slabs(d_own.at[at(1), :], lower)
+
+        def finish_out(s, upper, lower):
+            for part, terms in ((0, upper), (1, lower)):
+                at = pl.ds(part * (length // 2), length // 2)
+                extra = [
+                    part_reader(y_sum.at[at, :]),
+                    part_reader(x.at[at, pl.ds(0, width)]),
+                    part_reader(proj.at[at, pl.ds(0, width)]),
+                ]
+                add_slabs(layer_out.at[at, :], terms + extra)
+
+        steps = scatter_square(net, d_first, scratch, list(range(pieces)), finish, resident=True)
+        y_steps = scatter_square(net, y_in, y_scratch, [0], finish_out)
+        next(steps)
+        next(steps)
+        w_part[...] = matmul_tn(normed[...], d_proj[...]).astype(bf16)
+        by_place = lambda hops, core: w_part.at[
+            pl.ds((net.place(hops) * 2 + core) * col_width, col_width), :
+        ]
+        w_steps = scatter_columns(net, by_place, w_out, w_parts)
+        next(w_steps)
+        next(y_steps)
+        next(w_steps)
+        run_together(steps)
+
+        gain = gains[0:1, :width]
+        slab = 128
+        gain_own[...] = jnp.zeros_like(gain_own)
+
+        def unit_of(at):
+            values = x[at, :].astype(f32)
+            inverse = lax.rsqrt(jnp.mean(values * values, -1, keepdims=True) + NORM_EPS)
+            return values[:, :width] * inverse, inverse
+
+        for i in range(length // slab):
+            at = slice(i * slab, (i + 1) * slab)
+            unit, _ = unit_of(at)
+            d_normed = d_own[at, :]
+            share = jnp.sum(d_normed * gain * unit, -1, keepdims=True)
+            moment[:, at] = jnp.broadcast_to(share, (slab, 128)).T[:8]
+            gain_own[:8] += jnp.sum((d_normed * unit).reshape(slab // 8, 8, width), 0)
+        sends = [
+            net.send(moment, moments.at[bits - 1], (mo_s, mo_r), bits - 1, (net.flip(bits), net.c))
+            for bits in range(1, n_rows)
+        ]
+        gain_own[8:] = gain_two[...]
+        twin = net.send(gain_own, gain_twin, (gt_s, gt_r), 0, net.twin)
+        for copy in sends:
+            copy.wait_recv()
+        whole = moment[...] + moments[0] + moments[1] + moments[2]
+        for i in range(length // slab):
+            at = slice(i * slab, (i + 1) * slab)
+            unit, inverse = unit_of(at)
+            mean = jnp.broadcast_to(whole[:1, at], (128, slab)).T[:, :1] / model
+            grad_in[at, :] = d_resid[at, :] + inverse * (d_own[at, :] * gain - unit * mean)
+        twin.wait_recv()
+        mine = net.r * ring + net.z
+        gain_sums[mine] = gain_own[...] + gain_twin[...]
+        sends = [
+            net.send(gain_sums.at[mine], gain_sums.at[mine], (ga_s, ga_r), number, device)
+            for number, (hops, bits, device) in enumerate(others)
+        ]
+        next(w_steps)
+        run_together(y_steps)
+        for copy in sends:
+            copy.wait_recv()
+        total = gain_sums[net.z * ring]
+        for i in range(1, ring):
+            total = total + gain_sums[net.z * ring + i]
+        gain_out[0:1] = jnp.sum(total[:8], 0, keepdims=True)
+        gain_out[1:2] = jnp.sum(total[8:], 0, keepdims=True)
+        gain_out[2:8] = jnp.zeros((6, width), f32)
+        run_together(w_steps)
+        net.finish()
+
+    vmem = pltpu.VMEM
+    return remote_call(
+        kernel,
+        "last_phase",
+        7,
+        [
+            shape((length, width), bf16),
+            shape((length, width), f32),
+            shape((8, width), f32),
+            shape((col_width, in_width), f32),
+        ],
+        [
+            vmem((length, width), f32),
+            vmem((model, in_width), bf16),
+            vmem((8, length), f32),
+            vmem((n_rows - 1, 8, length), f32),
+            vmem((16, width), f32),
+            vmem((16, width), f32),
+            vmem((chips, 16, width), f32),
+        ]
+        + scatter_scratch(pieces, piece, width, resident=True)
+        + scatter_scratch(1, length, width)
+        + scatter_columns_scratch(ring, col_width, in_width)
+        + pair_sems(n_rows - 1)
+        + pair_sems(chips - 1)
+        + pair_sems(1),
+        (
+            d_first.reshape(pieces, piece, model), d_proj, normed, parts, part_sum, x, proj, d_resid,
+            gains, gain_part,
+        ),
+        in_vmem=(0, 1, 2, 4, 5, 6, 7, 8, 9),
+        out_vmem=(0, 1, 2, 3),
     )
 
 
 def expert_kernel(
-    info, rows, grads, slot_row, chosen, mine_hot, gate_own, gate_twin, up_own, up_twin, down_own,
-    down_twin, token_w, shared_down,
+    info, rows, grads, maps, gate_own, gate_twin, up_own, up_twin, down_own, down_twin, shared, router,
     d_rows_out, rows_out, slot_rows, d_part, e_act, d_gate, d_up, s_act, d_shared, probs_out, d_gates,
-    w_gate, w_up, w_down, slot_dx, part, sems,
+    w_gate, w_up, w_down, part, sems,
 ):
     tokens, model = rows.shape[1:]
     n_slots = slot_rows.shape[1]
     half_hidden = gate_own.shape[1]
     hidden = 2 * half_hidden
-    pad = shared_down.shape[1]
-    row = info[0]
+    pad = shared.shape[1] // 3
+    gate_up, down = slice(0, 2 * pad), slice(2 * pad, 3 * pad)
+    row, own_expert = info[0], info[1]
     width = model // 4
     bf16, f32 = jnp.bfloat16, jnp.float32
+    blocks, experts, block_rows = maps.shape[1:]
 
     @pl.when(pl.program_id(0) == 0)
     def _():
@@ -1113,8 +1621,19 @@
             copy.wait()
 
     x = rows[0]
+    slot_row, chosen = [], []
+    for b in range(blocks):
+        own_map = jnp.where(
+            lax.broadcasted_iota(jnp.int32, (experts, block_rows), 0) == own_expert, maps[0, b], 0.0
+        )
+        own_map = jnp.sum(own_map, 0, keepdims=True)
+        slot_row.append(jnp.where(own_map >= 0, own_map + b * (n_slots // blocks), -1.0))
+        filled = jnp.concatenate([maps[0, b], jnp.full((128 - experts, block_rows), -1.0, f32)], 0)
+        chosen.append(filled.T)
+    slot_row, chosen = jnp.concatenate(slot_row, 1), jnp.concatenate(chosen, 0)
+    mine_hot = (lax.broadcasted_iota(jnp.int32, (1, 128), 1) == own_expert).astype(f32)
     pick = (
-        lax.broadcasted_iota(jnp.int32, (n_slots, tokens), 0).astype(f32) == slot_row[0]
+        lax.broadcasted_iota(jnp.int32, (n_slots, tokens), 0).astype(f32) == slot_row
     ).astype(f32)
     pick_b = pick.astype(bf16)
     pick_t = pick.T.astype(bf16)
@@ -1122,16 +1641,16 @@
         a, b, (dims, ((), ())), precision=PRECISE, preferred_element_type=f32
     )
 
-    logits = matmul(x, token_w[:, 2 * pad :])
-    logits = jnp.where(chosen[0] > 0, logits, NEG_LARGE)
+    logits = matmul(x, router[...])
+    logits = jnp.where(chosen >= 0, logits, NEG_LARGE)
     logits = jnp.exp(logits - jnp.max(logits, -1, keepdims=True))
     probs = logits / jnp.sum(logits, -1, keepdims=True)
     probs_out[0] = probs
-    my_gate = jnp.sum(probs * mine_hot[...], -1, keepdims=True)
+    my_gate = jnp.sum(probs * mine_hot, -1, keepdims=True)
     slot_gate = exact(pick, jnp.broadcast_to(my_gate, (tokens, 128)), ((1,), (0,)))[:, :1]
-    s_gate = matmul(x, token_w[:, :pad])
-    s_up = matmul(x, token_w[:, pad : 2 * pad])
-    through = matmul(grads[0], shared_down[...])
+    s_gate = matmul(x, shared[:, :pad])
+    s_up = matmul(x, shared[:, pad : 2 * pad])
+    through = matmul(grads[0], shared[:, down])
     s_silu, s_slope = silu_parts(s_gate)
     s_act[0] = (s_silu * s_up).astype(bf16)
     d_shared[0, :, :pad] = (through * s_up * s_slope).astype(bf16)
@@ -1168,21 +1687,19 @@
         at = pl.ds(pl.multiple_of(t * tile, tile), tile)
         d_slot = matmul_nt(d_gate[0], w_gate[at, :]) + matmul_nt(d_up[0], w_up[at, :])
         d_rows_out[0, :, at] = (
-            matmul(pick_t, d_slot.astype(bf16)) + matmul_nt(d_shared[0], token_w[at, : 2 * pad])
+            matmul(pick_t, d_slot.astype(bf16)) + matmul_nt(d_shared[0], shared[at, gate_up])
         ).astype(bf16)
         out = (matmul(e_act[0], w_down[:, at]) * slot_gate).astype(bf16)
         rows_out[0, :, at] = (
-            matmul(pick_t, out) + matmul_nt(s_act[0], shared_down[at, :])
+            matmul(pick_t, out) + matmul_nt(s_act[0], shared[at, down])
         ).astype(bf16)
 
 
-def expert_chunks(
-    info, rows, grads, slot_row, chosen, mine_hot, experts_w, token_w, shared_down, slots
-):
+def expert_chunks(info, rows, grads, maps, experts_w, shared, router, slots):
     chunks, tokens, model = rows.shape
     half_hidden = experts_w[0].shape[1]
     hidden = 2 * half_hidden
-    pad = shared_down.shape[1]
+    pad = shared.shape[1] // 3
     by_chunk = lambda *dims: pl.BlockSpec((1, *dims), lambda i, s: (i, 0, 0))
     once = lambda *dims: pl.BlockSpec(dims, lambda i, s: (0, 0), pipeline_mode=pl.Buffered(1))
     anywhere = pl.BlockSpec(memory_space=pl.ANY)
@@ -1199,12 +1716,10 @@
             in_specs=[
                 by_chunk(tokens, model),
                 by_chunk(tokens, model),
-                by_chunk(1, tokens),
-                by_chunk(tokens, 128),
-                once(1, 128),
+                pl.BlockSpec((1, *maps.shape[1:]), lambda i, s: (i, 0, 0, 0)),
             ]
             + [anywhere] * 6
-            + [once(*token_w.shape), once(*shared_down.shape)],
+            + [once(*shared.shape), once(*router.shape)],
             out_specs=[
                 single(tokens, model),
                 single(tokens, model),
@@ -1216,13 +1731,12 @@
                 single(tokens, pad),
                 single(tokens, 2 * pad),
                 single(tokens, 128),
-                pl.BlockSpec((1, 1, tokens), lambda i, s: (s[1 + i], 0, 0)),
+                pl.BlockSpec((1, 1, tokens), lambda i, s: (s[2 + i], 0, 0)),
             ],
             scratch_shapes=[
                 pltpu.VMEM((model, hidden), bf16),
                 pltpu.VMEM((model, hidden), bf16),
                 pltpu.VMEM((hidden, model), bf16),
-                pltpu.VMEM((8, 128), bf16),
                 pltpu.VMEM((slots, model), bf16),
                 pltpu.SemaphoreType.DMA((24,)),
             ],
@@ -1247,98 +1761,7 @@
             transcendentals=chunks * slots * hidden,
         ),
         name="expert_chunks",
-    )(info, rows, grads, slot_row, chosen, mine_hot, *experts_w, token_w, shared_down)
-
-
-def attention_backward_kernel(
-    scale, block_ref, q_ref, k_ref, kt_ref, v_ref, go_ref, lse_ref, delta_ref, dq_ref, dkv_ref, dqt
-):
-    length, width = q_ref.shape
-    heads = width // HEAD_DIM
-    step = pl.program_id(0)
-    own = block_ref[0]
-
-    @pl.when(step == 0)
-    def _():
-        dqt[...] = jnp.zeros_like(dqt)
-
-    def one_block(masked):
-        keys = k_ref[...]
-        keys_t = kt_ref[...]
-        values = v_ref[...]
-        d_key = jnp.zeros((length, HEAD_DIM), jnp.float32)
-        d_value = jnp.zeros((length, HEAD_DIM), jnp.float32)
-        for head in range(heads):
-            columns = slice(head * HEAD_DIM, (head + 1) * HEAD_DIM)
-            queries = q_ref[:, columns]
-            grads = go_ref[:, columns]
-            probs = jnp.exp(scores_of(keys, queries, scale) - lse_ref[head])
-            if masked:
-                probs = jnp.where(causal_mask(probs), probs, 0.0)
-            d_probs = matmul_nt(values, grads)
-            d_scores = (probs * (d_probs - delta_ref[head])).astype(jnp.bfloat16)
-            d_value = d_value + matmul(probs.astype(jnp.bfloat16), grads)
-            d_key = d_key + matmul(d_scores, queries)
-            dqt[head] = dqt[head] + matmul(keys_t, d_scores)
-        dkv_ref[:, :HEAD_DIM] = (d_key * scale).astype(dkv_ref.dtype)
-        dkv_ref[:, HEAD_DIM:] = d_value.astype(dkv_ref.dtype)
-
-    @pl.when(step < own)
-    def _():
-        one_block(False)
-
-    @pl.when(step == own)
-    def _():
-        one_block(True)
-
-    @pl.when(step > own)
-    def _():
-        dkv_ref[...] = jnp.zeros_like(dkv_ref)
-
-    @pl.when(step == pl.num_programs(0) - 1)
-    def _():
-        for head in range(heads):
-            dq_ref[:, head * HEAD_DIM : (head + 1) * HEAD_DIM] = (dqt[head] * scale).T
-
-
-def attention_backward(block, queries, keys, keys_t, values, grads, lse, delta):
-    length, width = queries.shape
-    heads = width // HEAD_DIM
-    whole = keys.shape[0]
-    fixed = lambda b, s: (0, 0)
-    fixed_three = lambda b, s: (0, 0, 0)
-    return pl.pallas_call(
-        lambda *refs: attention_backward_kernel(1.0 / math.sqrt(HEAD_DIM), *refs),
-        grid_spec=pltpu.PrefetchScalarGridSpec(
-            num_scalar_prefetch=1,
-            grid=(whole // length,),
-            in_specs=[
-                pl.BlockSpec((length, width), fixed),
-                pl.BlockSpec((length, HEAD_DIM), lambda b, s: (jnp.minimum(b, s[0]), 0)),
-                pl.BlockSpec((HEAD_DIM, length), lambda b, s: (0, jnp.minimum(b, s[0]))),
-                pl.BlockSpec((length, HEAD_DIM), lambda b, s: (jnp.minimum(b, s[0]), 0)),
-                pl.BlockSpec((length, width), fixed),
-                pl.BlockSpec((heads, 1, length), fixed_three),
-                pl.BlockSpec((heads, 1, length), fixed_three),
-            ],
-            out_specs=[
-                pl.BlockSpec((length, width), fixed),
-                pl.BlockSpec((length, 2 * HEAD_DIM), lambda b, s: (b, 0)),
-            ],
-            scratch_shapes=[pltpu.VMEM((heads, HEAD_DIM, length), jnp.float32)],
-        ),
-        out_shape=[
-            jax.ShapeDtypeStruct((length, width), jnp.float32),
-            jax.ShapeDtypeStruct((whole, 2 * HEAD_DIM), jnp.bfloat16),
-        ],
-        compiler_params=pltpu.CompilerParams(vmem_limit_bytes=48 * 1024 * 1024),
-        cost_estimate=pl.CostEstimate(
-            flops=10 * length * width * whole,
-            bytes_accessed=6 * whole * HEAD_DIM * 2 + length * width * 8,
-            transcendentals=length * heads * whole,
-        ),
-        name="attention_backward",
-    )(block, queries, keys, keys_t, values, grads, lse, delta)
+    )(info, rows, grads, maps, *experts_w, shared, router)
 
 
 def add_bf16(left, right):
@@ -1496,98 +1919,51 @@
 
     small = jnp.concatenate([w_router, norm1_gain[:, None], norm2_gain[:, None]], 1)
     small = jnp.pad(small, ((0, 0), (0, 128 - small.shape[1])))
-    token_input, weights_in, small = front_gather(
-        n_rows, net.n_cols, layer_in[0],
-        jnp.concatenate([w_query, key_matrix, value_matrix], 1), small,
-    )
-    token_input = token_input[0].astype(jnp.float32)
-    weights_in = weights_in.reshape(model_width, -1)
-    small = small.reshape(model_width, 128)
-    router_full = small[:, :experts]
-    gains = small[:, experts : experts + 2].astype(jnp.float32).T
-    first_gain, second_gain = gains[0][None], gains[1][None]
-    first_inverse = lax.rsqrt(jnp.mean(token_input * token_input, -1, keepdims=True) + NORM_EPS)
-    first_unit = token_input * first_inverse
-    first_normed = (first_unit * first_gain).astype(jnp.bfloat16)
-    projected = matmul(first_normed, weights_in)
-    positions = c * length + jnp.arange(length, dtype=jnp.int32)
-    cosine_table, sine_table = rope_tables(positions, HEAD_DIM)
-    rotated = apply_rotary(
-        projected[:, : q_width + kv_width].reshape(length, -1, HEAD_DIM), cosine_table, sine_table
-    ).astype(jnp.bfloat16)
-    queries = rotated[:, :q_heads].reshape(length, q_width)
-    kv_local = jnp.concatenate(
-        [rotated[:, q_heads], projected[:, q_width + kv_width :].astype(jnp.bfloat16)], 1
-    )
-    block_no = c.astype(jnp.int32)[None]
-    attn_f32, log_total, kv_all, grad_rows, weights_out_t, slot_maps = attention_gather(
-        n_rows, net.n_cols, queries, kv_local, cotangent[0], w_out.T, slot_map
-    )
-    weights_out_t = weights_out_t.reshape(model_width, -1)
-    kv_all = kv_all.reshape(-1, 2 * HEAD_DIM)
-    keys_all, values_all = kv_all[:, :HEAD_DIM], kv_all[:, HEAD_DIM:]
-    attn_rows = attn_f32.astype(jnp.bfloat16)
-    proj = matmul_nt(attn_rows, weights_out_t).astype(jnp.bfloat16)
-    blocks_of = lambda whole: [
-        whole[:, j * row_width : (j + 1) * row_width] for j in range(n_rows)
-    ]
-    attn_proj = rows_sum(n_rows, net.n_cols, proj).astype(jnp.float32)
-    residual = token_input + attn_proj
-    second_inverse = lax.rsqrt(jnp.mean(residual * residual, -1, keepdims=True) + NORM_EPS)
-    second_unit = residual * second_inverse
-    second_normed = (second_unit * second_gain).astype(jnp.bfloat16)
-
     pad_to = -(-shared_hidden // 128) * 128
     padded = lambda w: jnp.pad(
         w.reshape(col_width, ring, shared_hidden), ((0, 0), (0, 0), (0, pad_to - shared_hidden))
     )
     packed = jnp.concatenate([padded(shared_gate), padded(shared_up), padded(shared_down.T)], 2)
     packed = jnp.swapaxes(packed, 0, 1)
-    shared_w = jnp.zeros((ring, 2) + packed.shape[1:], jnp.bfloat16)
-    for hops in range(ring):
-        piece = index(packed, net.chip(-hops), 0, False)
-        piece = net.along_z(piece, hops) if hops else piece
-        twin = net.sibling(piece)
-        spot = net.place(hops)
-        shared_w = lax.dynamic_update_slice(shared_w, piece[None, None], (spot, k, 0, 0))
-        shared_w = lax.dynamic_update_slice(shared_w, twin[None, None], (spot, 1 - k, 0, 0))
-    shared_w = shared_w.reshape(model_width, 3 * pad_to)
-    shared_down_t = shared_w[:, 2 * pad_to :]
-    token_w = jnp.concatenate(
-        [shared_w[:, : 2 * pad_to], jnp.pad(router_full, ((0, 0), (0, 128 - experts)))], 1
-    )
     experts_w = []
     for own in (expert_gate[0], expert_up[0], expert_down[0]):
         experts_w += [own, net.sibling(own)]
-
-    my_expert = r * ring + z
-    mine_hot = (jnp.arange(128, dtype=jnp.int32) == my_expert).astype(jnp.float32)[None]
-    my_map = index(slot_maps, my_expert, 2, False)
-    first_slot = (jnp.arange(n_rows, dtype=jnp.float32) * slots)[None, :, None]
-    slot_row = jnp.where(my_map >= 0, my_map + first_slot, -1.0).reshape(ring, 1, length)
-    chosen = jnp.swapaxes(slot_maps >= 0, 2, 3).reshape(ring, length, experts)
-    chosen = jnp.pad(chosen.astype(jnp.float32), ((0, 0), (0, 0), (0, 128 - experts)))
-    rows_all = token_gather(n_rows, net.n_cols, second_normed[:, :row_width])
-    info = jnp.stack([r] + [net.chip(hops) for hops in range(ring)]).astype(jnp.int32)
+    positions = c * length + jnp.arange(length, dtype=jnp.int32)
+    cosine_table, sine_table = rope_tables(positions, HEAD_DIM)
+    tables = (
+        jnp.concatenate([cosine_table, cosine_table], 1),
+        jnp.concatenate([-sine_table, sine_table], 1),
+    )
+
+    (
+        token_input, first_normed, weights_in, small, queries, kv_all, attn_f32, log_total,
+        weights_out_t, grad_rows, rows_all, slot_maps, shared_w, attn_proj, gains,
+    ) = first_phase(
+        n_rows, net.n_cols, layer_in[0], cotangent[0],
+        jnp.concatenate([w_query, key_matrix, value_matrix], 1), small, w_out.T, packed, slot_map,
+        tables,
+    )
+    info = jnp.stack([r, r * ring + z] + [net.chip(hops) for hops in range(ring)]).astype(jnp.int32)
     (
         d_rows, out_rows, slot_rows, d_part, e_act, d_e_gate, d_e_up, s_act, d_shared, gate_probs,
         d_gate_mine,
     ) = expert_chunks(
-        info, rows_all, grad_rows, slot_row, chosen, mine_hot, experts_w, token_w, shared_down_t,
-        n_rows * slots,
-    )
-
-    d_second, d_gate_all = token_sum(
-        n_rows, net.n_cols, d_rows, d_gate_mine.reshape(ring, length)
-    )
+        info, rows_all, grad_rows, slot_maps, experts_w, shared_w, small, n_rows * slots
+    )
+
+    joined = lambda whole: whole.reshape(-1, whole.shape[-1])
+    attn_proj = joined(attn_proj)
+    d_attn, d_resid, gain_part, d_gate_all, g_expert_gate, g_expert_up, g_expert_down = token_sum(
+        n_rows, net.n_cols, d_rows, d_gate_mine.reshape(ring, length),
+        [joined(part) for part in (slot_rows, d_part, e_act, d_e_gate, d_e_up)],
+        gate_probs[0], small, (token_input, attn_proj, grad_rows[0]), gains,
+    )[:7]
+
     grad_router = jnp.zeros((row_width, experts), jnp.float32)
-    d_logits_own = None
     for hops in range(ring):
         probs = gate_probs[hops][:, :experts]
         d_gates = index(d_gate_all, net.chip(hops), 1, False).T
         d_logits = probs * (d_gates - jnp.sum(probs * d_gates, -1, keepdims=True))
-        if hops == 0:
-            d_logits_own = d_logits
         quarter = lax.dynamic_slice(rows_all[hops], (r * rows_dev, 0), (rows_dev, model_width))
         quarter = lax.switch(
             r ^ z,
@@ -1605,71 +1981,18 @@
     g_router = index(grad_router, k, 0, False) + net.sibling(index(grad_router, 1 - k, 0, False))
     g_router = g_router + net.along_x(g_router)
     g_router = g_router + net.along_y(g_router)
-    high, low = split_terms(d_logits_own)
-    d_router_in = matmul_nt(
-        jnp.concatenate([high, low], 1), jnp.concatenate([router_full, router_full], 1)
-    )
-    d_second = d_second.astype(jnp.float32) + d_router_in
-    d_second_unit = d_second * second_gain
-    second_gain_grad = jnp.sum((d_second * second_unit)[:, :row_width], 0)
-    d_resid = grad_rows[0].astype(jnp.float32) + second_inverse * (
-        d_second_unit
-        - second_unit * jnp.mean(d_second_unit * second_unit, -1, keepdims=True)
-    )
-    d_attn = d_resid.astype(jnp.bfloat16)
-
-    d_heads = matmul(d_attn, weights_out_t).astype(jnp.bfloat16)
-    delta = jnp.sum(
-        (d_heads.astype(jnp.float32) * attn_f32).reshape(length, q_heads, HEAD_DIM), -1
-    ).T[:, None, :]
-    d_query, d_kv_all = attention_backward(
-        block_no, queries, keys_all, keys_all.T, values_all, d_heads, log_total, delta
-    )
-    d_kv = net.cols_scatter(d_kv_all.reshape(ring, 2, length, 2 * HEAD_DIM), net.chip)
-    d_rotated = jnp.concatenate([d_query, d_kv[:, :HEAD_DIM]], 1).reshape(length, -1, HEAD_DIM)
-    d_rotated = apply_rotary(d_rotated, cosine_table, -sine_table).reshape(length, -1)
-    d_projected = jnp.concatenate([d_rotated, d_kv[:, HEAD_DIM:]], 1).astype(jnp.bfloat16)
-    d_first = matmul_nt(d_projected, weights_in).astype(jnp.bfloat16)
-    d_first = net.rows_scatter(blocks_of(d_first))
-    unit_mine = first_unit[:, :row_width]
-    d_first_unit = d_first * first_gain[:, :row_width]
-    moment = jnp.sum(d_first_unit * unit_mine, -1).reshape(-1, 128)
-    moment = moment + net.along_x(moment)
-    moment = moment + net.along_y(moment)
-    moment = moment.reshape(length, 1) / model_width
-    grad_in = d_resid[:, :row_width] + first_inverse * (d_first_unit - unit_mine * moment)
-    first_gain_grad = jnp.sum(d_first * unit_mine, 0)
-    gain_grads = jnp.stack([first_gain_grad, second_gain_grad])
-    gain_grads = gain_grads + net.sibling(gain_grads)
-    bit = 1
-    while bit < ring:
-        gain_grads = gain_grads + net.across_z(gain_grads, bit)
-        bit *= 2
-    gain_grads = jnp.stack([gain_grads, net.along_x(gain_grads)])
-    gain_grads = jnp.concatenate([gain_grads, net.along_y(gain_grads)])
-    gain_grads = index(gain_grads, r ^ z, 0, False).reshape(2, 2, col_width)
-    gain_grads = index(gain_grads, k, 1, False)
+
+    d_projected, d_first, part_sum, g_out = attention_back(
+        n_rows, net.n_cols, d_attn, weights_out_t, weights_in, queries, kv_all, attn_f32, log_total,
+        tables, out_rows,
+    )
+    layer_out, grad_in, gain_grads, g_in = last_phase(
+        n_rows, net.n_cols, d_first, d_projected, first_normed, out_rows, part_sum, token_input,
+        attn_proj, d_resid, gains, gain_part,
+    )
+    gain_grads = index(gain_grads[:2].reshape(2, 2, col_width), k, 1, False)
 
     column_parts = lambda whole: whole.astype(jnp.bfloat16).reshape(ring, 2, col_width, -1)
-    joined = lambda whole: whole.reshape(-1, whole.shape[-1])
-    slot_rows, e_act, d_part = joined(slot_rows), joined(e_act), joined(d_part)
-    d_e_gate, d_e_up = joined(d_e_gate), joined(d_e_up)
-
-    def halves(left, right, axis):
-        own = lambda v: v[:, :half_hidden]
-        other = lambda v: v[:, half_hidden:]
-        if axis == 0:
-            mine = matmul_tn(left, own(right))
-            sent = matmul_tn(left, other(right)).astype(jnp.bfloat16)
-        else:
-            mine = matmul_tn(own(left), right)
-            sent = matmul_tn(other(left), right).astype(jnp.bfloat16)
-        return net.mixed(mine + net.sibling(sent).astype(jnp.float32), axis)[None]
-
-    g_expert_gate = halves(slot_rows, d_e_gate, 0)
-    g_expert_up = halves(slot_rows, d_e_up, 0)
-    g_expert_down = halves(e_act, d_part, 1)
-
     shared_parts = jnp.concatenate(
         [
             matmul_tn(joined(rows_all), joined(d_shared)),
@@ -1688,28 +2011,22 @@
         g_shared[:, :, n * pad_to : n * pad_to + shared_hidden], 0, 1
     ).reshape(col_width, -1)
 
-    weight_parts = jnp.concatenate(
-        [matmul_tn(first_normed, d_projected), matmul_tn(d_attn, attn_rows)], 1
-    )
-    out_mine, g_in = last_sums(n_rows, net.n_cols, out_rows, column_parts(weight_parts))
-    layer_out = (residual[:, :row_width] + out_mine).astype(jnp.bfloat16)
-    width_in = q_width + 2 * kv_width
     return (
         layer_out[None],
         grad_in[None],
         gain_grads[0],
         g_in[:, :q_width],
         g_in[:, q_width : q_width + kv_width],
-        g_in[:, q_width + kv_width : width_in],
-        g_in[:, width_in:].T,
+        g_in[:, q_width + kv_width :],
+        g_out.T,
         gain_grads[1],
         g_router,
         shared_cols(0),
         shared_cols(1),
         shared_cols(2).T,
-        g_expert_gate,
-        g_expert_up,
-        g_expert_down,
+        g_expert_gate[None],
+        g_expert_up[None],
+        g_expert_down[None],
     )
 
 

time: 1160 us -> 926 us (0.80)
  other arithmetic: 110 us -> 16.2 us
  matrix products: 97.2 us -> 19.2 us
  Pallas kernels: 725 us -> 794 us
  waiting for transfers between devices: 53.3 us -> 0.03 us
  local copies, waits for them, and re-layouts: 115 us -> 70 us
  starting transfers between devices: 44.1 us -> 14.4 us
    pallas_call x6 -> x4, Pallas kernels: 575 us -> 664 us  [remote_call(): pl.pallas_call(kernel, out_shape=out_shape, in_specs=[vmem if i in in_vme...]
    dot_general x14 -> x6, matrix products: 74.4 us -> 18.3 us  [matmul_tn(): lax.dot_general(left_op, right_op, (((0,), (0,)), ((), ())), preferred_el...]
    ppermute x35 -> x10, waiting for transfers between devices: 53.3 us -> 0.03 us  [move(): return lax.ppermute(values, ('rows', 'cols'), pairs)]
    add x12 -> x0, other arithmetic: 36.7 us -> none  [the longest x3 23 us: halves(): return net.mixed(mine + net.sibling(sent).astype(jnp.float32), axis)[None]]
    ppermute x35 -> x10, starting transfers between devices: 44.1 us -> 14.4 us  [move(): return lax.ppermute(values, ('rows', 'cols'), pairs)]
    slice x19 -> x3, local copies, waits for them, and re-layouts: 28.3 us -> 4.55 us  [the longest x1 2.09 us: gathered_layer(): g_in[:, :q_width]]
    dot_general x5 -> x0, matrix products: 21.2 us -> none  [the longest x3 12.6 us: matmul_nt(): lax.dot_general(left_op, right_op, (((1,), (1,)), ((), ())), preferred_el...]
    pallas_call x1 -> x0, Pallas kernels: 19.6 us -> none  [attention_backward(): pl.pallas_call(lambda *refs: attention_backward_kernel(1.0 / math.sqrt(HE...]
  transfers between devices with their start and end apart: 35 -> 10, of which waited for: 10 -> 0; matrix products, arithmetic and copies ran while one was open for 22% -> 5% of each run, Pallas kernels for 39% -> 59%
where the time goes in v3:
time: 926 us; the launch traced here: 916 us
  Pallas kernels  794 us (86%)
  local copies, waits for them, and re-layouts  70 us (8%)
  matrix products  19.2 us (2%)
  other arithmetic  16.2 us (2%)
  starting transfers between devices  14.4 us (2%)
    pallas_call x4, Pallas kernels, remote_call(): pl.pallas_call(kernel, out_shape=out_shape, in_specs=[vmem if i in in_vme...  664 us
    pallas_call x1, Pallas kernels, expert_chunks(): pl.pallas_call(expert_kernel, grid_spec=pltpu.PrefetchScalarGridSpec(num_...  130 us
    unnamed x55, local copies, waits for them, and re-layouts  28.9 us
  transfers between devices with their start and end apart: 10, of which 0 were waited for; matrix products, arithmetic and copies ran while one was open for 5% of the time, Pallas kernels for 59%

profile of v3, /device:TPU:18, one launch (start us, length us, event | category | flops | bytes accessed | tf_op | source)
XLA Modules:
  0.0 915.7 jit_solution(17024534501275424339)
XLA Ops:
  9.3 1.8 pad_maximum_fusion.w_in
  14.4 291.7 %first_phase.1 = (bf16[512,2560]{1,0:T(8,128)(2,1)}, bf16[512,2560]{1,0:T(8,128)(2,1)}, bf16[2560,896]{1,0:T(8,128)(2,1)}, bf16[2560,128]{1,0:T(8,128)(2,1)}, bf...) custom-call(bf16[512,640]{1,0:T(8,128)(2,1)} %bitcast.164, ...), custom_call_target="tpu_custom_call" | custom-call | tf_op jit(solution)/shard_map/first_phase/pallas_call | solution.py:801
  306.1 6.1 fusion.42
  316.9 3.4 slice_bitcast_fusion.g_in
  320.3 129.9 %expert_chunks.1 = (bf16[4,512,2560]{2,1,0:T(8,128)(2,1)}, bf16[4,512,2560]{2,1,0:T(8,128)(2,1)}, bf16[4,256,2560]{2,1,0:T(8,128)(2,1)}, bf16[4,256,2560]{2,1,0:...) custom-call(s32[6]{0:T(128)} %stack.27.info, ...), custom_call_target="tpu_custom_call" | custom-call | flops 80530636800 | bytes 41943040 | tf_op jit(solution)/shard_map/expert_chunks/pallas_call | solution.py:1711
  451.5 2.1 slice_bitcast_fusion.3
  453.5 127.9 %token_sum.1 = (bf16[512,2560]{1,0:T(8,128)(2,1)}, f32[512,640]{1,0:T(8,128)}, f32[8,640]{1,0:T(8,128)}, f32[16,4,512]{2,1,0:T(4,128)}, f32[2560,768]{1,0:T(8,12...) custom-call(bf16[4,512,2560]{2,1,0:T(8,128)(2,1)} %get-tuple-element, ...), custom_call_target="tpu_custom_call" | custom-call | tf_op jit(solution)/shard_map/token_sum/pallas_call | solution.py:801
  581.5 1.9 constant_dynamic-slice_fusion.7
  586.7 7.1 fusion.5
  593.8 8.8 bitcast_convert_fusion
  604.0 3.7 collective-permute-start.6
  618.7 2.1 fusion
  622.0 1.8 collective-permute-start.9
  623.8 2.0 collective-permute-start.8
  626.7 3.8 collective-permute-start.4
  630.4 140.3 %attention_back.1 = (bf16[512,896]{1,0:T(8,128)(2,1)}, bf16[512,2560]{1,0:T(8,128)(2,1)}, bf16[512,640]{1,0:T(8,128)(2,1)}, f32[320,640]{1,0:T(8,128)}) custom-call(bf16[512,2560]{1,0:T(8,128)(2,1)} %get-tuple-element.108.d_attn, bf16[2560,640]{1,0:T(8,128)(2,1)} %get-tuple-element.109.wo, bf16[2560,896]{1,0:T(8,128)(2,1)} %get-tuple-element.110.w_in, ...), custom_call_target="tpu_custom_call" | custom-call | tf_op jit(solution)/shard_map/attention_back/pallas_call | solution.py:801
  770.8 104.1 %last_phase.1 = (bf16[512,640]{1,0:T(8,128)(2,1)}, f32[512,640]{1,0:T(8,128)}, f32[8,640]{1,0:T(8,128)}, f32[320,896]{1,0:T(8,128)}) custom-call(bf16[2,256,2560]{2,1,0:T(8,128)(2,1)} %bitcast.150, bf16[512,896]{1,0:T(8,128)(2,1)} %get-tuple-element.117.d_proj, bf16[512,2560]{1,0:T(8,128)(2,1)} %get-tuple-element.118.normed, ...), custom_call_target="tpu_custom_call" | custom-call | tf_op jit(solution)/shard_map/last_phase/pallas_call | solution.py:801
  878.3 2.1 slice.145
  885.7 2.1 copy.149
  890.9 2.7 copy.154
  896.2 2.0 copy.200
  900.1 7.3 copy.203
  907.4 3.9 copy.204
  912.0 3.2 copy.205
  (150 shorter events, 53.7 us)
Async XLA Ops:
  0.6 5.8 copy-start.10
  0.7 6.4 copy-start.11
  0.7 319.6 %collective-permute-start = (bf16[2560,768]{1,0:T(8,128)(2,1)}, bf16[2560,768]{1,0:T(8,128)(2,1)}, u32[]{:S(2)}, u32[]{:S(2)}) collective-permute-start(bf16[2560,768]{1,0:T(8,128)(2,1)} %bitcast.171), channel_id=1, source_target_pairs={{0,1},{1,0},{2,3},{3,2},{4,5},{5,4},{6,7},{7,6},{8,9},{9,8},{10,11... | collective-permute-start | bytes 11796488 | tf_op jit(solution)/shard_map/ppermute | solution.py:1787
  0.7 319.5 %collective-permute-start.1 = (bf16[2560,768]{1,0:T(8,128)(2,1)}, bf16[2560,768]{1,0:T(8,128)(2,1)}, u32[]{:S(2)}, u32[]{:S(2)}) collective-permute-start(bf16[2560,768]{1,0:T(8,128)(2,1)} %bitcast.173), channel_id=1, source_target_pairs={{0,1},{1,0},{2,3},{3,2},{4,5},{5,4},{6,7},{7,6},{8,9},{9,8},{10,11... | collective-permute-start | bytes 11796488 | tf_op jit(solution)/shard_map/ppermute | solution.py:1787
  1.2 319.0 %collective-permute-start.2 = (bf16[768,2560]{1,0:T(8,128)(2,1)}, bf16[768,2560]{1,0:T(8,128)(2,1)}, u32[]{:S(2)}, u32[]{:S(2)}) collective-permute-start(bf16[768,2560]{1,0:T(8,128)(2,1)} %bitcast.175), channel_id=1, source_target_pairs={{0,1},{1,0},{2,3},{3,2},{4,5},{5,4},{6,7},{7,6},{8,9},{9,8},{10,11... | collective-permute-start | bytes 11796488 | tf_op jit(solution)/shard_map/ppermute | solution.py:1787
  7.3 4.7 copy-start.13
  453.5 130.0 %copy-start.2 = (f32[512,128]{1,0:T(8,128)S(1)}, f32[512,128]{1,0:T(8,128)}, u32[]{:S(2)}) copy-start(f32[512,128]{1,0:T(8,128)} %get-tuple-element.211.probs) | copy-start | bytes 786436
  581.4 5.2 copy-start.14
  586.7 7.1 copy-start.15
  593.7 8.8 copy-start
  604.0 14.7 %collective-permute-start.6 = (bf16[4,320,768]{2,1,0:T(8,128)(2,1)}, bf16[4,320,768]{2,1,0:T(8,128)(2,1)}, u32[]{:S(2)}, u32[]{:S(2)}) collective-permute-start(bf16[4,320,768]{2,1,0:T(8,128)(2,1)} %fusion.10), channel_id=1, source_target_pairs={{0,1},{1,0},{2,3},{3,2},{4,5},{5,4},{6,7},{7,6},{8,9},{9,8},{10,11... | collective-permute-start | bytes 5898248 | tf_op jit(solution)/shard_map/ppermute | solution.py:1787
  608.0 10.1 %copy-start.6 = (bf16[128,640]{1,0:T(8,128)(2,1)S(1)}, bf16[128,640]{1,0:T(8,128)(2,1)}, u32[]{:S(2)}) copy-start(bf16[128,640]{1,0:T(8,128)(2,1)} %get-tuple-element.263) | copy-start | bytes 491524
  608.0 10.2 %copy-start.8 = (bf16[128,640]{1,0:T(8,128)(2,1)S(1)}, bf16[128,640]{1,0:T(8,128)(2,1)}, u32[]{:S(2)}) copy-start(bf16[128,640]{1,0:T(8,128)(2,1)} %copy-done.7) | copy-start | bytes 491524
  618.6 8.1 collective-permute-start.3
  622.0 261.1 %collective-permute-start.9 = (bf16[320,768]{1,0:T(8,128)(2,1)}, bf16[320,768]{1,0:T(8,128)(2,1)}, u32[]{:S(2)}, u32[]{:S(2)}) collective-permute-start(bf16[320,768]{1,0:T(8,128)(2,1)} %get-tuple-element.202), channel_id=1, source_target_pairs={{0,6},{1,7},{2,0},{3,1},{4,2},{5,3},{6,4},{7,5},{8,14},{9,15},{10,... | collective-permute-start | bytes 1474568 | tf_op jit(solution)/shard_map/ppermute | solution.py:1787
  623.8 260.6 %collective-permute-start.8 = (bf16[320,768]{1,0:T(8,128)(2,1)}, bf16[320,768]{1,0:T(8,128)(2,1)}, u32[]{:S(2)}, u32[]{:S(2)}) collective-permute-start(bf16[320,768]{1,0:T(8,128)(2,1)} %get-tuple-element.203), channel_id=1, source_target_pairs={{0,4},{1,5},{2,6},{3,7},{4,0},{5,1},{6,2},{7,3},{8,12},{9,13},{10,... | collective-permute-start | bytes 1474568 | tf_op jit(solution)/shard_map/ppermute | solution.py:1787
  625.8 259.9 %collective-permute-start.7 = (bf16[320,768]{1,0:T(8,128)(2,1)}, bf16[320,768]{1,0:T(8,128)(2,1)}, u32[]{:S(2)}, u32[]{:S(2)}) collective-permute-start(bf16[320,768]{1,0:T(8,128)(2,1)} %get-tuple-element.204), channel_id=1, source_target_pairs={{0,2},{1,3},{2,4},{3,5},{4,6},{5,7},{6,0},{7,1},{8,10},{9,11},{10,... | collective-permute-start | bytes 1474568 | tf_op jit(solution)/shard_map/ppermute | solution.py:1787
  626.7 248.2 %collective-permute-start.4 = (f32[320,16]{0,1:T(8,128)S(1)}, f32[320,16]{0,1:T(8,128)S(1)}, u32[]{:S(2)}, u32[]{:S(2)}) collective-permute-start(f32[320,16]{0,1:T(8,128)S(1)} %bitcast_add_fusion), channel_id=1, source_target_pairs={{0,8},{1,9},{2,10},{3,11},{4,12},{5,13},{6,14},{7,15},{8,0},{9,1},... | collective-permute-start | bytes 61448 | tf_op jit(solution)/shard_map/ppermute | solution.py:1787
  874.9 6.9 collective-permute-start.5
  894.9 4.3 copy-start.4
  898.2 9.2 %slice-start.2 = ((s8[7864320]{0:T(1024)(128)(4,1)}), s8[4194304]{0:T(1024)(128)(4,1)S(1)}, s32[]{:S(2)}) async-start(s8[7864320]{0:T(1024)(128)(4,1)} %bitcast.136), calls=%async_computation.2 | async-start | bytes 8388608
  900.1 7.3 slice-start.3
  900.1 11.2 %slice-start = ((s8[7864320]{0:T(1024)(128)(4,1)}), s8[4194304]{0:T(1024)(128)(4,1)S(1)}, s32[]{:S(2)}) async-start(s8[7864320]{0:T(1024)(128)(4,1)} %bitcast.133), calls=%async_computation | async-start | bytes 8388608
  907.4 4.6 slice-start.1
  (6 other events, 16.7 us)

commit v4 on v3

--- a/solution.py
+++ b/solution.py
@@ -545,6 +545,11 @@
         self.started.append(copy)
         return copy
 
+    def settle(self, copies):
+        for copy in copies:
+            copy.wait_send()
+            self.started = [other for other in self.started if other is not copy]
+
     def finish(self):
         for copy in self.started:
             copy.wait_send()
@@ -560,65 +565,81 @@
     return [pltpu.SemaphoreType.DMA((count,)), pltpu.SemaphoreType.DMA((count,))]
 
 
-def gather_square(net, src, out, sems, local_sem, chunks, known=None):
-    rows, width = src.shape
-    half = rows // 2
-
-    def block(s, j, part=None):
-        columns = pl.ds(j * width, width)
+class SquareGather:
+    def __init__(self, net, src, out, sems, local_sem, chunks, known=None):
+        self.net, self.src, self.out, self.sems, self.chunks = net, src, out, sems, chunks
+        self.rows, self.width = src.shape
+        if known is None:
+            self.own = pltpu.make_async_copy(src, self.block(0, 0), local_sem)
+        else:
+            self.own = pltpu.make_async_copy(known, out.at[0], local_sem)
+        self.own.start()
+        self.ups, self.xs, self.ys, self.lasts = {}, {}, {}, {}
+
+    def block(self, s, j, part=None):
+        columns = pl.ds(j * self.width, self.width)
         if part is None:
-            return out.at[s, :, columns]
-        return out.at[s, pl.ds(part * half, half), columns]
-
-    def part_of(s, part):
-        return src.at[pl.ds(part * half, half), :] if s == 0 else block(s, 0, part)
-
-    if known is None:
-        own = pltpu.make_async_copy(src, block(0, 0), local_sem)
-    else:
-        own = pltpu.make_async_copy(known, out.at[0], local_sem)
-    own.start()
-    ups, xs, ys, lasts = {}, {}, {}, {}
-    first = 0 if known is None else 1
-
-    def send_up(s):
-        if s < chunks - 1:
-            whole = src if s == 0 else block(s, 0)
-            ups[s + 1] = net.send(whole, block(s + 1, 0), sems, 7 * s, net.up)
-
-    def send_chunk(s):
-        xs[s] = {p: net.send(part_of(s, p), block(s, 1, p), sems, 7 * s + 1 + p, net.x) for p in (0, 1)}
-        ys[s] = {p: net.send(part_of(s, p), block(s, 2, p), sems, 7 * s + 3 + p, net.y) for p in (1, 0)}
-
-    def forward(s):
-        xs[s][0].wait_recv()
-        one = net.send(block(s, 1, 0), block(s, 3, 0), sems, 7 * s + 5, net.y)
-        ys[s][1].wait_recv()
-        two = net.send(block(s, 2, 1), block(s, 3, 1), sems, 7 * s + 6, net.x)
-        lasts[s] = [one, two]
-
-    if known is None:
-        send_chunk(0)
+            return self.out.at[s, :, columns]
+        half = self.rows // 2
+        return self.out.at[s, pl.ds(part * half, half), columns]
+
+    def up(self, s):
+        if s:
+            self.ups[s].wait_recv()
+        if s < self.chunks - 1:
+            whole = self.src if s == 0 else self.block(s, 0)
+            self.ups[s + 1] = self.net.send(
+                whole, self.block(s + 1, 0), self.sems, 7 * s, self.net.up
+            )
+
+    def across(self, s):
+        half = self.rows // 2
+        part_of = lambda p: (
+            self.src.at[pl.ds(p * half, half), :] if s == 0 else self.block(s, 0, p)
+        )
+        send = self.net.send
+        self.xs[s] = {
+            p: send(part_of(p), self.block(s, 1, p), self.sems, 7 * s + 1 + p, self.net.x)
+            for p in (0, 1)
+        }
+        self.ys[s] = {
+            p: send(part_of(p), self.block(s, 2, p), self.sems, 7 * s + 3 + p, self.net.y)
+            for p in (1, 0)
+        }
+
+    def forward(self, s):
+        block, send = self.block, self.net.send
+        self.xs[s][0].wait_recv()
+        one = send(block(s, 1, 0), block(s, 3, 0), self.sems, 7 * s + 5, self.net.y)
+        self.ys[s][1].wait_recv()
+        two = send(block(s, 2, 1), block(s, 3, 1), self.sems, 7 * s + 6, self.net.x)
+        self.lasts[s] = [one, two]
+
+    def complete(self, s):
+        self.xs[s][1].wait_recv()
+        self.ys[s][0].wait_recv()
+        for copy in self.lasts[s]:
+            copy.wait_recv()
+
+
+def gather_square(net, src, out, sems, local_sem, chunks):
+    gather = SquareGather(net, src, out, sems, local_sem, chunks)
+    gather.across(0)
+    yield
+    if chunks > 1:
+        gather.up(0)
         yield
-    if chunks > 1:
-        send_up(0)
+    gather.forward(0)
+    yield
+    for s in range(1, chunks):
+        gather.up(s)
+        gather.across(s)
         yield
-    if known is None:
-        forward(0)
+        gather.forward(s)
         yield
-    for s in range(1, chunks):
-        ups[s].wait_recv()
-        send_up(s)
-        send_chunk(s)
-        yield
-        forward(s)
-        yield
-    own.wait()
-    for s in range(first, chunks):
-        xs[s][1].wait_recv()
-        ys[s][0].wait_recv()
-        lasts[s][0].wait_recv()
-        lasts[s][1].wait_recv()
+    gather.own.wait()
+    for s in range(chunks):
+        gather.complete(s)
 
 
 def gather_columns(net, src, spot, sems, local_sem=None):
@@ -671,71 +692,98 @@
         pltpu.VMEM((chunks, 2, half, width), jnp.bfloat16),
         pltpu.VMEM((chunks, 2, half, width), jnp.bfloat16),
         pltpu.SemaphoreType.DMA((chunks, 3)),
-    ] + pair_sems(5 * chunks)
+    ] + pair_sems(6 * chunks)
+
+
+class SquareScatter:
+    def __init__(self, net, scratch, resident=False):
+        self.net, self.resident = net, resident
+        self.my_up, self.my_low, self.got_x, self.got_y, self.got_last = scratch[:5]
+        self.stage, self.load_sems, *self.sems = scratch[5:]
+        self.half, self.width = self.got_x.shape[2:]
+        self.src, self.loads, self.sent = {}, {}, {}
+        self.left, self.right = pl.ds(0, self.width), pl.ds(self.width, self.width)
+
+    def part(self, i, part, j, count=1):
+        rows = pl.ds(part * self.half, self.half)
+        return self.src[i].at[rows, pl.ds(j * self.width, count * self.width)]
+
+    def mine(self, i, part, j):
+        if self.resident:
+            return part_reader(self.part(i, part, j))
+        if part == 0:
+            return part_reader(self.my_up, i, j // 2)
+        return part_reader(self.my_low, i, columns=(self.left, self.right)[j])
+
+    def give(self, i, src, j):
+        self.src[i] = src
+        net, sems = self.net, self.sems
+        sent = self.sent.setdefault(i, {})
+        if j & 1:
+            sent["x", j] = net.send(
+                self.part(i, 0, j), self.got_x.at[i, j // 2], sems, 6 * i + j // 2, net.x
+            )
+        if j & 2:
+            columns = pl.ds((j - 2) * self.width, self.width)
+            sent["y", j] = net.send(
+                self.part(i, 1, j), self.got_y.at[i, :, columns], sems, 6 * i + j, net.y
+            )
+
+    def first(self, i, src):
+        for j in (3, 1, 2):
+            self.give(i, src, j)
+        if not self.resident:
+            load = pltpu.make_async_copy
+            self.loads[i] = [
+                load(self.part(i, 0, 0), self.my_up.at[i, 0], self.load_sems.at[i, 0]),
+                load(self.part(i, 0, 2), self.my_up.at[i, 1], self.load_sems.at[i, 1]),
+                load(self.part(i, 1, 0, 2), self.my_low.at[i], self.load_sems.at[i, 2]),
+            ]
+            for copy in self.loads[i]:
+                copy.start()
+
+    def second(self, i):
+        net, sent, sems = self.net, self.sent[i], self.sems
+        for copy in self.loads.get(i, []):
+            copy.wait()
+        sent["x", 3].wait_recv()
+        add_slabs(self.stage.at[i, 0], [self.mine(i, 0, 2), part_reader(self.got_x, i, 1)])
+        sent["up"] = net.send(self.stage.at[i, 0], self.got_last.at[i, 0], sems, 6 * i + 4, net.y)
+        sent["y", 3].wait_recv()
+        add_slabs(
+            self.stage.at[i, 1],
+            [self.mine(i, 1, 1), part_reader(self.got_y, i, columns=self.right)],
+        )
+        sent["low"] = net.send(self.stage.at[i, 1], self.got_last.at[i, 1], sems, 6 * i + 5, net.x)
+
+    def third(self, i):
+        for key in (("x", 1), ("y", 2), "up", "low"):
+            self.sent[i][key].wait_recv()
+        upper = [
+            self.mine(i, 0, 0), part_reader(self.got_x, i, 0), part_reader(self.got_last, i, 0)
+        ]
+        lower = [
+            self.mine(i, 1, 0),
+            part_reader(self.got_y, i, columns=self.left),
+            part_reader(self.got_last, i, 1),
+        ]
+        return upper, lower
+
+    def release(self, i):
+        self.net.settle([self.sent[i][key] for key in (("x", 3), ("y", 3), ("x", 1), ("y", 2))])
 
 
 def scatter_square(net, src, scratch, order, finish, resident=False):
-    my_up, my_low, got_x, got_y, got_last, stage, load_sems, *sems = scratch
-    half, width = got_x.shape[2:]
-    upper, lower = pl.ds(0, half), pl.ds(half, half)
-    column = lambda j, count=1: pl.ds(j * width, count * width)
-    left, right = pl.ds(0, width), pl.ds(width, width)
-    loads, sent = {}, {}
-
-    def mine(i, part, j):
-        if resident:
-            return part_reader(src.at[order[i], upper if part == 0 else lower, column(j)])
-        if part == 0:
-            return part_reader(my_up, i, j // 2)
-        return part_reader(my_low, i, columns=(left, right)[j])
-
-    def first(i):
-        s = order[i]
-        loads[i] = [] if resident else [
-            pltpu.make_async_copy(src.at[s, upper, column(0)], my_up.at[i, 0], load_sems.at[i, 0]),
-            pltpu.make_async_copy(src.at[s, upper, column(2)], my_up.at[i, 1], load_sems.at[i, 1]),
-            pltpu.make_async_copy(src.at[s, lower, column(0, 2)], my_low.at[i], load_sems.at[i, 2]),
-        ]
-        sent[i] = [
-            net.send(src.at[s, upper, column(3)], got_x.at[i, 1], sems, 5 * i, net.x),
-            net.send(src.at[s, lower, column(2, 2)], got_y.at[i], sems, 5 * i + 1, net.y),
-            net.send(src.at[s, upper, column(1)], got_x.at[i, 0], sems, 5 * i + 2, net.x),
-        ]
-        for load in loads[i]:
-            load.start()
-
-    def second(i):
-        for load in loads[i]:
-            load.wait()
-        sent[i][0].wait_recv()
-        add_slabs(stage.at[i, 0], [mine(i, 0, 2), part_reader(got_x, i, 1)])
-        sent[i].append(net.send(stage.at[i, 0], got_last.at[i, 0], sems, 5 * i + 3, net.y))
-        sent[i][1].wait_recv()
-        add_slabs(stage.at[i, 1], [mine(i, 1, 1), part_reader(got_y, i, columns=right)])
-        sent[i].append(net.send(stage.at[i, 1], got_last.at[i, 1], sems, 5 * i + 4, net.x))
-
-    def third(i):
-        for copy in sent[i][2:]:
-            copy.wait_recv()
-        finish(
-            order[i],
-            [mine(i, 0, 0), part_reader(got_x, i, 0), part_reader(got_last, i, 0)],
-            [
-                mine(i, 1, 0),
-                part_reader(got_y, i, columns=left),
-                part_reader(got_last, i, 1),
-            ],
-        )
-
+    scatter = SquareScatter(net, scratch, resident)
     for i in range(len(order) + 2):
         if i < len(order):
-            first(i)
+            scatter.first(i, src.at[order[i]])
             yield
         if 0 <= i - 1 < len(order):
-            second(i - 1)
+            scatter.second(i - 1)
             yield
         if 0 <= i - 2:
-            third(i - 2)
+            finish(order[i - 2], *scatter.third(i - 2))
             yield
 
 
@@ -855,15 +903,15 @@
 
     def kernel(
         x_in, g_in, w_in, small_in, wo_in, packed_in, map_in, cosine, sine,
-        x_out, normed_out, w_out, small_out, q, kv_out, out, lse, wo_out, g_out, rows_out, map_out,
+        x_out, normed_out, w_out, small_out, q, kv_out, out, lse, wo_out, g_out, second, map_out,
         shared_out, sum_out, gains_out,
-        x, normed, w, small_all, kv, wo, proj, proj_sum, second, result, projected, top, total, acc,
+        x, normed, w, small_all, kv, wo, proj, proj_sum, result, projected, top, total, acc,
         *sems,
     ):
         scratch, sems = list(sems[:9]), list(sems[9:])
         pairs = lambda: (sems.pop(0), sems.pop(0))
         x_sems, g_sems, w_sems, small_sems, wo_sems, kv_sems = [pairs() for _ in range(6)]
-        map_sems, rows_sems, shared_sems, sum_sems, sum_sems_two = [pairs() for _ in range(5)]
+        map_sems, shared_sems, sum_sems, sum_sems_two = [pairs() for _ in range(4)]
         local = sems.pop(0)
         net = Links(n_rows, n_cols)
         others = net.spread_partners()
@@ -1024,16 +1072,7 @@
             run_together(gathers[s])
             second_norm(s)
         save(proj_sum, sum_out)
-        rows_steps = gather_square(
-            net, second.at[:, pl.ds(0, row_width)], rows_out, rows_sems, local.at[8 + 9], ring,
-            known=second,
-        )
-        next(rows_steps)
-        next(g_steps, None)
-        next(rows_steps)
-        next(shared_steps)
-        next(g_steps, None)
-        run_together(rows_steps, g_steps, shared_steps)
+        run_together(g_steps, shared_steps)
         own_map.wait()
         for copy in maps:
             copy.wait_recv()
@@ -1058,7 +1097,7 @@
             shape((heads, 1, length), f32),
             shape((model, q_width), bf16),
             shape((ring, length, model), bf16),
-            shape((ring, length, model), bf16),
+            shape((length, model), bf16),
             shape((ring, n_rows, *slot_map.shape), f32),
             shape((model, packed.shape[2]), bf16),
             shape((pieces, piece, model), bf16),
@@ -1073,7 +1112,6 @@
             vmem((model, q_width), bf16),
             vmem((pieces, piece, model), bf16),
             vmem((pieces, piece, model), bf16),
-            vmem((length, model), bf16),
             vmem((pieces, piece, row_width), bf16),
             vmem((length, in_width), f32),
             vmem((1, length), f32),
@@ -1088,158 +1126,402 @@
         + pair_sems(2 * ring)
         + pair_sems(2 * ring)
         + pair_sems(partners)
-        + pair_sems(7 * ring)
         + pair_sems(2 * ring)
         + pair_sems(7)
         + pair_sems(7)
         + [pltpu.SemaphoreType.DMA((18,))],
         (block, grads, weights, small, weights_out, packed, slot_map, *tables),
         in_vmem=(7, 8),
-        out_vmem=(4, 6, 7, 14),
-    )
-
-
-def token_sum(n_rows, n_cols, parts, gates, expert_rows, probs, router, token_rows, gains):
+        out_vmem=(4, 6, 7, 10, 14),
+    )
+
+
+def experts_phase(n_rows, n_cols, second, grads, maps, experts_w, shared, router, slots):
     ring = n_cols // 2
-    rows, model = parts.shape[1:]
+    tokens, model = second.shape
     width = model // n_rows
     experts = n_rows * ring
-    slot_rows, d_part, e_act, d_gate, d_up = expert_rows
-    n_slots, hidden = e_act.shape
-    half = hidden // 2
+    half_hidden = experts_w[0].shape[1]
+    hidden = 2 * half_hidden
+    pad = shared.shape[1] // 3
+    blocks, _, block_rows = maps.shape[1:]
+    n_slots = blocks * slots
     bf16, f32 = jnp.bfloat16, jnp.float32
     shape = jax.ShapeDtypeStruct
 
     def kernel(
-        src, gate, xr_in, dp_in, act_in, dg_in, du_in, probs, router, x_in, proj_in, g_in, gains,
-        d_attn, d_resid, gain_out, gate_out, out_g, out_u, out_d, land_g, land_u, land_d,
-        result, second, xr, dp, act, dg, du, leave_a, leave_b, landed_a, landed_b, full_a, full_b,
-        gate_own, high_ref, low_ref, *rest,
+        known, g_in, maps, gate_own, gate_twin, up_own, up_twin, down_own, down_twin, shared_in,
+        router_in,
+        result, rows_out, y_out, slot_out, d_part_out, act_out, d_gate_out, d_up_out, s_act_out,
+        d_shared_out, probs_out, gate_out,
+        w_gate, w_up, w_down, shared, router, x, g, slot_rows, part, e_act, d_gate, d_up, s_act,
+        d_shared, probs, d_x, d_gates, *rest,
+    ):
+        scratch, (landed, leaving, ring_s, ring_r) = rest[:9], rest[9:13]
+        xs, xr, ms, mr, local, w_sems, out_sems = rest[13:]
+        net = Links(n_rows, n_cols)
+        others = net.spread_partners()
+        net.greet([device for _, _, device in others])
+        mine = net.r * ring + net.z
+        gather = SquareGather(
+            net, known.at[:, pl.ds(0, width)], rows_out, (xs, xr), local.at[0], ring, known=known
+        )
+        gather.up(0)
+        x_load = lambda s: pltpu.make_async_copy(
+            known if s == 0 else rows_out.at[s], x, local.at[1]
+        )
+        g_load = lambda s: pltpu.make_async_copy(g_in.at[s], g, local.at[2])
+        x_load(0).start()
+        g_load(0).start()
+        shared_load = pltpu.make_async_copy(shared_in, shared, local.at[3])
+        shared_load.start()
+        router_load = pltpu.make_async_copy(router_in, router, local.at[4])
+        router_load.start()
+        weights = []
+        for j in range(n_rows):
+            there = pl.ds(pl.multiple_of(net.flip(j) * width, width), width)
+            here = pl.ds(j * width, width)
+            for h, sources in enumerate(((gate_own, up_own, down_own), (gate_twin, up_twin, down_twin))):
+                cols = pl.ds(h * half_hidden, half_hidden)
+                number = 6 * j + 3 * h
+                weights += [
+                    pltpu.make_async_copy(
+                        sources[0].at[there, :], w_gate.at[here, cols], w_sems.at[number]
+                    ),
+                    pltpu.make_async_copy(
+                        sources[1].at[there, :], w_up.at[here, cols], w_sems.at[number + 1]
+                    ),
+                    pltpu.make_async_copy(
+                        sources[2].at[:, there], w_down.at[cols, here], w_sems.at[number + 2]
+                    ),
+                ]
+        for copy in weights:
+            copy.start()
+
+        scatter = SquareScatter(net, scratch, resident=True)
+        ring_copies, stores = [], {}
+        kept = {
+            "slot": (slot_rows, slot_out), "part": (part, d_part_out), "act": (e_act, act_out),
+            "d_gate": (d_gate, d_gate_out), "d_up": (d_up, d_up_out), "s_act": (s_act, s_act_out),
+            "d_shared": (d_shared, d_shared_out), "probs": (probs, probs_out), "y": (g, y_out),
+        }
+
+        def store(s, *names):
+            for name in names:
+                source, target = kept[name]
+                number = list(kept).index(name)
+                stores[name] = pltpu.make_async_copy(source, target.at[s], out_sems.at[number])
+                stores[name].start()
+
+        def stored(*names):
+            for name in names:
+                if name in stores:
+                    stores.pop(name).wait()
+
+        def pass_on(s):
+            turn = s - 1
+            for p, terms in enumerate(scatter.third(s)):
+                at = pl.ds(p * (tokens // 2), tokens // 2)
+                if s == 0:
+                    add_slabs(result.at[at, :], terms)
+                    continue
+                if turn and not p:
+                    ring_copies[turn - 1].wait_recv()
+                if turn > 1 and not p:
+                    net.settle([ring_copies[turn - 2]])
+                if turn:
+                    terms = terms + [part_reader(landed.at[turn - 1, at, :])]
+                add_slabs(leaving.at[turn % 2, at, :], terms)
+            if s:
+                ring_copies.append(
+                    net.send(leaving.at[turn % 2], landed.at[turn], (ring_s, ring_r), turn, net.up)
+                )
+
+        def in_lanes(column):
+            high = column.astype(bf16)
+            rest = column - high.astype(f32)
+            middle = rest.astype(bf16)
+            low = (rest - middle.astype(f32)).astype(bf16)
+            lane = lax.broadcasted_iota(jnp.int32, (column.shape[0], 128), 1)
+            terms = jnp.where(lane == 0, high.astype(f32), 0.0)
+            terms = jnp.where(lane == 1, middle.astype(f32), terms)
+            return jnp.where(lane == 2, low.astype(f32), terms).astype(bf16)
+
+        tile = 512
+
+        def compute(s, ticks):
+            def tick(name):
+                for step in ticks.get(name, []):
+                    step()
+
+            lanes = lax.broadcasted_iota(jnp.int32, (1, 128), 1)
+            mine_hot = (lanes == mine).astype(f32)
+            slot_row, slot_column, chosen = [], [], []
+            for b in range(blocks):
+                own_map = jnp.where(
+                    lax.broadcasted_iota(jnp.int32, (experts, block_rows), 0) == mine, maps[s, b], 0.0
+                )
+                own_map = jnp.sum(own_map, 0, keepdims=True)
+                slot_row.append(jnp.where(own_map >= 0, own_map + b * slots, -1.0))
+                filled = jnp.concatenate(
+                    [maps[s, b], jnp.full((128 - experts, block_rows), -1.0, f32)], 0
+                ).T
+                chosen.append(filled)
+                own_map = jnp.sum(filled * mine_hot, -1, keepdims=True)
+                slot_column.append(jnp.where(own_map >= 0, own_map + b * slots, -1.0))
+            slot_row, chosen = jnp.concatenate(slot_row, 1), jnp.concatenate(chosen, 0)
+            slot_column = jnp.concatenate(slot_column, 0)
+            numbers = lambda dims, axis: lax.broadcasted_iota(jnp.int32, dims, axis).astype(f32)
+            pick = (numbers((n_slots, tokens), 0) == slot_row).astype(f32).astype(bf16)
+            pick_t = (numbers((tokens, n_slots), 1) == slot_column).astype(f32).astype(bf16)
+
+            stored("probs", "s_act", "d_shared", "y")
+            if s:
+                g_load(s).start()
+            x_load(s).wait()
+            if s == 0:
+                router_load.wait()
+                shared_load.wait()
+            logits = matmul(x[...], router[...])
+            logits = jnp.where(chosen >= 0, logits, NEG_LARGE)
+            logits = jnp.exp(logits - jnp.max(logits, -1, keepdims=True))
+            gate_probs = logits / jnp.sum(logits, -1, keepdims=True)
+            probs[...] = gate_probs
+            my_gate = jnp.sum(gate_probs * mine_hot, -1, keepdims=True)
+            slot_gate = jnp.sum(matmul(pick, in_lanes(my_gate)), -1, keepdims=True)
+            s_gate = matmul(x[...], shared[:, :pad])
+            s_up = matmul(x[...], shared[:, pad : 2 * pad])
+            g_load(s).wait()
+            through = matmul(g[...], shared[:, 2 * pad :])
+            s_silu, s_slope = silu_parts(s_gate)
+            s_act[...] = (s_silu * s_up).astype(bf16)
+            d_shared[:, :pad] = (through * s_up * s_slope).astype(bf16)
+            d_shared[:, pad:] = (through * s_silu).astype(bf16)
+            store(s, "probs", "s_act", "d_shared")
+            tick("shared")
+
+            stored("slot", "part", "act", "d_gate", "d_up")
+            for t in range(model // tile):
+                at = slice(t * tile, (t + 1) * tile)
+                slot_rows[:, at] = matmul(pick, x[:, at]).astype(bf16)
+                part[:, at] = matmul(pick, g[:, at]).astype(bf16)
+            if s == 0:
+                for copy in weights:
+                    copy.wait()
+            tick("picked")
+
+            step = half_hidden // 3
+
+            def hidden_tile(t, total):
+                at = pl.ds(pl.multiple_of(t * step, step), step)
+                e_gate = matmul(slot_rows[...], w_gate[:, at])
+                e_up = matmul(slot_rows[...], w_up[:, at])
+                through = matmul_nt(part[...], w_down[at, :])
+                e_silu, e_slope = silu_parts(e_gate)
+                act = e_silu * e_up
+                d_act = through * slot_gate
+                e_act[:, at] = act.astype(bf16)
+                d_gate[:, at] = (d_act * e_up * e_slope).astype(bf16)
+                d_up[:, at] = (d_act * e_silu).astype(bf16)
+                return total + jnp.sum(act * through, -1, keepdims=True)
+
+            d_slot_gate = lax.fori_loop(0, 3, hidden_tile, jnp.zeros((n_slots, 1), f32))
+            tick("half")
+            d_slot_gate = lax.fori_loop(3, 6, hidden_tile, d_slot_gate)
+            d_gates[net.chip(s)] = jnp.sum(
+                matmul_tn(in_lanes(d_slot_gate), pick), 0, keepdims=True
+            )
+            part[...] = (part[...].astype(f32) * slot_gate).astype(bf16)
+            store(s, "slot", "part", "act", "d_gate", "d_up")
+            tick("hidden")
+
+            d_chunk = d_x.at[s % 2]
+            if s >= 2:
+                scatter.release(s - 2)
+            def out_tile(t):
+                at = pl.ds(pl.multiple_of(t * tile, tile), tile)
+                d_slot = matmul_nt(d_gate[...], w_gate[at, :]) + matmul_nt(d_up[...], w_up[at, :])
+                d_chunk[:, at] = (
+                    matmul(pick_t, d_slot.astype(bf16))
+                    + matmul_nt(d_shared[...], shared[at, : 2 * pad])
+                ).astype(bf16)
+                out = (matmul(e_act[...], w_down[:, at]) * slot_gate).astype(bf16)
+                g[:, at] = (
+                    matmul(pick_t, out) + matmul_nt(s_act[...], shared[at, 2 * pad :])
+                ).astype(bf16)
+
+            pl.loop(2, 5)(out_tile)
+            scatter.give(s, d_chunk, 3)
+            scatter.give(s, d_chunk, 2)
+            tick("right")
+            pl.loop(0, 2)(out_tile)
+            scatter.give(s, d_chunk, 1)
+            store(s, "y")
+            tick("left")
+
+        def arrive(s):
+            def step():
+                gather.up(s)
+                gather.across(s)
+
+            return step
+
+        def take(s):
+            def step():
+                gather.complete(s)
+                x_load(s).start()
+
+            return step
+
+        pass_x = lambda s: lambda: gather.forward(s)
+        second_of = lambda s: lambda: scatter.second(s)
+        third_of = lambda s: lambda: pass_on(s)
+        compute(0, {"hidden": [arrive(1)], "left": [pass_x(1), arrive(2), take(1)]})
+        compute(
+            1,
+            {
+                "half": [pass_x(2), arrive(3)],
+                "hidden": [second_of(0)],
+                "left": [third_of(0), take(2)],
+            },
+        )
+        compute(2, {"picked": [pass_x(3)], "hidden": [second_of(1)], "left": [third_of(1), take(3)]})
+        compute(3, {"hidden": [second_of(2)], "left": [third_of(2)]})
+        copies = []
+        own = pltpu.make_async_copy(d_gates, gate_out.at[mine], local.at[5])
+        own.start()
+        for number, (hops, bits, device) in enumerate(others):
+            copies.append(net.send(d_gates, gate_out.at[mine], (ms, mr), number, device))
+        scatter.second(3)
+        pass_on(3)
+        ring_copies[-1].wait_recv()
+        add_slabs(result, [part_reader(result), part_reader(landed.at[ring - 2])])
+        stored(*kept)
+        own.wait()
+        gather.own.wait()
+        for copy in copies:
+            copy.wait_recv()
+        net.finish()
+
+    vmem = pltpu.VMEM
+    by_chunk = lambda dtype, *dims: shape((ring, *dims), dtype)
+    return remote_call(
+        kernel,
+        "experts_phase",
+        5,
+        [
+            shape((tokens, width), bf16),
+            by_chunk(bf16, tokens, model),
+            by_chunk(bf16, tokens, model),
+            by_chunk(bf16, n_slots, model),
+            by_chunk(bf16, n_slots, model),
+            by_chunk(bf16, n_slots, hidden),
+            by_chunk(bf16, n_slots, hidden),
+            by_chunk(bf16, n_slots, hidden),
+            by_chunk(bf16, tokens, pad),
+            by_chunk(bf16, tokens, 2 * pad),
+            by_chunk(f32, tokens, 128),
+            shape((experts, ring, 1, tokens), f32),
+        ],
+        [
+            vmem((model, hidden), bf16),
+            vmem((model, hidden), bf16),
+            vmem((hidden, model), bf16),
+            vmem(shared.shape, bf16),
+            vmem(router.shape, bf16),
+            vmem((tokens, model), bf16),
+            vmem((tokens, model), bf16),
+            vmem((n_slots, model), bf16),
+            vmem((n_slots, model), bf16),
+            vmem((n_slots, hidden), bf16),
+            vmem((n_slots, hidden), bf16),
+            vmem((n_slots, hidden), bf16),
+            vmem((tokens, pad), bf16),
+            vmem((tokens, 2 * pad), bf16),
+            vmem((tokens, 128), f32),
+            vmem((2, tokens, model), bf16),
+            vmem((ring, 1, tokens), f32),
+        ]
+        + scatter_scratch(ring, tokens, width, resident=True)
+        + [vmem((ring - 1, tokens, width), bf16), vmem((2, tokens, width), bf16)]
+        + pair_sems(ring - 1)
+        + pair_sems(7 * ring)
+        + pair_sems(experts - 1)
+        + [
+            pltpu.SemaphoreType.DMA((6,)),
+            pltpu.SemaphoreType.DMA((24,)),
+            pltpu.SemaphoreType.DMA((9,)),
+        ],
+        (second, grads, maps, *experts_w, shared, router),
+        in_vmem=(2,),
+        out_vmem=(0,),
+    )
+
+
+def attention_back(
+    n_rows, n_cols, d_block, d_gates, probs, router, token_rows, gains, weights_out, weights_in,
+    queries, kv, heads_out, lse, tables, parts,
+):
+    ring = n_cols // 2
+    length, model = token_rows[0].shape
+    experts = n_rows * ring
+    q_width = weights_out.shape[1]
+    in_width = weights_in.shape[1]
+    col_width = model // n_cols
+    width = model // n_rows
+    heads = q_width // HEAD_DIM
+    scale = 1.0 / math.sqrt(HEAD_DIM)
+    bf16, f32 = jnp.bfloat16, jnp.float32
+    shape = jax.ShapeDtypeStruct
+
+    def kernel(
+        block, gates, probs, router, x_in, proj_in, g_in, gains, wo_in, w_in, q, kv, out, lse, cosine,
+        sine, y_in,
+        d_proj, d_first, y_out, wo_out, d_resid, gain_out,
+        second, proj, g, high_ref, low_ref,
+        wo, w, go, delta, dqt, dkv, dkv_own, wo_part, *rest,
     ):
         scratch, ring_parts = rest[:9], rest[9:13]
-        gs, gr, ms, mr, es, er, local, sem = rest[13:]
-        leaving, landed, full = (leave_a, leave_b), (landed_a, landed_b), (full_a, full_b)
+        kv_parts, wo_parts, gs, gr, local = rest[13:20], rest[20:27], rest[27], rest[28], rest[29]
         net = Links(n_rows, n_cols)
-        others = net.spread_partners()
-        net.greet([device for _, _, device in others] + [net.twin])
-        mine = net.r * ring + net.z
-        order = list(range(1, ring)) + [0]
-        steps = scatter_square(net, src, scratch, order, ring_finish(net, ring_parts, result, []))
-        next(steps)
-        copies = []
-        own = pltpu.make_async_copy(gate, gate_out.at[mine], local.at[1])
-        own.start()
-        for number, (hops, bits, device) in enumerate(others):
-            copies.append(net.send(gate, gate_out.at[mine], (ms, mr), number, device))
-        next(steps)
-
+        net.greet([net.x, net.y, net.up, net.down, net.twin])
+        gather = gather_square(net, block, second, (gs, gr), local.at[1], 1)
+        next(gather)
+        x, d_attn = d_first, proj
         loads = [
-            pltpu.make_async_copy(a, b, sem.at[i])
-            for i, (a, b) in enumerate(
-                ((xr_in, xr), (dg_in, dg), (du_in, du), (act_in, act), (dp_in, dp))
-            )
+            pltpu.make_async_copy(a, b, local.at[2 + i])
+            for i, (a, b) in enumerate(((x_in, x), (proj_in, proj), (g_in.at[0], g)))
         ]
         for load in loads:
             load.start()
-        ours, theirs = slice(0, half), slice(half, hidden)
-        sends, leaves, stores = [], {}, {}
-
-        def slot_of(kind, j):
-            return kind // 2, j % 2 if kind < 2 else 0
-
-        def tile(kind, j, part):
-            columns = slice(j * width, (j + 1) * width)
-            if kind < 2:
-                return matmul_tn(xr[:, columns], (dg, du)[kind][:, part])
-            return matmul_tn(act[:, part], dp[:, columns])
-
-        def land(kind, j, order=False):
-            place = net.flip(j) if order else j
-            at = pl.ds(pl.multiple_of(place * width, width), width)
-            if kind < 2:
-                ref = ((land_g, land_u), (out_g, out_u))[order][kind]
-                return ref.at[at, :]
-            return (land_d, out_d)[order].at[:, at]
-
-        def give(kind, j):
-            group, slot = slot_of(kind, j)
-            if (group, slot) in leaves:
-                leaves[group, slot].wait_send()
-            buffer = leaving[group]
-            buffer[slot] = tile(kind, j, theirs).astype(bf16)
-            copy = net.send(buffer.at[slot], land(kind, j), (es, er), 4 * kind + j, net.twin)
-            net.started.pop()
-            leaves[group, slot] = copy
-            sends.append(copy)
-
-        def keep(kind, j):
-            group, slot = slot_of(kind, j)
-            buffer, got = full[group], landed[group]
-            sends[4 * kind + j].wait_recv()
-            load = pltpu.make_async_copy(land(kind, j), got.at[slot], sem.at[5 + slot])
-            load.start()
-            if (group, slot) in stores:
-                stores[group, slot].wait()
-            product = tile(kind, j, ours)
-            load.wait()
-            buffer[slot] = product + got[slot].astype(f32)
-            store = pltpu.make_async_copy(
-                buffer.at[slot], land(kind, j, True), sem.at[7 + 2 * group + slot]
-            )
-            store.start()
-            stores[group, slot] = store
-
-        for load in loads[:3]:
-            load.wait()
-        for kind in (0, 1):
-            for j in range(n_rows):
-                give(kind, j)
-            next(steps)
-        for load in loads[3:]:
-            load.wait()
-        for j in range(n_rows):
-            give(2, j)
-        next(steps)
-        next(steps)
-        for kind in (0, 1, 2):
-            next(steps)
-            for j in range(n_rows):
-                keep(kind, j)
-            next(steps)
-        for copy in leaves.values():
-            copy.wait_send()
-        for store in stores.values():
-            store.wait()
-
-        run_together(steps)
-
-        x, proj, g = xr.at[pl.ds(0, rows)], xr.at[pl.ds(rows, rows)], dp.at[pl.ds(0, rows)]
-        loads = [
-            pltpu.make_async_copy(a, b, sem.at[i])
-            for i, (a, b) in enumerate(((x_in, x), (proj_in, proj), (g_in, g)))
-        ]
-        for load in loads:
-            load.start()
-        gather = gather_square(net, result, second, (gs, gr), local.at[0], 1)
-        next(gather)
-        own.wait()
-        for copy in copies:
-            copy.wait_recv()
-        gate_load = pltpu.make_async_copy(gate_out.at[:, net.z], gate_own, sem.at[3])
-        gate_load.start()
-        gate_load.wait()
-        d_gates = jnp.concatenate([gate_own[...], jnp.zeros((128 - experts, rows), f32)], 0).T
+        wo_load = pltpu.make_async_copy(wo_in, wo, local.at[5])
+        wo_load.start()
+        w_load = pltpu.make_async_copy(w_in, w, local.at[0])
+        w_load.start()
+        d_gates = jnp.concatenate(
+            [gates[...].reshape(experts, length), jnp.zeros((128 - experts, length), f32)], 0
+        ).T
         d_logits = probs[...] * (d_gates - jnp.sum(probs[...] * d_gates, -1, keepdims=True))
         high = d_logits.astype(bf16)
         high_ref[...] = high
         low_ref[...] = (d_logits - high.astype(f32)).astype(bf16)
         for load in loads:
             load.wait()
+        copies = []
+        y_steps = scatter_square(
+            net, y_in, scratch, list(range(1, ring)), ring_finish(net, ring_parts, None, copies)
+        )
+        by_place = lambda ref: lambda hops, core: ref.at[
+            pl.ds((net.place(hops) * 2 + core) * col_width, col_width), :
+        ]
+
         run_together(gather)
+        next(y_steps)
+        next(y_steps)
         gain = gains[1:2]
         gain_out[...] = jnp.zeros_like(gain_out)
 
-        @pl.loop(0, rows // 128)
+        @pl.loop(0, length // 128)
         def _(i):
             at = pl.ds(pl.multiple_of(i * 128, 128), 128)
             values = x[at, :].astype(f32) + proj[at, :].astype(f32)
@@ -1256,90 +1538,7 @@
             along = (d_second[:, :width] * unit[:, :width]).reshape(16, 8, width)
             gain_out[...] += jnp.sum(along, 0)
 
-        net.finish()
-
-    x, proj, g = token_rows
-    return remote_call(
-        kernel,
-        "token_sum",
-        5,
-        [
-            shape((rows, model), bf16),
-            shape((rows, width), f32),
-            shape((8, width), f32),
-            shape((experts, *gates.shape), f32),
-            shape((model, half), f32),
-            shape((model, half), f32),
-            shape((half, model), f32),
-            shape((model, half), bf16),
-            shape((model, half), bf16),
-            shape((half, model), bf16),
-        ],
-        [
-            pltpu.VMEM((rows, width), bf16),
-            pltpu.VMEM((1, rows, model), bf16),
-            pltpu.VMEM((n_slots, model), bf16),
-            pltpu.VMEM((n_slots, model), bf16),
-            pltpu.VMEM((n_slots, hidden), bf16),
-            pltpu.VMEM((n_slots, hidden), bf16),
-            pltpu.VMEM((n_slots, hidden), bf16),
-            pltpu.VMEM((2, width, half), bf16),
-            pltpu.VMEM((1, half, width), bf16),
-            pltpu.VMEM((2, width, half), bf16),
-            pltpu.VMEM((1, half, width), bf16),
-            pltpu.VMEM((2, width, half), f32),
-            pltpu.VMEM((1, half, width), f32),
-            pltpu.VMEM((experts, rows), f32),
-            pltpu.VMEM((rows, 128), bf16),
-            pltpu.VMEM((rows, 128), bf16),
-        ]
-        + scatter_scratch(ring, rows, width)
-        + ring_scratch(ring, rows, width)
-        + pair_sems(7)
-        + pair_sems(experts - 1)
-        + pair_sems(3 * n_rows)
-        + [pltpu.SemaphoreType.DMA((2,)), pltpu.SemaphoreType.DMA((10,))],
-        (parts, gates, *expert_rows, probs, router, x, proj, g, gains),
-        in_vmem=(7, 8, 12),
-        out_vmem=(0, 1, 2),
-    )
-
-
-def attention_back(
-    n_rows, n_cols, d_attn, weights_out, weights_in, queries, kv, heads_out, lse, tables, parts
-):
-    ring = n_cols // 2
-    length, model = d_attn.shape
-    q_width = weights_out.shape[1]
-    in_width = weights_in.shape[1]
-    col_width = model // n_cols
-    width = model // n_rows
-    heads = q_width // HEAD_DIM
-    scale = 1.0 / math.sqrt(HEAD_DIM)
-    bf16, f32 = jnp.bfloat16, jnp.float32
-    shape = jax.ShapeDtypeStruct
-
-    def kernel(
-        d_attn, wo, w_in, q, kv, out, lse, cosine, sine, y_in,
-        d_proj, d_first, y_out, wo_out,
-        w, go, delta, dqt, dkv, dkv_own, wo_part, *rest,
-    ):
-        scratch, ring_parts = rest[:9], rest[9:13]
-        kv_parts, wo_parts, local = rest[13:20], rest[20:27], rest[27]
-        net = Links(n_rows, n_cols)
-        net.greet([net.x, net.y, net.up, net.down, net.twin])
-        w_load = pltpu.make_async_copy(w_in, w, local.at[0])
-        w_load.start()
-        copies = []
-        y_steps = scatter_square(
-            net, y_in, scratch, list(range(1, ring)), ring_finish(net, ring_parts, None, copies)
-        )
-        next(y_steps)
-        next(y_steps)
-        by_place = lambda ref: lambda hops, core: ref.at[
-            pl.ds((net.place(hops) * 2 + core) * col_width, col_width), :
-        ]
-
+        wo_load.wait()
         go[...] = matmul(d_attn[...], wo[...]).astype(bf16)
         wo_part[...] = matmul_tn(d_attn[...], out[...].astype(bf16)).astype(bf16)
         wo_steps = scatter_columns(net, by_place(wo_part), wo_out, wo_parts)
@@ -1351,6 +1550,7 @@
         dqt[...] = jnp.zeros_like(dqt)
         dkv[...] = jnp.zeros_like(dkv)
         next(wo_steps)
+        next(y_steps)
         next(y_steps)
 
         def one_block(number, masked):
@@ -1385,8 +1585,8 @@
         )
         next(kv_steps)
         next(kv_steps)
+        next(wo_steps)
         next(y_steps)
-        next(wo_steps)
 
         def turned_back(values):
             return (values * cosine[...] - pltpu.roll(values, HEAD_DIM // 2, 1) * sine[...]).astype(bf16)
@@ -1395,8 +1595,10 @@
             columns = slice(head * HEAD_DIM, (head + 1) * HEAD_DIM)
             d_proj[:, columns] = turned_back((dqt[head] * scale).T)
         next(kv_steps)
+        next(wo_steps)
         next(y_steps)
         next(kv_steps)
+        next(y_steps)
         run_together(kv_steps)
         d_proj[:, q_width : q_width + HEAD_DIM] = turned_back(dkv_own[:, :HEAD_DIM])
         d_proj[:, q_width + HEAD_DIM :] = dkv_own[:, HEAD_DIM:].astype(bf16)
@@ -1419,8 +1621,16 @@
             shape((length, model), bf16),
             shape((length, width), bf16),
             shape((col_width, q_width), f32),
+            shape((length, width), f32),
+            shape((8, width), f32),
         ],
         [
+            vmem((1, length, model), bf16),
+            vmem((length, model), bf16),
+            vmem((length, model), bf16),
+            vmem((length, 128), bf16),
+            vmem((length, 128), bf16),
+            vmem((model, q_width), bf16),
             vmem((model, in_width), bf16),
             vmem((length, q_width), bf16),
             vmem((heads, 1, length), f32),
@@ -1433,14 +1643,21 @@
         + ring_scratch(ring, length, width)
         + scatter_columns_scratch(ring, length, 2 * HEAD_DIM)
         + scatter_columns_scratch(ring, col_width, q_width)
-        + [pltpu.SemaphoreType.DMA((1,))],
-        (d_attn, weights_out, weights_in, queries, kv, heads_out, lse, *tables, parts),
-        in_vmem=(0, 1, 3, 4, 5, 6, 7, 8),
-        out_vmem=(0, 1, 2, 3),
-    )
-
-
-def last_phase(n_rows, n_cols, d_first, d_proj, normed, parts, part_sum, x, proj, d_resid, gains, gain_part):
+        + pair_sems(7)
+        + [pltpu.SemaphoreType.DMA((6,))],
+        (
+            d_block, d_gates, probs, router, *token_rows, gains, weights_out, weights_in, queries, kv,
+            heads_out, lse, *tables, parts,
+        ),
+        in_vmem=(1, 2, 3, 7, 10, 11, 12, 13, 14, 15),
+        out_vmem=(0, 1, 2, 3, 4, 5),
+    )
+
+
+def last_phase(
+    n_rows, n_cols, d_first, d_proj, normed, parts, part_sum, x, proj, d_resid, gains, gain_part,
+    expert_rows, router_rows,
+):
     ring = n_cols // 2
     length, model = d_first.shape
     width = model // n_rows
@@ -1451,15 +1668,24 @@
     bf16, f32 = jnp.bfloat16, jnp.float32
     shape = jax.ShapeDtypeStruct
     chips = n_rows * ring
+    slot_rows, d_part, e_act, d_gate, d_up = expert_rows
+    n_slots, hidden = e_act.shape
+    half = hidden // 2
+    experts = router_rows[2].shape[0]
+    rows_dev = length // n_rows
 
     def kernel(
-        d_first, d_proj, normed, y_in, y_sum, x, proj, d_resid, gains, gain_two,
-        layer_out, grad_in, gain_out, w_out,
-        d_own, w_part, moment, moments, gain_own, gain_twin, gain_sums, *rest,
+        d_first, d_proj, normed, y_in, y_sum, x, proj_in, d_resid, gains, gain_two,
+        xr_in, dp_in, act_in, dg_in, du_in, rows_in, probs_in, gates_in,
+        layer_out, grad_in, gain_out, w_out, router_out, out_g, out_u, out_d, land_g, land_u, land_d,
+        d_own, w_part, moment, moments, gain_own, gain_twin, gain_sums, proj,
+        xr, dg, du, leave_a, leave_b, landed_a, landed_b, full_a, full_b,
+        x_q, probs_q, gates_q, router_part, router_got, router_sum, *rest,
     ):
         scratch, y_scratch = rest[:9], rest[9:18]
         w_parts = rest[18:25]
-        mo_s, mo_r, ga_s, ga_r, gt_s, gt_r = rest[25:]
+        mo_s, mo_r, ga_s, ga_r, gt_s, gt_r, es, er, sem, ro_s, ro_r, router_sems = rest[25:]
+        leaving, landed, full = (leave_a, leave_b), (landed_a, landed_b), (full_a, full_b)
         net = Links(n_rows, n_cols)
         others = net.spread_partners()
         net.greet([device for _, _, device in others] + [net.twin])
@@ -1475,7 +1701,7 @@
                 extra = [
                     part_reader(y_sum.at[at, :]),
                     part_reader(x.at[at, pl.ds(0, width)]),
-                    part_reader(proj.at[at, pl.ds(0, width)]),
+                    part_reader(proj.at[at, :]),
                 ]
                 add_slabs(layer_out.at[at, :], terms + extra)
 
@@ -1483,14 +1709,93 @@
         y_steps = scatter_square(net, y_in, y_scratch, [0], finish_out)
         next(steps)
         next(steps)
+        loads = [
+            pltpu.make_async_copy(a, b, sem.at[i])
+            for i, (a, b) in enumerate(
+                ((xr_in, xr), (dg_in, dg), (du_in, du), (act_in, dg), (dp_in, xr))
+            )
+        ]
+        for load in loads[:3]:
+            load.start()
+        ours, theirs = slice(0, half), slice(half, hidden)
+        given, leaves, stores = [], {}, {}
+
+        def slot_of(kind, j):
+            return kind // 2, j % 2 if kind < 2 else 0
+
+        def tile(kind, j, part):
+            columns = slice(j * width, (j + 1) * width)
+            if kind < 2:
+                return matmul_tn(xr[:, columns], (dg, du)[kind][:, part])
+            return matmul_tn(dg[:, part], xr[:, columns])
+
+        def land(kind, j, order=False):
+            place = net.flip(j) if order else j
+            at = pl.ds(pl.multiple_of(place * width, width), width)
+            if kind < 2:
+                ref = ((land_g, land_u), (out_g, out_u))[order][kind]
+                return ref.at[at, :]
+            return (land_d, out_d)[order].at[:, at]
+
+        def give(kind, j):
+            group, slot = slot_of(kind, j)
+            if (group, slot) in leaves:
+                leaves[group, slot].wait_send()
+            buffer = leaving[group]
+            buffer[slot] = tile(kind, j, theirs).astype(bf16)
+            copy = net.send(buffer.at[slot], land(kind, j), (es, er), 4 * kind + j, net.twin)
+            net.started.pop()
+            leaves[group, slot] = copy
+            given.append(copy)
+
+        def keep(kind, j):
+            group, slot = slot_of(kind, j)
+            buffer, got = full[group], landed[group]
+            given[4 * kind + j].wait_recv()
+            load = pltpu.make_async_copy(land(kind, j), got.at[slot], sem.at[5 + slot])
+            load.start()
+            if (group, slot) in stores:
+                stores[group, slot].wait()
+            product = tile(kind, j, ours)
+            load.wait()
+            buffer[slot] = product + got[slot].astype(f32)
+            store = pltpu.make_async_copy(
+                buffer.at[slot], land(kind, j, True), sem.at[7 + 2 * group + slot]
+            )
+            store.start()
+            stores[group, slot] = store
+
+        proj_load = pltpu.make_async_copy(proj_in.at[:, pl.ds(0, width)], proj, sem.at[10])
+        proj_load.start()
+        quarter = pl.ds(pl.multiple_of(net.r * rows_dev, rows_dev), rows_dev)
+        column = pl.ds(pl.multiple_of(net.place(0) * width, width), width)
+        router_loads = []
+        for s in range(ring):
+            router_loads += [
+                pltpu.make_async_copy(
+                    rows_in.at[s, quarter, column], x_q.at[s], router_sems.at[s, 0]
+                ),
+                pltpu.make_async_copy(probs_in.at[s, quarter, :], probs_q.at[s], router_sems.at[s, 1]),
+                pltpu.make_async_copy(
+                    gates_in.at[:, net.chip(s), 0, quarter], gates_q.at[s], router_sems.at[s, 2]
+                ),
+            ]
+        for load in router_loads:
+            load.start()
         w_part[...] = matmul_tn(normed[...], d_proj[...]).astype(bf16)
         by_place = lambda hops, core: w_part.at[
             pl.ds((net.place(hops) * 2 + core) * col_width, col_width), :
         ]
         w_steps = scatter_columns(net, by_place, w_out, w_parts)
         next(w_steps)
+        next(steps)
+        next(w_steps)
+        next(steps)
         next(y_steps)
-        next(w_steps)
+        for load in loads[:3]:
+            load.wait()
+        for j in range(2):
+            give(0, j)
         run_together(steps)
 
         gain = gains[0:1, :width]
@@ -1515,6 +1820,9 @@
         ]
         gain_own[8:] = gain_two[...]
         twin = net.send(gain_own, gain_twin, (gt_s, gt_r), 0, net.twin)
+        for j in range(2, n_rows):
+            give(0, j)
+        next(w_steps)
         for copy in sends:
             copy.wait_recv()
         whole = moment[...] + moments[0] + moments[1] + moments[2]
@@ -1530,10 +1838,53 @@
             net.send(gain_sums.at[mine], gain_sums.at[mine], (ga_s, ga_r), number, device)
             for number, (hops, bits, device) in enumerate(others)
         ]
+        proj_load.wait()
+        next(y_steps)
+        for j in range(n_rows):
+            give(1, j)
         next(w_steps)
-        run_together(y_steps)
+        next(y_steps)
+        for load in router_loads:
+            load.wait()
+        for s in range(ring):
+            d_gates = jnp.concatenate([gates_q[s], jnp.zeros((128 - experts, rows_dev), f32)], 0).T
+            d_logits = probs_q[s] * (d_gates - jnp.sum(probs_q[s] * d_gates, -1, keepdims=True))
+            high = d_logits.astype(bf16)
+            low = (d_logits - high.astype(f32)).astype(bf16)
+            part = matmul_tn(x_q[s], high) + matmul_tn(x_q[s], low)
+            for core in range(2):
+                rows = part[core * col_width : (core + 1) * col_width]
+                router_part[core] = rows if s == 0 else router_part[core] + rows
+        router_twin = net.send(router_part.at[1 - net.k], router_got.at[0], (ro_s, ro_r), 0, net.twin)
+        for kind in (0, 1):
+            for j in range(n_rows):
+                keep(kind, j)
+            if kind == 0:
+                router_twin.wait_recv()
+                router_sum[0] = router_part[net.k] + router_got[0]
+                router_x = net.send(router_sum.at[0], router_got.at[1], (ro_s, ro_r), 1, net.x)
+            next(w_steps, None)
+        router_x.wait_recv()
+        router_sum[1] = router_sum[0] + router_got[1]
+        router_y = net.send(router_sum.at[1], router_got.at[2], (ro_s, ro_r), 2, net.y)
+        for load in loads[3:]:
+            load.start()
+        next(y_steps, None)
+        for load in loads[3:]:
+            load.wait()
+        for j in range(n_rows):
+            give(2, j)
+        run_together(y_steps, w_steps)
+        for j in range(n_rows):
+            keep(2, j)
+        for copy in leaves.values():
+            copy.wait_send()
+        for store in stores.values():
+            store.wait()
         for copy in sends:
             copy.wait_recv()
+        router_y.wait_recv()
+        router_out[...] = router_sum[1] + router_got[2]
         total = gain_sums[net.z * ring]
         for i in range(1, ring):
             total = total + gain_sums[net.z * ring + i]
@@ -1553,6 +1904,13 @@
             shape((length, width), f32),
             shape((8, width), f32),
             shape((col_width, in_width), f32),
+            shape((col_width, 128), f32),
+            shape((model, half), f32),
+            shape((model, half), f32),
+            shape((half, model), f32),
+            shape((model, half), bf16),
+            shape((model, half), bf16),
+            shape((half, model), bf16),
         ],
         [
             vmem((length, width), f32),
@@ -1562,206 +1920,40 @@
             vmem((16, width), f32),
             vmem((16, width), f32),
             vmem((chips, 16, width), f32),
+            vmem((length, width), bf16),
+            vmem((n_slots, model), bf16),
+            vmem((n_slots, hidden), bf16),
+            vmem((n_slots, hidden), bf16),
+            vmem((2, width, half), bf16),
+            vmem((1, half, width), bf16),
+            vmem((2, width, half), bf16),
+            vmem((1, half, width), bf16),
+            vmem((2, width, half), f32),
+            vmem((1, half, width), f32),
+            vmem((ring, rows_dev, width), bf16),
+            vmem((ring, rows_dev, 128), f32),
+            vmem((ring, experts, rows_dev), f32),
+            vmem((2, col_width, 128), f32),
+            vmem((3, col_width, 128), f32),
+            vmem((2, col_width, 128), f32),
         ]
         + scatter_scratch(pieces, piece, width, resident=True)
         + scatter_scratch(1, length, width)
         + scatter_columns_scratch(ring, col_width, in_width)
         + pair_sems(n_rows - 1)
         + pair_sems(chips - 1)
-        + pair_sems(1),
+        + pair_sems(1)
+        + pair_sems(3 * n_rows)
+        + [pltpu.SemaphoreType.DMA((11,))]
+        + pair_sems(3)
+        + [pltpu.SemaphoreType.DMA((ring, 3))],
         (
             d_first.reshape(pieces, piece, model), d_proj, normed, parts, part_sum, x, proj, d_resid,
-            gains, gain_part,
+            gains, gain_part, *expert_rows, *router_rows,
         ),
-        in_vmem=(0, 1, 2, 4, 5, 6, 7, 8, 9),
-        out_vmem=(0, 1, 2, 3),
-    )
-
-
-def expert_kernel(
-    info, rows, grads, maps, gate_own, gate_twin, up_own, up_twin, down_own, down_twin, shared, router,
-    d_rows_out, rows_out, slot_rows, d_part, e_act, d_gate, d_up, s_act, d_shared, probs_out, d_gates,
-    w_gate, w_up, w_down, part, sems,
-):
-    tokens, model = rows.shape[1:]
-    n_slots = slot_rows.shape[1]
-    half_hidden = gate_own.shape[1]
-    hidden = 2 * half_hidden
-    pad = shared.shape[1] // 3
-    gate_up, down = slice(0, 2 * pad), slice(2 * pad, 3 * pad)
-    row, own_expert = info[0], info[1]
-    width = model // 4
-    bf16, f32 = jnp.bfloat16, jnp.float32
-    blocks, experts, block_rows = maps.shape[1:]
-
-    @pl.when(pl.program_id(0) == 0)
-    def _():
-        copies = []
-        for j in range(4):
-            flipped = row + (1 - 2 * lax.rem(row, 2)) * (j & 1) + (2 - 4 * lax.div(row, 2)) * (j >> 1)
-            there = pl.ds(pl.multiple_of(flipped * width, width), width)
-            here = pl.ds(j * width, width)
-            for h, sources in enumerate(((gate_own, up_own, down_own), (gate_twin, up_twin, down_twin))):
-                cols = pl.ds(h * half_hidden, half_hidden)
-                number = 6 * j + 3 * h
-                copies += [
-                    pltpu.make_async_copy(
-                        sources[0].at[there, :], w_gate.at[here, cols], sems.at[number]
-                    ),
-                    pltpu.make_async_copy(
-                        sources[1].at[there, :], w_up.at[here, cols], sems.at[number + 1]
-                    ),
-                    pltpu.make_async_copy(
-                        sources[2].at[:, there], w_down.at[cols, here], sems.at[number + 2]
-                    ),
-                ]
-        for copy in copies:
-            copy.start()
-        for copy in copies:
-            copy.wait()
-
-    x = rows[0]
-    slot_row, chosen = [], []
-    for b in range(blocks):
-        own_map = jnp.where(
-            lax.broadcasted_iota(jnp.int32, (experts, block_rows), 0) == own_expert, maps[0, b], 0.0
-        )
-        own_map = jnp.sum(own_map, 0, keepdims=True)
-        slot_row.append(jnp.where(own_map >= 0, own_map + b * (n_slots // blocks), -1.0))
-        filled = jnp.concatenate([maps[0, b], jnp.full((128 - experts, block_rows), -1.0, f32)], 0)
-        chosen.append(filled.T)
-    slot_row, chosen = jnp.concatenate(slot_row, 1), jnp.concatenate(chosen, 0)
-    mine_hot = (lax.broadcasted_iota(jnp.int32, (1, 128), 1) == own_expert).astype(f32)
-    pick = (
-        lax.broadcasted_iota(jnp.int32, (n_slots, tokens), 0).astype(f32) == slot_row
-    ).astype(f32)
-    pick_b = pick.astype(bf16)
-    pick_t = pick.T.astype(bf16)
-    exact = lambda a, b, dims: lax.dot_general(
-        a, b, (dims, ((), ())), precision=PRECISE, preferred_element_type=f32
-    )
-
-    logits = matmul(x, router[...])
-    logits = jnp.where(chosen >= 0, logits, NEG_LARGE)
-    logits = jnp.exp(logits - jnp.max(logits, -1, keepdims=True))
-    probs = logits / jnp.sum(logits, -1, keepdims=True)
-    probs_out[0] = probs
-    my_gate = jnp.sum(probs * mine_hot, -1, keepdims=True)
-    slot_gate = exact(pick, jnp.broadcast_to(my_gate, (tokens, 128)), ((1,), (0,)))[:, :1]
-    s_gate = matmul(x, shared[:, :pad])
-    s_up = matmul(x, shared[:, pad : 2 * pad])
-    through = matmul(grads[0], shared[:, down])
-    s_silu, s_slope = silu_parts(s_gate)
-    s_act[0] = (s_silu * s_up).astype(bf16)
-    d_shared[0, :, :pad] = (through * s_up * s_slope).astype(bf16)
-    d_shared[0, :, pad:] = (through * s_silu).astype(bf16)
-
-    tile = 512
-    for t in range(model // tile):
-        at = slice(t * tile, (t + 1) * tile)
-        slot_rows[0, :, at] = matmul(pick_b, rows[0, :, at]).astype(bf16)
-        picked = matmul(pick_b, grads[0, :, at])
-        part[:, at] = picked.astype(bf16)
-        d_part[0, :, at] = (picked * slot_gate).astype(bf16)
-
-    step = 256
-
-    def hidden_tile(t, total):
-        at = pl.ds(pl.multiple_of(t * step, step), step)
-        e_gate = matmul(slot_rows[0], w_gate[:, at])
-        e_up = matmul(slot_rows[0], w_up[:, at])
-        through = matmul_nt(part[...], w_down[at, :])
-        e_silu, e_slope = silu_parts(e_gate)
-        act = e_silu * e_up
-        d_act = through * slot_gate
-        e_act[0, :, at] = act.astype(bf16)
-        d_gate[0, :, at] = (d_act * e_up * e_slope).astype(bf16)
-        d_up[0, :, at] = (d_act * e_silu).astype(bf16)
-        return total + jnp.sum(act * through, -1, keepdims=True)
-
-    d_gate_slot = lax.fori_loop(0, hidden // step, hidden_tile, jnp.zeros((n_slots, 1), f32))
-    d_gates[0] = exact(jnp.broadcast_to(d_gate_slot, (n_slots, 128)), pick, ((0,), (0,)))[:1]
-
-    @pl.loop(0, model // tile)
-    def _(t):
-        at = pl.ds(pl.multiple_of(t * tile, tile), tile)
-        d_slot = matmul_nt(d_gate[0], w_gate[at, :]) + matmul_nt(d_up[0], w_up[at, :])
-        d_rows_out[0, :, at] = (
-            matmul(pick_t, d_slot.astype(bf16)) + matmul_nt(d_shared[0], shared[at, gate_up])
-        ).astype(bf16)
-        out = (matmul(e_act[0], w_down[:, at]) * slot_gate).astype(bf16)
-        rows_out[0, :, at] = (
-            matmul(pick_t, out) + matmul_nt(s_act[0], shared[at, down])
-        ).astype(bf16)
-
-
-def expert_chunks(info, rows, grads, maps, experts_w, shared, router, slots):
-    chunks, tokens, model = rows.shape
-    half_hidden = experts_w[0].shape[1]
-    hidden = 2 * half_hidden
-    pad = shared.shape[1] // 3
-    by_chunk = lambda *dims: pl.BlockSpec((1, *dims), lambda i, s: (i, 0, 0))
-    once = lambda *dims: pl.BlockSpec(dims, lambda i, s: (0, 0), pipeline_mode=pl.Buffered(1))
-    anywhere = pl.BlockSpec(memory_space=pl.ANY)
-    single = lambda *dims: pl.BlockSpec(
-        (1, *dims), lambda i, s: (i, 0, 0), pipeline_mode=pl.Buffered(1)
-    )
-    bf16, f32 = jnp.bfloat16, jnp.float32
-    shape = lambda dtype, *dims: jax.ShapeDtypeStruct((chunks, *dims), dtype)
-    return pl.pallas_call(
-        expert_kernel,
-        grid_spec=pltpu.PrefetchScalarGridSpec(
-            num_scalar_prefetch=1,
-            grid=(chunks,),
-            in_specs=[
-                by_chunk(tokens, model),
-                by_chunk(tokens, model),
-                pl.BlockSpec((1, *maps.shape[1:]), lambda i, s: (i, 0, 0, 0)),
-            ]
-            + [anywhere] * 6
-            + [once(*shared.shape), once(*router.shape)],
-            out_specs=[
-                single(tokens, model),
-                single(tokens, model),
-                single(slots, model),
-                single(slots, model),
-                single(slots, hidden),
-                single(slots, hidden),
-                single(slots, hidden),
-                single(tokens, pad),
-                single(tokens, 2 * pad),
-                single(tokens, 128),
-                pl.BlockSpec((1, 1, tokens), lambda i, s: (s[2 + i], 0, 0)),
-            ],
-            scratch_shapes=[
-                pltpu.VMEM((model, hidden), bf16),
-                pltpu.VMEM((model, hidden), bf16),
-                pltpu.VMEM((hidden, model), bf16),
-                pltpu.VMEM((slots, model), bf16),
-                pltpu.SemaphoreType.DMA((24,)),
-            ],
-        ),
-        out_shape=[
-            shape(bf16, tokens, model),
-            shape(bf16, tokens, model),
-            shape(bf16, slots, model),
-            shape(bf16, slots, model),
-            shape(bf16, slots, hidden),
-            shape(bf16, slots, hidden),
-            shape(bf16, slots, hidden),
-            shape(bf16, tokens, pad),
-            shape(bf16, tokens, 2 * pad),
-            shape(f32, tokens, 128),
-            shape(f32, 1, tokens),
-        ],
-        compiler_params=pltpu.CompilerParams(vmem_limit_bytes=63 * MIB),
-        cost_estimate=pl.CostEstimate(
-            flops=chunks * 2 * tokens * model * (4 * hidden + 6 * pad),
-            bytes_accessed=40 * MIB,
-            transcendentals=chunks * slots * hidden,
-        ),
-        name="expert_chunks",
-    )(info, rows, grads, maps, *experts_w, shared, router)
+        in_vmem=(0, 1, 2, 4, 5, 7, 8, 9),
+        out_vmem=(0, 1, 2, 3, 4),
+    )
 
 
 def add_bf16(left, right):
@@ -1937,59 +2129,31 @@
 
     (
         token_input, first_normed, weights_in, small, queries, kv_all, attn_f32, log_total,
-        weights_out_t, grad_rows, rows_all, slot_maps, shared_w, attn_proj, gains,
+        weights_out_t, grad_rows, second_normed, slot_maps, shared_w, attn_proj, gains,
     ) = first_phase(
         n_rows, net.n_cols, layer_in[0], cotangent[0],
         jnp.concatenate([w_query, key_matrix, value_matrix], 1), small, w_out.T, packed, slot_map,
         tables,
     )
-    info = jnp.stack([r, r * ring + z] + [net.chip(hops) for hops in range(ring)]).astype(jnp.int32)
-    (
-        d_rows, out_rows, slot_rows, d_part, e_act, d_e_gate, d_e_up, s_act, d_shared, gate_probs,
-        d_gate_mine,
-    ) = expert_chunks(
-        info, rows_all, grad_rows, slot_maps, experts_w, shared_w, small, n_rows * slots
-    )
-
     joined = lambda whole: whole.reshape(-1, whole.shape[-1])
     attn_proj = joined(attn_proj)
-    d_attn, d_resid, gain_part, d_gate_all, g_expert_gate, g_expert_up, g_expert_down = token_sum(
-        n_rows, net.n_cols, d_rows, d_gate_mine.reshape(ring, length),
-        [joined(part) for part in (slot_rows, d_part, e_act, d_e_gate, d_e_up)],
-        gate_probs[0], small, (token_input, attn_proj, grad_rows[0]), gains,
-    )[:7]
-
-    grad_router = jnp.zeros((row_width, experts), jnp.float32)
-    for hops in range(ring):
-        probs = gate_probs[hops][:, :experts]
-        d_gates = index(d_gate_all, net.chip(hops), 1, False).T
-        d_logits = probs * (d_gates - jnp.sum(probs * d_gates, -1, keepdims=True))
-        quarter = lax.dynamic_slice(rows_all[hops], (r * rows_dev, 0), (rows_dev, model_width))
-        quarter = lax.switch(
-            r ^ z,
-            [
-                lambda rows, j=j: rows[:, j * row_width : (j + 1) * row_width]
-                for j in range(n_rows)
-            ],
-            quarter,
-        )
-        d_quarter = lax.dynamic_slice_in_dim(d_logits, r * rows_dev, rows_dev, 0)
-        high, low = split_terms(d_quarter)
-        both = matmul_tn(quarter, jnp.concatenate([high, low], 1))
-        grad_router = grad_router + both[:, :experts] + both[:, experts:]
-    grad_router = grad_router.reshape(2, col_width, experts)
-    g_router = index(grad_router, k, 0, False) + net.sibling(index(grad_router, 1 - k, 0, False))
-    g_router = g_router + net.along_x(g_router)
-    g_router = g_router + net.along_y(g_router)
-
-    d_projected, d_first, part_sum, g_out = attention_back(
-        n_rows, net.n_cols, d_attn, weights_out_t, weights_in, queries, kv_all, attn_f32, log_total,
-        tables, out_rows,
-    )
-    layer_out, grad_in, gain_grads, g_in = last_phase(
+    (
+        d_block, rows_all, out_rows, slot_rows, d_part, e_act, d_e_gate, d_e_up, s_act, d_shared,
+        gate_probs, d_gate_all,
+    ) = experts_phase(
+        n_rows, net.n_cols, second_normed, grad_rows, slot_maps, experts_w, shared_w, small, slots
+    )
+    d_projected, d_first, part_sum, g_out, d_resid, gain_part = attention_back(
+        n_rows, net.n_cols, d_block, index(d_gate_all, z, 1, False)[:, 0], gate_probs[0], small,
+        (token_input, attn_proj, grad_rows), gains, weights_out_t, weights_in, queries, kv_all,
+        attn_f32, log_total, tables, out_rows,
+    )
+    layer_out, grad_in, gain_grads, g_in, g_router, *g_experts = last_phase(
         n_rows, net.n_cols, d_first, d_projected, first_normed, out_rows, part_sum, token_input,
         attn_proj, d_resid, gains, gain_part,
-    )
+        [joined(part) for part in (slot_rows, d_part, e_act, d_e_gate, d_e_up)],
+        (rows_all, gate_probs, d_gate_all),
+    )[:8]
     gain_grads = index(gain_grads[:2].reshape(2, 2, col_width), k, 1, False)
 
     column_parts = lambda whole: whole.astype(jnp.bfloat16).reshape(ring, 2, col_width, -1)
@@ -2020,13 +2184,13 @@
         g_in[:, q_width + kv_width :],
         g_out.T,
         gain_grads[1],
-        g_router,
+        g_router[:, :experts],
         shared_cols(0),
         shared_cols(1),
         shared_cols(2).T,
-        g_expert_gate[None],
-        g_expert_up[None],
-        g_expert_down[None],
+        g_experts[0][None],
+        g_experts[1][None],
+        g_experts[2][None],
     )
 
 

time: 926 us -> 795 us (0.86)
  Pallas kernels: 794 us -> 704 us
  local copies, waits for them, and re-layouts: 70 us -> 49.1 us
  starting transfers between devices: 14.4 us -> 4.69 us
    pallas_call x1 -> x0, Pallas kernels: 130 us -> none  [expert_chunks(): pl.pallas_call(expert_kernel, grid_spec=pltpu.PrefetchScalarGridSpec(num_...]
    pallas_call x4, Pallas kernels: 664 us -> 704 us  [remote_call(): pl.pallas_call(kernel, out_shape=out_shape, in_specs=[vmem if i in in_vme...]
    ppermute x10 -> x7, starting transfers between devices: 14.4 us -> 4.69 us  [move(): return lax.ppermute(values, ('rows', 'cols'), pairs)]
    unnamed x55 -> x51, local copies, waits for them, and re-layouts: 28.9 us -> 29.9 us
  transfers between devices with their start and end apart: 10 -> 7, of which waited for: 0 -> 1; matrix products, arithmetic and copies ran while one was open for 5% -> 3% of each run, Pallas kernels for 59% -> 63%
where the time goes in v4:
time: 795 us; the launch traced here: 785 us
  Pallas kernels  704 us (89%)
  local copies, waits for them, and re-layouts  49.1 us (6%)
  matrix products  14.1 us (2%)
    pallas_call x4, Pallas kernels, remote_call(): pl.pallas_call(kernel, out_shape=out_shape, in_specs=[vmem if i in in_vme...  704 us
    unnamed x51, local copies, waits for them, and re-layouts  29.9 us
  transfers between devices with their start and end apart: 7, of which 1 were waited for; matrix products, arithmetic and copies ran while one was open for 3% of the time, Pallas kernels for 63%

profile of v4, /device:TPU:18, one launch (start us, length us, event | category | flops | bytes accessed | tf_op | source)
XLA Modules:
  0.0 784.6 jit_solution(2486609610898053315)
XLA Ops:
  10.2 1.4 fusion.8.packed_in
  11.6 217.2 %first_phase.1 = (bf16[512,2560]{1,0:T(8,128)(2,1)}, bf16[512,2560]{1,0:T(8,128)(2,1)}, bf16[2560,896]{1,0:T(8,128)(2,1)}, bf16[2560,128]{1,0:T(8,128)(2,1)}, bf...) custom-call(bf16[512,640]{1,0:T(8,128)(2,1)} %bitcast.114, ...), custom_call_target="tpu_custom_call" | custom-call | tf_op jit(solution)/shard_map/first_phase/pallas_call | solution.py:849
  228.9 212.4 %experts_phase.1 = (bf16[512,640]{1,0:T(8,128)(2,1)}, bf16[4,512,2560]{2,1,0:T(8,128)(2,1)}, bf16[4,512,2560]{2,1,0:T(8,128)(2,1)}, bf16[4,256,2560]{2,1,0:T(8,1...) custom-call(bf16[512,2560]{1,0:T(8,128)(2,1)} %get-tuple-element.56., ...), custom_call_target="tpu_custom_call" | custom-call | tf_op jit(solution)/shard_map/experts_phase/pallas_call | solution.py:849
  441.2 7.3 fusion.5
  449.1 5.9 bitcast_convert_fusion
  455.0 1.4 fusion.10
  457.8 2.9 collective-permute-done.3
  460.8 2.1 fusion
  464.6 2.3 collective-permute-start.5
  468.1 1.7 slice_bitcast_fusion.probs
  469.8 152.2 %attention_back.1 = (bf16[512,896]{1,0:T(8,128)(2,1)}, bf16[512,2560]{1,0:T(8,128)(2,1)}, bf16[512,640]{1,0:T(8,128)(2,1)}, f32[320,640]{1,0:T(8,128)}, f32[512,640]{1,0:T(8,128)}, /*index=5*/f32[8,640]{1,0:T(8,128)}) custom-call(bf16[512,640]{1,0:T(8,128)(2,1)} %get-tuple-element.61.block, f32[16,512]{1,0:T(8,128)} %bitcast.119, ...), custom_call_target="tpu_custom_call" | custom-call | tf_op jit(solution)/shard_map/attention_back/pallas_call | solution.py:849
  621.9 122.8 %last_phase.1 = (bf16[512,640]{1,0:T(8,128)(2,1)}, f32[512,640]{1,0:T(8,128)}, f32[8,640]{1,0:T(8,128)}, f32[320,896]{1,0:T(8,128)}, f32[320,128]{1,0:T(8,128)},...) custom-call(bf16[2,256,2560]{2,1,0:T(8,128)(2,1)} %bitcast.108, ...), custom_call_target="tpu_custom_call" | custom-call | tf_op jit(solution)/shard_map/last_phase/pallas_call | solution.py:849
  744.7 2.1 slice.38
  747.6 1.6 copy.96
  749.8 1.7 fusion.23
  752.2 1.3 copy.93
  753.6 1.3 copy.94
  754.9 2.1 copy.95
  758.1 1.7 fusion.22
  759.9 2.7 copy.97
  765.1 2.0 copy.121
  769.1 7.3 copy.124
  776.4 3.9 copy.125
  781.0 3.2 copy.126
  (86 shorter events, 22.7 us)
Async XLA Ops:
  0.6 2.3 copy-start.6
  0.7 2.9 copy-start.7
  0.7 228.2 %collective-permute-start = (bf16[2560,768]{1,0:T(8,128)(2,1)}, bf16[2560,768]{1,0:T(8,128)(2,1)}, u32[]{:S(2)}, u32[]{:S(2)}) collective-permute-start(bf16[2560,768]{1,0:T(8,128)(2,1)} %bitcast.99), channel_id=1, source_target_pairs={{0,1},{1,0},{2,3},{3,2},{4,5},{5,4},{6,7},{7,6},{8,9},{9,8},{10,11... | collective-permute-start | bytes 11796488 | tf_op jit(solution)/shard_map/ppermute | solution.py:1979
  0.8 228.1 %collective-permute-start.1 = (bf16[2560,768]{1,0:T(8,128)(2,1)}, bf16[2560,768]{1,0:T(8,128)(2,1)}, u32[]{:S(2)}, u32[]{:S(2)}) collective-permute-start(bf16[2560,768]{1,0:T(8,128)(2,1)} %bitcast.101), channel_id=1, source_target_pairs={{0,1},{1,0},{2,3},{3,2},{4,5},{5,4},{6,7},{7,6},{8,9},{9,8},{10,11... | collective-permute-start | bytes 11796488 | tf_op jit(solution)/shard_map/ppermute | solution.py:1979
  1.2 227.6 %collective-permute-start.2 = (bf16[768,2560]{1,0:T(8,128)(2,1)}, bf16[768,2560]{1,0:T(8,128)(2,1)}, u32[]{:S(2)}, u32[]{:S(2)}) collective-permute-start(bf16[768,2560]{1,0:T(8,128)(2,1)} %bitcast.103), channel_id=1, source_target_pairs={{0,1},{1,0},{2,3},{3,2},{4,5},{5,4},{6,7},{7,6},{8,9},{9,8},{10,11... | collective-permute-start | bytes 11796488 | tf_op jit(solution)/shard_map/ppermute | solution.py:1979
  3.0 2.6 copy-start.11
  3.0 2.8 copy-start.12
  3.6 4.9 copy-start.8
  3.6 4.9 copy-start.9
  3.9 4.5 copy-start.10
  441.2 7.3 copy-start
  441.2 7.8 %copy-start.13 = (bf16[4,512,512]{2,1,0:T(8,128)(2,1)S(1)}, bf16[4,512,512]{2,1,0:T(8,128)(2,1)}, u32[]{:S(2)}) copy-start(bf16[4,512,512]{2,1,0:T(8,128)(2,1)} %get-tuple-element.92) | copy-start | bytes 6291460
  448.5 6.5 copy-start.1
  456.5 4.3 collective-permute-start.3
  464.1 288.1 %collective-permute-start.4 = (bf16[320,768]{1,0:T(8,128)(2,1)}, bf16[320,768]{1,0:T(8,128)(2,1)}, u32[]{:S(2)}, u32[]{:S(2)}) collective-permute-start(bf16[320,768]{1,0:T(8,128)(2,1)} %get-tuple-element.164), channel_id=1, source_target_pairs={{0,2},{1,3},{2,4},{3,5},{4,6},{5,7},{6,0},{7,1},{8,10},{9,11},{10,... | collective-permute-start | bytes 1474568 | tf_op jit(solution)/shard_map/ppermute | solution.py:1979
  464.6 288.9 %collective-permute-start.5 = (bf16[320,768]{1,0:T(8,128)(2,1)}, bf16[320,768]{1,0:T(8,128)(2,1)}, u32[]{:S(2)}, u32[]{:S(2)}) collective-permute-start(bf16[320,768]{1,0:T(8,128)(2,1)} %get-tuple-element.163), channel_id=1, source_target_pairs={{0,4},{1,5},{2,6},{3,7},{4,0},{5,1},{6,2},{7,3},{8,12},{9,13},{10,... | collective-permute-start | bytes 1474568 | tf_op jit(solution)/shard_map/ppermute | solution.py:1979
  467.0 287.9 %collective-permute-start.6 = (bf16[320,768]{1,0:T(8,128)(2,1)}, bf16[320,768]{1,0:T(8,128)(2,1)}, u32[]{:S(2)}, u32[]{:S(2)}) collective-permute-start(bf16[320,768]{1,0:T(8,128)(2,1)} %get-tuple-element.162), channel_id=1, source_target_pairs={{0,6},{1,7},{2,0},{3,1},{4,2},{5,3},{6,4},{7,5},{8,14},{9,15},{10,... | collective-permute-start | bytes 1474568 | tf_op jit(solution)/shard_map/ppermute | solution.py:1979
  759.9 2.7 copy-start.2
  763.8 3.3 copy-start.4
  763.8 4.3 copy-start.5
  767.1 9.2 %slice-start.2 = ((s8[7864320]{0:T(1024)(128)(4,1)}), s8[4194304]{0:T(1024)(128)(4,1)S(1)}, s32[]{:S(2)}) async-start(s8[7864320]{0:T(1024)(128)(4,1)} %bitcast.88), calls=%async_computation.2 | async-start | bytes 8388608
  769.1 7.3 slice-start.3
  769.1 11.2 %slice-start = ((s8[7864320]{0:T(1024)(128)(4,1)}), s8[4194304]{0:T(1024)(128)(4,1)S(1)}, s32[]{:S(2)}) async-start(s8[7864320]{0:T(1024)(128)(4,1)} %bitcast.85), calls=%async_computation | async-start | bytes 8388608
  776.4 4.6 slice-start.1
  (1 other events, 1.1 us)

commit v5 on v4

--- a/solution.py
+++ b/solution.py
@@ -904,7 +904,7 @@
     def kernel(
         x_in, g_in, w_in, small_in, wo_in, packed_in, map_in, cosine, sine,
         x_out, normed_out, w_out, small_out, q, kv_out, out, lse, wo_out, g_out, second, map_out,
-        shared_out, sum_out, gains_out,
+        shared_out, sum_out, gains_out, scale_out,
         x, normed, w, small_all, kv, wo, proj, proj_sum, result, projected, top, total, acc,
         *sems,
     ):
@@ -961,6 +961,7 @@
             values = x[0, at, :].astype(f32)
             inverse = lax.rsqrt(jnp.mean(values * values, -1, keepdims=True) + NORM_EPS)
             normed[at, :] = (values * inverse * first_gain).astype(bf16)
+            scale_out[at, :] = jnp.broadcast_to(inverse, (64, 128))
 
         save(normed, normed_out)
         next(wo_steps)
@@ -1102,6 +1103,7 @@
             shape((model, packed.shape[2]), bf16),
             shape((pieces, piece, model), bf16),
             shape((8, model), f32),
+            shape((length, 128), f32),
         ],
         [
             vmem((1, length, model), bf16),
@@ -1132,7 +1134,7 @@
         + [pltpu.SemaphoreType.DMA((18,))],
         (block, grads, weights, small, weights_out, packed, slot_map, *tables),
         in_vmem=(7, 8),
-        out_vmem=(4, 6, 7, 10, 14),
+        out_vmem=(4, 6, 7, 10, 14, 15),
     )
 
 
@@ -1460,7 +1462,7 @@
 
 def attention_back(
     n_rows, n_cols, d_block, d_gates, probs, router, token_rows, gains, weights_out, weights_in,
-    queries, kv, heads_out, lse, tables, parts,
+    queries, kv, heads_out, lse, tables, parts, expert_rows,
 ):
     ring = n_cols // 2
     length, model = token_rows[0].shape
@@ -1471,22 +1473,34 @@
     width = model // n_rows
     heads = q_width // HEAD_DIM
     scale = 1.0 / math.sqrt(HEAD_DIM)
+    half = expert_rows[2].shape[1] // 2
+    n_slots = expert_rows[2].shape[0]
     bf16, f32 = jnp.bfloat16, jnp.float32
     shape = jax.ShapeDtypeStruct
 
     def kernel(
         block, gates, probs, router, x_in, proj_in, g_in, gains, wo_in, w_in, q, kv, out, lse, cosine,
-        sine, y_in,
-        d_proj, d_first, y_out, wo_out, d_resid, gain_out,
+        sine, y_in, xr_in, dp_in, act_in, dg_in, du_in,
+        d_proj, d_first, y_out, wo_out, d_resid, gain_out, xr_out, dp_out, act_out, dg_out, du_out,
         second, proj, g, high_ref, low_ref,
-        wo, w, go, delta, dqt, dkv, dkv_own, wo_part, *rest,
+        wo, w, go, delta, dqt, dkv, dkv_own, wo_part, y_hold, y_landed, *rest,
     ):
-        scratch, ring_parts = rest[:9], rest[9:13]
-        kv_parts, wo_parts, gs, gr, local = rest[13:20], rest[20:27], rest[27], rest[28], rest[29]
+        scratch, kv_parts, wo_parts = rest[:9], rest[9:16], rest[16:23]
+        gs, gr, yr_s, yr_r, es, er, local = rest[23:]
         net = Links(n_rows, n_cols)
         net.greet([net.x, net.y, net.up, net.down, net.twin])
         gather = gather_square(net, block, second, (gs, gr), local.at[1], 1)
         next(gather)
+        others = pl.ds(half, half)
+        twins = [
+            net.send(source, target, (es, er), number, net.twin)
+            for number, (source, target) in enumerate(
+                (
+                    (xr_in, xr_out), (dg_in.at[:, others], dg_out), (du_in.at[:, others], du_out),
+                    (act_in.at[:, others], act_out), (dp_in, dp_out),
+                )
+            )
+        ]
         x, d_attn = d_first, proj
         loads = [
             pltpu.make_async_copy(a, b, local.at[2 + i])
@@ -1507,10 +1521,18 @@
         low_ref[...] = (d_logits - high.astype(f32)).astype(bf16)
         for load in loads:
             load.wait()
-        copies = []
-        y_steps = scatter_square(
-            net, y_in, scratch, list(range(1, ring)), ring_finish(net, ring_parts, None, copies)
-        )
+
+        hop = []
+
+        def keep_sum(s, upper, lower):
+            half = length // 2
+            target = y_hold if s == 1 else y_out.at[s - 1]
+            add_slabs(target.at[pl.ds(0, half), :], upper)
+            add_slabs(target.at[pl.ds(half, half), :], lower)
+            if s == 1:
+                hop.append(net.send(y_hold, y_landed, (yr_s, yr_r), 0, net.up))
+
+        y_steps = scatter_square(net, y_in, scratch, list(range(1, ring)), keep_sum)
         by_place = lambda ref: lambda hops, core: ref.at[
             pl.ds((net.place(hops) * 2 + core) * col_width, col_width), :
         ]
@@ -1575,17 +1597,26 @@
             dkv[number, :, HEAD_DIM:] = d_value.astype(bf16)
 
         one_block(net.c, True)
-
-        @pl.loop(0, net.c)
+        middle = lax.div(net.c, 2)
+
+        @pl.loop(0, middle)
         def _(number):
             one_block(number, False)
 
+        next(y_steps)
+        next(y_steps)
+        next(wo_steps)
+
+        @pl.loop(middle, net.c)
+        def _(number):
+            one_block(number, False)
+
+        next(wo_steps)
         kv_steps = scatter_columns(
             net, lambda hops, core: dkv.at[2 * net.chip(hops) + core], dkv_own, kv_parts
         )
         next(kv_steps)
         next(kv_steps)
-        next(wo_steps)
         next(y_steps)
 
         def turned_back(values):
@@ -1595,11 +1626,11 @@
             columns = slice(head * HEAD_DIM, (head + 1) * HEAD_DIM)
             d_proj[:, columns] = turned_back((dqt[head] * scale).T)
         next(kv_steps)
-        next(wo_steps)
         next(y_steps)
         next(kv_steps)
-        next(y_steps)
+        next(wo_steps)
         run_together(kv_steps)
+        next(y_steps, None)
         d_proj[:, q_width : q_width + HEAD_DIM] = turned_back(dkv_own[:, :HEAD_DIM])
         d_proj[:, q_width + HEAD_DIM :] = dkv_own[:, HEAD_DIM:].astype(bf16)
         w_load.wait()
@@ -1607,8 +1638,10 @@
             at = slice(j * width, (j + 1) * width)
             d_first[:, at] = matmul_nt(d_proj[...], w[at, :]).astype(bf16)
         run_together(y_steps, wo_steps)
-        copies[-1].wait_recv()
-        y_out[...] = ring_parts[0][ring - 2]
+        hop[0].wait_recv()
+        y_out[0] = y_landed[...]
+        for copy in twins:
+            copy.wait_recv()
         net.finish()
 
     vmem = pltpu.VMEM
@@ -1619,10 +1652,15 @@
         [
             shape((length, in_width), bf16),
             shape((length, model), bf16),
-            shape((length, width), bf16),
+            shape((ring - 1, length, width), bf16),
             shape((col_width, q_width), f32),
             shape((length, width), f32),
             shape((8, width), f32),
+            shape((n_slots, model), bf16),
+            shape((n_slots, model), bf16),
+            shape((n_slots, half), bf16),
+            shape((n_slots, half), bf16),
+            shape((n_slots, half), bf16),
         ],
         [
             vmem((1, length, model), bf16),
@@ -1638,16 +1676,19 @@
             vmem((n_cols, length, 2 * HEAD_DIM), bf16),
             vmem((length, 2 * HEAD_DIM), f32),
             vmem((model, q_width), bf16),
+            vmem((length, width), bf16),
+            vmem((length, width), bf16),
         ]
         + scatter_scratch(ring - 1, length, width)
-        + ring_scratch(ring, length, width)
         + scatter_columns_scratch(ring, length, 2 * HEAD_DIM)
         + scatter_columns_scratch(ring, col_width, q_width)
         + pair_sems(7)
+        + pair_sems(1)
+        + pair_sems(5)
         + [pltpu.SemaphoreType.DMA((6,))],
         (
             d_block, d_gates, probs, router, *token_rows, gains, weights_out, weights_in, queries, kv,
-            heads_out, lse, *tables, parts,
+            heads_out, lse, *tables, parts, *expert_rows,
         ),
         in_vmem=(1, 2, 3, 7, 10, 11, 12, 13, 14, 15),
         out_vmem=(0, 1, 2, 3, 4, 5),
@@ -1656,7 +1697,7 @@
 
 def last_phase(
     n_rows, n_cols, d_first, d_proj, normed, parts, part_sum, x, proj, d_resid, gains, gain_part,
-    expert_rows, router_rows,
+    x_scale, expert_rows, twin_rows, router_rows,
 ):
     ring = n_cols // 2
     length, model = d_first.shape
@@ -1675,17 +1716,18 @@
     rows_dev = length // n_rows
 
     def kernel(
-        d_first, d_proj, normed, y_in, y_sum, x, proj_in, d_resid, gains, gain_two,
-        xr_in, dp_in, act_in, dg_in, du_in, rows_in, probs_in, gates_in,
-        layer_out, grad_in, gain_out, w_out, router_out, out_g, out_u, out_d, land_g, land_u, land_d,
-        d_own, w_part, moment, moments, gain_own, gain_twin, gain_sums, proj,
-        xr, dg, du, leave_a, leave_b, landed_a, landed_b, full_a, full_b,
-        x_q, probs_q, gates_q, router_part, router_got, router_sum, *rest,
+        d_first, d_proj, normed, y_in, y_sum, x_in, proj_in, d_resid, gains, gain_two, x_scale,
+        xr_in, dp_in, act_in, dg_in, du_in, xr_twin, dp_twin, act_twin, dg_twin, du_twin,
+        rows_in, probs_in, gates_in,
+        layer_out, grad_in, gain_out, w_out, router_out, out_g, out_u, out_d,
+        d_own, w_part, moment, moments, gain_own, gain_twin, gain_sums, proj, x,
+        xr, dg, du, full_a, full_b,
+        x_q, probs_q, gates_q, router_part, router_got, router_sum, y_landed, y_leaving, *rest,
     ):
         scratch, y_scratch = rest[:9], rest[9:18]
         w_parts = rest[18:25]
-        mo_s, mo_r, ga_s, ga_r, gt_s, gt_r, es, er, sem, ro_s, ro_r, router_sems = rest[25:]
-        leaving, landed, full = (leave_a, leave_b), (landed_a, landed_b), (full_a, full_b)
+        mo_s, mo_r, ga_s, ga_r, gt_s, gt_r, sem, ro_s, ro_r, router_sems, yr_s, yr_r = rest[25:]
+        full = (full_a, full_b)
         net = Links(n_rows, n_cols)
         others = net.spread_partners()
         net.greet([device for _, _, device in others] + [net.twin])
@@ -1695,12 +1737,30 @@
             add_slabs(d_own.at[at(0), :], upper)
             add_slabs(d_own.at[at(1), :], lower)
 
+        ring_copies = []
+
+        def pass_on(turn):
+            if turn == 1:
+                before = part_reader(y_sum, 0)
+            else:
+                ring_copies[turn - 2].wait_recv()
+                before = part_reader(y_landed, turn - 2)
+            add_slabs(y_leaving.at[turn - 1], [part_reader(y_sum, turn), before])
+            ring_copies.append(
+                net.send(
+                    y_leaving.at[turn - 1], y_landed.at[turn - 1], (yr_s, yr_r), turn - 1, net.up
+                )
+            )
+
+        pass_on(1)
+
         def finish_out(s, upper, lower):
+            ring_copies[-1].wait_recv()
             for part, terms in ((0, upper), (1, lower)):
                 at = pl.ds(part * (length // 2), length // 2)
                 extra = [
-                    part_reader(y_sum.at[at, :]),
-                    part_reader(x.at[at, pl.ds(0, width)]),
+                    part_reader(y_landed.at[ring - 3, at, :]),
+                    part_reader(x.at[at, :]),
                     part_reader(proj.at[at, :]),
                 ]
                 add_slabs(layer_out.at[at, :], terms + extra)
@@ -1709,64 +1769,44 @@
         y_steps = scatter_square(net, y_in, y_scratch, [0], finish_out)
         next(steps)
         next(steps)
+        ours, mine, twins = pl.ds(0, half), pl.ds(0, n_slots), pl.ds(n_slots, n_slots)
         loads = [
             pltpu.make_async_copy(a, b, sem.at[i])
             for i, (a, b) in enumerate(
-                ((xr_in, xr), (dg_in, dg), (du_in, du), (act_in, dg), (dp_in, xr))
+                (
+                    (xr_in, xr.at[mine]), (xr_twin, xr.at[twins]),
+                    (dg_in.at[:, ours], dg.at[mine]), (dg_twin, dg.at[twins]),
+                    (du_in.at[:, ours], du.at[mine]), (du_twin, du.at[twins]),
+                    (act_in.at[:, ours], dg.at[mine]), (act_twin, dg.at[twins]),
+                    (dp_in, xr.at[mine]), (dp_twin, xr.at[twins]),
+                )
             )
         ]
-        for load in loads[:3]:
+        early, late = loads[:6], loads[6:]
+        for load in early:
             load.start()
-        ours, theirs = slice(0, half), slice(half, hidden)
-        given, leaves, stores = [], {}, {}
-
-        def slot_of(kind, j):
-            return kind // 2, j % 2 if kind < 2 else 0
-
-        def tile(kind, j, part):
+        stores = {}
+
+        def make(kind, j):
+            group, slot = kind // 2, j % 2 if kind < 2 else 0
             columns = slice(j * width, (j + 1) * width)
-            if kind < 2:
-                return matmul_tn(xr[:, columns], (dg, du)[kind][:, part])
-            return matmul_tn(dg[:, part], xr[:, columns])
-
-        def land(kind, j, order=False):
-            place = net.flip(j) if order else j
-            at = pl.ds(pl.multiple_of(place * width, width), width)
-            if kind < 2:
-                ref = ((land_g, land_u), (out_g, out_u))[order][kind]
-                return ref.at[at, :]
-            return (land_d, out_d)[order].at[:, at]
-
-        def give(kind, j):
-            group, slot = slot_of(kind, j)
-            if (group, slot) in leaves:
-                leaves[group, slot].wait_send()
-            buffer = leaving[group]
-            buffer[slot] = tile(kind, j, theirs).astype(bf16)
-            copy = net.send(buffer.at[slot], land(kind, j), (es, er), 4 * kind + j, net.twin)
-            net.started.pop()
-            leaves[group, slot] = copy
-            given.append(copy)
-
-        def keep(kind, j):
-            group, slot = slot_of(kind, j)
-            buffer, got = full[group], landed[group]
-            given[4 * kind + j].wait_recv()
-            load = pltpu.make_async_copy(land(kind, j), got.at[slot], sem.at[5 + slot])
-            load.start()
+            at = pl.ds(pl.multiple_of(net.flip(j) * width, width), width)
             if (group, slot) in stores:
                 stores[group, slot].wait()
-            product = tile(kind, j, ours)
-            load.wait()
-            buffer[slot] = product + got[slot].astype(f32)
-            store = pltpu.make_async_copy(
-                buffer.at[slot], land(kind, j, True), sem.at[7 + 2 * group + slot]
-            )
+            if kind < 2:
+                full[group][slot] = matmul_tn(xr[:, columns], (dg, du)[kind][...])
+                target = (out_g, out_u)[kind].at[at, :]
+            else:
+                full[group][slot] = matmul_tn(dg[...], xr[:, columns])
+                target = out_d.at[:, at]
+            store = pltpu.make_async_copy(full[group].at[slot], target, sem.at[12 + 2 * group + slot])
             store.start()
             stores[group, slot] = store
 
         proj_load = pltpu.make_async_copy(proj_in.at[:, pl.ds(0, width)], proj, sem.at[10])
         proj_load.start()
+        x_load = pltpu.make_async_copy(x_in.at[:, pl.ds(0, width)], x, sem.at[11])
+        x_load.start()
         quarter = pl.ds(pl.multiple_of(net.r * rows_dev, rows_dev), rows_dev)
         column = pl.ds(pl.multiple_of(net.place(0) * width, width), width)
         router_loads = []
@@ -1789,23 +1829,24 @@
         w_steps = scatter_columns(net, by_place, w_out, w_parts)
         next(w_steps)
         next(steps)
+        for load in early:
+            load.wait()
+        make(0, 0)
         next(w_steps)
         next(steps)
         next(y_steps)
-        for load in loads[:3]:
-            load.wait()
-        for j in range(2):
-            give(0, j)
+        make(0, 1)
+        pass_on(2)
         run_together(steps)
 
+        x_load.wait()
         gain = gains[0:1, :width]
         slab = 128
         gain_own[...] = jnp.zeros_like(gain_own)
 
         def unit_of(at):
-            values = x[at, :].astype(f32)
-            inverse = lax.rsqrt(jnp.mean(values * values, -1, keepdims=True) + NORM_EPS)
-            return values[:, :width] * inverse, inverse
+            inverse = x_scale[at, :1]
+            return x[at, :].astype(f32) * inverse, inverse
 
         for i in range(length // slab):
             at = slice(i * slab, (i + 1) * slab)
@@ -1820,9 +1861,8 @@
         ]
         gain_own[8:] = gain_two[...]
         twin = net.send(gain_own, gain_twin, (gt_s, gt_r), 0, net.twin)
-        for j in range(2, n_rows):
-            give(0, j)
         next(w_steps)
+        make(0, 2)
         for copy in sends:
             copy.wait_recv()
         whole = moment[...] + moments[0] + moments[1] + moments[2]
@@ -1838,12 +1878,11 @@
             net.send(gain_sums.at[mine], gain_sums.at[mine], (ga_s, ga_r), number, device)
             for number, (hops, bits, device) in enumerate(others)
         ]
-        proj_load.wait()
+        make(0, 3)
+        next(w_steps)
+        make(1, 0)
         next(y_steps)
-        for j in range(n_rows):
-            give(1, j)
-        next(w_steps)
-        next(y_steps)
+        make(1, 1)
         for load in router_loads:
             load.wait()
         for s in range(ring):
@@ -1856,29 +1895,23 @@
                 rows = part[core * col_width : (core + 1) * col_width]
                 router_part[core] = rows if s == 0 else router_part[core] + rows
         router_twin = net.send(router_part.at[1 - net.k], router_got.at[0], (ro_s, ro_r), 0, net.twin)
-        for kind in (0, 1):
-            for j in range(n_rows):
-                keep(kind, j)
-            if kind == 0:
-                router_twin.wait_recv()
-                router_sum[0] = router_part[net.k] + router_got[0]
-                router_x = net.send(router_sum.at[0], router_got.at[1], (ro_s, ro_r), 1, net.x)
-            next(w_steps, None)
+        make(1, 2)
+        router_twin.wait_recv()
+        router_sum[0] = router_part[net.k] + router_got[0]
+        router_x = net.send(router_sum.at[0], router_got.at[1], (ro_s, ro_r), 1, net.x)
+        proj_load.wait()
+        next(y_steps)
+        make(1, 3)
+        for load in late:
+            load.start()
         router_x.wait_recv()
         router_sum[1] = router_sum[0] + router_got[1]
         router_y = net.send(router_sum.at[1], router_got.at[2], (ro_s, ro_r), 2, net.y)
-        for load in loads[3:]:
-            load.start()
-        next(y_steps, None)
-        for load in loads[3:]:
+        run_together(y_steps, w_steps)
+        for load in late:
             load.wait()
         for j in range(n_rows):
-            give(2, j)
-        run_together(y_steps, w_steps)
-        for j in range(n_rows):
-            keep(2, j)
-        for copy in leaves.values():
-            copy.wait_send()
+            make(2, j)
         for store in stores.values():
             store.wait()
         for copy in sends:
@@ -1908,9 +1941,6 @@
             shape((model, half), f32),
             shape((model, half), f32),
             shape((half, model), f32),
-            shape((model, half), bf16),
-            shape((model, half), bf16),
-            shape((half, model), bf16),
         ],
         [
             vmem((length, width), f32),
@@ -1921,13 +1951,10 @@
             vmem((16, width), f32),
             vmem((chips, 16, width), f32),
             vmem((length, width), bf16),
-            vmem((n_slots, model), bf16),
-            vmem((n_slots, hidden), bf16),
-            vmem((n_slots, hidden), bf16),
-            vmem((2, width, half), bf16),
-            vmem((1, half, width), bf16),
-            vmem((2, width, half), bf16),
-            vmem((1, half, width), bf16),
+            vmem((length, width), bf16),
+            vmem((2 * n_slots, model), bf16),
+            vmem((2 * n_slots, half), bf16),
+            vmem((2 * n_slots, half), bf16),
             vmem((2, width, half), f32),
             vmem((1, half, width), f32),
             vmem((ring, rows_dev, width), bf16),
@@ -1936,6 +1963,8 @@
             vmem((2, col_width, 128), f32),
             vmem((3, col_width, 128), f32),
             vmem((2, col_width, 128), f32),
+            vmem((ring - 2, length, width), bf16),
+            vmem((ring - 2, length, width), bf16),
         ]
         + scatter_scratch(pieces, piece, width, resident=True)
         + scatter_scratch(1, length, width)
@@ -1943,15 +1972,15 @@
         + pair_sems(n_rows - 1)
         + pair_sems(chips - 1)
         + pair_sems(1)
-        + pair_sems(3 * n_rows)
-        + [pltpu.SemaphoreType.DMA((11,))]
+        + [pltpu.SemaphoreType.DMA((16,))]
         + pair_sems(3)
-        + [pltpu.SemaphoreType.DMA((ring, 3))],
+        + [pltpu.SemaphoreType.DMA((ring, 3))]
+        + pair_sems(ring - 2),
         (
             d_first.reshape(pieces, piece, model), d_proj, normed, parts, part_sum, x, proj, d_resid,
-            gains, gain_part, *expert_rows, *router_rows,
+            gains, gain_part, x_scale, *expert_rows, *twin_rows, *router_rows,
         ),
-        in_vmem=(0, 1, 2, 4, 5, 7, 8, 9),
+        in_vmem=(0, 1, 2, 4, 7, 8, 9, 10),
         out_vmem=(0, 1, 2, 3, 4),
     )
 
@@ -2130,6 +2159,7 @@
     (
         token_input, first_normed, weights_in, small, queries, kv_all, attn_f32, log_total,
         weights_out_t, grad_rows, second_normed, slot_maps, shared_w, attn_proj, gains,
+        first_scale,
     ) = first_phase(
         n_rows, net.n_cols, layer_in[0], cotangent[0],
         jnp.concatenate([w_query, key_matrix, value_matrix], 1), small, w_out.T, packed, slot_map,
@@ -2143,17 +2173,17 @@
     ) = experts_phase(
         n_rows, net.n_cols, second_normed, grad_rows, slot_maps, experts_w, shared_w, small, slots
     )
-    d_projected, d_first, part_sum, g_out, d_resid, gain_part = attention_back(
+    expert_rows = [joined(part) for part in (slot_rows, d_part, e_act, d_e_gate, d_e_up)]
+    d_projected, d_first, part_sum, g_out, d_resid, gain_part, *twin_rows = attention_back(
         n_rows, net.n_cols, d_block, index(d_gate_all, z, 1, False)[:, 0], gate_probs[0], small,
         (token_input, attn_proj, grad_rows), gains, weights_out_t, weights_in, queries, kv_all,
-        attn_f32, log_total, tables, out_rows,
+        attn_f32, log_total, tables, out_rows, expert_rows,
     )
     layer_out, grad_in, gain_grads, g_in, g_router, *g_experts = last_phase(
         n_rows, net.n_cols, d_first, d_projected, first_normed, out_rows, part_sum, token_input,
-        attn_proj, d_resid, gains, gain_part,
-        [joined(part) for part in (slot_rows, d_part, e_act, d_e_gate, d_e_up)],
-        (rows_all, gate_probs, d_gate_all),
-    )[:8]
+        attn_proj, d_resid, gains, gain_part, first_scale,
+        expert_rows, twin_rows, (rows_all, gate_probs, d_gate_all),
+    )
     gain_grads = index(gain_grads[:2].reshape(2, 2, col_width), k, 1, False)
 
     column_parts = lambda whole: whole.astype(jnp.bfloat16).reshape(ring, 2, col_width, -1)

time: 795 us -> 757 us (0.952)
  Pallas kernels: 704 us -> 667 us
    pallas_call x4, Pallas kernels: 704 us -> 667 us  [remote_call(): pl.pallas_call(kernel, out_shape=out_shape, in_specs=[vmem if i in in_vme...]
  transfers between devices with their start and end apart: 7 -> 7, of which waited for: 1 -> 1; matrix products, arithmetic and copies ran while one was open for 3% -> 3% of each run, Pallas kernels for 63% -> 61%
where the time goes in v5:
time: 757 us; the launch traced here: 747 us
  Pallas kernels  667 us (88%)
  local copies, waits for them, and re-layouts  49.1 us (6%)
  matrix products  14.1 us (2%)
  other arithmetic  7.85 us (1%)
    pallas_call x4, Pallas kernels, remote_call(): pl.pallas_call(kernel, out_shape=out_shape, in_specs=[vmem if i in in_vme...  667 us
    unnamed x51, local copies, waits for them, and re-layouts  29.9 us
  transfers between devices with their start and end apart: 7, of which 1 were waited for; matrix products, arithmetic and copies ran while one was open for 3% of the time, Pallas kernels for 61%

profile of v5, /device:TPU:18, one launch (start us, length us, event | category | flops | bytes accessed | tf_op | source)
XLA Modules:
  0.0 746.8 jit_solution(18345836191841862587)
XLA Ops:
  10.2 1.4 fusion.8.packed_in
  11.6 217.4 %first_phase.1 = (bf16[512,2560]{1,0:T(8,128)(2,1)}, bf16[512,2560]{1,0:T(8,128)(2,1)}, bf16[2560,896]{1,0:T(8,128)(2,1)}, bf16[2560,128]{1,0:T(8,128)(2,1)}, bf...) custom-call(bf16[512,640]{1,0:T(8,128)(2,1)} %bitcast.119, ...), custom_call_target="tpu_custom_call" | custom-call | tf_op jit(solution)/shard_map/first_phase/pallas_call | solution.py:849
  229.0 212.2 %experts_phase.1 = (bf16[512,640]{1,0:T(8,128)(2,1)}, bf16[4,512,2560]{2,1,0:T(8,128)(2,1)}, bf16[4,512,2560]{2,1,0:T(8,128)(2,1)}, bf16[4,256,2560]{2,1,0:T(8,1...) custom-call(bf16[512,2560]{1,0:T(8,128)(2,1)} %get-tuple-element.62., ...), custom_call_target="tpu_custom_call" | custom-call | tf_op jit(solution)/shard_map/experts_phase/pallas_call | solution.py:849
  441.3 7.3 fusion.5
  449.1 5.9 bitcast_convert_fusion
  455.1 1.4 fusion.10
  457.9 2.9 collective-permute-done.3
  460.8 2.1 fusion
  464.6 2.4 collective-permute-start.5
  468.1 1.7 slice_bitcast_fusion.probs
  469.8 127.3 %attention_back.1 = (bf16[512,896]{1,0:T(8,128)(2,1)}, bf16[512,2560]{1,0:T(8,128)(2,1)}, bf16[3,512,640]{2,1,0:T(8,128)(2,1)}, f32[320,640]{1,0:T(8,128)}, f32[...) custom-call(bf16[512,640]{1,0:T(8,128)(2,1)} %get-tuple-element.67.b, ...), custom_call_target="tpu_custom_call" | custom-call | tf_op jit(solution)/shard_map/attention_back/pallas_call | solution.py:849
  597.1 109.9 %last_phase.1 = (bf16[512,640]{1,0:T(8,128)(2,1)}, f32[512,640]{1,0:T(8,128)}, f32[8,640]{1,0:T(8,128)}, f32[320,896]{1,0:T(8,128)}, f32[320,128]{1,0:T(8,128)},...) custom-call(bf16[2,256,2560]{2,1,0:T(8,128)(2,1)} %bitcast.113, ...), custom_call_target="tpu_custom_call" | custom-call | tf_op jit(solution)/shard_map/last_phase/pallas_call | solution.py:849
  707.0 2.1 slice.38
  709.9 1.6 copy.96
  712.1 1.7 fusion.23
  714.5 1.3 copy.93
  715.8 1.3 copy.94
  717.2 2.1 copy.95
  720.4 1.7 fusion.22
  722.1 2.7 copy.97
  727.4 2.0 copy.121
  731.3 7.3 copy.124
  738.6 3.9 copy.125
  743.2 3.2 copy.126
  (86 shorter events, 22.6 us)
Async XLA Ops:
  0.6 2.3 copy-start.6
  0.7 2.9 copy-start.7
  0.7 228.3 %collective-permute-start = (bf16[2560,768]{1,0:T(8,128)(2,1)}, bf16[2560,768]{1,0:T(8,128)(2,1)}, u32[]{:S(2)}, u32[]{:S(2)}) collective-permute-start(bf16[2560,768]{1,0:T(8,128)(2,1)} %bitcast.107), channel_id=1, source_target_pairs={{0,1},{1,0},{2,3},{3,2},{4,5},{5,4},{6,7},{7,6},{8,9},{9,8},{10,11... | collective-permute-start | bytes 11796488 | tf_op jit(solution)/shard_map/ppermute | solution.py:2008
  0.8 228.3 %collective-permute-start.1 = (bf16[2560,768]{1,0:T(8,128)(2,1)}, bf16[2560,768]{1,0:T(8,128)(2,1)}, u32[]{:S(2)}, u32[]{:S(2)}) collective-permute-start(bf16[2560,768]{1,0:T(8,128)(2,1)} %bitcast.109), channel_id=1, source_target_pairs={{0,1},{1,0},{2,3},{3,2},{4,5},{5,4},{6,7},{7,6},{8,9},{9,8},{10,11... | collective-permute-start | bytes 11796488 | tf_op jit(solution)/shard_map/ppermute | solution.py:2008
  1.2 227.8 %collective-permute-start.2 = (bf16[768,2560]{1,0:T(8,128)(2,1)}, bf16[768,2560]{1,0:T(8,128)(2,1)}, u32[]{:S(2)}, u32[]{:S(2)}) collective-permute-start(bf16[768,2560]{1,0:T(8,128)(2,1)} %bitcast.111), channel_id=1, source_target_pairs={{0,1},{1,0},{2,3},{3,2},{4,5},{5,4},{6,7},{7,6},{8,9},{9,8},{10,11... | collective-permute-start | bytes 11796488 | tf_op jit(solution)/shard_map/ppermute | solution.py:2008
  3.0 2.6 copy-start.11
  3.0 2.8 copy-start.12
  3.6 4.9 copy-start.8
  3.6 4.9 copy-start.9
  3.9 4.5 copy-start.10
  441.2 7.3 copy-start
  441.2 7.8 %copy-start.13 = (bf16[4,512,512]{2,1,0:T(8,128)(2,1)S(1)}, bf16[4,512,512]{2,1,0:T(8,128)(2,1)}, u32[]{:S(2)}) copy-start(bf16[4,512,512]{2,1,0:T(8,128)(2,1)} %get-tuple-element.104) | copy-start | bytes 6291460
  448.6 6.5 copy-start.1
  456.5 4.3 collective-permute-start.3
  464.1 250.4 %collective-permute-start.4 = (bf16[320,768]{1,0:T(8,128)(2,1)}, bf16[320,768]{1,0:T(8,128)(2,1)}, u32[]{:S(2)}, u32[]{:S(2)}) collective-permute-start(bf16[320,768]{1,0:T(8,128)(2,1)} %get-tuple-element.176), channel_id=1, source_target_pairs={{0,2},{1,3},{2,4},{3,5},{4,6},{5,7},{6,0},{7,1},{8,10},{9,11},{10,... | collective-permute-start | bytes 1474568 | tf_op jit(solution)/shard_map/ppermute | solution.py:2008
  464.6 251.2 %collective-permute-start.5 = (bf16[320,768]{1,0:T(8,128)(2,1)}, bf16[320,768]{1,0:T(8,128)(2,1)}, u32[]{:S(2)}, u32[]{:S(2)}) collective-permute-start(bf16[320,768]{1,0:T(8,128)(2,1)} %get-tuple-element.175), channel_id=1, source_target_pairs={{0,4},{1,5},{2,6},{3,7},{4,0},{5,1},{6,2},{7,3},{8,12},{9,13},{10,... | collective-permute-start | bytes 1474568 | tf_op jit(solution)/shard_map/ppermute | solution.py:2008
  467.0 250.2 %collective-permute-start.6 = (bf16[320,768]{1,0:T(8,128)(2,1)}, bf16[320,768]{1,0:T(8,128)(2,1)}, u32[]{:S(2)}, u32[]{:S(2)}) collective-permute-start(bf16[320,768]{1,0:T(8,128)(2,1)} %get-tuple-element.174), channel_id=1, source_target_pairs={{0,6},{1,7},{2,0},{3,1},{4,2},{5,3},{6,4},{7,5},{8,14},{9,15},{10,... | collective-permute-start | bytes 1474568 | tf_op jit(solution)/shard_map/ppermute | solution.py:2008
  722.1 2.7 copy-start.2
  726.1 3.3 copy-start.4
  726.1 4.3 copy-start.5
  729.4 9.2 %slice-start.2 = ((s8[7864320]{0:T(1024)(128)(4,1)}), s8[4194304]{0:T(1024)(128)(4,1)S(1)}, s32[]{:S(2)}) async-start(s8[7864320]{0:T(1024)(128)(4,1)} %bitcast.98), calls=%async_computation.2 | async-start | bytes 8388608
  731.3 7.3 slice-start.3
  731.3 11.2 %slice-start = ((s8[7864320]{0:T(1024)(128)(4,1)}), s8[4194304]{0:T(1024)(128)(4,1)S(1)}, s32[]{:S(2)}) async-start(s8[7864320]{0:T(1024)(128)(4,1)} %bitcast.95), calls=%async_computation | async-start | bytes 8388608
  738.6 4.6 slice-start.1
  (1 other events, 1.1 us)

commit v6 on v5

--- a/solution.py
+++ b/solution.py
@@ -911,18 +911,20 @@
         scratch, sems = list(sems[:9]), list(sems[9:])
         pairs = lambda: (sems.pop(0), sems.pop(0))
         x_sems, g_sems, w_sems, small_sems, wo_sems, kv_sems = [pairs() for _ in range(6)]
-        map_sems, shared_sems, sum_sems, sum_sems_two = [pairs() for _ in range(4)]
+        map_sems, shared_sems, sum_sems, sum_sems_two, u_sems = [pairs() for _ in range(5)]
         local = sems.pop(0)
         net = Links(n_rows, n_cols)
         others = net.spread_partners()
         net.greet([device for _, _, device in others] + [net.twin])
-        by_place = lambda ref: lambda hops, core: ref.at[
-            pl.ds((net.place(hops) * 2 + core) * col_width, col_width), :
+        by_place = lambda ref, columns=slice(None): lambda hops, core: ref.at[
+            pl.ds((net.place(hops) * 2 + core) * col_width, col_width), columns
         ]
+        for_q, for_kv = pl.ds(0, q_width), pl.ds(q_width, 2 * HEAD_DIM)
 
         x_steps = gather_square(net, x_in, x, x_sems, local.at[0], 1)
         small_steps = gather_columns(net, small_in, by_place(small_all), small_sems, local.at[1])
-        w_steps = gather_columns(net, w_in, by_place(w), w_sems, local.at[2])
+        w_steps = gather_columns(net, w_in.at[:, for_q], by_place(w, for_q), w_sems, local.at[2])
+        u_steps = gather_columns(net, w_in.at[:, for_kv], by_place(w, for_kv), u_sems, local.at[18])
         wo_steps = gather_columns(net, wo_in, by_place(wo), wo_sems, local.at[3])
         g_steps = gather_square(net, g_in, g_out, g_sems, local.at[4], ring)
         saves = []
@@ -933,6 +935,7 @@
             saves.append(copy)
 
         next(small_steps)
+        next(u_steps)
         next(x_steps)
         next(w_steps)
         maps = []
@@ -941,11 +944,14 @@
         own_map = pltpu.make_async_copy(map_in, map_out.at[0, net.r], local.at[5])
         own_map.start()
         next(small_steps)
+        next(u_steps)
         next(w_steps)
         next(x_steps)
         next(g_steps)
         next(small_steps)
+        next(u_steps)
         next(small_steps)
+        next(u_steps)
         next(w_steps)
         run_together(x_steps, small_steps)
         save(x.at[0], x_out)
@@ -964,40 +970,37 @@
             scale_out[at, :] = jnp.broadcast_to(inverse, (64, 128))
 
         save(normed, normed_out)
-        next(wo_steps)
-        next(w_steps)
-        run_together(w_steps)
-        save(w, w_out)
-        next(g_steps)
-
-        projected[...] = matmul(normed[...], w[...])
-        next(wo_steps)
-
         def rotate(columns):
             values = projected[:, columns]
             turned = pltpu.roll(values, HEAD_DIM // 2, 1)
             return (values * cosine[...] + turned * sine[...]).astype(bf16)
 
-        for head in range(heads + 1):
-            columns = slice(head * HEAD_DIM, (head + 1) * HEAD_DIM)
-            if head < heads:
-                q[:, columns] = rotate(columns)
-            else:
-                kv[net.c, :, :HEAD_DIM] = rotate(columns)
+        run_together(u_steps)
+        projected[:, for_kv] = matmul(normed[...], w[:, for_kv])
+        kv[net.c, :, :HEAD_DIM] = rotate(slice(q_width, q_width + HEAD_DIM))
         kv[net.c, :, HEAD_DIM:] = projected[:, q_width + HEAD_DIM :].astype(bf16)
         kv_steps = gather_columns(
             net, kv.at[net.c], lambda hops, core: kv.at[2 * net.chip(hops) + core], kv_sems
         )
         next(kv_steps)
+        next(w_steps)
+        next(kv_steps)
+        run_together(w_steps)
+        save(w, w_out)
+        next(wo_steps)
         next(g_steps)
-        next(kv_steps)
-        next(wo_steps)
+        projected[:, for_q] = matmul(normed[...], w[:, for_q])
+        for head in range(heads):
+            columns = slice(head * HEAD_DIM, (head + 1) * HEAD_DIM)
+            q[:, columns] = rotate(columns)
         next(kv_steps)
         next(g_steps)
         next(kv_steps)
         next(wo_steps)
         run_together(kv_steps)
         save(kv, kv_out)
+        next(wo_steps)
+        next(g_steps)
 
         for head in range(heads):
             columns = slice(head * HEAD_DIM, (head + 1) * HEAD_DIM)
@@ -1026,7 +1029,11 @@
 
             out[:, columns] = (acc[...] / total[...]).T
             lse[head] = top[...] + jnp.log(total[...])
-            if head in (0, 3):
+            if head == 0:
+                next(g_steps)
+            if head == 2:
+                next(wo_steps)
+            if head == 3:
                 next(g_steps)
 
         run_together(wo_steps)
@@ -1131,7 +1138,8 @@
         + pair_sems(2 * ring)
         + pair_sems(7)
         + pair_sems(7)
-        + [pltpu.SemaphoreType.DMA((18,))],
+        + pair_sems(2 * ring)
+        + [pltpu.SemaphoreType.DMA((19,))],
         (block, grads, weights, small, weights_out, packed, slot_map, *tables),
         in_vmem=(7, 8),
         out_vmem=(4, 6, 7, 10, 14, 15),
@@ -1197,11 +1205,8 @@
                         sources[2].at[:, there], w_down.at[cols, here], w_sems.at[number + 2]
                     ),
                 ]
-        for copy in weights:
-            copy.start()
-
         scatter = SquareScatter(net, scratch, resident=True)
-        ring_copies, stores = [], {}
+        ring_copies, stores = {}, {}
         kept = {
             "slot": (slot_rows, slot_out), "part": (part, d_part_out), "act": (e_act, act_out),
             "d_gate": (d_gate, d_gate_out), "d_up": (d_up, d_up_out), "s_act": (s_act, s_act_out),
@@ -1227,16 +1232,15 @@
                 if s == 0:
                     add_slabs(result.at[at, :], terms)
                     continue
-                if turn and not p:
-                    ring_copies[turn - 1].wait_recv()
-                if turn > 1 and not p:
-                    net.settle([ring_copies[turn - 2]])
                 if turn:
+                    ring_copies[turn - 1, p].wait_recv()
                     terms = terms + [part_reader(landed.at[turn - 1, at, :])]
+                if turn > 1:
+                    net.settle([ring_copies[turn - 2, p]])
                 add_slabs(leaving.at[turn % 2, at, :], terms)
-            if s:
-                ring_copies.append(
-                    net.send(leaving.at[turn % 2], landed.at[turn], (ring_s, ring_r), turn, net.up)
+                ring_copies[turn, p] = net.send(
+                    leaving.at[turn % 2, at, :], landed.at[turn, at, :], (ring_s, ring_r),
+                    2 * turn + p, net.up,
                 )
 
         def in_lanes(column):
@@ -1284,6 +1288,9 @@
             if s == 0:
                 router_load.wait()
                 shared_load.wait()
+                g_load(0).wait()
+                for copy in weights:
+                    copy.start()
             logits = matmul(x[...], router[...])
             logits = jnp.where(chosen >= 0, logits, NEG_LARGE)
             logits = jnp.exp(logits - jnp.max(logits, -1, keepdims=True))
@@ -1293,7 +1300,8 @@
             slot_gate = jnp.sum(matmul(pick, in_lanes(my_gate)), -1, keepdims=True)
             s_gate = matmul(x[...], shared[:, :pad])
             s_up = matmul(x[...], shared[:, pad : 2 * pad])
-            g_load(s).wait()
+            if s:
+                g_load(s).wait()
             through = matmul(g[...], shared[:, 2 * pad :])
             s_silu, s_slope = silu_parts(s_gate)
             s_act[...] = (s_silu * s_up).astype(bf16)
@@ -1396,8 +1404,12 @@
             copies.append(net.send(d_gates, gate_out.at[mine], (ms, mr), number, device))
         scatter.second(3)
         pass_on(3)
-        ring_copies[-1].wait_recv()
-        add_slabs(result, [part_reader(result), part_reader(landed.at[ring - 2])])
+        for p in range(2):
+            at = pl.ds(p * (tokens // 2), tokens // 2)
+            ring_copies[ring - 2, p].wait_recv()
+            add_slabs(
+                result.at[at, :], [part_reader(result.at[at, :]), part_reader(landed.at[ring - 2, at, :])]
+            )
         stored(*kept)
         own.wait()
         gather.own.wait()
@@ -1446,7 +1458,7 @@
         ]
         + scatter_scratch(ring, tokens, width, resident=True)
         + [vmem((ring - 1, tokens, width), bf16), vmem((2, tokens, width), bf16)]
-        + pair_sems(ring - 1)
+        + pair_sems(2 * (ring - 1))
         + pair_sems(7 * ring)
         + pair_sems(experts - 1)
         + [
@@ -1479,10 +1491,10 @@
     shape = jax.ShapeDtypeStruct
 
     def kernel(
-        block, gates, probs, router, x_in, proj_in, g_in, gains, wo_in, w_in, q, kv, out, lse, cosine,
+        block, gates, probs_in, router, x_in, proj_in, g_in, gains, wo_in, w_in, q, kv, out, lse, cosine,
         sine, y_in, xr_in, dp_in, act_in, dg_in, du_in,
         d_proj, d_first, y_out, wo_out, d_resid, gain_out, xr_out, dp_out, act_out, dg_out, du_out,
-        second, proj, g, high_ref, low_ref,
+        second, proj, g, probs, high_ref, low_ref,
         wo, w, go, delta, dqt, dkv, dkv_own, wo_part, y_hold, y_landed, *rest,
     ):
         scratch, kv_parts, wo_parts = rest[:9], rest[9:16], rest[16:23]
@@ -1506,6 +1518,8 @@
             pltpu.make_async_copy(a, b, local.at[2 + i])
             for i, (a, b) in enumerate(((x_in, x), (proj_in, proj), (g_in.at[0], g)))
         ]
+        probs_load = pltpu.make_async_copy(probs_in.at[0], probs, local.at[6])
+        probs_load.start()
         for load in loads:
             load.start()
         wo_load = pltpu.make_async_copy(wo_in, wo, local.at[5])
@@ -1515,6 +1529,7 @@
         d_gates = jnp.concatenate(
             [gates[...].reshape(experts, length), jnp.zeros((128 - experts, length), f32)], 0
         ).T
+        probs_load.wait()
         d_logits = probs[...] * (d_gates - jnp.sum(probs[...] * d_gates, -1, keepdims=True))
         high = d_logits.astype(bf16)
         high_ref[...] = high
@@ -1666,6 +1681,7 @@
             vmem((1, length, model), bf16),
             vmem((length, model), bf16),
             vmem((length, model), bf16),
+            vmem((length, 128), f32),
             vmem((length, 128), bf16),
             vmem((length, 128), bf16),
             vmem((model, q_width), bf16),
@@ -1685,12 +1701,12 @@
         + pair_sems(7)
         + pair_sems(1)
         + pair_sems(5)
-        + [pltpu.SemaphoreType.DMA((6,))],
+        + [pltpu.SemaphoreType.DMA((7,))],
         (
             d_block, d_gates, probs, router, *token_rows, gains, weights_out, weights_in, queries, kv,
             heads_out, lse, *tables, parts, *expert_rows,
         ),
-        in_vmem=(1, 2, 3, 7, 10, 11, 12, 13, 14, 15),
+        in_vmem=(1, 3, 7, 10, 11, 12, 13, 14, 15),
         out_vmem=(0, 1, 2, 3, 4, 5),
     )
 
@@ -2175,7 +2191,7 @@
     )
     expert_rows = [joined(part) for part in (slot_rows, d_part, e_act, d_e_gate, d_e_up)]
     d_projected, d_first, part_sum, g_out, d_resid, gain_part, *twin_rows = attention_back(
-        n_rows, net.n_cols, d_block, index(d_gate_all, z, 1, False)[:, 0], gate_probs[0], small,
+        n_rows, net.n_cols, d_block, index(d_gate_all, z, 1, False)[:, 0], gate_probs, small,
         (token_input, attn_proj, grad_rows), gains, weights_out_t, weights_in, queries, kv_all,
         attn_f32, log_total, tables, out_rows, expert_rows,
     )

time: 757 us -> 733 us (0.968)
  Pallas kernels: 667 us -> 644 us
    pallas_call x4, Pallas kernels: 667 us -> 644 us  [remote_call(): pl.pallas_call(kernel, out_shape=out_shape, in_specs=[vmem if i in in_vme...]
  transfers between devices with their start and end apart: 7 -> 7, of which waited for: 1 -> 1; matrix products, arithmetic and copies ran while one was open for 3% -> 3% of each run, Pallas kernels for 61% -> 63%
where the time goes in v6:
time: 733 us; the launch traced here: 724 us
  Pallas kernels  644 us (88%)
  local copies, waits for them, and re-layouts  47.4 us (6%)
  matrix products  14.1 us (2%)
  other arithmetic  7.85 us (1%)
    pallas_call x4, Pallas kernels, remote_call(): pl.pallas_call(kernel, out_shape=out_shape, in_specs=[vmem if i in in_vme...  644 us
    unnamed x51, local copies, waits for them, and re-layouts  29.9 us
  transfers between devices with their start and end apart: 7, of which 1 were waited for; matrix products, arithmetic and copies ran while one was open for 3% of the time, Pallas kernels for 63%

profile of v6, /device:TPU:18, one launch (start us, length us, event | category | flops | bytes accessed | tf_op | source)
XLA Modules:
  0.0 723.8 jit_solution(5386830007813828930)
XLA Ops:
  10.2 1.4 fusion.8.packed_in
  11.6 216.9 %first_phase.1 = (bf16[512,2560]{1,0:T(8,128)(2,1)}, bf16[512,2560]{1,0:T(8,128)(2,1)}, bf16[2560,896]{1,0:T(8,128)(2,1)}, bf16[2560,128]{1,0:T(8,128)(2,1)}, bf...) custom-call(bf16[512,640]{1,0:T(8,128)(2,1)} %bitcast.117, ...), custom_call_target="tpu_custom_call" | custom-call | tf_op jit(solution)/shard_map/first_phase/pallas_call | solution.py:849
  228.6 190.7 %experts_phase.1 = (bf16[512,640]{1,0:T(8,128)(2,1)}, bf16[4,512,2560]{2,1,0:T(8,128)(2,1)}, bf16[4,512,2560]{2,1,0:T(8,128)(2,1)}, bf16[4,256,2560]{2,1,0:T(8,1...) custom-call(bf16[512,2560]{1,0:T(8,128)(2,1)} %get-tuple-element.62., ...), custom_call_target="tpu_custom_call" | custom-call | tf_op jit(solution)/shard_map/experts_phase/pallas_call | solution.py:849
  419.3 7.3 %fusion.5 = bf16[2560,256]{1,0:T(8,128)(2,1)S(1)} fusion(bf16[4,512,2560]{2,1,0:T(8,128)(2,1)} %get-tuple-element.63.g_in, bf16[4,512,256]{2,1,0:T(8,128)(2,1)} %get-tuple-element.105), kind=kOutput, calls=%fused_computation.16 | convolution fusion | flops 2685009920 | bytes 12845056 | tf_op jit(solution)/shard_map/dot_general | solution.py:42
  427.1 6.0 bitcast_convert_fusion
  433.1 1.4 fusion.10
  434.5 4.3 collective-permute-done.3
  438.8 2.1 fusion
  442.3 2.6 collective-permute-start.5
  444.9 1.6 collective-permute-start.6
  447.9 126.3 %attention_back.1 = (bf16[512,896]{1,0:T(8,128)(2,1)}, bf16[512,2560]{1,0:T(8,128)(2,1)}, bf16[3,512,640]{2,1,0:T(8,128)(2,1)}, f32[320,640]{1,0:T(8,128)}, f32[...) custom-call(bf16[512,640]{1,0:T(8,128)(2,1)} %get-tuple-element.67.b, ...), custom_call_target="tpu_custom_call" | custom-call | tf_op jit(solution)/shard_map/attention_back/pallas_call | solution.py:849
  574.2 109.8 %last_phase.1 = (bf16[512,640]{1,0:T(8,128)(2,1)}, f32[512,640]{1,0:T(8,128)}, f32[8,640]{1,0:T(8,128)}, f32[320,896]{1,0:T(8,128)}, f32[320,128]{1,0:T(8,128)},...) custom-call(bf16[2,256,2560]{2,1,0:T(8,128)(2,1)} %bitcast.111, ...), custom_call_target="tpu_custom_call" | custom-call | tf_op jit(solution)/shard_map/last_phase/pallas_call | solution.py:849
  684.0 2.1 slice.34
  686.9 1.6 copy.96
  689.2 1.7 fusion.23
  691.6 1.3 copy.93
  692.9 1.3 copy.94
  694.3 2.1 copy.95
  697.5 1.7 fusion.22
  699.2 2.7 copy.97
  704.5 2.0 copy.121
  708.4 7.3 %copy.124 = f32[1,2560,768]{2,1,0:T(8,128)} copy(f32[1,2560,768]{2,1,0:T(8,128)} %bitcast.99) | data formatting | bytes 15728640
  715.7 3.9 copy.125
  720.3 3.2 copy.126
  (85 shorter events, 21.2 us)
Async XLA Ops:
  0.6 2.3 copy-start.6
  0.7 2.9 copy-start.7
  0.7 227.9 %collective-permute-start = (bf16[2560,768]{1,0:T(8,128)(2,1)}, bf16[2560,768]{1,0:T(8,128)(2,1)}, u32[]{:S(2)}, u32[]{:S(2)}) collective-permute-start(bf16[2560,768]{1,0:T(8,128)(2,1)} %bitcast.105), channel_id=1, source_target_pairs={{0,1},{1,0},{2,3},{3,2},{4,5},{5,4},{6,7},{7,6},{8,9},{9,8},{10,11... | collective-permute-start | bytes 11796488 | tf_op jit(solution)/shard_map/ppermute | solution.py:2024
  0.8 227.8 %collective-permute-start.1 = (bf16[2560,768]{1,0:T(8,128)(2,1)}, bf16[2560,768]{1,0:T(8,128)(2,1)}, u32[]{:S(2)}, u32[]{:S(2)}) collective-permute-start(bf16[2560,768]{1,0:T(8,128)(2,1)} %bitcast.107), channel_id=1, source_target_pairs={{0,1},{1,0},{2,3},{3,2},{4,5},{5,4},{6,7},{7,6},{8,9},{9,8},{10,11... | collective-permute-start | bytes 11796488 | tf_op jit(solution)/shard_map/ppermute | solution.py:2024
  1.2 227.3 %collective-permute-start.2 = (bf16[768,2560]{1,0:T(8,128)(2,1)}, bf16[768,2560]{1,0:T(8,128)(2,1)}, u32[]{:S(2)}, u32[]{:S(2)}) collective-permute-start(bf16[768,2560]{1,0:T(8,128)(2,1)} %bitcast.109), channel_id=1, source_target_pairs={{0,1},{1,0},{2,3},{3,2},{4,5},{5,4},{6,7},{7,6},{8,9},{9,8},{10,11... | collective-permute-start | bytes 11796488 | tf_op jit(solution)/shard_map/ppermute | solution.py:2024
  3.0 2.6 copy-start.11
  3.0 2.8 copy-start.12
  3.6 4.9 copy-start.8
  3.6 4.9 copy-start.9
  3.9 4.5 copy-start.10
  419.2 7.3 %copy-start = (bf16[4,512,2560]{2,1,0:T(8,128)(2,1)S(1)}, bf16[4,512,2560]{2,1,0:T(8,128)(2,1)}, u32[]{:S(2)}) copy-start(bf16[4,512,2560]{2,1,0:T(8,128)(2,1)} %get-tuple-element.97.rows_in) | copy-start | bytes 31457284
  419.3 7.8 %copy-start.13 = (bf16[4,512,512]{2,1,0:T(8,128)(2,1)S(1)}, bf16[4,512,512]{2,1,0:T(8,128)(2,1)}, u32[]{:S(2)}) copy-start(bf16[4,512,512]{2,1,0:T(8,128)(2,1)} %get-tuple-element.104) | copy-start | bytes 6291460
  426.6 6.5 copy-start.1
  434.5 4.3 collective-permute-start.3
  442.1 249.5 %collective-permute-start.4 = (bf16[320,768]{1,0:T(8,128)(2,1)}, bf16[320,768]{1,0:T(8,128)(2,1)}, u32[]{:S(2)}, u32[]{:S(2)}) collective-permute-start(bf16[320,768]{1,0:T(8,128)(2,1)} %get-tuple-element.176), channel_id=1, source_target_pairs={{0,2},{1,3},{2,4},{3,5},{4,6},{5,7},{6,0},{7,1},{8,10},{9,11},{10,... | collective-permute-start | bytes 1474568 | tf_op jit(solution)/shard_map/ppermute | solution.py:2024
  442.3 250.6 %collective-permute-start.5 = (bf16[320,768]{1,0:T(8,128)(2,1)}, bf16[320,768]{1,0:T(8,128)(2,1)}, u32[]{:S(2)}, u32[]{:S(2)}) collective-permute-start(bf16[320,768]{1,0:T(8,128)(2,1)} %get-tuple-element.175), channel_id=1, source_target_pairs={{0,4},{1,5},{2,6},{3,7},{4,0},{5,1},{6,2},{7,3},{8,12},{9,13},{10,... | collective-permute-start | bytes 1474568 | tf_op jit(solution)/shard_map/ppermute | solution.py:2024
  444.9 249.4 %collective-permute-start.6 = (bf16[320,768]{1,0:T(8,128)(2,1)}, bf16[320,768]{1,0:T(8,128)(2,1)}, u32[]{:S(2)}, u32[]{:S(2)}) collective-permute-start(bf16[320,768]{1,0:T(8,128)(2,1)} %get-tuple-element.174), channel_id=1, source_target_pairs={{0,6},{1,7},{2,0},{3,1},{4,2},{5,3},{6,4},{7,5},{8,14},{9,15},{10,... | collective-permute-start | bytes 1474568 | tf_op jit(solution)/shard_map/ppermute | solution.py:2024
  699.2 2.7 copy-start.2
  703.2 3.3 copy-start.4
  703.2 4.3 copy-start.5
  706.5 9.2 %slice-start.2 = ((s8[7864320]{0:T(1024)(128)(4,1)}), s8[4194304]{0:T(1024)(128)(4,1)S(1)}, s32[]{:S(2)}) async-start(s8[7864320]{0:T(1024)(128)(4,1)} %bitcast.96), calls=%async_computation.2 | async-start | bytes 8388608
  708.4 7.3 %slice-start.3 = ((s8[7864320]{0:T(1024)(128)(4,1)}), s8[3670016]{0:T(1024)(128)(4,1)S(1)}, s32[]{:S(2)}) async-start(s8[7864320]{0:T(1024)(128)(4,1)} %bitcast.96), calls=%async_computation.3 | async-start | bytes 7340032
  708.4 11.2 %slice-start = ((s8[7864320]{0:T(1024)(128)(4,1)}), s8[4194304]{0:T(1024)(128)(4,1)S(1)}, s32[]{:S(2)}) async-start(s8[7864320]{0:T(1024)(128)(4,1)} %bitcast.93), calls=%async_computation | async-start | bytes 8388608
  715.7 4.6 slice-start.1
  (1 other events, 1.1 us)

commit v7 on v6

--- a/solution.py
+++ b/solution.py
@@ -1361,9 +1361,9 @@
                 ).astype(bf16)
 
             pl.loop(2, 5)(out_tile)
+            tick("right")
             scatter.give(s, d_chunk, 3)
             scatter.give(s, d_chunk, 2)
-            tick("right")
             pl.loop(0, 2)(out_tile)
             scatter.give(s, d_chunk, 1)
             store(s, "y")
@@ -1386,7 +1386,7 @@
         pass_x = lambda s: lambda: gather.forward(s)
         second_of = lambda s: lambda: scatter.second(s)
         third_of = lambda s: lambda: pass_on(s)
-        compute(0, {"hidden": [arrive(1)], "left": [pass_x(1), arrive(2), take(1)]})
+        compute(0, {"hidden": [arrive(1)], "right": [pass_x(1)], "left": [arrive(2), take(1)]})
         compute(
             1,
             {

time: 733 us -> 735 us (level)
  transfers between devices with their start and end apart: 7 -> 7, of which waited for: 1 -> 1; matrix products, arithmetic and copies ran while one was open for 3% -> 3% of each run, Pallas kernels for 63% -> 62%
where the time goes in v7:
time: 735 us; the launch traced here: 722 us
  Pallas kernels  640 us (87%)
  local copies, waits for them, and re-layouts  47.4 us (6%)
  matrix products  14.1 us (2%)
  other arithmetic  7.85 us (1%)
    pallas_call x4, Pallas kernels, remote_call(): pl.pallas_call(kernel, out_shape=out_shape, in_specs=[vmem if i in in_vme...  640 us
    unnamed x51, local copies, waits for them, and re-layouts  29.9 us
  transfers between devices with their start and end apart: 7, of which 1 were waited for; matrix products, arithmetic and copies ran while one was open for 3% of the time, Pallas kernels for 62%

profile of v7, /device:TPU:18, one launch (start us, length us, event | category | flops | bytes accessed | tf_op | source)
XLA Modules:
  0.0 722.1 jit_solution(6227708358194910819)
XLA Ops:
  10.2 1.4 fusion.8.packed_in
  11.6 216.9 %first_phase.1 = (bf16[512,2560]{1,0:T(8,128)(2,1)}, bf16[512,2560]{1,0:T(8,128)(2,1)}, bf16[2560,896]{1,0:T(8,128)(2,1)}, bf16[2560,128]{1,0:T(8,128)(2,1)}, bf...) custom-call(bf16[512,640]{1,0:T(8,128)(2,1)} %bitcast.117, ...), custom_call_target="tpu_custom_call" | custom-call | tf_op jit(solution)/shard_map/first_phase/pallas_call | solution.py:849
  228.6 190.1 %experts_phase.1 = (bf16[512,640]{1,0:T(8,128)(2,1)}, bf16[4,512,2560]{2,1,0:T(8,128)(2,1)}, bf16[4,512,2560]{2,1,0:T(8,128)(2,1)}, bf16[4,256,2560]{2,1,0:T(8,1...) custom-call(bf16[512,2560]{1,0:T(8,128)(2,1)} %get-tuple-element.62., ...), custom_call_target="tpu_custom_call" | custom-call | tf_op jit(solution)/shard_map/experts_phase/pallas_call | solution.py:849
  418.7 7.3 %fusion.5 = bf16[2560,256]{1,0:T(8,128)(2,1)S(1)} fusion(bf16[4,512,2560]{2,1,0:T(8,128)(2,1)} %get-tuple-element.63.g_in, bf16[4,512,256]{2,1,0:T(8,128)(2,1)} %get-tuple-element.105), kind=kOutput, calls=%fused_computation.16 | convolution fusion | flops 2685009920 | bytes 12845056 | tf_op jit(solution)/shard_map/dot_general | solution.py:42
  426.5 5.9 bitcast_convert_fusion
  432.5 1.4 fusion.10
  433.9 4.3 collective-permute-done.3
  438.2 2.1 fusion
  442.5 2.3 collective-permute-start.5
  444.8 2.9 collective-permute-start.6
  449.1 125.5 %attention_back.1 = (bf16[512,896]{1,0:T(8,128)(2,1)}, bf16[512,2560]{1,0:T(8,128)(2,1)}, bf16[3,512,640]{2,1,0:T(8,128)(2,1)}, f32[320,640]{1,0:T(8,128)}, f32[...) custom-call(bf16[512,640]{1,0:T(8,128)(2,1)} %get-tuple-element.67.b, ...), custom_call_target="tpu_custom_call" | custom-call | tf_op jit(solution)/shard_map/attention_back/pallas_call | solution.py:849
  574.6 107.8 %last_phase.1 = (bf16[512,640]{1,0:T(8,128)(2,1)}, f32[512,640]{1,0:T(8,128)}, f32[8,640]{1,0:T(8,128)}, f32[320,896]{1,0:T(8,128)}, f32[320,128]{1,0:T(8,128)},...) custom-call(bf16[2,256,2560]{2,1,0:T(8,128)(2,1)} %bitcast.111, ...), custom_call_target="tpu_custom_call" | custom-call | tf_op jit(solution)/shard_map/last_phase/pallas_call | solution.py:849
  682.4 2.1 slice.34
  685.3 1.6 copy.96
  687.5 1.7 fusion.23
  689.9 1.3 copy.93
  691.2 1.3 copy.94
  692.6 2.1 copy.95
  695.8 1.7 fusion.22
  697.5 2.7 copy.97
  702.8 2.0 copy.121
  706.8 7.3 %copy.124 = f32[1,2560,768]{2,1,0:T(8,128)} copy(f32[1,2560,768]{2,1,0:T(8,128)} %bitcast.99) | data formatting | bytes 15728640
  714.0 3.9 copy.125
  718.6 3.2 copy.126
  (85 shorter events, 21.9 us)
Async XLA Ops:
  0.6 2.3 copy-start.6
  0.7 2.9 copy-start.7
  0.7 227.9 %collective-permute-start = (bf16[2560,768]{1,0:T(8,128)(2,1)}, bf16[2560,768]{1,0:T(8,128)(2,1)}, u32[]{:S(2)}, u32[]{:S(2)}) collective-permute-start(bf16[2560,768]{1,0:T(8,128)(2,1)} %bitcast.105), channel_id=1, source_target_pairs={{0,1},{1,0},{2,3},{3,2},{4,5},{5,4},{6,7},{7,6},{8,9},{9,8},{10,11... | collective-permute-start | bytes 11796488 | tf_op jit(solution)/shard_map/ppermute | solution.py:2024
  0.8 227.8 %collective-permute-start.1 = (bf16[2560,768]{1,0:T(8,128)(2,1)}, bf16[2560,768]{1,0:T(8,128)(2,1)}, u32[]{:S(2)}, u32[]{:S(2)}) collective-permute-start(bf16[2560,768]{1,0:T(8,128)(2,1)} %bitcast.107), channel_id=1, source_target_pairs={{0,1},{1,0},{2,3},{3,2},{4,5},{5,4},{6,7},{7,6},{8,9},{9,8},{10,11... | collective-permute-start | bytes 11796488 | tf_op jit(solution)/shard_map/ppermute | solution.py:2024
  1.2 227.3 %collective-permute-start.2 = (bf16[768,2560]{1,0:T(8,128)(2,1)}, bf16[768,2560]{1,0:T(8,128)(2,1)}, u32[]{:S(2)}, u32[]{:S(2)}) collective-permute-start(bf16[768,2560]{1,0:T(8,128)(2,1)} %bitcast.109), channel_id=1, source_target_pairs={{0,1},{1,0},{2,3},{3,2},{4,5},{5,4},{6,7},{7,6},{8,9},{9,8},{10,11... | collective-permute-start | bytes 11796488 | tf_op jit(solution)/shard_map/ppermute | solution.py:2024
  3.0 2.6 copy-start.11
  3.0 2.8 copy-start.12
  3.6 4.9 copy-start.8
  3.6 4.9 copy-start.9
  3.9 4.5 copy-start.10
  418.7 7.3 %copy-start = (bf16[4,512,2560]{2,1,0:T(8,128)(2,1)S(1)}, bf16[4,512,2560]{2,1,0:T(8,128)(2,1)}, u32[]{:S(2)}) copy-start(bf16[4,512,2560]{2,1,0:T(8,128)(2,1)} %get-tuple-element.97.rows_in) | copy-start | bytes 31457284
  418.7 7.8 %copy-start.13 = (bf16[4,512,512]{2,1,0:T(8,128)(2,1)S(1)}, bf16[4,512,512]{2,1,0:T(8,128)(2,1)}, u32[]{:S(2)}) copy-start(bf16[4,512,512]{2,1,0:T(8,128)(2,1)} %get-tuple-element.104) | copy-start | bytes 6291460
  426.0 6.5 copy-start.1
  433.9 4.3 collective-permute-start.3
  441.5 248.4 %collective-permute-start.4 = (bf16[320,768]{1,0:T(8,128)(2,1)}, bf16[320,768]{1,0:T(8,128)(2,1)}, u32[]{:S(2)}, u32[]{:S(2)}) collective-permute-start(bf16[320,768]{1,0:T(8,128)(2,1)} %get-tuple-element.176), channel_id=1, source_target_pairs={{0,2},{1,3},{2,4},{3,5},{4,6},{5,7},{6,0},{7,1},{8,10},{9,11},{10,... | collective-permute-start | bytes 1474568 | tf_op jit(solution)/shard_map/ppermute | solution.py:2024
  442.5 248.8 %collective-permute-start.5 = (bf16[320,768]{1,0:T(8,128)(2,1)}, bf16[320,768]{1,0:T(8,128)(2,1)}, u32[]{:S(2)}, u32[]{:S(2)}) collective-permute-start(bf16[320,768]{1,0:T(8,128)(2,1)} %get-tuple-element.175), channel_id=1, source_target_pairs={{0,4},{1,5},{2,6},{3,7},{4,0},{5,1},{6,2},{7,3},{8,12},{9,13},{10,... | collective-permute-start | bytes 1474568 | tf_op jit(solution)/shard_map/ppermute | solution.py:2024
  444.8 247.8 %collective-permute-start.6 = (bf16[320,768]{1,0:T(8,128)(2,1)}, bf16[320,768]{1,0:T(8,128)(2,1)}, u32[]{:S(2)}, u32[]{:S(2)}) collective-permute-start(bf16[320,768]{1,0:T(8,128)(2,1)} %get-tuple-element.174), channel_id=1, source_target_pairs={{0,6},{1,7},{2,0},{3,1},{4,2},{5,3},{6,4},{7,5},{8,14},{9,15},{10,... | collective-permute-start | bytes 1474568 | tf_op jit(solution)/shard_map/ppermute | solution.py:2024
  697.5 2.7 copy-start.2
  701.5 3.3 copy-start.4
  701.5 4.3 copy-start.5
  704.8 9.2 %slice-start.2 = ((s8[7864320]{0:T(1024)(128)(4,1)}), s8[4194304]{0:T(1024)(128)(4,1)S(1)}, s32[]{:S(2)}) async-start(s8[7864320]{0:T(1024)(128)(4,1)} %bitcast.96), calls=%async_computation.2 | async-start | bytes 8388608
  706.7 7.3 %slice-start.3 = ((s8[7864320]{0:T(1024)(128)(4,1)}), s8[3670016]{0:T(1024)(128)(4,1)S(1)}, s32[]{:S(2)}) async-start(s8[7864320]{0:T(1024)(128)(4,1)} %bitcast.96), calls=%async_computation.3 | async-start | bytes 7340032
  706.7 11.2 %slice-start = ((s8[7864320]{0:T(1024)(128)(4,1)}), s8[4194304]{0:T(1024)(128)(4,1)S(1)}, s32[]{:S(2)}) async-start(s8[7864320]{0:T(1024)(128)(4,1)} %bitcast.93), calls=%async_computation | async-start | bytes 8388608
  714.0 4.6 slice-start.1
  (1 other events, 1.1 us)
